TPU v7x, 128 devices: a whole 4x4x4 slice. The times are simulated.
128 devices in a mesh: row: 8 (over x, z_hi), col: 16 (over y, z_lo, core).
Axes of the slice: x: 4, y: 4, z: 4 (z_hi: 2, z_lo: 2; z = z_hi * 2 + z_lo), core: 2. Of those that a mesh axis runs over, the one named last changes fastest.
Arguments:
- tokens: bfloat16 [512, 16384], P(('row', 'col')), may hold values from -6 to 6
- gate_weight: bfloat16 [16384, 26624], P('col', 'row'), may hold values from -0.046875 to 0.046875
- up_weight: bfloat16 [16384, 26624], P('col', 'row'), may hold values from -0.046875 to 0.046875
- down_weight: bfloat16 [26624, 16384], P('row', 'col'), may hold values from -0.0390625 to 0.0390625
Outputs:
- mixed: bfloat16 [512, 16384], P('row', 'col')
All inputs are finite; a program needn't handle non-finite values.
Results may differ from a plain program's by a relative error of at most 0.005.
Values may be sent and summed in bfloat16 or wider, within the bound.
No kernel may reach another device: no remote copies, remote signals or barrier semaphores. Data moves between devices by JAX's collectives and lax.ppermute only.
A program may use at most 128 MiB of HBM per device.

v0:
```python
import jax
import jax.numpy as jnp
from jax import lax
from jax.sharding import PartitionSpec as P


def per_device(tokens, gate_weight, up_weight, down_weight):
    split_rows = lax.all_to_all(tokens, "col", split_axis=1, concat_axis=0, tiled=True)
    features = lax.all_gather(split_rows, "row", axis=0, tiled=True)
    hidden_width = gate_weight.shape[1]
    selected = features
    gate_term = jnp.dot(selected, gate_weight, preferred_element_type=jnp.float32)
    up_term = jnp.dot(selected, up_weight, preferred_element_type=jnp.float32)
    combined = lax.psum_scatter(
        jnp.concatenate((gate_term, up_term), axis=1), "col", scatter_dimension=0, tiled=True
    )
    hidden = (jax.nn.silu(combined[:, :hidden_width]) * combined[:, hidden_width:]).astype(
        jnp.bfloat16
    )
    hidden_all = lax.all_gather(hidden, "col", axis=0, tiled=True)
    selected = hidden_all
    mixed = lax.psum_scatter(
        jnp.dot(selected, down_weight, preferred_element_type=jnp.float32),
        "row",
        scatter_dimension=0,
        tiled=True,
    )
    return mixed.astype(jnp.bfloat16)


def solution(mesh):
    placed = (P(("row", "col"), None), P("col", "row"), P("col", "row"), P("row", "col"))
    return jax.shard_map(
        per_device, mesh=mesh, in_specs=placed, out_specs=P("row", "col"), check_vma=False
    )
```

profile of v0, /device:TPU:1, one launch (start us, length us, event | category | flops | bytes accessed | tf_op | source)
XLA Modules:
  0.0 364.6 jit_solution(6556024873480419130)
XLA Ops:
  6.5 0.0 all-gather.3.cloned.1.call-start
  6.5 13.5 %all_to_all.19 = bf16[4,16,1024]{2,0,1:T(4,128)(2,1)S(1)} all-to-all(bf16[4,16,1024]{2,0,1:T(4,128)(2,1)} %bitcast.9), channel_id=1, replica_groups=mesh['row'=8,'col'=16] {'col'}, dimensions={1} | all-to-all | bytes 262144 | tf_op jit(solution)/shard_map/all_to_all | solution.py:8
  20.0 0.7 all_to_all.17
  20.7 0.0 all-gather.3.cloned.1.call-update
  20.8 0.0 reduce-scatter.3.cloned.1.call-start
  20.8 46.2 %all-gather.3.cloned.1.call-done = bf16[512,1024]{1,0:T(8,128)(2,1)} async-done(((bf16[64,1024]{1,0:T(8,128)(2,1)}), bf16[512,1024]{1,0:T(8,128)(2,1)}) %all-gather.3.cloned.1.call-update) | async-done | bytes 1048592 | tf_op jit(solution)/shard_map/all_gather | solution.py:9
  67.0 0.0 copy-start
  67.0 7.3 %fusion.2 = f32[512,3328]{1,0:T(8,128)S(1)} fusion(bf16[512,1024]{1,0:T(8,128)(2,1)} %all-gather.3.cloned.1.call-done, bf16[1024,3328]{1,0:T(8,128)(2,1)} %param.6), kind=kOutput, calls=%fused_computation.4 | convolution fusion | flops 3489660928 | bytes 14680064 | tf_op jit(solution)/shard_map/dot_general | solution.py:13
  74.3 0.0 copy-done
  74.3 6.1 %fusion.1 = f32[512,3328]{1,0:T(8,128)S(1)} fusion(bf16[512,1024]{1,0:T(8,128)(2,1)S(1)} %copy-done, bf16[1024,3328]{1,0:T(8,128)(2,1)} %param.5), kind=kOutput, calls=%fused_computation.3 | convolution fusion | flops 3489660928 | bytes 14680064 | tf_op jit(solution)/shard_map/dot_general | solution.py:12
  80.5 5.5 %pad_maximum_fusion = f32[512,6656]{1,0:T(8,128)} fusion(f32[512,3328]{1,0:T(8,128)S(1)} %fusion.2, f32[512,3328]{1,0:T(8,128)S(1)} %fusion.1), kind=kLoop, calls=%fused_computation | loop fusion | flops 3407872 | bytes 27262976 | tf_op jit(solution)/shard_map/concatenate | solution.py:15
  85.9 0.0 reduce-scatter.3.cloned.1.call-update
  86.0 0.0 all-gather.5.cloned.1.call-start
  86.0 149.8 %reduce-scatter.3.cloned.1.call-done = f32[32,6656]{1,0:T(8,128)} async-done(((f32[512,6656]{1,0:T(8,128)}), f32[32,6656]{1,0:T(8,128)}) %reduce-scatter.3.cloned.1.call-update) | async-done | bytes 851984 | tf_op jit(solution)/shard_map/reduce_scatter | solution.py:14
  235.8 1.9 fusion
  237.8 0.0 all-gather.5.cloned.1.call-update
  237.8 0.0 reduce-scatter.5.cloned.1.call-start
  237.8 36.0 %all-gather.5.cloned.1.call-done = bf16[512,3328]{1,0:T(8,128)(2,1)} async-done(((bf16[32,3328]{1,0:T(8,128)(2,1)}), bf16[512,3328]{1,0:T(8,128)(2,1)}) %all-gather.5.cloned.1.call-update) | async-done | bytes 3407888 | tf_op jit(solution)/shard_map/all_gather | solution.py:20
  273.8 9.0 %fusion.3 = f32[512,1024]{1,0:T(8,128)} fusion(bf16[512,3328]{1,0:T(8,128)(2,1)} %all-gather.5.cloned.1.call-done, bf16[3328,1024]{1,0:T(8,128)(2,1)} %param.7), kind=kOutput, calls=%fused_computation.5 | convolution fusion | flops 3489660928 | bytes 12320768 | tf_op jit(solution)/shard_map/dot_general | solution.py:23
  282.8 0.0 reduce-scatter.5.cloned.1.call-update
  282.9 73.6 %reduce-scatter.5.cloned.1.call-done = f32[64,1024]{1,0:T(8,128)} async-done(((f32[512,1024]{1,0:T(8,128)}), f32[64,1024]{1,0:T(8,128)}) %reduce-scatter.5.cloned.1.call-update) | async-done | bytes 262160 | tf_op jit(solution)/shard_map/reduce_scatter | solution.py:22
  356.5 1.6 convert_element_type.7
Async XLA Ops:
  6.5 60.5 %all-gather.3.cloned.1.call-start = ((), (), s32[]{:S(2)}) async-start(), calls=%async_computation.3 | async-start | bytes 1179648 | tf_op jit(solution)/shard_map/all_gather | solution.py:9
  20.8 215.1 %reduce-scatter.3.cloned.1.call-start = ((), (), s32[]{:S(2)}) async-start(), calls=%async_computation.4 | async-start | bytes 14483456 | tf_op jit(solution)/shard_map/reduce_scatter | solution.py:14
  67.0 7.3 %copy-start = (bf16[512,1024]{1,0:T(8,128)(2,1)S(1)}, bf16[512,1024]{1,0:T(8,128)(2,1)}, u32[]{:S(2)}) copy-start(bf16[512,1024]{1,0:T(8,128)(2,1)} %all-gather.3.cloned.1.call-done) | copy-start | bytes 3145732
  86.0 187.9 %all-gather.5.cloned.1.call-start = ((), (), s32[]{:S(2)}) async-start(), calls=%async_computation.5 | async-start | bytes 3620864 | tf_op jit(solution)/shard_map/all_gather | solution.py:20
  237.8 118.7 %reduce-scatter.5.cloned.1.call-start = ((), (), s32[]{:S(2)}) async-start(), calls=%async_computation.6 | async-start | bytes 2359296 | tf_op jit(solution)/shard_map/reduce_scatter | solution.py:22
Sparse Core Ops, SparseCore 0:
  20.9 46.1 all-gather.2
  86.1 149.6 reduce-scatter.2
  237.9 35.8 all-gather.4
  283.0 73.4 reduce-scatter.4
where the time goes:
time: 366 us; the launch traced here: 365 us
  waiting for transfers between devices  306 us (84%)
  matrix products  22.4 us (6%)
  blocking collectives  13.5 us (4%)
  between operations  13.2 us (4%)
  other arithmetic  9.02 us (2%)
    reduce_scatter x1, waiting for transfers between devices, per_device(): lax.psum_scatter(jnp.concatenate((gate_term, up_term), axis=1), 'col', sc...  150 us
    reduce_scatter x1, waiting for transfers between devices, per_device(): lax.psum_scatter(jnp.dot(selected, down_weight, preferred_element_type=jn...  73.6 us
    all_gather x1, waiting for transfers between devices, per_device(): features = lax.all_gather(split_rows, 'row', axis=0, tiled=True)  46.2 us
    all_gather x1, waiting for transfers between devices, per_device(): hidden_all = lax.all_gather(hidden, 'col', axis=0, tiled=True)  36 us
    all_to_all x1, blocking collectives, per_device(): lax.all_to_all(tokens, 'col', split_axis=1, concat_axis=0, tiled=True)  13.5 us
    dot_general x1, matrix products, per_device(): jnp.dot(selected, down_weight, preferred_element_type=jnp.float32)  9.01 us
  transfers between devices with their start and end apart: 4, of which 4 were waited for; matrix products, arithmetic and copies ran while one was open for 0% of the time, Pallas kernels for 0%

commit v1 on v0

v1 whole, which is shorter than its diff:
```python
import jax
import jax.numpy as jnp
from jax import lax
from jax.sharding import PartitionSpec as P

F32, BF16, F16 = jnp.float32, jnp.bfloat16, jnp.float16
LIFT = 8.0
CHUNKS = ((2, 1), (3, 0))


def along(axis, size, move):
    pairs = [(i, move(i)) for i in range(size)]
    return lambda v: lax.ppermute(v, axis, pairs)


def lifted(v):
    return (v * LIFT).astype(F16)


def lowered(v):
    return v.astype(F32) * (1 / LIFT)


def per_device(tokens, gate_weight, up_weight, down_weight):
    row, col = lax.axis_index("row"), lax.axis_index("col")
    z_hi, x = row % 2, row // 2
    core, z_lo, y = col % 2, (col // 2) % 2, col // 4
    to_core = along("col", 16, lambda c: c ^ 1)
    to_z = along("col", 16, lambda c: c ^ 2)
    y_up = along("col", 16, lambda c: (c + 4) % 16)
    y_down = along("col", 16, lambda c: (c + 12) % 16)

    features = tokens.shape[1] // 16
    blocks = tokens.reshape(4, 16, features).transpose(1, 0, 2).reshape(1, 64, features)
    blocks = jnp.broadcast_to(blocks, (8, 64, features)).reshape(512, features)
    every = lax.all_to_all(blocks, ("row", "col"), split_axis=0, concat_axis=0, tiled=True)
    every = every.reshape(4, 2, 4, 16, features)

    def tokens_of(j, half):
        block = lax.dynamic_slice(
            every, ((x + j) % 4, half, 0, 0, 0), (1, 1, 4, 16, features)
        ).reshape(4, 16, features)
        doubled = jnp.concatenate((block, block), axis=0)
        return lax.dynamic_slice_in_dim(doubled, y, 4, 0)

    half_hidden = gate_weight.shape[1] // 2
    arrived = []
    for chunk in CHUNKS:
        n = 16 * len(chunk)

        def rows_of(half):
            parts = [tokens_of(j, half) for j in chunk]
            return jnp.stack(parts, axis=1).reshape(4 * n, features)

        away, kept = rows_of(1 - core), rows_of(core)

        def project(weight):
            sent = to_core(lifted(jnp.dot(away, weight, preferred_element_type=F32)))
            return jnp.dot(kept, weight, preferred_element_type=F32) + lowered(sent)

        gate, up = project(gate_weight), project(up_weight)
        g = [gate[n * k : n * (k + 1)] for k in range(4)]
        u = [up[n * k : n * (k + 1)] for k in range(4)]
        first_up = y_up(jnp.stack((lifted(g[2]), lifted(u[1]))))
        first_down = y_down(jnp.stack((lifted(u[2]), lifted(g[3]))))
        second_up = y_up(lifted(g[1] + lowered(first_up[0])))
        second_down = y_down(lifted(u[3] + lowered(first_down[0])))
        gate = g[0] + lowered(first_down[1]) + lowered(second_up)
        up = u[0] + lowered(first_up[1]) + lowered(second_down)
        both = jnp.stack((gate, up))
        lo, hi = both[:, :, :half_hidden], both[:, :, half_hidden:]
        beside = to_z(lifted(jnp.where(z_lo == 0, hi, lo)))
        total = jnp.where(z_lo == 0, lo, hi) + lowered(beside)
        hidden = (jax.nn.silu(total[0]) * total[1]).astype(BF16)
        beside = to_z(hidden)
        hidden = jnp.concatenate(
            (jnp.where(z_lo == 0, hidden, beside), jnp.where(z_lo == 0, beside, hidden)), axis=1
        )
        from_below, from_above = y_up(hidden), y_down(hidden)
        far_lo = y_up(from_below[:, :half_hidden])
        far_hi = y_down(from_above[:, half_hidden:])
        far = jnp.concatenate((far_lo, far_hi), axis=1)
        kept = jnp.concatenate((hidden, from_above, far, from_below), axis=0)
        away = to_core(kept)

        def down(rows):
            mixed = jnp.dot(rows, down_weight, preferred_element_type=F32)
            return mixed.reshape(4, len(chunk), 16, -1)

        kept, away = down(kept), down(away)
        same = jnp.where(z_hi == core, kept, away)
        cross = jnp.where(z_hi == core, away, kept)
        for k, j in enumerate(chunk):
            straight = along("row", 8, lambda r: (r + 2 * j) % 8)
            turned = along("row", 8, lambda r: ((r + 2 * j) % 8) ^ 1)
            here = same[:, k].reshape(64, -1)
            arrived.append(here if j == 0 else straight(here.astype(BF16)).astype(F32))
            arrived.append(turned(cross[:, k].reshape(64, -1).astype(BF16)).astype(F32))

    out = sum(arrived).astype(BF16)
    doubled = jnp.concatenate((out, out), axis=0)
    return lax.dynamic_slice_in_dim(doubled, 64 - y * 16, 64, 0)


def solution(mesh):
    placed = (P(("row", "col"), None), P("col", "row"), P("col", "row"), P("row", "col"))
    return jax.shard_map(
        per_device, mesh=mesh, in_specs=placed, out_specs=P("row", "col"), check_vma=False
    )
```

time: 366 us -> 151 us (0.41)
  waiting for transfers between devices: 306 us -> 63.2 us
  starting transfers between devices: 0.13 us -> 56.9 us
  blocking collectives: 13.5 us -> 0 us
  between operations: 13.2 us -> 0.72 us
  local copies, waits for them, and re-layouts: 0.69 us -> 6.37 us
  other arithmetic: 9.02 us -> 3.66 us
    reduce_scatter x2 -> x0, waiting for transfers between devices: 223 us -> none  [the longest x1 150 us: per_device(): lax.psum_scatter(jnp.concatenate((gate_term, up_term), axis=1), 'col', sc...]
    all_gather x2 -> x0, waiting for transfers between devices: 82.2 us -> none  [the longest x1 46.2 us: per_device(): features = lax.all_gather(split_rows, 'row', axis=0, tiled=True)]
    ppermute x0 -> x33, starting transfers between devices: none -> 44.9 us  [along(): return lambda v: lax.ppermute(v, axis, pairs)]
    ppermute x0 -> x33, waiting for transfers between devices: none -> 44.4 us  [along(): return lambda v: lax.ppermute(v, axis, pairs)]
    all_to_all x0 -> x1, waiting for transfers between devices: none -> 18.8 us  [per_device(): lax.all_to_all(blocks, ('row', 'col'), split_axis=0, concat_axis=0, tiled...]
    all_to_all x1 -> x0, blocking collectives: 13.5 us -> none  [per_device(): lax.all_to_all(tokens, 'col', split_axis=1, concat_axis=0, tiled=True)]
    all_to_all x0 -> x1, starting transfers between devices: none -> 12 us  [per_device(): lax.all_to_all(blocks, ('row', 'col'), split_axis=0, concat_axis=0, tiled...]
    concatenate x1 -> x5, other arithmetic: 5.47 us -> 0.9 us  [the longest x1 0.73 us: per_device(): doubled = jnp.concatenate((out, out), axis=0)]
  transfers between devices with their start and end apart: 4 -> 34, of which waited for: 4 -> 18; matrix products, arithmetic and copies ran while one was open for 0% -> 12% of each run, Pallas kernels for 0% -> 0%
where the time goes in v1:
time: 151 us; the launch traced here: 150 us
  waiting for transfers between devices  63.2 us (42%)
  starting transfers between devices  56.9 us (38%)
  matrix products  19.2 us (13%)
  local copies, waits for them, and re-layouts  6.37 us (4%)
  other arithmetic  3.66 us (2%)
    ppermute x33, starting transfers between devices, along(): return lambda v: lax.ppermute(v, axis, pairs)  44.9 us
    ppermute x33, waiting for transfers between devices, along(): return lambda v: lax.ppermute(v, axis, pairs)  44.4 us
    all_to_all x1, waiting for transfers between devices, per_device(): lax.all_to_all(blocks, ('row', 'col'), split_axis=0, concat_axis=0, tiled...  18.8 us
    all_to_all x1, starting transfers between devices, per_device(): lax.all_to_all(blocks, ('row', 'col'), split_axis=0, concat_axis=0, tiled...  12 us
    dot_general x4, matrix products, project(): sent = to_core(lifted(jnp.dot(away, weight, preferred_element_type=F32)))  7.39 us
    dot_general x4, matrix products, down(): mixed = jnp.dot(rows, down_weight, preferred_element_type=F32)  7.32 us
    dot_general x4, matrix products, project(): return jnp.dot(kept, weight, preferred_element_type=F32) + lowered(sent)  4.5 us
  transfers between devices with their start and end apart: 34, of which 18 were waited for; matrix products, arithmetic and copies ran while one was open for 12% of the time, Pallas kernels for 0%

profile of v1, /device:TPU:1, one launch (start us, length us, event | category | flops | bytes accessed | tf_op | source)
XLA Modules:
  0.0 150.1 jit_solution(10054786080084274460)
XLA Ops:
  0.0 0.9 broadcast_in_dim.7
  1.1 1.2 all_to_all.6
  2.3 12.0 %all-to-all-start = ((bf16[128,4,1024]{2,1,0:T(4,128)(2,1)}), bf16[128,4,1024]{2,1,0:T(4,128)(2,1)}, u32[]{:S(2)}, u32[]{:S(2)}) async-start(bf16[128,4,1024]{2,1,0:T(4,128)(2,1)} %all_to_all.6), calls=%async_computation | async-start | bytes 2097152 | tf_op jit(solution)/shard_map/all_to_all | solution.py:36
  14.4 18.8 %all-to-all-done = bf16[128,4,1024]{2,1,0:T(4,128)(2,1)} async-done(((bf16[128,4,1024]{2,1,0:T(4,128)(2,1)}), bf16[128,4,1024]{2,1,0:T(4,128)(2,1)}, u32[]{:S(2)}, u32[]{:S(2)}) %all-to-all-start) | async-done | bytes 1048608 | tf_op jit(solution)/shard_map/all_to_all | solution.py:36
  33.2 2.3 %reshape.93 = bf16[4,2,4,16,1024]{4,3,2,1,0:T(8,128)(2,1)} reshape(bf16[128,4,1024]{2,1,0:T(4,128)(2,1)} %all-to-all-done) | data formatting | bytes 2097152 | tf_op jit(solution)/shard_map/reshape | solution.py:37
  35.6 1.4 dynamic-slice_bitcast_fusion.5
  37.1 4.2 %fusion = f16[128,3328]{1,0:T(8,128)(2,1)S(1)} fusion(bf16[128,1024]{1,0:T(8,128)(2,1)S(1)} %bitcast.152, bf16[1024,3328]{1,0:T(8,128)(2,1)} %param.5), kind=kOutput, calls=%fused_computation.4 | convolution fusion | flops 873267200 | bytes 7929856 | tf_op jit(solution)/shard_map/dot_general | solution.py:58
  41.8 1.1 fusion.1
  43.4 1.1 fusion.2
  45.0 1.1 fusion.3
  46.6 1.1 multiply_add_fusion.2
  47.8 1.1 multiply_add_fusion.3
  49.1 0.6 collective-permute-start.3
  49.7 1.1 multiply_add_fusion.1
  50.9 1.1 multiply_add_fusion
  52.2 0.9 collective-permute-start.20
  53.1 8.5 %collective-permute-done.3 = f16[2,32,3328]{2,1,0:T(8,128)(2,1)S(1)} collective-permute-done((f16[2,32,3328]{2,1,0:T(8,128)(2,1)S(1)}, f16[2,32,3328]{2,1,0:T(8,128)(2,1)S(1)}, u32[]{:S(2)}, u32[]{:S(2)}) %collective-permute-start.3) | collective-permute-done | bytes 426016 | tf_op jit(solution)/shard_map/ppermute | solution.py:13
  61.9 1.5 collective-permute-start.4
  63.3 7.4 %collective-permute-done.20 = f16[2,32,3328]{2,1,0:T(8,128)(2,1)S(1)} collective-permute-done((f16[2,32,3328]{2,1,0:T(8,128)(2,1)S(1)}, f16[2,32,3328]{2,1,0:T(8,128)(2,1)S(1)}, u32[]{:S(2)}, u32[]{:S(2)}) %collective-permute-start.20) | collective-permute-done | bytes 426016 | tf_op jit(solution)/shard_map/ppermute | solution.py:13
  71.0 1.5 collective-permute-start.21
  72.5 2.8 %collective-permute-done.4 = f16[32,3328]{1,0:T(8,128)(2,1)S(1)} collective-permute-done((f16[32,3328]{1,0:T(8,128)(2,1)S(1)}, f16[32,3328]{1,0:T(8,128)(2,1)S(1)}, u32[]{:S(2)}, u32[]{:S(2)}) %collective-permute-start.4) | collective-permute-done | bytes 213024 | tf_op jit(solution)/shard_map/ppermute | solution.py:13
  75.5 3.5 %collective-permute-done.21 = f16[32,3328]{1,0:T(8,128)(2,1)S(1)} collective-permute-done((f16[32,3328]{1,0:T(8,128)(2,1)S(1)}, f16[32,3328]{1,0:T(8,128)(2,1)S(1)}, u32[]{:S(2)}, u32[]{:S(2)}) %collective-permute-start.21) | collective-permute-done | bytes 213024 | tf_op jit(solution)/shard_map/ppermute | solution.py:13
  79.0 1.2 collective-permute-done.19
  80.4 1.3 collective-permute-start.22
  81.7 3.1 %collective-permute-done.5 = f16[32,3328]{1,0:T(8,128)(2,1)S(1)} collective-permute-done((f16[32,3328]{1,0:T(8,128)(2,1)S(1)}, f16[32,3328]{1,0:T(8,128)(2,1)S(1)}, u32[]{:S(2)}, u32[]{:S(2)}) %collective-permute-start.5) | collective-permute-done | bytes 213024 | tf_op jit(solution)/shard_map/ppermute | solution.py:13
  85.4 4.0 %collective-permute-done.22 = f16[32,3328]{1,0:T(8,128)(2,1)S(1)} collective-permute-done((f16[32,3328]{1,0:T(8,128)(2,1)S(1)}, f16[32,3328]{1,0:T(8,128)(2,1)S(1)}, u32[]{:S(2)}, u32[]{:S(2)}) %collective-permute-start.22) | collective-permute-done | bytes 213024 | tf_op jit(solution)/shard_map/ppermute | solution.py:13
  90.2 1.1 collective-permute-start.7
  91.3 4.4 %collective-permute-done.23 = f16[2,32,1664]{2,1,0:T(8,128)(2,1)S(1)} collective-permute-done((f16[2,32,1664]{2,1,0:T(8,128)(2,1)S(1)}, f16[2,32,1664]{2,1,0:T(8,128)(2,1)S(1)}, u32[]{:S(2)}, u32[]{:S(2)}) %collective-permute-start.23) | collective-permute-done | bytes 213024 | tf_op jit(solution)/shard_map/ppermute | solution.py:13
  96.2 1.8 %collective-permute-done.7 = bf16[32,1664]{1,0:T(8,128)(2,1)S(1)} collective-permute-done((bf16[32,1664]{1,0:T(8,128)(2,1)S(1)}, bf16[32,1664]{1,0:T(8,128)(2,1)S(1)}, u32[]{:S(2)}, u32[]{:S(2)}) %collective-permute-start.7) | collective-permute-done | bytes 106528 | tf_op jit(solution)/shard_map/ppermute | solution.py:13
  98.2 2.7 %collective-permute-start.8 = (bf16[32,3328]{1,0:T(8,128)(2,1)S(1)}, bf16[32,3328]{1,0:T(8,128)(2,1)S(1)}, u32[]{:S(2)}, u32[]{:S(2)}) collective-permute-start(bf16[32,3328]{1,0:T(8,128)(2,1)S(1)} %pad_maximum_fusion.12), channel_id=1, source_target_pairs={{0,12},{1,13},{2,14},{3,15},{4,0},{5,1},{6,2},{7,3},{8,4},{9,5},{1... | collective-permute-start | bytes 638984 | tf_op jit(solution)/shard_map/ppermute | solution.py:13
  101.2 2.7 %collective-permute-start.25 = (bf16[32,3328]{1,0:T(8,128)(2,1)S(1)}, bf16[32,3328]{1,0:T(8,128)(2,1)S(1)}, u32[]{:S(2)}, u32[]{:S(2)}) collective-permute-start(bf16[32,3328]{1,0:T(8,128)(2,1)S(1)} %pad_maximum_fusion.13), channel_id=1, source_target_pairs={{0,12},{1,13},{2,14},{3,15},{4,0},{5,1},{6,2},{7,3},{8,4},{9,5},{1... | collective-permute-start | bytes 638984 | tf_op jit(solution)/shard_map/ppermute | solution.py:13
  104.2 2.7 %collective-permute-start.11 = (bf16[32,1664]{1,0:T(8,128)(2,1)S(1)}, bf16[32,1664]{1,0:T(8,128)(2,1)S(1)}, u32[]{:S(2)}, u32[]{:S(2)}) collective-permute-start(bf16[32,1664]{1,0:T(8,128)(2,1)S(1)} %slice.200), channel_id=1, source_target_pairs={{0,12},{1,13},{2,14},{3,15},{4,0},{5,1},{6,2},{7,3},{8,4},{9,5},{1... | collective-permute-start | bytes 319496 | tf_op jit(solution)/shard_map/ppermute | solution.py:13
  107.2 2.7 %collective-permute-start.28 = (bf16[32,1664]{1,0:T(8,128)(2,1)S(1)}, bf16[32,1664]{1,0:T(8,128)(2,1)S(1)}, u32[]{:S(2)}, u32[]{:S(2)}) collective-permute-start(bf16[32,1664]{1,0:T(8,128)(2,1)S(1)} %slice.222), channel_id=1, source_target_pairs={{0,12},{1,13},{2,14},{3,15},{4,0},{5,1},{6,2},{7,3},{8,4},{9,5},{1... | collective-permute-start | bytes 319496 | tf_op jit(solution)/shard_map/ppermute | solution.py:13
  110.5 8.5 %collective-permute-start.12 = (bf16[128,3328]{1,0:T(8,128)(2,1)S(1)}, bf16[128,3328]{1,0:T(8,128)(2,1)S(1)}, u32[]{:S(2)}, u32[]{:S(2)}) collective-permute-start(bf16[128,3328]{1,0:T(8,128)(2,1)S(1)} %pad_maximum_fusion), channel_id=1, source_target_pairs={{0,1},{1,0},{2,3},{3,2},{4,5},{5,4},{6,7},{7,6},{8,9},{9,8},{10,11... | collective-permute-start | bytes 2555912 | tf_op jit(solution)/shard_map/ppermute | solution.py:13
  119.0 2.7 %collective-permute-start.29 = (bf16[128,3328]{1,0:T(8,128)(2,1)S(1)}, bf16[128,3328]{1,0:T(8,128)(2,1)S(1)}, u32[]{:S(2)}, u32[]{:S(2)}) collective-permute-start(bf16[128,3328]{1,0:T(8,128)(2,1)S(1)} %pad_maximum_fusion.1), channel_id=1, source_target_pairs={{0,1},{1,0},{2,3},{3,2},{4,5},{5,4},{6,7},{7,6},{8,9},{9,8},{10,11... | collective-permute-start | bytes 2555912 | tf_op jit(solution)/shard_map/ppermute | solution.py:13
  121.8 4.0 %fusion.61 = f32[128,1024]{1,0:T(8,128)S(1)} fusion(bf16[3328,1024]{1,0:T(8,128)(2,1)} %param.7, bf16[32,3328]{1,0:T(8,128)(2,1)S(1)} %collective-permute-done.26, bf16[32,1664]{1,0:T(8,128)(2,1)S(1)} %collective-permute-done.28, bf16[32,1664]{1,0:T(8,128)(2,1)S(1)} %collective-permute-done.27, bf16[32,3328]{1,0:T(8,128)(2,1)S(1)} %collective-permute-done.25, ...), kind=kOutput, calls=%fused_computation.147 | convolution fusion | flops 877527040 | bytes 8192000 | tf_op jit(solution)/shard_map/dot_general | solution.py:87
  125.8 1.1 fusion.66
  127.0 1.1 select_convert_fusion.2
  128.1 1.0 collective-permute-start.13
  129.1 3.1 %collective-permute-start.14 = (bf16[64,1024]{1,0:T(8,128)(2,1)S(1)}, bf16[64,1024]{1,0:T(8,128)(2,1)S(1)}, u32[]{:S(2)}, u32[]{:S(2)}) collective-permute-start(bf16[64,1024]{1,0:T(8,128)(2,1)S(1)} %bitcast.172), channel_id=1, source_target_pairs={{0,80},{16,64},{32,112},{48,96},{64,16},{80,0},{96,48},{112,32},{1... | collective-permute-start | bytes 393224 | tf_op jit(solution)/shard_map/ppermute | solution.py:13
  132.7 3.0 %collective-permute-start.16 = (bf16[64,1024]{1,0:T(8,128)(2,1)S(1)}, bf16[64,1024]{1,0:T(8,128)(2,1)S(1)}, u32[]{:S(2)}, u32[]{:S(2)}) collective-permute-start(bf16[64,1024]{1,0:T(8,128)(2,1)S(1)} %bitcast.168), channel_id=1, source_target_pairs={{0,48},{16,32},{32,80},{48,64},{64,112},{80,96},{96,16},{112,0},{1... | collective-permute-start | bytes 393224 | tf_op jit(solution)/shard_map/ppermute | solution.py:13
  135.7 1.1 select_convert_fusion
  136.9 2.7 %collective-permute-start.30 = (bf16[64,1024]{1,0:T(8,128)(2,1)S(1)}, bf16[64,1024]{1,0:T(8,128)(2,1)S(1)}, u32[]{:S(2)}, u32[]{:S(2)}) collective-permute-start(bf16[64,1024]{1,0:T(8,128)(2,1)S(1)} %bitcast.166), channel_id=1, source_target_pairs={{0,96},{16,112},{32,0},{48,16},{64,32},{80,48},{96,64},{112,80},{1... | collective-permute-start | bytes 393224 | tf_op jit(solution)/shard_map/ppermute | solution.py:13
  140.1 2.3 %collective-permute-start.32 = (bf16[64,1024]{1,0:T(8,128)(2,1)S(1)}, bf16[64,1024]{1,0:T(8,128)(2,1)S(1)}, u32[]{:S(2)}, u32[]{:S(2)}) collective-permute-start(bf16[64,1024]{1,0:T(8,128)(2,1)S(1)} %bitcast.169), channel_id=1, source_target_pairs={{0,16},{16,0},{32,48},{48,32},{64,80},{80,64},{96,112},{112,96},{1... | collective-permute-start | bytes 393224 | tf_op jit(solution)/shard_map/ppermute | solution.py:13
  142.4 1.5 %collective-permute-done.16 = bf16[64,1024]{1,0:T(8,128)(2,1)S(1)} collective-permute-done((bf16[64,1024]{1,0:T(8,128)(2,1)S(1)}, bf16[64,1024]{1,0:T(8,128)(2,1)S(1)}, u32[]{:S(2)}, u32[]{:S(2)}) %collective-permute-start.16) | collective-permute-done | bytes 131104 | tf_op jit(solution)/shard_map/ppermute | solution.py:13
  144.0 2.0 %collective-permute-done.31 = bf16[64,1024]{1,0:T(8,128)(2,1)S(1)} collective-permute-done((bf16[64,1024]{1,0:T(8,128)(2,1)S(1)}, bf16[64,1024]{1,0:T(8,128)(2,1)S(1)}, u32[]{:S(2)}, u32[]{:S(2)}) %collective-permute-start.31) | collective-permute-done | bytes 131104 | tf_op jit(solution)/shard_map/ppermute | solution.py:13
  145.9 3.2 %collective-permute-done.32 = bf16[64,1024]{1,0:T(8,128)(2,1)S(1)} collective-permute-done((bf16[64,1024]{1,0:T(8,128)(2,1)S(1)}, bf16[64,1024]{1,0:T(8,128)(2,1)S(1)}, u32[]{:S(2)}, u32[]{:S(2)}) %collective-permute-start.32) | collective-permute-done | bytes 131104 | tf_op jit(solution)/shard_map/ppermute | solution.py:13
  149.3 0.7 fusion.44
  (98 shorter events, 8.5 us)
Async XLA Ops:
  2.3 30.9 %all-to-all-start = ((bf16[128,4,1024]{2,1,0:T(4,128)(2,1)}), bf16[128,4,1024]{2,1,0:T(4,128)(2,1)}, u32[]{:S(2)}, u32[]{:S(2)}) async-start(bf16[128,4,1024]{2,1,0:T(4,128)(2,1)} %all_to_all.6), calls=%async_computation | async-start | bytes 2097152 | tf_op jit(solution)/shard_map/all_to_all | solution.py:36
  33.2 8.5 %slice-start.2 = ((s8[6815744]{0:T(1024)(128)(4,1)}), s8[2621440]{0:T(1024)(128)(4,1)S(1)}, s32[]{:S(2)}) async-start(s8[6815744]{0:T(1024)(128)(4,1)} %bitcast.148), calls=%async_computation.3 | async-start | bytes 5242880
  37.1 4.7 %slice-start.3 = ((s8[6815744]{0:T(1024)(128)(4,1)}), s8[4194304]{0:T(1024)(128)(4,1)S(1)}, s32[]{:S(2)}) async-start(s8[6815744]{0:T(1024)(128)(4,1)} %bitcast.148), calls=%async_computation.4 | async-start | bytes 8388608
  37.1 6.1 %slice-start = ((s8[6815744]{0:T(1024)(128)(4,1)}), s8[4194304]{0:T(1024)(128)(4,1)S(1)}, s32[]{:S(2)}) async-start(s8[6815744]{0:T(1024)(128)(4,1)} %bitcast.146), calls=%async_computation.1 | async-start | bytes 8388608
  41.3 2.2 %slice-start.1 = ((s8[6815744]{0:T(1024)(128)(4,1)}), s8[2621440]{0:T(1024)(128)(4,1)S(1)}, s32[]{:S(2)}) async-start(s8[6815744]{0:T(1024)(128)(4,1)} %bitcast.146), calls=%async_computation.2 | async-start | bytes 5242880
  41.3 6.6 %collective-permute-start = (f16[128,3328]{1,0:T(8,128)(2,1)S(1)}, f16[128,3328]{1,0:T(8,128)(2,1)S(1)}, u32[]{:S(2)}, u32[]{:S(2)}) collective-permute-start(f16[128,3328]{1,0:T(8,128)(2,1)S(1)} %fusion), channel_id=1, source_target_pairs={{0,1},{1,0},{2,3},{3,2},{4,5},{5,4},{6,7},{7,6},{8,9},{9,8},{10,11... | collective-permute-start | bytes 2555912 | tf_op jit(solution)/shard_map/ppermute | solution.py:13
  42.8 3.8 %collective-permute-start.1 = (f16[128,3328]{1,0:T(8,128)(2,1)S(1)}, f16[128,3328]{1,0:T(8,128)(2,1)S(1)}, u32[]{:S(2)}, u32[]{:S(2)}) collective-permute-start(f16[128,3328]{1,0:T(8,128)(2,1)S(1)} %fusion.1), channel_id=1, source_target_pairs={{0,1},{1,0},{2,3},{3,2},{4,5},{5,4},{6,7},{7,6},{8,9},{9,8},{10,11... | collective-permute-start | bytes 2555912 | tf_op jit(solution)/shard_map/ppermute | solution.py:13
  44.5 5.2 %collective-permute-start.17 = (f16[128,3328]{1,0:T(8,128)(2,1)S(1)}, f16[128,3328]{1,0:T(8,128)(2,1)S(1)}, u32[]{:S(2)}, u32[]{:S(2)}) collective-permute-start(f16[128,3328]{1,0:T(8,128)(2,1)S(1)} %fusion.2), channel_id=1, source_target_pairs={{0,1},{1,0},{2,3},{3,2},{4,5},{5,4},{6,7},{7,6},{8,9},{9,8},{10,11... | collective-permute-start | bytes 2555912 | tf_op jit(solution)/shard_map/ppermute | solution.py:13
  46.1 4.8 %collective-permute-start.18 = (f16[128,3328]{1,0:T(8,128)(2,1)S(1)}, f16[128,3328]{1,0:T(8,128)(2,1)S(1)}, u32[]{:S(2)}, u32[]{:S(2)}) collective-permute-start(f16[128,3328]{1,0:T(8,128)(2,1)S(1)} %fusion.3), channel_id=1, source_target_pairs={{0,1},{1,0},{2,3},{3,2},{4,5},{5,4},{6,7},{7,6},{8,9},{9,8},{10,11... | collective-permute-start | bytes 2555912 | tf_op jit(solution)/shard_map/ppermute | solution.py:13
  49.1 12.5 %collective-permute-start.3 = (f16[2,32,3328]{2,1,0:T(8,128)(2,1)S(1)}, f16[2,32,3328]{2,1,0:T(8,128)(2,1)S(1)}, u32[]{:S(2)}, u32[]{:S(2)}) collective-permute-start(f16[2,32,3328]{2,1,0:T(8,128)(2,1)S(1)} %pad_maximum_fusion.5), channel_id=1, source_target_pairs={{0,4},{1,5},{2,6},{3,7},{4,8},{5,9},{6,10},{7,11},{8,12},{9,13},{1... | collective-permute-start | bytes 1277960 | tf_op jit(solution)/shard_map/ppermute | solution.py:13
  52.2 18.5 %collective-permute-start.20 = (f16[2,32,3328]{2,1,0:T(8,128)(2,1)S(1)}, f16[2,32,3328]{2,1,0:T(8,128)(2,1)S(1)}, u32[]{:S(2)}, u32[]{:S(2)}) collective-permute-start(f16[2,32,3328]{2,1,0:T(8,128)(2,1)S(1)} %pad_maximum_fusion.7), channel_id=1, source_target_pairs={{0,4},{1,5},{2,6},{3,7},{4,8},{5,9},{6,10},{7,11},{8,12},{9,13},{1... | collective-permute-start | bytes 1277960 | tf_op jit(solution)/shard_map/ppermute | solution.py:13
  61.8 13.5 %collective-permute-start.2 = (f16[2,32,3328]{2,1,0:T(8,128)(2,1)S(1)}, f16[2,32,3328]{2,1,0:T(8,128)(2,1)S(1)}, u32[]{:S(2)}, u32[]{:S(2)}) collective-permute-start(f16[2,32,3328]{2,1,0:T(8,128)(2,1)S(1)} %pad_maximum_fusion.4), channel_id=1, source_target_pairs={{0,12},{1,13},{2,14},{3,15},{4,0},{5,1},{6,2},{7,3},{8,4},{9,5},{1... | collective-permute-start | bytes 1277960 | tf_op jit(solution)/shard_map/ppermute | solution.py:13
  61.9 13.4 %collective-permute-start.4 = (f16[32,3328]{1,0:T(8,128)(2,1)S(1)}, f16[32,3328]{1,0:T(8,128)(2,1)S(1)}, u32[]{:S(2)}, u32[]{:S(2)}) collective-permute-start(f16[32,3328]{1,0:T(8,128)(2,1)S(1)} %get-tuple-element.5), channel_id=1, source_target_pairs={{0,4},{1,5},{2,6},{3,7},{4,8},{5,9},{6,10},{7,11},{8,12},{9,13},{1... | collective-permute-start | bytes 638984 | tf_op jit(solution)/shard_map/ppermute | solution.py:13
  70.9 9.3 %collective-permute-start.19 = (f16[2,32,3328]{2,1,0:T(8,128)(2,1)S(1)}, f16[2,32,3328]{2,1,0:T(8,128)(2,1)S(1)}, u32[]{:S(2)}, u32[]{:S(2)}) collective-permute-start(f16[2,32,3328]{2,1,0:T(8,128)(2,1)S(1)} %pad_maximum_fusion.6), channel_id=1, source_target_pairs={{0,12},{1,13},{2,14},{3,15},{4,0},{5,1},{6,2},{7,3},{8,4},{9,5},{1... | collective-permute-start | bytes 1277960 | tf_op jit(solution)/shard_map/ppermute | solution.py:13
  71.0 8.0 %collective-permute-start.21 = (f16[32,3328]{1,0:T(8,128)(2,1)S(1)}, f16[32,3328]{1,0:T(8,128)(2,1)S(1)}, u32[]{:S(2)}, u32[]{:S(2)}) collective-permute-start(f16[32,3328]{1,0:T(8,128)(2,1)S(1)} %get-tuple-element.9), channel_id=1, source_target_pairs={{0,4},{1,5},{2,6},{3,7},{4,8},{5,9},{6,10},{7,11},{8,12},{9,13},{1... | collective-permute-start | bytes 638984 | tf_op jit(solution)/shard_map/ppermute | solution.py:13
  75.4 9.4 %collective-permute-start.5 = (f16[32,3328]{1,0:T(8,128)(2,1)S(1)}, f16[32,3328]{1,0:T(8,128)(2,1)S(1)}, u32[]{:S(2)}, u32[]{:S(2)}) collective-permute-start(f16[32,3328]{1,0:T(8,128)(2,1)S(1)} %get-tuple-element.24), channel_id=1, source_target_pairs={{0,12},{1,13},{2,14},{3,15},{4,0},{5,1},{6,2},{7,3},{8,4},{9,5},{1... | collective-permute-start | bytes 638984 | tf_op jit(solution)/shard_map/ppermute | solution.py:13
  80.4 9.0 %collective-permute-start.22 = (f16[32,3328]{1,0:T(8,128)(2,1)S(1)}, f16[32,3328]{1,0:T(8,128)(2,1)S(1)}, u32[]{:S(2)}, u32[]{:S(2)}) collective-permute-start(f16[32,3328]{1,0:T(8,128)(2,1)S(1)} %get-tuple-element.26), channel_id=1, source_target_pairs={{0,12},{1,13},{2,14},{3,15},{4,0},{5,1},{6,2},{7,3},{8,4},{9,5},{1... | collective-permute-start | bytes 638984 | tf_op jit(solution)/shard_map/ppermute | solution.py:13
  85.0 5.1 %collective-permute-start.6 = (f16[2,32,1664]{2,1,0:T(8,128)(2,1)S(1)}, f16[2,32,1664]{2,1,0:T(8,128)(2,1)S(1)}, u32[]{:S(2)}, u32[]{:S(2)}) collective-permute-start(f16[2,32,1664]{2,1,0:T(8,128)(2,1)S(1)} %multiply_convert_fusion.1), channel_id=1, source_target_pairs={{0,2},{1,3},{2,0},{3,1},{4,6},{5,7},{6,4},{7,5},{8,10},{9,11},{10,... | collective-permute-start | bytes 638984 | tf_op jit(solution)/shard_map/ppermute | solution.py:13
  89.5 6.2 %collective-permute-start.23 = (f16[2,32,1664]{2,1,0:T(8,128)(2,1)S(1)}, f16[2,32,1664]{2,1,0:T(8,128)(2,1)S(1)}, u32[]{:S(2)}, u32[]{:S(2)}) collective-permute-start(f16[2,32,1664]{2,1,0:T(8,128)(2,1)S(1)} %multiply_convert_fusion), channel_id=1, source_target_pairs={{0,2},{1,3},{2,0},{3,1},{4,6},{5,7},{6,4},{7,5},{8,10},{9,11},{10,... | collective-permute-start | bytes 638984 | tf_op jit(solution)/shard_map/ppermute | solution.py:13
  90.2 7.8 %collective-permute-start.7 = (bf16[32,1664]{1,0:T(8,128)(2,1)S(1)}, bf16[32,1664]{1,0:T(8,128)(2,1)S(1)}, u32[]{:S(2)}, u32[]{:S(2)}) collective-permute-start(bf16[32,1664]{1,0:T(8,128)(2,1)S(1)} %fusion.43), channel_id=1, source_target_pairs={{0,2},{1,3},{2,0},{3,1},{4,6},{5,7},{6,4},{7,5},{8,10},{9,11},{10,... | collective-permute-start | bytes 319496 | tf_op jit(solution)/shard_map/ppermute | solution.py:13
  95.9 5.1 %collective-permute-start.24 = (bf16[32,1664]{1,0:T(8,128)(2,1)S(1)}, bf16[32,1664]{1,0:T(8,128)(2,1)S(1)}, u32[]{:S(2)}, u32[]{:S(2)}) collective-permute-start(bf16[32,1664]{1,0:T(8,128)(2,1)S(1)} %fusion.41), channel_id=1, source_target_pairs={{0,2},{1,3},{2,0},{3,1},{4,6},{5,7},{6,4},{7,5},{8,10},{9,11},{10,... | collective-permute-start | bytes 319496 | tf_op jit(solution)/shard_map/ppermute | solution.py:13
  98.1 6.0 %collective-permute-start.9 = (bf16[32,3328]{1,0:T(8,128)(2,1)S(1)}, bf16[32,3328]{1,0:T(8,128)(2,1)S(1)}, u32[]{:S(2)}, u32[]{:S(2)}) collective-permute-start(bf16[32,3328]{1,0:T(8,128)(2,1)S(1)} %pad_maximum_fusion.12), channel_id=1, source_target_pairs={{0,4},{1,5},{2,6},{3,7},{4,8},{5,9},{6,10},{7,11},{8,12},{9,13},{1... | collective-permute-start | bytes 638984 | tf_op jit(solution)/shard_map/ppermute | solution.py:13
  98.2 6.0 %collective-permute-start.8 = (bf16[32,3328]{1,0:T(8,128)(2,1)S(1)}, bf16[32,3328]{1,0:T(8,128)(2,1)S(1)}, u32[]{:S(2)}, u32[]{:S(2)}) collective-permute-start(bf16[32,3328]{1,0:T(8,128)(2,1)S(1)} %pad_maximum_fusion.12), channel_id=1, source_target_pairs={{0,12},{1,13},{2,14},{3,15},{4,0},{5,1},{6,2},{7,3},{8,4},{9,5},{1... | collective-permute-start | bytes 638984 | tf_op jit(solution)/shard_map/ppermute | solution.py:13
  101.1 6.0 %collective-permute-start.26 = (bf16[32,3328]{1,0:T(8,128)(2,1)S(1)}, bf16[32,3328]{1,0:T(8,128)(2,1)S(1)}, u32[]{:S(2)}, u32[]{:S(2)}) collective-permute-start(bf16[32,3328]{1,0:T(8,128)(2,1)S(1)} %pad_maximum_fusion.13), channel_id=1, source_target_pairs={{0,4},{1,5},{2,6},{3,7},{4,8},{5,9},{6,10},{7,11},{8,12},{9,13},{1... | collective-permute-start | bytes 638984 | tf_op jit(solution)/shard_map/ppermute | solution.py:13
  101.2 6.0 %collective-permute-start.25 = (bf16[32,3328]{1,0:T(8,128)(2,1)S(1)}, bf16[32,3328]{1,0:T(8,128)(2,1)S(1)}, u32[]{:S(2)}, u32[]{:S(2)}) collective-permute-start(bf16[32,3328]{1,0:T(8,128)(2,1)S(1)} %pad_maximum_fusion.13), channel_id=1, source_target_pairs={{0,12},{1,13},{2,14},{3,15},{4,0},{5,1},{6,2},{7,3},{8,4},{9,5},{1... | collective-permute-start | bytes 638984 | tf_op jit(solution)/shard_map/ppermute | solution.py:13
  104.1 6.3 %collective-permute-start.10 = (bf16[32,1664]{1,0:T(8,128)(2,1)S(1)}, bf16[32,1664]{1,0:T(8,128)(2,1)S(1)}, u32[]{:S(2)}, u32[]{:S(2)}) collective-permute-start(bf16[32,1664]{1,0:T(8,128)(2,1)S(1)} %slice.199), channel_id=1, source_target_pairs={{0,4},{1,5},{2,6},{3,7},{4,8},{5,9},{6,10},{7,11},{8,12},{9,13},{1... | collective-permute-start | bytes 319496 | tf_op jit(solution)/shard_map/ppermute | solution.py:13
  104.2 6.2 %collective-permute-start.11 = (bf16[32,1664]{1,0:T(8,128)(2,1)S(1)}, bf16[32,1664]{1,0:T(8,128)(2,1)S(1)}, u32[]{:S(2)}, u32[]{:S(2)}) collective-permute-start(bf16[32,1664]{1,0:T(8,128)(2,1)S(1)} %slice.200), channel_id=1, source_target_pairs={{0,12},{1,13},{2,14},{3,15},{4,0},{5,1},{6,2},{7,3},{8,4},{9,5},{1... | collective-permute-start | bytes 319496 | tf_op jit(solution)/shard_map/ppermute | solution.py:13
  107.1 11.8 %collective-permute-start.27 = (bf16[32,1664]{1,0:T(8,128)(2,1)S(1)}, bf16[32,1664]{1,0:T(8,128)(2,1)S(1)}, u32[]{:S(2)}, u32[]{:S(2)}) collective-permute-start(bf16[32,1664]{1,0:T(8,128)(2,1)S(1)} %slice.221), channel_id=1, source_target_pairs={{0,4},{1,5},{2,6},{3,7},{4,8},{5,9},{6,10},{7,11},{8,12},{9,13},{1... | collective-permute-start | bytes 319496 | tf_op jit(solution)/shard_map/ppermute | solution.py:13
  107.2 11.7 %collective-permute-start.28 = (bf16[32,1664]{1,0:T(8,128)(2,1)S(1)}, bf16[32,1664]{1,0:T(8,128)(2,1)S(1)}, u32[]{:S(2)}, u32[]{:S(2)}) collective-permute-start(bf16[32,1664]{1,0:T(8,128)(2,1)S(1)} %slice.222), channel_id=1, source_target_pairs={{0,12},{1,13},{2,14},{3,15},{4,0},{5,1},{6,2},{7,3},{8,4},{9,5},{1... | collective-permute-start | bytes 319496 | tf_op jit(solution)/shard_map/ppermute | solution.py:13
  110.5 15.4 %collective-permute-start.12 = (bf16[128,3328]{1,0:T(8,128)(2,1)S(1)}, bf16[128,3328]{1,0:T(8,128)(2,1)S(1)}, u32[]{:S(2)}, u32[]{:S(2)}) collective-permute-start(bf16[128,3328]{1,0:T(8,128)(2,1)S(1)} %pad_maximum_fusion), channel_id=1, source_target_pairs={{0,1},{1,0},{2,3},{3,2},{4,5},{5,4},{6,7},{7,6},{8,9},{9,8},{10,11... | collective-permute-start | bytes 2555912 | tf_op jit(solution)/shard_map/ppermute | solution.py:13
  119.0 6.9 %slice-start.4 = ((s8[6815744]{0:T(1024)(128)(4,1)}), s8[4194304]{0:T(1024)(128)(4,1)S(1)}, s32[]{:S(2)}) async-start(s8[6815744]{0:T(1024)(128)(4,1)} %bitcast.150), calls=%async_computation.5 | async-start | bytes 8388608
  119.0 6.8 %slice-start.5 = ((s8[6815744]{0:T(1024)(128)(4,1)}), s8[2621440]{0:T(1024)(128)(4,1)S(1)}, s32[]{:S(2)}) async-start(s8[6815744]{0:T(1024)(128)(4,1)} %bitcast.150), calls=%async_computation.6 | async-start | bytes 5242880
  119.0 16.6 %collective-permute-start.29 = (bf16[128,3328]{1,0:T(8,128)(2,1)S(1)}, bf16[128,3328]{1,0:T(8,128)(2,1)S(1)}, u32[]{:S(2)}, u32[]{:S(2)}) collective-permute-start(bf16[128,3328]{1,0:T(8,128)(2,1)S(1)} %pad_maximum_fusion.1), channel_id=1, source_target_pairs={{0,1},{1,0},{2,3},{3,2},{4,5},{5,4},{6,7},{7,6},{8,9},{9,8},{10,11... | collective-permute-start | bytes 2555912 | tf_op jit(solution)/shard_map/ppermute | solution.py:13
  128.1 11.5 %collective-permute-start.13 = (bf16[64,1024]{1,0:T(8,128)(2,1)S(1)}, bf16[64,1024]{1,0:T(8,128)(2,1)S(1)}, u32[]{:S(2)}, u32[]{:S(2)}) collective-permute-start(bf16[64,1024]{1,0:T(8,128)(2,1)S(1)} %bitcast.170), channel_id=1, source_target_pairs={{0,64},{16,80},{32,96},{48,112},{64,0},{80,16},{96,32},{112,48},{1... | collective-permute-start | bytes 393224 | tf_op jit(solution)/shard_map/ppermute | solution.py:13
  129.1 11.0 %collective-permute-start.14 = (bf16[64,1024]{1,0:T(8,128)(2,1)S(1)}, bf16[64,1024]{1,0:T(8,128)(2,1)S(1)}, u32[]{:S(2)}, u32[]{:S(2)}) collective-permute-start(bf16[64,1024]{1,0:T(8,128)(2,1)S(1)} %bitcast.172), channel_id=1, source_target_pairs={{0,80},{16,64},{32,112},{48,96},{64,16},{80,0},{96,48},{112,32},{1... | collective-permute-start | bytes 393224 | tf_op jit(solution)/shard_map/ppermute | solution.py:13
  132.2 10.2 %collective-permute-start.15 = (bf16[64,1024]{1,0:T(8,128)(2,1)S(1)}, bf16[64,1024]{1,0:T(8,128)(2,1)S(1)}, u32[]{:S(2)}, u32[]{:S(2)}) collective-permute-start(bf16[64,1024]{1,0:T(8,128)(2,1)S(1)} %bitcast.167), channel_id=1, source_target_pairs={{0,32},{16,48},{32,64},{48,80},{64,96},{80,112},{96,0},{112,16},{1... | collective-permute-start | bytes 393224 | tf_op jit(solution)/shard_map/ppermute | solution.py:13
  132.7 11.3 %collective-permute-start.16 = (bf16[64,1024]{1,0:T(8,128)(2,1)S(1)}, bf16[64,1024]{1,0:T(8,128)(2,1)S(1)}, u32[]{:S(2)}, u32[]{:S(2)}) collective-permute-start(bf16[64,1024]{1,0:T(8,128)(2,1)S(1)} %bitcast.168), channel_id=1, source_target_pairs={{0,48},{16,32},{32,80},{48,64},{64,112},{80,96},{96,16},{112,0},{1... | collective-permute-start | bytes 393224 | tf_op jit(solution)/shard_map/ppermute | solution.py:13
  136.9 7.1 %collective-permute-start.30 = (bf16[64,1024]{1,0:T(8,128)(2,1)S(1)}, bf16[64,1024]{1,0:T(8,128)(2,1)S(1)}, u32[]{:S(2)}, u32[]{:S(2)}) collective-permute-start(bf16[64,1024]{1,0:T(8,128)(2,1)S(1)} %bitcast.166), channel_id=1, source_target_pairs={{0,96},{16,112},{32,0},{48,16},{64,32},{80,48},{96,64},{112,80},{1... | collective-permute-start | bytes 393224 | tf_op jit(solution)/shard_map/ppermute | solution.py:13
  139.6 6.3 %collective-permute-start.31 = (bf16[64,1024]{1,0:T(8,128)(2,1)S(1)}, bf16[64,1024]{1,0:T(8,128)(2,1)S(1)}, u32[]{:S(2)}, u32[]{:S(2)}) collective-permute-start(bf16[64,1024]{1,0:T(8,128)(2,1)S(1)} %bitcast.171), channel_id=1, source_target_pairs={{0,112},{16,96},{32,16},{48,0},{64,48},{80,32},{96,80},{112,64},{1... | collective-permute-start | bytes 393224 | tf_op jit(solution)/shard_map/ppermute | solution.py:13
  140.1 9.1 %collective-permute-start.32 = (bf16[64,1024]{1,0:T(8,128)(2,1)S(1)}, bf16[64,1024]{1,0:T(8,128)(2,1)S(1)}, u32[]{:S(2)}, u32[]{:S(2)}) collective-permute-start(bf16[64,1024]{1,0:T(8,128)(2,1)S(1)} %bitcast.169), channel_id=1, source_target_pairs={{0,16},{16,0},{32,48},{48,32},{64,80},{80,64},{96,112},{112,96},{1... | collective-permute-start | bytes 393224 | tf_op jit(solution)/shard_map/ppermute | solution.py:13

commit v2 on v0

v2 whole, which is shorter than its diff:
```python
import jax
import jax.numpy as jnp
from jax import lax
from jax.experimental import pallas as pl
from jax.experimental.pallas import tpu as pltpu
from jax.sharding import Mesh, PartitionSpec as P

F32, BF16, F16 = jnp.float32, jnp.bfloat16, jnp.float16
LIFT = 8.0
TILE = 256
AXES = ("x", "z_hi", "y", "z_lo", "core")
CHUNKS = ((0,), (1,), (3,), (2,))
ORDER = (
    (1, -1), (0, 0), (2, -1), (3, -1), (0, 2), (1, 0), (2, 0), (1, 2), (0, 3), (2, 2), (3, 0),
    (1, 3), (0, 4), (3, 2), (2, 3), (0, 5), (1, 4), (3, 3), (2, 4), (0, 6), (1, 5), (3, 4),
    (2, 5), (1, 6), (0, 7), (2, 6), (3, 5), (0, 8), (1, 7), (3, 6), (2, 7), (1, 8), (3, 7),
    (2, 8), (3, 8),
)


def permute(axes, sizes, move):
    def flat(place):
        index = 0
        for size, part in zip(sizes, place):
            index = index * size + part % size
        return index

    places = [()]
    for size in sizes:
        places = [p + (i,) for p in places for i in range(size)]
    pairs = [(flat(p), flat(move(*p))) for p in places]
    return lambda v: lax.ppermute(v, axes, pairs)


def lifted(v):
    return (v * LIFT).astype(F16)


def lowered(v):
    return v.astype(F32) * (1 / LIFT)


def multiply(rows, *refs):
    half = len(refs) // 2
    for weight, out in zip(refs[:half], refs[half:]):

        @pl.loop(0, weight.shape[1] // TILE)
        def _(i):
            columns = pl.ds(pl.multiple_of(i * TILE, TILE), TILE)
            out[:, columns] = jnp.dot(rows[...], weight[:, columns], preferred_element_type=F32)


def product(rows, *weights):
    vmem = pl.BlockSpec(memory_space=pltpu.VMEM)
    return pl.pallas_call(
        multiply,
        out_shape=[jax.ShapeDtypeStruct((rows.shape[0], w.shape[1]), F32) for w in weights],
        in_specs=[vmem] * (1 + len(weights)),
        out_specs=[vmem] * len(weights),
        compiler_params=pltpu.CompilerParams(vmem_limit_bytes=48 * 2**20),
        cost_estimate=pl.CostEstimate(flops=0, bytes_accessed=0, transcendentals=0),
    )(rows, *weights)


def per_device(tokens, gate_weight, up_weight, down_weight):
    z_hi, y, core = (lax.axis_index(a) for a in ("z_hi", "y", "core"))
    swap_core = permute(("core",), (2,), lambda c: (1 - c,))
    swap_z = permute(("z_lo",), (2,), lambda z: (1 - z,))
    swap_first = permute(("y", "core"), (4, 2), lambda y, c: (y ^ (3 if c else 1), c))
    swap_second = permute(("y", "core"), (4, 2), lambda y, c: (y ^ (1 if c else 3), c))
    along_x = {j: permute(("x",), (4,), lambda x, j=j: (x + j,)) for j in (1, 2, 3)}
    along_row = {
        (j, t): permute(("x", "z_hi"), (4, 2), lambda x, z, j=j, t=t: (x + j, z ^ t))
        for j in range(4)
        for t in range(2)
    }

    features = tokens.shape[1] // 16
    blocks = tokens.reshape(4, 16, features).transpose(1, 0, 2).reshape(1, 64, features)
    blocks = jnp.broadcast_to(blocks, (2, 64, features)).reshape(128, features)
    mine = lax.all_to_all(blocks, AXES[1:], split_axis=0, concat_axis=0, tiled=True)
    mine = mine.reshape(2, 4, 16, features)

    def ordered(half):
        own = lax.dynamic_index_in_dim(mine, half, 0, keepdims=False)
        first = jnp.where(half == 0, 1, 3)
        places = (y, y ^ (4 - first), y ^ first, y ^ 2)
        return [lax.dynamic_index_in_dim(own, p, 0, keepdims=False) for p in places]

    own = jnp.stack(ordered(1 - core) + ordered(core)).reshape(2, 4, 16, features)
    rows = {0: own}

    state = [{} for _ in CHUNKS]
    last = [own]
    arrived = {}

    def tie(*values):
        *values, last[0] = lax.optimization_barrier((*values, last[0]))
        return values

    def step(k, s):
        chunk, st = CHUNKS[k], state[k]
        n = 16 * len(chunk)
        if s == -1:
            for j in chunk:
                rows[j] = along_x[4 - j](*tie(own))
        elif s == 0:
            parts = tie(*[rows[j] for j in chunk])
            both = jnp.stack(parts, axis=2).reshape(8 * n, features)
            terms = product(both, gate_weight, up_weight)
            send = jnp.stack([lifted(v[: 4 * n]) for v in terms])
            send, *st["kept"] = tie(send, *[v[4 * n :] for v in terms])
            st["flight"] = swap_core(send)
        elif s == 2:
            (got,) = tie(st["flight"])
            total = [v + lowered(g) for v, g in zip(st["kept"], got)]
            send = jnp.stack([lifted(v[2 * n :]) for v in total])
            send, *st["kept"] = tie(send, *[v[: 2 * n] for v in total])
            st["flight"] = swap_first(send)
        elif s == 3:
            (got,) = tie(st["flight"])
            total = [v + lowered(g) for v, g in zip(st["kept"], got)]
            send = jnp.stack([lifted(v[n:]) for v in total])
            send, *st["kept"] = tie(send, *[v[:n] for v in total])
            st["flight"] = swap_second(send)
        elif s == 4:
            (got,) = tie(st["flight"])
            total = [v + lowered(g) for v, g in zip(st["kept"], got)]
            send, *st["kept"] = tie(jnp.stack([lifted(v) for v in total]), *total)
            st["flight"] = swap_z(send)
        elif s == 5:
            (got,) = tie(st["flight"])
            gate, up = [v + lowered(g) for v, g in zip(st["kept"], got)]
            (st["hidden"],) = tie((jax.nn.silu(gate) * up).astype(BF16))
            st["flight"] = swap_second(st["hidden"])
        elif s == 6:
            (got,) = tie(st["flight"])
            (st["hidden"],) = tie(jnp.concatenate((st["hidden"], got)))
            st["flight"] = swap_first(st["hidden"])
        elif s == 7:
            (got,) = tie(st["flight"])
            (st["hidden"],) = tie(jnp.concatenate((st["hidden"], got)))
            st["flight"] = swap_core(st["hidden"])
        elif s == 8:
            (got,) = tie(st["flight"])
            both = jnp.concatenate((got, st["hidden"]))
            (mixed,) = product(both, down_weight)
            mixed = mixed.reshape(2, 4, len(chunk), 16, -1)
            stays = z_hi == core
            same = jnp.where(stays, mixed[1], mixed[0])
            cross = jnp.where(stays, mixed[0], mixed[1])
            sends = []
            for i, j in enumerate(chunk):
                here = same[:, i].reshape(64, -1)
                sends.append(here if j == 0 else here.astype(BF16))
                sends.append(cross[:, i].reshape(64, -1).astype(BF16))
            sends = tie(*sends)
            for i, j in enumerate(chunk):
                here, there = sends[2 * i : 2 * i + 2]
                arrived[j, 0] = here if j == 0 else along_row[j, 0](here).astype(F32)
                arrived[j, 1] = along_row[j, 1](there).astype(F32)

    for k, s in ORDER:
        step(k, s)

    out = sum(arrived.values()).astype(BF16).reshape(4, 16, -1)
    first = jnp.where(z_hi == 0, 1, 3)
    where = jnp.stack([jnp.where(e == 0, 0, jnp.where(e == 2, 3, jnp.where(e == first, 2, 1))) for e in range(4)])
    blocks = [lax.dynamic_index_in_dim(out, where[y ^ p], 0, keepdims=False) for p in range(4)]
    return jnp.concatenate(blocks)


def solution(mesh):
    grid = Mesh(mesh.devices.reshape(4, 2, 4, 2, 2), AXES)
    row, col = AXES[:2], AXES[2:]
    placed = (P(AXES, None), P(col, row), P(col, row), P(row, col))
    return jax.shard_map(
        per_device, mesh=grid, in_specs=placed, out_specs=P(row, col), check_vma=False
    )
```

time: 366 us -> 189 us (0.52)
  waiting for transfers between devices: 306 us -> 55.7 us
  Pallas kernels: 0 us -> 63.2 us
  starting transfers between devices: 0.13 us -> 51.4 us
  matrix products: 22.4 us -> 0 us
  blocking collectives: 13.5 us -> 0 us
  between operations: 13.2 us -> 8.25 us
    reduce_scatter x2 -> x0, waiting for transfers between devices: 223 us -> none  [the longest x1 150 us: per_device(): lax.psum_scatter(jnp.concatenate((gate_term, up_term), axis=1), 'col', sc...]
    all_gather x2 -> x0, waiting for transfers between devices: 82.2 us -> none  [the longest x1 46.2 us: per_device(): features = lax.all_gather(split_rows, 'row', axis=0, tiled=True)]
    pallas_call x0 -> x8, Pallas kernels: none -> 63.2 us  [product(): pl.pallas_call(multiply, out_shape=[jax.ShapeDtypeStruct((rows.shape[0],...]
    ppermute x0 -> x38, waiting for transfers between devices: none -> 47 us  [permute(): return lambda v: lax.ppermute(v, axes, pairs)]
    ppermute x0 -> x38, starting transfers between devices: none -> 41.8 us  [permute(): return lambda v: lax.ppermute(v, axes, pairs)]
    dot_general x3 -> x0, matrix products: 22.4 us -> none  [the longest x1 9.01 us: per_device(): jnp.dot(selected, down_weight, preferred_element_type=jnp.float32)]
    all_to_all x1 -> x0, blocking collectives: 13.5 us -> none  [per_device(): lax.all_to_all(tokens, 'col', split_axis=1, concat_axis=0, tiled=True)]
    all_to_all x0 -> x1, starting transfers between devices: none -> 9.6 us  [per_device(): lax.all_to_all(blocks, AXES[1:], split_axis=0, concat_axis=0, tiled=True)]
  transfers between devices with their start and end apart: 4 -> 39, of which waited for: 4 -> 13; matrix products, arithmetic and copies ran while one was open for 0% -> 3% of each run, Pallas kernels for 0% -> 22%
where the time goes in v2:
time: 189 us
  Pallas kernels  63.2 us (33%)
  waiting for transfers between devices  55.7 us (29%)
  starting transfers between devices  51.4 us (27%)
  between operations  8.25 us (4%)
  other arithmetic  7.47 us (4%)
  local copies, waits for them, and re-layouts  2.64 us (1%)
    pallas_call x8, Pallas kernels, product(): pl.pallas_call(multiply, out_shape=[jax.ShapeDtypeStruct((rows.shape[0],...  63.2 us
    ppermute x38, waiting for transfers between devices, permute(): return lambda v: lax.ppermute(v, axes, pairs)  47 us
    ppermute x38, starting transfers between devices, permute(): return lambda v: lax.ppermute(v, axes, pairs)  41.8 us
    all_to_all x1, starting transfers between devices, per_device(): lax.all_to_all(blocks, AXES[1:], split_axis=0, concat_axis=0, tiled=True)  9.6 us
    all_to_all x1, waiting for transfers between devices, per_device(): lax.all_to_all(blocks, AXES[1:], split_axis=0, concat_axis=0, tiled=True)  8.79 us
  transfers between devices with their start and end apart: 39, of which 13 were waited for; matrix products, arithmetic and copies ran while one was open for 3% of the time, Pallas kernels for 22%

profile of v2, /device:TPU:1, one launch (start us, length us, event | category | flops | bytes accessed | tf_op | source)
XLA Modules:
  0.0 188.7 jit_solution(11656338381450892342)
XLA Ops:
  0.0 0.9 broadcast_in_dim.7
  1.0 0.8 all_to_all.6
  1.8 9.6 %all-to-all-start = ((bf16[32,4,1024]{2,1,0:T(4,128)(2,1)}), bf16[32,4,1024]{2,1,0:T(4,128)(2,1)S(1)}, u32[]{:S(2)}, u32[]{:S(2)}) async-start(bf16[32,4,1024]{2,1,0:T(4,128)(2,1)} %all_to_all.6), calls=%async_computation | async-start | bytes 524288 | tf_op jit(solution)/shard_map/all_to_all | solution.py:81
  11.5 8.8 %all-to-all-done = bf16[32,4,1024]{2,1,0:T(4,128)(2,1)S(1)} async-done(((bf16[32,4,1024]{2,1,0:T(4,128)(2,1)}), bf16[32,4,1024]{2,1,0:T(4,128)(2,1)S(1)}, u32[]{:S(2)}, u32[]{:S(2)}) %all-to-all-start) | async-done | bytes 262176 | tf_op jit(solution)/shard_map/all_to_all | solution.py:81
  20.5 11.1 %shard_map.46 = (f32[128,3328]{1,0:T(8,128)S(1)}, f32[128,3328]{1,0:T(8,128)S(1)}) custom-call(bf16[128,1024]{1,0:T(8,128)(2,1)S(1)} %bitcast.199, bf16[1024,3328]{1,0:T(8,128)(2,1)} %refs_0_.11, bf16[1024,3328]{1,0:T(8,128)(2,1)} %refs_1_.7), custom_call_target="tpu_custom_call" | custom-call | tf_op jit(solution)/shard_map/pallas_call | solution.py:55
  31.8 1.1 pad_maximum_fusion
  33.0 0.9 collective-permute-start
  33.9 2.5 %collective-permute-start.2 = (bf16[2,4,16,1024]{3,2,1,0:T(8,128)(2,1)S(1)}, bf16[2,4,16,1024]{3,2,1,0:T(8,128)(2,1)S(1)}, u32[]{:S(2)}, u32[]{:S(2)}) collective-permute-start(bf16[2,4,16,1024]{3,2,1,0:T(8,128)(2,1)S(1)} %bitcast.200), channel_id=1, source_target_pairs={{0,96},{32,0},{64,32},{96,64},{1,97},{33,1},{65,33},{97,65},{2,98}... | collective-permute-start | bytes 786440 | tf_op jit(solution)/shard_map/ppermute | solution.py:32
  36.4 1.7 collective-permute-start.7
  38.6 9.0 %collective-permute-done.2 = bf16[2,4,16,1024]{3,2,1,0:T(8,128)(2,1)S(1)} collective-permute-done((bf16[2,4,16,1024]{3,2,1,0:T(8,128)(2,1)S(1)}, bf16[2,4,16,1024]{3,2,1,0:T(8,128)(2,1)S(1)}, u32[]{:S(2)}, u32[]{:S(2)}) %collective-permute-start.2) | collective-permute-done | bytes 262176 | tf_op jit(solution)/shard_map/ppermute | solution.py:32
  47.6 11.1 %shard_map.47 = (f32[128,3328]{1,0:T(8,128)S(1)}, f32[128,3328]{1,0:T(8,128)S(1)}) custom-call(bf16[128,1024]{1,0:T(8,128)(2,1)S(1)} %bitcast.205, bf16[1024,3328]{1,0:T(8,128)(2,1)} %refs_0_.11, bf16[1024,3328]{1,0:T(8,128)(2,1)} %refs_1_.7), custom_call_target="tpu_custom_call" | custom-call | tf_op jit(solution)/shard_map/pallas_call | solution.py:55
  59.2 11.1 %shard_map.48 = (f32[128,3328]{1,0:T(8,128)S(1)}, f32[128,3328]{1,0:T(8,128)S(1)}) custom-call(bf16[128,1024]{1,0:T(8,128)(2,1)S(1)} %bitcast.204, bf16[1024,3328]{1,0:T(8,128)(2,1)} %refs_0_.11, bf16[1024,3328]{1,0:T(8,128)(2,1)} %refs_1_.7), custom_call_target="tpu_custom_call" | custom-call | tf_op jit(solution)/shard_map/pallas_call | solution.py:55
  70.4 1.0 collective-permute-start.3
  72.6 0.9 collective-permute-done.3
  73.9 6.1 %collective-permute-done.1 = f16[2,32,3328]{2,1,0:T(8,128)(2,1)S(1)} collective-permute-done((f16[2,32,3328]{2,1,0:T(8,128)(2,1)S(1)}, f16[2,32,3328]{2,1,0:T(8,128)(2,1)S(1)}, u32[]{:S(2)}, u32[]{:S(2)}) %collective-permute-start.1) | collective-permute-done | bytes 426016 | tf_op jit(solution)/shard_map/ppermute | solution.py:32
  80.7 11.1 %shard_map.49 = (f32[128,3328]{1,0:T(8,128)S(1)}, f32[128,3328]{1,0:T(8,128)S(1)}) custom-call(bf16[128,1024]{1,0:T(8,128)(2,1)S(1)} %bitcast.203, bf16[1024,3328]{1,0:T(8,128)(2,1)} %refs_0_.11, bf16[1024,3328]{1,0:T(8,128)(2,1)} %refs_1_.7), custom_call_target="tpu_custom_call" | custom-call | tf_op jit(solution)/shard_map/pallas_call | solution.py:55
  92.7 1.0 collective-permute-start.11
  93.7 2.4 %collective-permute-start.10 = (f16[2,32,3328]{2,1,0:T(8,128)(2,1)S(1)}, f16[2,32,3328]{2,1,0:T(8,128)(2,1)S(1)}, u32[]{:S(2)}, u32[]{:S(2)}) collective-permute-start(f16[2,32,3328]{2,1,0:T(8,128)(2,1)S(1)} %pad_maximum_fusion.10), channel_id=1, source_target_pairs={{0,4},{1,13},{4,0},{5,9},{8,12},{9,5},{12,8},{13,1},{2,6},{3,15},{... | collective-permute-start | bytes 1277960 | tf_op jit(solution)/shard_map/ppermute | solution.py:32
  96.1 6.6 %collective-permute-done.6 = f16[2,32,3328]{2,1,0:T(8,128)(2,1)S(1)} collective-permute-done((f16[2,32,3328]{2,1,0:T(8,128)(2,1)S(1)}, f16[2,32,3328]{2,1,0:T(8,128)(2,1)S(1)}, u32[]{:S(2)}, u32[]{:S(2)}) %collective-permute-start.6) | collective-permute-done | bytes 426016 | tf_op jit(solution)/shard_map/ppermute | solution.py:32
  103.8 3.4 %collective-permute-done.10 = f16[2,32,3328]{2,1,0:T(8,128)(2,1)S(1)} collective-permute-done((f16[2,32,3328]{2,1,0:T(8,128)(2,1)S(1)}, f16[2,32,3328]{2,1,0:T(8,128)(2,1)S(1)}, u32[]{:S(2)}, u32[]{:S(2)}) %collective-permute-start.10) | collective-permute-done | bytes 426016 | tf_op jit(solution)/shard_map/ppermute | solution.py:32
  107.4 2.7 %collective-permute-done.9 = f16[2,16,3328]{2,1,0:T(8,128)(2,1)S(1)} collective-permute-done((f16[2,16,3328]{2,1,0:T(8,128)(2,1)S(1)}, f16[2,16,3328]{2,1,0:T(8,128)(2,1)S(1)}, u32[]{:S(2)}, u32[]{:S(2)}) %collective-permute-start.9) | collective-permute-done | bytes 213024 | tf_op jit(solution)/shard_map/ppermute | solution.py:32
  111.1 1.1 collective-permute-start.13
  112.2 1.6 collective-permute-done.12
  114.4 1.8 collective-permute-done.17
  116.3 2.3 %collective-permute-start.18 = (bf16[16,3328]{1,0:T(8,128)(2,1)S(1)}, bf16[16,3328]{1,0:T(8,128)(2,1)S(1)}, u32[]{:S(2)}, u32[]{:S(2)}) collective-permute-start(bf16[16,3328]{1,0:T(8,128)(2,1)S(1)} %fusion.37), channel_id=1, source_target_pairs={{0,12},{1,5},{4,8},{5,1},{8,4},{9,13},{12,0},{13,9},{2,14},{3,7},{... | collective-permute-start | bytes 319496 | tf_op jit(solution)/shard_map/ppermute | solution.py:32
  118.5 7.3 %collective-permute-done.16 = bf16[32,3328]{1,0:T(8,128)(2,1)S(1)} collective-permute-done((bf16[32,3328]{1,0:T(8,128)(2,1)S(1)}, bf16[32,3328]{1,0:T(8,128)(2,1)S(1)}, u32[]{:S(2)}, u32[]{:S(2)}) %collective-permute-start.16) | collective-permute-done | bytes 213024 | tf_op jit(solution)/shard_map/ppermute | solution.py:32
  126.0 1.1 collective-permute-start.25
  127.4 1.3 collective-permute-start.19
  129.0 3.0 %collective-permute-done.25 = bf16[32,3328]{1,0:T(8,128)(2,1)S(1)} collective-permute-done((bf16[32,3328]{1,0:T(8,128)(2,1)S(1)}, bf16[32,3328]{1,0:T(8,128)(2,1)S(1)}, u32[]{:S(2)}, u32[]{:S(2)}) %collective-permute-start.25) | collective-permute-done | bytes 213024 | tf_op jit(solution)/shard_map/ppermute | solution.py:32
  132.0 0.9 collective-permute-start.26
  132.9 1.8 collective-permute-done.19
  135.1 0.8 collective-permute-start.22
  135.9 4.7 %shard_map.50 = f32[128,1024]{1,0:T(8,128)S(1)} custom-call(bf16[128,3328]{1,0:T(8,128)(2,1)S(1)} %pad_maximum_fusion.4.rows, bf16[3328,1024]{1,0:T(8,128)(2,1)} %refs_0_.15), custom_call_target="tpu_custom_call" | custom-call | tf_op jit(solution)/shard_map/pallas_call | solution.py:55
  140.7 1.2 collective-permute-start.24
  142.0 1.7 collective-permute-start.29
  143.8 0.9 collective-permute-start.33
  144.8 4.7 %shard_map.51 = f32[128,1024]{1,0:T(8,128)S(1)} custom-call(bf16[128,3328]{1,0:T(8,128)(2,1)S(1)} %pad_maximum_fusion.5.rows, bf16[3328,1024]{1,0:T(8,128)(2,1)} %refs_0_.15), custom_call_target="tpu_custom_call" | custom-call | tf_op jit(solution)/shard_map/pallas_call | solution.py:55
  149.7 1.1 collective-permute-start.34
  150.9 2.1 %collective-permute-start.30 = (bf16[64,3328]{1,0:T(8,128)(2,1)S(1)}, bf16[64,3328]{1,0:T(8,128)(2,1)S(1)}, u32[]{:S(2)}, u32[]{:S(2)}) collective-permute-start(bf16[64,3328]{1,0:T(8,128)(2,1)S(1)} %pad_maximum_fusion.14), channel_id=1, source_target_pairs={{0,1},{1,0},{2,3},{3,2},{4,5},{5,4},{6,7},{7,6},{8,9},{9,8},{10,11... | collective-permute-start | bytes 1277960 | tf_op jit(solution)/shard_map/ppermute | solution.py:32
  153.0 2.7 %collective-permute-done.34 = bf16[32,3328]{1,0:T(8,128)(2,1)S(1)} collective-permute-done((bf16[32,3328]{1,0:T(8,128)(2,1)S(1)}, bf16[32,3328]{1,0:T(8,128)(2,1)S(1)}, u32[]{:S(2)}, u32[]{:S(2)}) %collective-permute-start.34) | collective-permute-done | bytes 213024 | tf_op jit(solution)/shard_map/ppermute | solution.py:32
  155.7 1.7 collective-permute-start.35
  157.5 4.7 %shard_map.52 = f32[128,1024]{1,0:T(8,128)S(1)} custom-call(bf16[128,3328]{1,0:T(8,128)(2,1)S(1)} %pad_maximum_fusion.6.rows, bf16[3328,1024]{1,0:T(8,128)(2,1)} %refs_0_.15), custom_call_target="tpu_custom_call" | custom-call | tf_op jit(solution)/shard_map/pallas_call | solution.py:55
  162.2 5.0 %collective-permute-start.31 = (bf16[64,1024]{1,0:T(8,128)(2,1)S(1)}, bf16[64,1024]{1,0:T(8,128)(2,1)S(1)}, u32[]{:S(2)}, u32[]{:S(2)}) collective-permute-start(bf16[64,1024]{1,0:T(8,128)(2,1)S(1)} %get-tuple-element.304), channel_id=1, source_target_pairs={{0,96},{16,112},{32,0},{48,16},{64,32},{80,48},{96,64},{112,80},{1... | collective-permute-start | bytes 393224 | tf_op jit(solution)/shard_map/ppermute | solution.py:32
  167.3 2.5 %collective-permute-start.32 = (bf16[64,1024]{1,0:T(8,128)(2,1)S(1)}, bf16[64,1024]{1,0:T(8,128)(2,1)S(1)}, u32[]{:S(2)}, u32[]{:S(2)}) collective-permute-start(bf16[64,1024]{1,0:T(8,128)(2,1)S(1)} %get-tuple-element.305), channel_id=1, source_target_pairs={{0,112},{16,96},{32,16},{48,0},{64,48},{80,32},{96,80},{112,64},{1... | collective-permute-start | bytes 393224 | tf_op jit(solution)/shard_map/ppermute | solution.py:32
  169.9 4.7 %shard_map.53 = f32[128,1024]{1,0:T(8,128)S(1)} custom-call(bf16[128,3328]{1,0:T(8,128)(2,1)S(1)} %pad_maximum_fusion.7.rows, bf16[3328,1024]{1,0:T(8,128)(2,1)} %refs_0_.15), custom_call_target="tpu_custom_call" | custom-call | tf_op jit(solution)/shard_map/pallas_call | solution.py:55
  174.6 1.6 collective-permute-start.36
  176.1 3.5 %collective-permute-start.37 = (bf16[64,1024]{1,0:T(8,128)(2,1)S(1)}, bf16[64,1024]{1,0:T(8,128)(2,1)S(1)}, u32[]{:S(2)}, u32[]{:S(2)}) collective-permute-start(bf16[64,1024]{1,0:T(8,128)(2,1)S(1)} %get-tuple-element.308), channel_id=1, source_target_pairs={{0,80},{16,64},{32,112},{48,96},{64,16},{80,0},{96,48},{112,32},{1... | collective-permute-start | bytes 393224 | tf_op jit(solution)/shard_map/ppermute | solution.py:32
  188.0 0.7 pad_maximum_fusion.28
  (127 shorter events, 9.9 us)
Async XLA Ops:
  1.8 18.5 %all-to-all-start = ((bf16[32,4,1024]{2,1,0:T(4,128)(2,1)}), bf16[32,4,1024]{2,1,0:T(4,128)(2,1)S(1)}, u32[]{:S(2)}, u32[]{:S(2)}) async-start(bf16[32,4,1024]{2,1,0:T(4,128)(2,1)} %all_to_all.6), calls=%async_computation | async-start | bytes 524288 | tf_op jit(solution)/shard_map/all_to_all | solution.py:81
  33.0 5.2 %collective-permute-start = (f16[2,64,3328]{2,1,0:T(8,128)(2,1)}, f16[2,64,3328]{2,1,0:T(8,128)(2,1)S(1)}, u32[]{:S(2)}, u32[]{:S(2)}) collective-permute-start(f16[2,64,3328]{2,1,0:T(8,128)(2,1)} %pad_maximum_fusion), channel_id=1, source_target_pairs={{0,1},{1,0},{2,3},{3,2},{4,5},{5,4},{6,7},{7,6},{8,9},{9,8},{10,11... | collective-permute-start | bytes 2555912 | tf_op jit(solution)/shard_map/ppermute | solution.py:32
  33.9 13.7 %collective-permute-start.2 = (bf16[2,4,16,1024]{3,2,1,0:T(8,128)(2,1)S(1)}, bf16[2,4,16,1024]{3,2,1,0:T(8,128)(2,1)S(1)}, u32[]{:S(2)}, u32[]{:S(2)}) collective-permute-start(bf16[2,4,16,1024]{3,2,1,0:T(8,128)(2,1)S(1)} %bitcast.200), channel_id=1, source_target_pairs={{0,96},{32,0},{64,32},{96,64},{1,97},{33,1},{65,33},{97,65},{2,98}... | collective-permute-start | bytes 786440 | tf_op jit(solution)/shard_map/ppermute | solution.py:32
  36.4 22.8 %collective-permute-start.4 = (bf16[2,4,16,1024]{3,2,1,0:T(8,128)(2,1)S(1)}, bf16[2,4,16,1024]{3,2,1,0:T(8,128)(2,1)S(1)}, u32[]{:S(2)}, u32[]{:S(2)}) collective-permute-start(bf16[2,4,16,1024]{3,2,1,0:T(8,128)(2,1)S(1)} %bitcast.201), channel_id=1, source_target_pairs={{0,32},{32,64},{64,96},{96,0},{1,33},{33,65},{65,97},{97,1},{2,34}... | collective-permute-start | bytes 786440 | tf_op jit(solution)/shard_map/ppermute | solution.py:32
  36.4 44.3 %collective-permute-start.7 = (bf16[2,4,16,1024]{3,2,1,0:T(8,128)(2,1)S(1)}, bf16[2,4,16,1024]{3,2,1,0:T(8,128)(2,1)S(1)}, u32[]{:S(2)}, u32[]{:S(2)}) collective-permute-start(bf16[2,4,16,1024]{3,2,1,0:T(8,128)(2,1)S(1)} %bitcast.202), channel_id=1, source_target_pairs={{0,64},{32,96},{64,0},{96,32},{1,65},{33,97},{65,1},{97,33},{2,66}... | collective-permute-start | bytes 786440 | tf_op jit(solution)/shard_map/ppermute | solution.py:32
  70.4 3.1 %collective-permute-start.3 = (f16[2,64,3328]{2,1,0:T(8,128)(2,1)S(1)}, f16[2,64,3328]{2,1,0:T(8,128)(2,1)S(1)}, u32[]{:S(2)}, u32[]{:S(2)}) collective-permute-start(f16[2,64,3328]{2,1,0:T(8,128)(2,1)S(1)} %pad_maximum_fusion.1), channel_id=1, source_target_pairs={{0,1},{1,0},{2,3},{3,2},{4,5},{5,4},{6,7},{7,6},{8,9},{9,8},{10,11... | collective-permute-start | bytes 2555912 | tf_op jit(solution)/shard_map/ppermute | solution.py:32
  71.8 8.3 %collective-permute-start.1 = (f16[2,32,3328]{2,1,0:T(8,128)(2,1)S(1)}, f16[2,32,3328]{2,1,0:T(8,128)(2,1)S(1)}, u32[]{:S(2)}, u32[]{:S(2)}) collective-permute-start(f16[2,32,3328]{2,1,0:T(8,128)(2,1)S(1)} %pad_maximum_fusion.8), channel_id=1, source_target_pairs={{0,4},{1,13},{4,0},{5,9},{8,12},{9,5},{12,8},{13,1},{2,6},{3,15},{... | collective-permute-start | bytes 1277960 | tf_op jit(solution)/shard_map/ppermute | solution.py:32
  72.1 8.2 %collective-permute-start.8 = (f16[2,64,3328]{2,1,0:T(8,128)(2,1)S(1)}, f16[2,64,3328]{2,1,0:T(8,128)(2,1)S(1)}, u32[]{:S(2)}, u32[]{:S(2)}) collective-permute-start(f16[2,64,3328]{2,1,0:T(8,128)(2,1)S(1)} %pad_maximum_fusion.2), channel_id=1, source_target_pairs={{0,1},{1,0},{2,3},{3,2},{4,5},{5,4},{6,7},{7,6},{8,9},{9,8},{10,11... | collective-permute-start | bytes 2555912 | tf_op jit(solution)/shard_map/ppermute | solution.py:32
  92.1 10.6 %collective-permute-start.6 = (f16[2,32,3328]{2,1,0:T(8,128)(2,1)S(1)}, f16[2,32,3328]{2,1,0:T(8,128)(2,1)S(1)}, u32[]{:S(2)}, u32[]{:S(2)}) collective-permute-start(f16[2,32,3328]{2,1,0:T(8,128)(2,1)S(1)} %pad_maximum_fusion.9), channel_id=1, source_target_pairs={{0,4},{1,13},{4,0},{5,9},{8,12},{9,5},{12,8},{13,1},{2,6},{3,15},{... | collective-permute-start | bytes 1277960 | tf_op jit(solution)/shard_map/ppermute | solution.py:32
  92.6 10.3 %collective-permute-start.5 = (f16[2,16,3328]{2,1,0:T(8,128)(2,1)S(1)}, f16[2,16,3328]{2,1,0:T(8,128)(2,1)S(1)}, u32[]{:S(2)}, u32[]{:S(2)}) collective-permute-start(f16[2,16,3328]{2,1,0:T(8,128)(2,1)S(1)} %pad_maximum_fusion.16), channel_id=1, source_target_pairs={{0,12},{1,5},{4,8},{5,1},{8,4},{9,13},{12,0},{13,9},{2,14},{3,7},{... | collective-permute-start | bytes 638984 | tf_op jit(solution)/shard_map/ppermute | solution.py:32
  92.7 10.7 %collective-permute-start.11 = (f16[2,64,3328]{2,1,0:T(8,128)(2,1)S(1)}, f16[2,64,3328]{2,1,0:T(8,128)(2,1)S(1)}, u32[]{:S(2)}, u32[]{:S(2)}) collective-permute-start(f16[2,64,3328]{2,1,0:T(8,128)(2,1)S(1)} %pad_maximum_fusion.3), channel_id=1, source_target_pairs={{0,1},{1,0},{2,3},{3,2},{4,5},{5,4},{6,7},{7,6},{8,9},{9,8},{10,11... | collective-permute-start | bytes 2555912 | tf_op jit(solution)/shard_map/ppermute | solution.py:32
  93.7 13.5 %collective-permute-start.10 = (f16[2,32,3328]{2,1,0:T(8,128)(2,1)S(1)}, f16[2,32,3328]{2,1,0:T(8,128)(2,1)S(1)}, u32[]{:S(2)}, u32[]{:S(2)}) collective-permute-start(f16[2,32,3328]{2,1,0:T(8,128)(2,1)S(1)} %pad_maximum_fusion.10), channel_id=1, source_target_pairs={{0,4},{1,13},{4,0},{5,9},{8,12},{9,5},{12,8},{13,1},{2,6},{3,15},{... | collective-permute-start | bytes 1277960 | tf_op jit(solution)/shard_map/ppermute | solution.py:32
  103.0 7.1 %collective-permute-start.9 = (f16[2,16,3328]{2,1,0:T(8,128)(2,1)S(1)}, f16[2,16,3328]{2,1,0:T(8,128)(2,1)S(1)}, u32[]{:S(2)}, u32[]{:S(2)}) collective-permute-start(f16[2,16,3328]{2,1,0:T(8,128)(2,1)S(1)} %pad_maximum_fusion.18), channel_id=1, source_target_pairs={{0,2},{2,0},{1,3},{3,1},{4,6},{6,4},{5,7},{7,5},{8,10},{10,8},{9,1... | collective-permute-start | bytes 638984 | tf_op jit(solution)/shard_map/ppermute | solution.py:32
  103.3 7.0 %collective-permute-start.15 = (f16[2,16,3328]{2,1,0:T(8,128)(2,1)S(1)}, f16[2,16,3328]{2,1,0:T(8,128)(2,1)S(1)}, u32[]{:S(2)}, u32[]{:S(2)}) collective-permute-start(f16[2,16,3328]{2,1,0:T(8,128)(2,1)S(1)} %pad_maximum_fusion.17), channel_id=1, source_target_pairs={{0,12},{1,5},{4,8},{5,1},{8,4},{9,13},{12,0},{13,9},{2,14},{3,7},{... | collective-permute-start | bytes 638984 | tf_op jit(solution)/shard_map/ppermute | solution.py:32
  110.2 3.6 %collective-permute-start.12 = (bf16[16,3328]{1,0:T(8,128)(2,1)S(1)}, bf16[16,3328]{1,0:T(8,128)(2,1)S(1)}, u32[]{:S(2)}, u32[]{:S(2)}) collective-permute-start(bf16[16,3328]{1,0:T(8,128)(2,1)S(1)} %fusion.39), channel_id=1, source_target_pairs={{0,12},{1,5},{4,8},{5,1},{8,4},{9,13},{12,0},{13,9},{2,14},{3,7},{... | collective-permute-start | bytes 319496 | tf_op jit(solution)/shard_map/ppermute | solution.py:32
  110.5 5.7 %collective-permute-start.17 = (f16[2,16,3328]{2,1,0:T(8,128)(2,1)S(1)}, f16[2,16,3328]{2,1,0:T(8,128)(2,1)S(1)}, u32[]{:S(2)}, u32[]{:S(2)}) collective-permute-start(f16[2,16,3328]{2,1,0:T(8,128)(2,1)S(1)} %pad_maximum_fusion.20), channel_id=1, source_target_pairs={{0,2},{2,0},{1,3},{3,1},{4,6},{6,4},{5,7},{7,5},{8,10},{10,8},{9,1... | collective-permute-start | bytes 638984 | tf_op jit(solution)/shard_map/ppermute | solution.py:32
  110.8 16.3 %collective-permute-start.14 = (f16[2,32,3328]{2,1,0:T(8,128)(2,1)S(1)}, f16[2,32,3328]{2,1,0:T(8,128)(2,1)S(1)}, u32[]{:S(2)}, u32[]{:S(2)}) collective-permute-start(f16[2,32,3328]{2,1,0:T(8,128)(2,1)S(1)} %pad_maximum_fusion.11), channel_id=1, source_target_pairs={{0,4},{1,13},{4,0},{5,9},{8,12},{9,5},{12,8},{13,1},{2,6},{3,15},{... | collective-permute-start | bytes 1277960 | tf_op jit(solution)/shard_map/ppermute | solution.py:32
  111.1 16.1 %collective-permute-start.13 = (f16[2,16,3328]{2,1,0:T(8,128)(2,1)S(1)}, f16[2,16,3328]{2,1,0:T(8,128)(2,1)S(1)}, u32[]{:S(2)}, u32[]{:S(2)}) collective-permute-start(f16[2,16,3328]{2,1,0:T(8,128)(2,1)S(1)} %pad_maximum_fusion.19), channel_id=1, source_target_pairs={{0,12},{1,5},{4,8},{5,1},{8,4},{9,13},{12,0},{13,9},{2,14},{3,7},{... | collective-permute-start | bytes 638984 | tf_op jit(solution)/shard_map/ppermute | solution.py:32
  113.9 11.9 %collective-permute-start.16 = (bf16[32,3328]{1,0:T(8,128)(2,1)S(1)}, bf16[32,3328]{1,0:T(8,128)(2,1)S(1)}, u32[]{:S(2)}, u32[]{:S(2)}) collective-permute-start(bf16[32,3328]{1,0:T(8,128)(2,1)S(1)} %pad_maximum_fusion.23), channel_id=1, source_target_pairs={{0,4},{1,13},{4,0},{5,9},{8,12},{9,5},{12,8},{13,1},{2,6},{3,15},{... | collective-permute-start | bytes 638984 | tf_op jit(solution)/shard_map/ppermute | solution.py:32
  116.3 9.7 %collective-permute-start.18 = (bf16[16,3328]{1,0:T(8,128)(2,1)S(1)}, bf16[16,3328]{1,0:T(8,128)(2,1)S(1)}, u32[]{:S(2)}, u32[]{:S(2)}) collective-permute-start(bf16[16,3328]{1,0:T(8,128)(2,1)S(1)} %fusion.37), channel_id=1, source_target_pairs={{0,12},{1,5},{4,8},{5,1},{8,4},{9,13},{12,0},{13,9},{2,14},{3,7},{... | collective-permute-start | bytes 319496 | tf_op jit(solution)/shard_map/ppermute | solution.py:32
  125.8 10.1 %collective-permute-start.21 = (bf16[64,3328]{1,0:T(8,128)(2,1)S(1)}, bf16[64,3328]{1,0:T(8,128)(2,1)S(1)}, u32[]{:S(2)}, u32[]{:S(2)}) collective-permute-start(bf16[64,3328]{1,0:T(8,128)(2,1)S(1)} %pad_maximum_fusion.12), channel_id=1, source_target_pairs={{0,1},{1,0},{2,3},{3,2},{4,5},{5,4},{6,7},{7,6},{8,9},{9,8},{10,11... | collective-permute-start | bytes 1277960 | tf_op jit(solution)/shard_map/ppermute | solution.py:32
  126.0 6.0 %collective-permute-start.25 = (bf16[32,3328]{1,0:T(8,128)(2,1)S(1)}, bf16[32,3328]{1,0:T(8,128)(2,1)S(1)}, u32[]{:S(2)}, u32[]{:S(2)}) collective-permute-start(bf16[32,3328]{1,0:T(8,128)(2,1)S(1)} %pad_maximum_fusion.24), channel_id=1, source_target_pairs={{0,4},{1,13},{4,0},{5,9},{8,12},{9,5},{12,8},{13,1},{2,6},{3,15},{... | collective-permute-start | bytes 638984 | tf_op jit(solution)/shard_map/ppermute | solution.py:32
  127.4 7.3 %collective-permute-start.19 = (f16[2,16,3328]{2,1,0:T(8,128)(2,1)S(1)}, f16[2,16,3328]{2,1,0:T(8,128)(2,1)S(1)}, u32[]{:S(2)}, u32[]{:S(2)}) collective-permute-start(f16[2,16,3328]{2,1,0:T(8,128)(2,1)S(1)} %pad_maximum_fusion.22), channel_id=1, source_target_pairs={{0,2},{2,0},{1,3},{3,1},{4,6},{6,4},{5,7},{7,5},{8,10},{10,8},{9,1... | collective-permute-start | bytes 638984 | tf_op jit(solution)/shard_map/ppermute | solution.py:32
  128.8 6.2 %collective-permute-start.20 = (f16[2,16,3328]{2,1,0:T(8,128)(2,1)S(1)}, f16[2,16,3328]{2,1,0:T(8,128)(2,1)S(1)}, u32[]{:S(2)}, u32[]{:S(2)}) collective-permute-start(f16[2,16,3328]{2,1,0:T(8,128)(2,1)S(1)} %pad_maximum_fusion.21), channel_id=1, source_target_pairs={{0,12},{1,5},{4,8},{5,1},{8,4},{9,13},{12,0},{13,9},{2,14},{3,7},{... | collective-permute-start | bytes 638984 | tf_op jit(solution)/shard_map/ppermute | solution.py:32
  132.0 12.7 %collective-permute-start.26 = (bf16[64,3328]{1,0:T(8,128)(2,1)S(1)}, bf16[64,3328]{1,0:T(8,128)(2,1)S(1)}, u32[]{:S(2)}, u32[]{:S(2)}) collective-permute-start(bf16[64,3328]{1,0:T(8,128)(2,1)S(1)} %pad_maximum_fusion.13), channel_id=1, source_target_pairs={{0,1},{1,0},{2,3},{3,2},{4,5},{5,4},{6,7},{7,6},{8,9},{9,8},{10,11... | collective-permute-start | bytes 1277960 | tf_op jit(solution)/shard_map/ppermute | solution.py:32
  134.9 7.1 %collective-permute-start.23 = (bf16[16,3328]{1,0:T(8,128)(2,1)S(1)}, bf16[16,3328]{1,0:T(8,128)(2,1)S(1)}, u32[]{:S(2)}, u32[]{:S(2)}) collective-permute-start(bf16[16,3328]{1,0:T(8,128)(2,1)S(1)} %fusion.35), channel_id=1, source_target_pairs={{0,12},{1,5},{4,8},{5,1},{8,4},{9,13},{12,0},{13,9},{2,14},{3,7},{... | collective-permute-start | bytes 319496 | tf_op jit(solution)/shard_map/ppermute | solution.py:32
  135.1 8.5 %collective-permute-start.22 = (f16[2,16,3328]{2,1,0:T(8,128)(2,1)S(1)}, f16[2,16,3328]{2,1,0:T(8,128)(2,1)S(1)}, u32[]{:S(2)}, u32[]{:S(2)}) collective-permute-start(f16[2,16,3328]{2,1,0:T(8,128)(2,1)S(1)} %pad_maximum_fusion.26), channel_id=1, source_target_pairs={{0,2},{2,0},{1,3},{3,1},{4,6},{6,4},{5,7},{7,5},{8,10},{10,8},{9,1... | collective-permute-start | bytes 638984 | tf_op jit(solution)/shard_map/ppermute | solution.py:32
  140.7 33.9 %collective-permute-start.24 = (bf16[64,1024]{1,0:T(8,128)(2,1)S(1)}, bf16[64,1024]{1,0:T(8,128)(2,1)S(1)}, u32[]{:S(2)}, u32[]{:S(2)}) collective-permute-start(bf16[64,1024]{1,0:T(8,128)(2,1)S(1)} %select_convert_fusion.6), channel_id=1, source_target_pairs={{0,16},{16,0},{32,48},{48,32},{64,80},{80,64},{96,112},{112,96},{1... | collective-permute-start | bytes 393224 | tf_op jit(solution)/shard_map/ppermute | solution.py:32
  142.0 8.9 %collective-permute-start.29 = (bf16[32,3328]{1,0:T(8,128)(2,1)S(1)}, bf16[32,3328]{1,0:T(8,128)(2,1)S(1)}, u32[]{:S(2)}, u32[]{:S(2)}) collective-permute-start(bf16[32,3328]{1,0:T(8,128)(2,1)S(1)} %pad_maximum_fusion.25), channel_id=1, source_target_pairs={{0,4},{1,13},{4,0},{5,9},{8,12},{9,5},{12,8},{13,1},{2,6},{3,15},{... | collective-permute-start | bytes 638984 | tf_op jit(solution)/shard_map/ppermute | solution.py:32
  143.8 5.9 %collective-permute-start.33 = (bf16[16,3328]{1,0:T(8,128)(2,1)S(1)}, bf16[16,3328]{1,0:T(8,128)(2,1)S(1)}, u32[]{:S(2)}, u32[]{:S(2)}) collective-permute-start(bf16[16,3328]{1,0:T(8,128)(2,1)S(1)} %fusion.33), channel_id=1, source_target_pairs={{0,12},{1,5},{4,8},{5,1},{8,4},{9,13},{12,0},{13,9},{2,14},{3,7},{... | collective-permute-start | bytes 319496 | tf_op jit(solution)/shard_map/ppermute | solution.py:32
  149.5 26.7 %collective-permute-start.27 = (bf16[64,1024]{1,0:T(8,128)(2,1)S(1)}, bf16[64,1024]{1,0:T(8,128)(2,1)S(1)}, u32[]{:S(2)}, u32[]{:S(2)}) collective-permute-start(bf16[64,1024]{1,0:T(8,128)(2,1)S(1)} %get-tuple-element.301), channel_id=1, source_target_pairs={{0,32},{16,48},{32,64},{48,80},{64,96},{80,112},{96,0},{112,16},{1... | collective-permute-start | bytes 393224 | tf_op jit(solution)/shard_map/ppermute | solution.py:32
  149.6 38.2 %collective-permute-start.28 = (bf16[64,1024]{1,0:T(8,128)(2,1)S(1)}, bf16[64,1024]{1,0:T(8,128)(2,1)S(1)}, u32[]{:S(2)}, u32[]{:S(2)}) collective-permute-start(bf16[64,1024]{1,0:T(8,128)(2,1)S(1)} %get-tuple-element.302), channel_id=1, source_target_pairs={{0,48},{16,32},{32,80},{48,64},{64,112},{80,96},{96,16},{112,0},{1... | collective-permute-start | bytes 393224 | tf_op jit(solution)/shard_map/ppermute | solution.py:32
  149.7 6.0 %collective-permute-start.34 = (bf16[32,3328]{1,0:T(8,128)(2,1)S(1)}, bf16[32,3328]{1,0:T(8,128)(2,1)S(1)}, u32[]{:S(2)}, u32[]{:S(2)}) collective-permute-start(bf16[32,3328]{1,0:T(8,128)(2,1)S(1)} %pad_maximum_fusion.27), channel_id=1, source_target_pairs={{0,4},{1,13},{4,0},{5,9},{8,12},{9,5},{12,8},{13,1},{2,6},{3,15},{... | collective-permute-start | bytes 638984 | tf_op jit(solution)/shard_map/ppermute | solution.py:32
  150.9 6.6 %collective-permute-start.30 = (bf16[64,3328]{1,0:T(8,128)(2,1)S(1)}, bf16[64,3328]{1,0:T(8,128)(2,1)S(1)}, u32[]{:S(2)}, u32[]{:S(2)}) collective-permute-start(bf16[64,3328]{1,0:T(8,128)(2,1)S(1)} %pad_maximum_fusion.14), channel_id=1, source_target_pairs={{0,1},{1,0},{2,3},{3,2},{4,5},{5,4},{6,7},{7,6},{8,9},{9,8},{10,11... | collective-permute-start | bytes 1277960 | tf_op jit(solution)/shard_map/ppermute | solution.py:32
  155.7 11.5 %collective-permute-start.35 = (bf16[64,3328]{1,0:T(8,128)(2,1)S(1)}, bf16[64,3328]{1,0:T(8,128)(2,1)S(1)}, u32[]{:S(2)}, u32[]{:S(2)}) collective-permute-start(bf16[64,3328]{1,0:T(8,128)(2,1)S(1)} %pad_maximum_fusion.15), channel_id=1, source_target_pairs={{0,1},{1,0},{2,3},{3,2},{4,5},{5,4},{6,7},{7,6},{8,9},{9,8},{10,11... | collective-permute-start | bytes 1277960 | tf_op jit(solution)/shard_map/ppermute | solution.py:32
  162.2 25.6 %collective-permute-start.31 = (bf16[64,1024]{1,0:T(8,128)(2,1)S(1)}, bf16[64,1024]{1,0:T(8,128)(2,1)S(1)}, u32[]{:S(2)}, u32[]{:S(2)}) collective-permute-start(bf16[64,1024]{1,0:T(8,128)(2,1)S(1)} %get-tuple-element.304), channel_id=1, source_target_pairs={{0,96},{16,112},{32,0},{48,16},{64,32},{80,48},{96,64},{112,80},{1... | collective-permute-start | bytes 393224 | tf_op jit(solution)/shard_map/ppermute | solution.py:32
  167.3 20.6 %collective-permute-start.32 = (bf16[64,1024]{1,0:T(8,128)(2,1)S(1)}, bf16[64,1024]{1,0:T(8,128)(2,1)S(1)}, u32[]{:S(2)}, u32[]{:S(2)}) collective-permute-start(bf16[64,1024]{1,0:T(8,128)(2,1)S(1)} %get-tuple-element.305), channel_id=1, source_target_pairs={{0,112},{16,96},{32,16},{48,0},{64,48},{80,32},{96,80},{112,64},{1... | collective-permute-start | bytes 393224 | tf_op jit(solution)/shard_map/ppermute | solution.py:32
  174.6 13.2 %collective-permute-start.36 = (bf16[64,1024]{1,0:T(8,128)(2,1)S(1)}, bf16[64,1024]{1,0:T(8,128)(2,1)S(1)}, u32[]{:S(2)}, u32[]{:S(2)}) collective-permute-start(bf16[64,1024]{1,0:T(8,128)(2,1)S(1)} %get-tuple-element.307), channel_id=1, source_target_pairs={{0,64},{16,80},{32,96},{48,112},{64,0},{80,16},{96,32},{112,48},{1... | collective-permute-start | bytes 393224 | tf_op jit(solution)/shard_map/ppermute | solution.py:32
  176.1 11.7 %collective-permute-start.37 = (bf16[64,1024]{1,0:T(8,128)(2,1)S(1)}, bf16[64,1024]{1,0:T(8,128)(2,1)S(1)}, u32[]{:S(2)}, u32[]{:S(2)}) collective-permute-start(bf16[64,1024]{1,0:T(8,128)(2,1)S(1)} %get-tuple-element.308), channel_id=1, source_target_pairs={{0,80},{16,64},{32,112},{48,96},{64,16},{80,0},{96,48},{112,32},{1... | collective-permute-start | bytes 393224 | tf_op jit(solution)/shard_map/ppermute | solution.py:32

commit v3 on v2

--- a/solution.py
+++ b/solution.py
@@ -7,14 +7,13 @@
 
 F32, BF16, F16 = jnp.float32, jnp.bfloat16, jnp.float16
 LIFT = 8.0
-TILE = 256
 AXES = ("x", "z_hi", "y", "z_lo", "core")
-CHUNKS = ((0,), (1,), (3,), (2,))
+CHUNKS = ((0,), (1,), (2,), (3,))
 ORDER = (
-    (1, -1), (0, 0), (2, -1), (3, -1), (0, 2), (1, 0), (2, 0), (1, 2), (0, 3), (2, 2), (3, 0),
-    (1, 3), (0, 4), (3, 2), (2, 3), (0, 5), (1, 4), (3, 3), (2, 4), (0, 6), (1, 5), (3, 4),
-    (2, 5), (1, 6), (0, 7), (2, 6), (3, 5), (0, 8), (1, 7), (3, 6), (2, 7), (1, 8), (3, 7),
-    (2, 8), (3, 8),
+    (1, -1), (2, -1), (0, 0), (3, -1), (0, 2), (1, 0), (1, 2), (2, 0), (0, 3), (2, 2), (1, 3),
+    (0, 4), (3, 0), (2, 3), (1, 4), (3, 2), (0, 5), (2, 4), (1, 5), (3, 3), (0, 6), (2, 5),
+    (1, 6), (3, 4), (0, 7), (2, 6), (0, 8), (1, 7), (3, 5), (1, 8), (2, 7), (3, 6), (2, 8),
+    (3, 7), (3, 8),
 )
 
 
@@ -40,26 +39,35 @@
     return v.astype(F32) * (1 / LIFT)
 
 
-def multiply(rows, *refs):
-    half = len(refs) // 2
-    for weight, out in zip(refs[:half], refs[half:]):
+def copy_in(*refs):
+    half = (len(refs) - 1) // 2
+    sems = refs[-1]
+    copies = [
+        pltpu.make_async_copy(here, there, sems.at[i])
+        for i, (here, there) in enumerate(zip(refs[:half], refs[half : 2 * half]))
+    ]
+    for copy in copies:
+        copy.start()
+    for copy in copies:
+        copy.wait()
 
-        @pl.loop(0, weight.shape[1] // TILE)
-        def _(i):
-            columns = pl.ds(pl.multiple_of(i * TILE, TILE), TILE)
-            out[:, columns] = jnp.dot(rows[...], weight[:, columns], preferred_element_type=F32)
+
+def held(*weights):
+    return pl.pallas_call(
+        copy_in,
+        out_shape=[pltpu.VMEM(w.shape, w.dtype) for w in weights],
+        in_specs=[pl.BlockSpec(memory_space=pltpu.HBM)] * len(weights),
+        out_specs=[pl.BlockSpec(memory_space=pltpu.VMEM)] * len(weights),
+        scratch_shapes=[pltpu.SemaphoreType.DMA((len(weights),))],
+        compiler_params=pltpu.CompilerParams(vmem_limit_bytes=2**20),
+        cost_estimate=pl.CostEstimate(
+            flops=0, bytes_accessed=sum(2 * w.size for w in weights), transcendentals=0
+        ),
+    )(*weights)
 
 
 def product(rows, *weights):
-    vmem = pl.BlockSpec(memory_space=pltpu.VMEM)
-    return pl.pallas_call(
-        multiply,
-        out_shape=[jax.ShapeDtypeStruct((rows.shape[0], w.shape[1]), F32) for w in weights],
-        in_specs=[vmem] * (1 + len(weights)),
-        out_specs=[vmem] * len(weights),
-        compiler_params=pltpu.CompilerParams(vmem_limit_bytes=48 * 2**20),
-        cost_estimate=pl.CostEstimate(flops=0, bytes_accessed=0, transcendentals=0),
-    )(rows, *weights)
+    return [jnp.dot(rows, w, preferred_element_type=F32) for w in weights]
 
 
 def per_device(tokens, gate_weight, up_weight, down_weight):
@@ -78,7 +86,9 @@
     features = tokens.shape[1] // 16
     blocks = tokens.reshape(4, 16, features).transpose(1, 0, 2).reshape(1, 64, features)
     blocks = jnp.broadcast_to(blocks, (2, 64, features)).reshape(128, features)
+    blocks, *weights = lax.optimization_barrier((blocks, gate_weight, up_weight, down_weight))
     mine = lax.all_to_all(blocks, AXES[1:], split_axis=0, concat_axis=0, tiled=True)
+    mine, gate_weight, up_weight, down_weight = lax.optimization_barrier((mine, *held(*weights)))
     mine = mine.reshape(2, 4, 16, features)
 
     def ordered(half):

time: 189 us -> 167 us (0.88)
  Pallas kernels: 63.2 us -> 1.39 us
  waiting for transfers between devices: 55.7 us -> 34.2 us
  starting transfers between devices: 51.4 us -> 71.9 us
  local copies, waits for them, and re-layouts: 2.64 us -> 22.4 us
  matrix products: 0 us -> 15.8 us
  other arithmetic: 7.47 us -> 12.5 us
    pallas_call x8 -> x1, Pallas kernels: 63.2 us -> 1.39 us  [held(): pl.pallas_call(copy_in, out_shape=[pltpu.VMEM(w.shape, w.dtype) for w in...]
    ppermute x38, starting transfers between devices: 41.8 us -> 62.3 us  [permute(): return lambda v: lax.ppermute(v, axes, pairs)]
    unnamed x7 -> x41, local copies, waits for them, and re-layouts: 0.09 us -> 19.9 us
    dot_general x0 -> x12, matrix products: none -> 15.8 us  [product(): return [jnp.dot(rows, w, preferred_element_type=F32) for w in weights]]
    ppermute x38, waiting for transfers between devices: 47 us -> 34.2 us  [permute(): return lambda v: lax.ppermute(v, axes, pairs)]
    all_to_all x1, waiting for transfers between devices: 8.79 us -> 0.01 us  [per_device(): lax.all_to_all(blocks, AXES[1:], split_axis=0, concat_axis=0, tiled=True)]
  transfers between devices with their start and end apart: 39 -> 39, of which waited for: 13 -> 11; matrix products, arithmetic and copies ran while one was open for 3% -> 9% of each run, Pallas kernels for 22% -> 1%
where the time goes in v3:
time: 167 us
  starting transfers between devices  71.9 us (43%)
  waiting for transfers between devices  34.2 us (20%)
  local copies, waits for them, and re-layouts  22.4 us (13%)
  matrix products  15.8 us (9%)
  other arithmetic  12.5 us (7%)
  between operations  8.68 us (5%)
    ppermute x38, starting transfers between devices, permute(): return lambda v: lax.ppermute(v, axes, pairs)  62.3 us
    ppermute x38, waiting for transfers between devices, permute(): return lambda v: lax.ppermute(v, axes, pairs)  34.2 us
    unnamed x41, local copies, waits for them, and re-layouts  19.9 us
    dot_general x12, matrix products, product(): return [jnp.dot(rows, w, preferred_element_type=F32) for w in weights]  15.8 us
    all_to_all x1, starting transfers between devices, per_device(): lax.all_to_all(blocks, AXES[1:], split_axis=0, concat_axis=0, tiled=True)  9.6 us
  transfers between devices with their start and end apart: 39, of which 11 were waited for; matrix products, arithmetic and copies ran while one was open for 9% of the time, Pallas kernels for 1%

profile of v3, /device:TPU:1, one launch (start us, length us, event | category | flops | bytes accessed | tf_op | source)
XLA Modules:
  0.0 166.9 jit_solution(15755834535510913441)
XLA Ops:
  1.8 9.6 %all-to-all-start = ((bf16[32,4,1024]{2,1,0:T(4,128)(2,1)}), bf16[32,4,1024]{2,1,0:T(4,128)(2,1)S(1)}, u32[]{:S(2)}, u32[]{:S(2)}) async-start(bf16[32,4,1024]{2,1,0:T(4,128)(2,1)} %all_to_all.8), calls=%async_computation | async-start | bytes 524288 | tf_op jit(solution)/shard_map/all_to_all | solution.py:90
  11.5 2.9 %copy-done.3 = bf16[1024,3328]{1,0:T(8,128)(2,1)S(1)} copy-done((bf16[1024,3328]{1,0:T(8,128)(2,1)S(1)}, bf16[1024,3328]{1,0:T(8,128)(2,1)}, u32[]{:S(2)}) %copy-start.3) | copy-done | bytes 6815768
  14.4 2.9 %copy-done.4 = bf16[1024,3328]{1,0:T(8,128)(2,1)S(1)} copy-done((bf16[1024,3328]{1,0:T(8,128)(2,1)S(1)}, bf16[1024,3328]{1,0:T(8,128)(2,1)}, u32[]{:S(2)}) %copy-start.4) | copy-done | bytes 6815768
  17.3 2.9 %copy-done.5 = bf16[3328,1024]{1,0:T(8,128)(2,1)S(1)} copy-done((bf16[3328,1024]{1,0:T(8,128)(2,1)S(1)}, bf16[3328,1024]{1,0:T(8,128)(2,1)}, u32[]{:S(2)}) %copy-start.5) | copy-done | bytes 6815768
  20.3 1.4 shard_map.46
  21.7 2.8 %copy-done = bf16[1024,3328]{1,0:T(8,128)(2,1)} copy-done((bf16[1024,3328]{1,0:T(8,128)(2,1)}, bf16[1024,3328]{1,0:T(8,128)(2,1)S(1)}, u32[]{:S(2)}) %copy-start) | copy-done | bytes 6815768
  24.5 2.8 %copy-done.1 = bf16[1024,3328]{1,0:T(8,128)(2,1)} copy-done((bf16[1024,3328]{1,0:T(8,128)(2,1)}, bf16[1024,3328]{1,0:T(8,128)(2,1)S(1)}, u32[]{:S(2)}) %copy-start.1) | copy-done | bytes 6815768
  27.3 2.7 %copy-done.2 = bf16[3328,1024]{1,0:T(8,128)(2,1)} copy-done((bf16[3328,1024]{1,0:T(8,128)(2,1)}, bf16[3328,1024]{1,0:T(8,128)(2,1)S(1)}, u32[]{:S(2)}) %copy-start.2) | copy-done | bytes 6815768
  30.3 4.1 %fusion.109 = f32[128,3328]{1,0:T(8,128)S(1)} fusion(bf16[128,1024]{1,0:T(8,128)(2,1)S(1)} %bitcast.231, bf16[1024,3328]{1,0:T(8,128)(2,1)} %copy-done.1), kind=kOutput, calls=%fused_computation.220 | convolution fusion | flops 872415232 | bytes 8781824 | tf_op jit(solution)/shard_map/dot_general | solution.py:70
  35.2 1.1 fusion.110
  37.0 2.5 %collective-permute-start.3 = (bf16[2,4,16,1024]{3,2,1,0:T(8,128)(2,1)S(1)}, bf16[2,4,16,1024]{3,2,1,0:T(8,128)(2,1)S(1)}, u32[]{:S(2)}, u32[]{:S(2)}) collective-permute-start(bf16[2,4,16,1024]{3,2,1,0:T(8,128)(2,1)S(1)} %bitcast.233), channel_id=1, source_target_pairs={{0,96},{32,0},{64,32},{96,64},{1,97},{33,1},{65,33},{97,65},{2,98}... | collective-permute-start | bytes 786440 | tf_op jit(solution)/shard_map/ppermute | solution.py:31
  41.5 3.4 %collective-permute-done.3 = bf16[2,4,16,1024]{3,2,1,0:T(8,128)(2,1)S(1)} collective-permute-done((bf16[2,4,16,1024]{3,2,1,0:T(8,128)(2,1)S(1)}, bf16[2,4,16,1024]{3,2,1,0:T(8,128)(2,1)S(1)}, u32[]{:S(2)}, u32[]{:S(2)}) %collective-permute-start.3) | collective-permute-done | bytes 262176 | tf_op jit(solution)/shard_map/ppermute | solution.py:31
  49.1 1.2 pad_maximum_fusion.1
  50.3 1.1 collective-permute-start.4
  51.4 2.5 %collective-permute-start.2 = (bf16[2,4,16,1024]{3,2,1,0:T(8,128)(2,1)S(1)}, bf16[2,4,16,1024]{3,2,1,0:T(8,128)(2,1)S(1)}, u32[]{:S(2)}, u32[]{:S(2)}) collective-permute-start(bf16[2,4,16,1024]{3,2,1,0:T(8,128)(2,1)S(1)} %bitcast.234), channel_id=1, source_target_pairs={{0,64},{32,96},{64,0},{96,32},{1,65},{33,97},{65,1},{97,33},{2,66}... | collective-permute-start | bytes 786440 | tf_op jit(solution)/shard_map/ppermute | solution.py:31
  53.9 1.5 collective-permute-start.9
  55.4 2.7 %collective-permute-start.1 = (f16[2,32,3328]{2,1,0:T(8,128)(2,1)}, f16[2,32,3328]{2,1,0:T(8,128)(2,1)S(1)}, u32[]{:S(2)}, u32[]{:S(2)}) collective-permute-start(f16[2,32,3328]{2,1,0:T(8,128)(2,1)} %pad_maximum_fusion.4), channel_id=1, source_target_pairs={{0,4},{1,13},{4,0},{5,9},{8,12},{9,5},{12,8},{13,1},{2,6},{3,15},{... | collective-permute-start | bytes 1277960 | tf_op jit(solution)/shard_map/ppermute | solution.py:31
  58.1 1.9 %bitcast_add_fusion.5 = (f32[64,3328]{1,0:T(8,128)S(1)}, f32[64,3328]{1,0:T(8,128)S(1)}) fusion(f32[64,3328]{1,0:T(8,128)} %get-tuple-element.188, f16[2,64,3328]{2,1,0:T(8,128)(2,1)} %collective-permute-done.4, f32[64,3328]{1,0:T(8,128)} %get-tuple-element.192), kind=kLoop, calls=%fused_computation.41 | loop fusion | flops 1277952 | bytes 4259840 | tf_op jit(solution)/shard_map/add | solution.py:126
  60.9 1.1 fusion.113
  63.3 1.1 fusion.114
  66.2 2.8 %collective-permute-start.6 = (f16[2,32,3328]{2,1,0:T(8,128)(2,1)S(1)}, f16[2,32,3328]{2,1,0:T(8,128)(2,1)S(1)}, u32[]{:S(2)}, u32[]{:S(2)}) collective-permute-start(f16[2,32,3328]{2,1,0:T(8,128)(2,1)S(1)} %pad_maximum_fusion.5), channel_id=1, source_target_pairs={{0,4},{1,13},{4,0},{5,9},{8,12},{9,5},{12,8},{13,1},{2,6},{3,15},{... | collective-permute-start | bytes 1277960 | tf_op jit(solution)/shard_map/ppermute | solution.py:31
  69.5 7.6 %collective-permute-done.6 = f16[2,32,3328]{2,1,0:T(8,128)(2,1)S(1)} collective-permute-done((f16[2,32,3328]{2,1,0:T(8,128)(2,1)S(1)}, f16[2,32,3328]{2,1,0:T(8,128)(2,1)S(1)}, u32[]{:S(2)}, u32[]{:S(2)}) %collective-permute-start.6) | collective-permute-done | bytes 426016 | tf_op jit(solution)/shard_map/ppermute | solution.py:31
  78.6 1.1 fusion.116
  79.9 2.5 %collective-permute-start.12 = (f16[2,32,3328]{2,1,0:T(8,128)(2,1)S(1)}, f16[2,32,3328]{2,1,0:T(8,128)(2,1)S(1)}, u32[]{:S(2)}, u32[]{:S(2)}) collective-permute-start(f16[2,32,3328]{2,1,0:T(8,128)(2,1)S(1)} %pad_maximum_fusion.6), channel_id=1, source_target_pairs={{0,4},{1,13},{4,0},{5,9},{8,12},{9,5},{12,8},{13,1},{2,6},{3,15},{... | collective-permute-start | bytes 1277960 | tf_op jit(solution)/shard_map/ppermute | solution.py:31
  83.6 1.2 collective-permute-start.8
  84.8 5.9 %collective-permute-done.12 = f16[2,32,3328]{2,1,0:T(8,128)(2,1)S(1)} collective-permute-done((f16[2,32,3328]{2,1,0:T(8,128)(2,1)S(1)}, f16[2,32,3328]{2,1,0:T(8,128)(2,1)S(1)}, u32[]{:S(2)}, u32[]{:S(2)}) %collective-permute-start.12) | collective-permute-done | bytes 426016 | tf_op jit(solution)/shard_map/ppermute | solution.py:31
  91.2 1.3 collective-permute-start.15
  93.0 1.5 collective-permute-start.13
  94.4 1.7 %collective-permute-done.16 = f16[2,16,3328]{2,1,0:T(8,128)(2,1)S(1)} collective-permute-done((f16[2,16,3328]{2,1,0:T(8,128)(2,1)S(1)}, f16[2,16,3328]{2,1,0:T(8,128)(2,1)S(1)}, u32[]{:S(2)}, u32[]{:S(2)}) %collective-permute-start.16) | collective-permute-done | bytes 213024 | tf_op jit(solution)/shard_map/ppermute | solution.py:31
  96.4 2.8 %collective-permute-start.19 = (bf16[16,3328]{1,0:T(8,128)(2,1)S(1)}, bf16[16,3328]{1,0:T(8,128)(2,1)S(1)}, u32[]{:S(2)}, u32[]{:S(2)}) collective-permute-start(bf16[16,3328]{1,0:T(8,128)(2,1)S(1)} %fusion.61), channel_id=1, source_target_pairs={{0,12},{1,5},{4,8},{5,1},{8,4},{9,13},{12,0},{13,9},{2,14},{3,7},{... | collective-permute-start | bytes 319496 | tf_op jit(solution)/shard_map/ppermute | solution.py:31
  99.2 1.2 collective-permute-start.20
  100.4 3.0 %collective-permute-start.14 = (f16[2,32,3328]{2,1,0:T(8,128)(2,1)S(1)}, f16[2,32,3328]{2,1,0:T(8,128)(2,1)S(1)}, u32[]{:S(2)}, u32[]{:S(2)}) collective-permute-start(f16[2,32,3328]{2,1,0:T(8,128)(2,1)S(1)} %pad_maximum_fusion.7), channel_id=1, source_target_pairs={{0,4},{1,13},{4,0},{5,9},{8,12},{9,5},{12,8},{13,1},{2,6},{3,15},{... | collective-permute-start | bytes 1277960 | tf_op jit(solution)/shard_map/ppermute | solution.py:31
  103.6 2.7 %collective-permute-start.24 = (bf16[32,3328]{1,0:T(8,128)(2,1)S(1)}, bf16[32,3328]{1,0:T(8,128)(2,1)S(1)}, u32[]{:S(2)}, u32[]{:S(2)}) collective-permute-start(bf16[32,3328]{1,0:T(8,128)(2,1)S(1)} %pad_maximum_fusion.19), channel_id=1, source_target_pairs={{0,4},{1,13},{4,0},{5,9},{8,12},{9,5},{12,8},{13,1},{2,6},{3,15},{... | collective-permute-start | bytes 638984 | tf_op jit(solution)/shard_map/ppermute | solution.py:31
  106.5 4.9 %collective-permute-done.17 = bf16[32,3328]{1,0:T(8,128)(2,1)S(1)} collective-permute-done((bf16[32,3328]{1,0:T(8,128)(2,1)S(1)}, bf16[32,3328]{1,0:T(8,128)(2,1)S(1)}, u32[]{:S(2)}, u32[]{:S(2)}) %collective-permute-start.17) | collective-permute-done | bytes 213024 | tf_op jit(solution)/shard_map/ppermute | solution.py:31
  111.4 3.2 %collective-permute-start.21 = (bf16[64,3328]{1,0:T(8,128)(2,1)S(1)}, bf16[64,3328]{1,0:T(8,128)(2,1)S(1)}, u32[]{:S(2)}, u32[]{:S(2)}) collective-permute-start(bf16[64,3328]{1,0:T(8,128)(2,1)S(1)} %pad_maximum_fusion.8), channel_id=1, source_target_pairs={{0,1},{1,0},{2,3},{3,2},{4,5},{5,4},{6,7},{7,6},{8,9},{9,8},{10,11... | collective-permute-start | bytes 1277960 | tf_op jit(solution)/shard_map/ppermute | solution.py:31
  114.8 2.1 %collective-permute-start.25 = (bf16[64,3328]{1,0:T(8,128)(2,1)S(1)}, bf16[64,3328]{1,0:T(8,128)(2,1)S(1)}, u32[]{:S(2)}, u32[]{:S(2)}) collective-permute-start(bf16[64,3328]{1,0:T(8,128)(2,1)S(1)} %pad_maximum_fusion.9), channel_id=1, source_target_pairs={{0,1},{1,0},{2,3},{3,2},{4,5},{5,4},{6,7},{7,6},{8,9},{9,8},{10,11... | collective-permute-start | bytes 1277960 | tf_op jit(solution)/shard_map/ppermute | solution.py:31
  118.2 5.4 %collective-permute-done.28 = bf16[32,3328]{1,0:T(8,128)(2,1)S(1)} collective-permute-done((bf16[32,3328]{1,0:T(8,128)(2,1)S(1)}, bf16[32,3328]{1,0:T(8,128)(2,1)S(1)}, u32[]{:S(2)}, u32[]{:S(2)}) %collective-permute-start.28) | collective-permute-done | bytes 213024 | tf_op jit(solution)/shard_map/ppermute | solution.py:31
  123.6 1.1 collective-permute-start.29
  126.5 2.8 %collective-permute-start.23 = (bf16[64,1024]{1,0:T(8,128)(2,1)S(1)}, bf16[64,1024]{1,0:T(8,128)(2,1)S(1)}, u32[]{:S(2)}, u32[]{:S(2)}) collective-permute-start(bf16[64,1024]{1,0:T(8,128)(2,1)S(1)} %select_convert_fusion.6), channel_id=1, source_target_pairs={{0,16},{16,0},{32,48},{48,32},{64,80},{80,64},{96,112},{112,96},{1... | collective-permute-start | bytes 393224 | tf_op jit(solution)/shard_map/ppermute | solution.py:31
  129.3 1.4 collective-permute-done.32
  130.8 2.7 %collective-permute-start.33 = (bf16[16,3328]{1,0:T(8,128)(2,1)S(1)}, bf16[16,3328]{1,0:T(8,128)(2,1)S(1)}, u32[]{:S(2)}, u32[]{:S(2)}) collective-permute-start(bf16[16,3328]{1,0:T(8,128)(2,1)S(1)} %fusion.57), channel_id=1, source_target_pairs={{0,12},{1,5},{4,8},{5,1},{8,4},{9,13},{12,0},{13,9},{2,14},{3,7},{... | collective-permute-start | bytes 319496 | tf_op jit(solution)/shard_map/ppermute | solution.py:31
  134.6 1.3 collective-permute-done.33
  136.7 3.6 %collective-permute-start.27 = (bf16[64,1024]{1,0:T(8,128)(2,1)S(1)}, bf16[64,1024]{1,0:T(8,128)(2,1)S(1)}, u32[]{:S(2)}, u32[]{:S(2)}) collective-permute-start(bf16[64,1024]{1,0:T(8,128)(2,1)S(1)} %get-tuple-element.306), channel_id=1, source_target_pairs={{0,48},{16,32},{32,80},{48,64},{64,112},{80,96},{96,16},{112,0},{1... | collective-permute-start | bytes 393224 | tf_op jit(solution)/shard_map/ppermute | solution.py:31
  140.3 1.7 %collective-permute-done.34 = bf16[32,3328]{1,0:T(8,128)(2,1)S(1)} collective-permute-done((bf16[32,3328]{1,0:T(8,128)(2,1)S(1)}, bf16[32,3328]{1,0:T(8,128)(2,1)S(1)}, u32[]{:S(2)}, u32[]{:S(2)}) %collective-permute-start.34) | collective-permute-done | bytes 213024 | tf_op jit(solution)/shard_map/ppermute | solution.py:31
  142.1 4.6 %collective-permute-start.35 = (bf16[64,3328]{1,0:T(8,128)(2,1)S(1)}, bf16[64,3328]{1,0:T(8,128)(2,1)S(1)}, u32[]{:S(2)}, u32[]{:S(2)}) collective-permute-start(bf16[64,3328]{1,0:T(8,128)(2,1)S(1)} %pad_maximum_fusion.11), channel_id=1, source_target_pairs={{0,1},{1,0},{2,3},{3,2},{4,5},{5,4},{6,7},{7,6},{8,9},{9,8},{10,11... | collective-permute-start | bytes 1277960 | tf_op jit(solution)/shard_map/ppermute | solution.py:31
  147.7 2.5 %collective-permute-start.30 = (bf16[64,1024]{1,0:T(8,128)(2,1)S(1)}, bf16[64,1024]{1,0:T(8,128)(2,1)S(1)}, u32[]{:S(2)}, u32[]{:S(2)}) collective-permute-start(bf16[64,1024]{1,0:T(8,128)(2,1)S(1)} %get-tuple-element.308), channel_id=1, source_target_pairs={{0,64},{16,80},{32,96},{48,112},{64,0},{80,16},{96,32},{112,48},{1... | collective-permute-start | bytes 393224 | tf_op jit(solution)/shard_map/ppermute | solution.py:31
  150.3 3.1 %collective-permute-start.31 = (bf16[64,1024]{1,0:T(8,128)(2,1)S(1)}, bf16[64,1024]{1,0:T(8,128)(2,1)S(1)}, u32[]{:S(2)}, u32[]{:S(2)}) collective-permute-start(bf16[64,1024]{1,0:T(8,128)(2,1)S(1)} %get-tuple-element.309), channel_id=1, source_target_pairs={{0,80},{16,64},{32,112},{48,96},{64,16},{80,0},{96,48},{112,32},{1... | collective-permute-start | bytes 393224 | tf_op jit(solution)/shard_map/ppermute | solution.py:31
  154.4 3.1 %collective-permute-start.36 = (bf16[64,1024]{1,0:T(8,128)(2,1)S(1)}, bf16[64,1024]{1,0:T(8,128)(2,1)S(1)}, u32[]{:S(2)}, u32[]{:S(2)}) collective-permute-start(bf16[64,1024]{1,0:T(8,128)(2,1)S(1)} %get-tuple-element.313), channel_id=1, source_target_pairs={{0,96},{16,112},{32,0},{48,16},{64,32},{80,48},{96,64},{112,80},{1... | collective-permute-start | bytes 393224 | tf_op jit(solution)/shard_map/ppermute | solution.py:31
  (167 shorter events, 27.2 us)
Async XLA Ops:
  1.8 28.2 %all-to-all-start = ((bf16[32,4,1024]{2,1,0:T(4,128)(2,1)}), bf16[32,4,1024]{2,1,0:T(4,128)(2,1)S(1)}, u32[]{:S(2)}, u32[]{:S(2)}) async-start(bf16[32,4,1024]{2,1,0:T(4,128)(2,1)} %all_to_all.8), calls=%async_computation | async-start | bytes 524288 | tf_op jit(solution)/shard_map/all_to_all | solution.py:90
  11.5 2.9 %copy-start.3 = (bf16[1024,3328]{1,0:T(8,128)(2,1)S(1)}, bf16[1024,3328]{1,0:T(8,128)(2,1)}, u32[]{:S(2)}) copy-start(bf16[1024,3328]{1,0:T(8,128)(2,1)} %refs_0_) | copy-start | bytes 20447236
  30.2 4.2 %slice-start = ((s8[6815744]{0:T(1024)(128)(4,1)}), s8[4194304]{0:T(1024)(128)(4,1)S(1)}, s32[]{:S(2)}) async-start(s8[6815744]{0:T(1024)(128)(4,1)} %bitcast.221), calls=%async_computation.1 | async-start | bytes 8388608
  30.3 4.9 %slice-start.1 = ((s8[6815744]{0:T(1024)(128)(4,1)}), s8[2621440]{0:T(1024)(128)(4,1)S(1)}, s32[]{:S(2)}) async-start(s8[6815744]{0:T(1024)(128)(4,1)} %bitcast.221), calls=%async_computation.2 | async-start | bytes 5242880
  36.3 8.7 %slice-start.4 = ((s8[6815744]{0:T(1024)(128)(4,1)}), s8[4194304]{0:T(1024)(128)(4,1)S(1)}, s32[]{:S(2)}) async-start(s8[6815744]{0:T(1024)(128)(4,1)} %bitcast.225), calls=%async_computation.5 | async-start | bytes 8388608
  36.7 8.2 %slice-start.5 = ((s8[6815744]{0:T(1024)(128)(4,1)}), s8[2621440]{0:T(1024)(128)(4,1)S(1)}, s32[]{:S(2)}) async-start(s8[6815744]{0:T(1024)(128)(4,1)} %bitcast.225), calls=%async_computation.6 | async-start | bytes 5242880
  36.7 2.8 %collective-permute-start = (f16[2,64,3328]{2,1,0:T(8,128)(2,1)S(1)}, f16[2,64,3328]{2,1,0:T(8,128)(2,1)S(1)}, u32[]{:S(2)}, u32[]{:S(2)}) collective-permute-start(f16[2,64,3328]{2,1,0:T(8,128)(2,1)S(1)} %pad_maximum_fusion), channel_id=1, source_target_pairs={{0,1},{1,0},{2,3},{3,2},{4,5},{5,4},{6,7},{7,6},{8,9},{9,8},{10,11... | collective-permute-start | bytes 2555912 | tf_op jit(solution)/shard_map/ppermute | solution.py:31
  37.0 7.9 %collective-permute-start.3 = (bf16[2,4,16,1024]{3,2,1,0:T(8,128)(2,1)S(1)}, bf16[2,4,16,1024]{3,2,1,0:T(8,128)(2,1)S(1)}, u32[]{:S(2)}, u32[]{:S(2)}) collective-permute-start(bf16[2,4,16,1024]{3,2,1,0:T(8,128)(2,1)S(1)} %bitcast.233), channel_id=1, source_target_pairs={{0,96},{32,0},{64,32},{96,64},{1,97},{33,1},{65,33},{97,65},{2,98}... | collective-permute-start | bytes 786440 | tf_op jit(solution)/shard_map/ppermute | solution.py:31
  48.1 12.8 %slice-start.6 = ((s8[6815744]{0:T(1024)(128)(4,1)}), s8[2621440]{0:T(1024)(128)(4,1)S(1)}, s32[]{:S(2)}) async-start(s8[6815744]{0:T(1024)(128)(4,1)} %bitcast.227), calls=%async_computation.7 | async-start | bytes 5242880
  50.3 7.8 %collective-permute-start.4 = (f16[2,64,3328]{2,1,0:T(8,128)(2,1)}, f16[2,64,3328]{2,1,0:T(8,128)(2,1)}, u32[]{:S(2)}, u32[]{:S(2)}) collective-permute-start(f16[2,64,3328]{2,1,0:T(8,128)(2,1)} %pad_maximum_fusion.1), channel_id=1, source_target_pairs={{0,1},{1,0},{2,3},{3,2},{4,5},{5,4},{6,7},{7,6},{8,9},{9,8},{10,11... | collective-permute-start | bytes 2555912 | tf_op jit(solution)/shard_map/ppermute | solution.py:31
  51.4 9.5 %slice-start.7 = ((s8[6815744]{0:T(1024)(128)(4,1)}), s8[4194304]{0:T(1024)(128)(4,1)S(1)}, s32[]{:S(2)}) async-start(s8[6815744]{0:T(1024)(128)(4,1)} %bitcast.227), calls=%async_computation.8 | async-start | bytes 8388608
  51.4 9.5 %collective-permute-start.2 = (bf16[2,4,16,1024]{3,2,1,0:T(8,128)(2,1)S(1)}, bf16[2,4,16,1024]{3,2,1,0:T(8,128)(2,1)S(1)}, u32[]{:S(2)}, u32[]{:S(2)}) collective-permute-start(bf16[2,4,16,1024]{3,2,1,0:T(8,128)(2,1)S(1)} %bitcast.234), channel_id=1, source_target_pairs={{0,64},{32,96},{64,0},{96,32},{1,65},{33,97},{65,1},{97,33},{2,66}... | collective-permute-start | bytes 786440 | tf_op jit(solution)/shard_map/ppermute | solution.py:31
  53.9 23.7 %collective-permute-start.9 = (bf16[2,4,16,1024]{3,2,1,0:T(8,128)(2,1)S(1)}, bf16[2,4,16,1024]{3,2,1,0:T(8,128)(2,1)S(1)}, u32[]{:S(2)}, u32[]{:S(2)}) collective-permute-start(bf16[2,4,16,1024]{3,2,1,0:T(8,128)(2,1)S(1)} %bitcast.235), channel_id=1, source_target_pairs={{0,32},{32,64},{64,96},{96,0},{1,33},{33,65},{65,97},{97,1},{2,34}... | collective-permute-start | bytes 786440 | tf_op jit(solution)/shard_map/ppermute | solution.py:31
  55.4 9.4 %collective-permute-start.1 = (f16[2,32,3328]{2,1,0:T(8,128)(2,1)}, f16[2,32,3328]{2,1,0:T(8,128)(2,1)S(1)}, u32[]{:S(2)}, u32[]{:S(2)}) collective-permute-start(f16[2,32,3328]{2,1,0:T(8,128)(2,1)} %pad_maximum_fusion.4), channel_id=1, source_target_pairs={{0,4},{1,13},{4,0},{5,9},{8,12},{9,5},{12,8},{13,1},{2,6},{3,15},{... | collective-permute-start | bytes 1277960 | tf_op jit(solution)/shard_map/ppermute | solution.py:31
  65.5 3.5 %collective-permute-start.7 = (f16[2,64,3328]{2,1,0:T(8,128)(2,1)S(1)}, f16[2,64,3328]{2,1,0:T(8,128)(2,1)S(1)}, u32[]{:S(2)}, u32[]{:S(2)}) collective-permute-start(f16[2,64,3328]{2,1,0:T(8,128)(2,1)S(1)} %pad_maximum_fusion.2), channel_id=1, source_target_pairs={{0,1},{1,0},{2,3},{3,2},{4,5},{5,4},{6,7},{7,6},{8,9},{9,8},{10,11... | collective-permute-start | bytes 2555912 | tf_op jit(solution)/shard_map/ppermute | solution.py:31
  66.2 10.9 %collective-permute-start.6 = (f16[2,32,3328]{2,1,0:T(8,128)(2,1)S(1)}, f16[2,32,3328]{2,1,0:T(8,128)(2,1)S(1)}, u32[]{:S(2)}, u32[]{:S(2)}) collective-permute-start(f16[2,32,3328]{2,1,0:T(8,128)(2,1)S(1)} %pad_maximum_fusion.5), channel_id=1, source_target_pairs={{0,4},{1,13},{4,0},{5,9},{8,12},{9,5},{12,8},{13,1},{2,6},{3,15},{... | collective-permute-start | bytes 1277960 | tf_op jit(solution)/shard_map/ppermute | solution.py:31
  69.0 8.3 %collective-permute-start.5 = (f16[2,16,3328]{2,1,0:T(8,128)(2,1)S(1)}, f16[2,16,3328]{2,1,0:T(8,128)(2,1)S(1)}, u32[]{:S(2)}, u32[]{:S(2)}) collective-permute-start(f16[2,16,3328]{2,1,0:T(8,128)(2,1)S(1)} %pad_maximum_fusion.12), channel_id=1, source_target_pairs={{0,12},{1,5},{4,8},{5,1},{8,4},{9,13},{12,0},{13,9},{2,14},{3,7},{... | collective-permute-start | bytes 638984 | tf_op jit(solution)/shard_map/ppermute | solution.py:31
  79.9 10.8 %collective-permute-start.12 = (f16[2,32,3328]{2,1,0:T(8,128)(2,1)S(1)}, f16[2,32,3328]{2,1,0:T(8,128)(2,1)S(1)}, u32[]{:S(2)}, u32[]{:S(2)}) collective-permute-start(f16[2,32,3328]{2,1,0:T(8,128)(2,1)S(1)} %pad_maximum_fusion.6), channel_id=1, source_target_pairs={{0,4},{1,13},{4,0},{5,9},{8,12},{9,5},{12,8},{13,1},{2,6},{3,15},{... | collective-permute-start | bytes 1277960 | tf_op jit(solution)/shard_map/ppermute | solution.py:31
  82.6 8.4 %collective-permute-start.11 = (f16[2,16,3328]{2,1,0:T(8,128)(2,1)S(1)}, f16[2,16,3328]{2,1,0:T(8,128)(2,1)S(1)}, u32[]{:S(2)}, u32[]{:S(2)}) collective-permute-start(f16[2,16,3328]{2,1,0:T(8,128)(2,1)S(1)} %pad_maximum_fusion.13), channel_id=1, source_target_pairs={{0,12},{1,5},{4,8},{5,1},{8,4},{9,13},{12,0},{13,9},{2,14},{3,7},{... | collective-permute-start | bytes 638984 | tf_op jit(solution)/shard_map/ppermute | solution.py:31
  82.7 9.8 %collective-permute-start.10 = (f16[2,64,3328]{2,1,0:T(8,128)(2,1)S(1)}, f16[2,64,3328]{2,1,0:T(8,128)(2,1)S(1)}, u32[]{:S(2)}, u32[]{:S(2)}) collective-permute-start(f16[2,64,3328]{2,1,0:T(8,128)(2,1)S(1)} %pad_maximum_fusion.3), channel_id=1, source_target_pairs={{0,1},{1,0},{2,3},{3,2},{4,5},{5,4},{6,7},{7,6},{8,9},{9,8},{10,11... | collective-permute-start | bytes 2555912 | tf_op jit(solution)/shard_map/ppermute | solution.py:31
  83.6 9.3 %collective-permute-start.8 = (f16[2,16,3328]{2,1,0:T(8,128)(2,1)S(1)}, f16[2,16,3328]{2,1,0:T(8,128)(2,1)S(1)}, u32[]{:S(2)}, u32[]{:S(2)}) collective-permute-start(f16[2,16,3328]{2,1,0:T(8,128)(2,1)S(1)} %pad_maximum_fusion.14), channel_id=1, source_target_pairs={{0,2},{2,0},{1,3},{3,1},{4,6},{6,4},{5,7},{7,5},{8,10},{10,8},{9,1... | collective-permute-start | bytes 638984 | tf_op jit(solution)/shard_map/ppermute | solution.py:31
  91.1 5.1 %collective-permute-start.16 = (f16[2,16,3328]{2,1,0:T(8,128)(2,1)S(1)}, f16[2,16,3328]{2,1,0:T(8,128)(2,1)S(1)}, u32[]{:S(2)}, u32[]{:S(2)}) collective-permute-start(f16[2,16,3328]{2,1,0:T(8,128)(2,1)S(1)} %pad_maximum_fusion.15), channel_id=1, source_target_pairs={{0,12},{1,5},{4,8},{5,1},{8,4},{9,13},{12,0},{13,9},{2,14},{3,7},{... | collective-permute-start | bytes 638984 | tf_op jit(solution)/shard_map/ppermute | solution.py:31
  91.2 5.1 %collective-permute-start.15 = (f16[2,16,3328]{2,1,0:T(8,128)(2,1)S(1)}, f16[2,16,3328]{2,1,0:T(8,128)(2,1)S(1)}, u32[]{:S(2)}, u32[]{:S(2)}) collective-permute-start(f16[2,16,3328]{2,1,0:T(8,128)(2,1)S(1)} %pad_maximum_fusion.16), channel_id=1, source_target_pairs={{0,2},{2,0},{1,3},{3,1},{4,6},{6,4},{5,7},{7,5},{8,10},{10,8},{9,1... | collective-permute-start | bytes 638984 | tf_op jit(solution)/shard_map/ppermute | solution.py:31
  92.8 32.6 %slice-start.8 = ((s8[6815744]{0:T(1024)(128)(4,1)}), s8[4194304]{0:T(1024)(128)(4,1)S(1)}, s32[]{:S(2)}) async-start(s8[6815744]{0:T(1024)(128)(4,1)} %bitcast.229), calls=%async_computation.9 | async-start | bytes 8388608
  93.0 10.4 %collective-permute-start.13 = (bf16[16,3328]{1,0:T(8,128)(2,1)S(1)}, bf16[16,3328]{1,0:T(8,128)(2,1)S(1)}, u32[]{:S(2)}, u32[]{:S(2)}) collective-permute-start(bf16[16,3328]{1,0:T(8,128)(2,1)S(1)} %fusion.63), channel_id=1, source_target_pairs={{0,12},{1,5},{4,8},{5,1},{8,4},{9,13},{12,0},{13,9},{2,14},{3,7},{... | collective-permute-start | bytes 319496 | tf_op jit(solution)/shard_map/ppermute | solution.py:31
  96.4 7.1 %collective-permute-start.19 = (bf16[16,3328]{1,0:T(8,128)(2,1)S(1)}, bf16[16,3328]{1,0:T(8,128)(2,1)S(1)}, u32[]{:S(2)}, u32[]{:S(2)}) collective-permute-start(bf16[16,3328]{1,0:T(8,128)(2,1)S(1)} %fusion.61), channel_id=1, source_target_pairs={{0,12},{1,5},{4,8},{5,1},{8,4},{9,13},{12,0},{13,9},{2,14},{3,7},{... | collective-permute-start | bytes 319496 | tf_op jit(solution)/shard_map/ppermute | solution.py:31
  99.2 7.1 %collective-permute-start.20 = (f16[2,16,3328]{2,1,0:T(8,128)(2,1)S(1)}, f16[2,16,3328]{2,1,0:T(8,128)(2,1)S(1)}, u32[]{:S(2)}, u32[]{:S(2)}) collective-permute-start(f16[2,16,3328]{2,1,0:T(8,128)(2,1)S(1)} %pad_maximum_fusion.18), channel_id=1, source_target_pairs={{0,2},{2,0},{1,3},{3,1},{4,6},{6,4},{5,7},{7,5},{8,10},{10,8},{9,1... | collective-permute-start | bytes 638984 | tf_op jit(solution)/shard_map/ppermute | solution.py:31
  100.4 17.4 %collective-permute-start.14 = (f16[2,32,3328]{2,1,0:T(8,128)(2,1)S(1)}, f16[2,32,3328]{2,1,0:T(8,128)(2,1)S(1)}, u32[]{:S(2)}, u32[]{:S(2)}) collective-permute-start(f16[2,32,3328]{2,1,0:T(8,128)(2,1)S(1)} %pad_maximum_fusion.7), channel_id=1, source_target_pairs={{0,4},{1,13},{4,0},{5,9},{8,12},{9,5},{12,8},{13,1},{2,6},{3,15},{... | collective-permute-start | bytes 1277960 | tf_op jit(solution)/shard_map/ppermute | solution.py:31
  103.4 8.0 %collective-permute-start.17 = (bf16[32,3328]{1,0:T(8,128)(2,1)S(1)}, bf16[32,3328]{1,0:T(8,128)(2,1)S(1)}, u32[]{:S(2)}, u32[]{:S(2)}) collective-permute-start(bf16[32,3328]{1,0:T(8,128)(2,1)S(1)} %pad_maximum_fusion.17), channel_id=1, source_target_pairs={{0,4},{1,13},{4,0},{5,9},{8,12},{9,5},{12,8},{13,1},{2,6},{3,15},{... | collective-permute-start | bytes 638984 | tf_op jit(solution)/shard_map/ppermute | solution.py:31
  103.6 11.3 %collective-permute-start.24 = (bf16[32,3328]{1,0:T(8,128)(2,1)S(1)}, bf16[32,3328]{1,0:T(8,128)(2,1)S(1)}, u32[]{:S(2)}, u32[]{:S(2)}) collective-permute-start(bf16[32,3328]{1,0:T(8,128)(2,1)S(1)} %pad_maximum_fusion.19), channel_id=1, source_target_pairs={{0,4},{1,13},{4,0},{5,9},{8,12},{9,5},{12,8},{13,1},{2,6},{3,15},{... | collective-permute-start | bytes 638984 | tf_op jit(solution)/shard_map/ppermute | solution.py:31
  106.4 10.6 %collective-permute-start.22 = (bf16[16,3328]{1,0:T(8,128)(2,1)S(1)}, bf16[16,3328]{1,0:T(8,128)(2,1)S(1)}, u32[]{:S(2)}, u32[]{:S(2)}) collective-permute-start(bf16[16,3328]{1,0:T(8,128)(2,1)S(1)} %fusion.59), channel_id=1, source_target_pairs={{0,12},{1,5},{4,8},{5,1},{8,4},{9,13},{12,0},{13,9},{2,14},{3,7},{... | collective-permute-start | bytes 319496 | tf_op jit(solution)/shard_map/ppermute | solution.py:31
  111.4 13.9 %slice-start.9 = ((s8[6815744]{0:T(1024)(128)(4,1)}), s8[2621440]{0:T(1024)(128)(4,1)S(1)}, s32[]{:S(2)}) async-start(s8[6815744]{0:T(1024)(128)(4,1)} %bitcast.229), calls=%async_computation.10 | async-start | bytes 5242880
  111.4 13.9 %collective-permute-start.21 = (bf16[64,3328]{1,0:T(8,128)(2,1)S(1)}, bf16[64,3328]{1,0:T(8,128)(2,1)S(1)}, u32[]{:S(2)}, u32[]{:S(2)}) collective-permute-start(bf16[64,3328]{1,0:T(8,128)(2,1)S(1)} %pad_maximum_fusion.8), channel_id=1, source_target_pairs={{0,1},{1,0},{2,3},{3,2},{4,5},{5,4},{6,7},{7,6},{8,9},{9,8},{10,11... | collective-permute-start | bytes 1277960 | tf_op jit(solution)/shard_map/ppermute | solution.py:31
  114.8 14.5 %collective-permute-start.25 = (bf16[64,3328]{1,0:T(8,128)(2,1)S(1)}, bf16[64,3328]{1,0:T(8,128)(2,1)S(1)}, u32[]{:S(2)}, u32[]{:S(2)}) collective-permute-start(bf16[64,3328]{1,0:T(8,128)(2,1)S(1)} %pad_maximum_fusion.9), channel_id=1, source_target_pairs={{0,1},{1,0},{2,3},{3,2},{4,5},{5,4},{6,7},{7,6},{8,9},{9,8},{10,11... | collective-permute-start | bytes 1277960 | tf_op jit(solution)/shard_map/ppermute | solution.py:31
  117.0 6.6 %collective-permute-start.28 = (bf16[32,3328]{1,0:T(8,128)(2,1)S(1)}, bf16[32,3328]{1,0:T(8,128)(2,1)S(1)}, u32[]{:S(2)}, u32[]{:S(2)}) collective-permute-start(bf16[32,3328]{1,0:T(8,128)(2,1)S(1)} %pad_maximum_fusion.20), channel_id=1, source_target_pairs={{0,4},{1,13},{4,0},{5,9},{8,12},{9,5},{12,8},{13,1},{2,6},{3,15},{... | collective-permute-start | bytes 638984 | tf_op jit(solution)/shard_map/ppermute | solution.py:31
  118.1 6.7 %collective-permute-start.18 = (f16[2,16,3328]{2,1,0:T(8,128)(2,1)S(1)}, f16[2,16,3328]{2,1,0:T(8,128)(2,1)S(1)}, u32[]{:S(2)}, u32[]{:S(2)}) collective-permute-start(f16[2,16,3328]{2,1,0:T(8,128)(2,1)S(1)} %pad_maximum_fusion.21), channel_id=1, source_target_pairs={{0,12},{1,5},{4,8},{5,1},{8,4},{9,13},{12,0},{13,9},{2,14},{3,7},{... | collective-permute-start | bytes 638984 | tf_op jit(solution)/shard_map/ppermute | solution.py:31
  123.6 16.7 %collective-permute-start.29 = (bf16[64,3328]{1,0:T(8,128)(2,1)S(1)}, bf16[64,3328]{1,0:T(8,128)(2,1)S(1)}, u32[]{:S(2)}, u32[]{:S(2)}) collective-permute-start(bf16[64,3328]{1,0:T(8,128)(2,1)S(1)} %pad_maximum_fusion.10), channel_id=1, source_target_pairs={{0,1},{1,0},{2,3},{3,2},{4,5},{5,4},{6,7},{7,6},{8,9},{9,8},{10,11... | collective-permute-start | bytes 1277960 | tf_op jit(solution)/shard_map/ppermute | solution.py:31
  125.0 5.7 %collective-permute-start.32 = (f16[2,16,3328]{2,1,0:T(8,128)(2,1)S(1)}, f16[2,16,3328]{2,1,0:T(8,128)(2,1)S(1)}, u32[]{:S(2)}, u32[]{:S(2)}) collective-permute-start(f16[2,16,3328]{2,1,0:T(8,128)(2,1)S(1)} %pad_maximum_fusion.22), channel_id=1, source_target_pairs={{0,2},{2,0},{1,3},{3,1},{4,6},{6,4},{5,7},{7,5},{8,10},{10,8},{9,1... | collective-permute-start | bytes 638984 | tf_op jit(solution)/shard_map/ppermute | solution.py:31
  126.5 28.0 %collective-permute-start.23 = (bf16[64,1024]{1,0:T(8,128)(2,1)S(1)}, bf16[64,1024]{1,0:T(8,128)(2,1)S(1)}, u32[]{:S(2)}, u32[]{:S(2)}) collective-permute-start(bf16[64,1024]{1,0:T(8,128)(2,1)S(1)} %select_convert_fusion.6), channel_id=1, source_target_pairs={{0,16},{16,0},{32,48},{48,32},{64,80},{80,64},{96,112},{112,96},{1... | collective-permute-start | bytes 393224 | tf_op jit(solution)/shard_map/ppermute | solution.py:31
  130.8 5.1 %collective-permute-start.33 = (bf16[16,3328]{1,0:T(8,128)(2,1)S(1)}, bf16[16,3328]{1,0:T(8,128)(2,1)S(1)}, u32[]{:S(2)}, u32[]{:S(2)}) collective-permute-start(bf16[16,3328]{1,0:T(8,128)(2,1)S(1)} %fusion.57), channel_id=1, source_target_pairs={{0,12},{1,5},{4,8},{5,1},{8,4},{9,13},{12,0},{13,9},{2,14},{3,7},{... | collective-permute-start | bytes 319496 | tf_op jit(solution)/shard_map/ppermute | solution.py:31
  135.9 6.1 %collective-permute-start.34 = (bf16[32,3328]{1,0:T(8,128)(2,1)S(1)}, bf16[32,3328]{1,0:T(8,128)(2,1)S(1)}, u32[]{:S(2)}, u32[]{:S(2)}) collective-permute-start(bf16[32,3328]{1,0:T(8,128)(2,1)S(1)} %pad_maximum_fusion.23), channel_id=1, source_target_pairs={{0,4},{1,13},{4,0},{5,9},{8,12},{9,5},{12,8},{13,1},{2,6},{3,15},{... | collective-permute-start | bytes 638984 | tf_op jit(solution)/shard_map/ppermute | solution.py:31
  136.0 21.5 %collective-permute-start.26 = (bf16[64,1024]{1,0:T(8,128)(2,1)S(1)}, bf16[64,1024]{1,0:T(8,128)(2,1)S(1)}, u32[]{:S(2)}, u32[]{:S(2)}) collective-permute-start(bf16[64,1024]{1,0:T(8,128)(2,1)S(1)} %get-tuple-element.305), channel_id=1, source_target_pairs={{0,32},{16,48},{32,64},{48,80},{64,96},{80,112},{96,0},{112,16},{1... | collective-permute-start | bytes 393224 | tf_op jit(solution)/shard_map/ppermute | solution.py:31
  136.7 29.3 %collective-permute-start.27 = (bf16[64,1024]{1,0:T(8,128)(2,1)S(1)}, bf16[64,1024]{1,0:T(8,128)(2,1)S(1)}, u32[]{:S(2)}, u32[]{:S(2)}) collective-permute-start(bf16[64,1024]{1,0:T(8,128)(2,1)S(1)} %get-tuple-element.306), channel_id=1, source_target_pairs={{0,48},{16,32},{32,80},{48,64},{64,112},{80,96},{96,16},{112,0},{1... | collective-permute-start | bytes 393224 | tf_op jit(solution)/shard_map/ppermute | solution.py:31
  142.1 8.2 %collective-permute-start.35 = (bf16[64,3328]{1,0:T(8,128)(2,1)S(1)}, bf16[64,3328]{1,0:T(8,128)(2,1)S(1)}, u32[]{:S(2)}, u32[]{:S(2)}) collective-permute-start(bf16[64,3328]{1,0:T(8,128)(2,1)S(1)} %pad_maximum_fusion.11), channel_id=1, source_target_pairs={{0,1},{1,0},{2,3},{3,2},{4,5},{5,4},{6,7},{7,6},{8,9},{9,8},{10,11... | collective-permute-start | bytes 1277960 | tf_op jit(solution)/shard_map/ppermute | solution.py:31
  147.7 18.3 %collective-permute-start.30 = (bf16[64,1024]{1,0:T(8,128)(2,1)S(1)}, bf16[64,1024]{1,0:T(8,128)(2,1)S(1)}, u32[]{:S(2)}, u32[]{:S(2)}) collective-permute-start(bf16[64,1024]{1,0:T(8,128)(2,1)S(1)} %get-tuple-element.308), channel_id=1, source_target_pairs={{0,64},{16,80},{32,96},{48,112},{64,0},{80,16},{96,32},{112,48},{1... | collective-permute-start | bytes 393224 | tf_op jit(solution)/shard_map/ppermute | solution.py:31
  150.3 15.8 %collective-permute-start.31 = (bf16[64,1024]{1,0:T(8,128)(2,1)S(1)}, bf16[64,1024]{1,0:T(8,128)(2,1)S(1)}, u32[]{:S(2)}, u32[]{:S(2)}) collective-permute-start(bf16[64,1024]{1,0:T(8,128)(2,1)S(1)} %get-tuple-element.309), channel_id=1, source_target_pairs={{0,80},{16,64},{32,112},{48,96},{64,16},{80,0},{96,48},{112,32},{1... | collective-permute-start | bytes 393224 | tf_op jit(solution)/shard_map/ppermute | solution.py:31
  154.4 11.6 %collective-permute-start.36 = (bf16[64,1024]{1,0:T(8,128)(2,1)S(1)}, bf16[64,1024]{1,0:T(8,128)(2,1)S(1)}, u32[]{:S(2)}, u32[]{:S(2)}) collective-permute-start(bf16[64,1024]{1,0:T(8,128)(2,1)S(1)} %get-tuple-element.313), channel_id=1, source_target_pairs={{0,96},{16,112},{32,0},{48,16},{64,32},{80,48},{96,64},{112,80},{1... | collective-permute-start | bytes 393224 | tf_op jit(solution)/shard_map/ppermute | solution.py:31
  157.5 8.6 %collective-permute-start.37 = (bf16[64,1024]{1,0:T(8,128)(2,1)S(1)}, bf16[64,1024]{1,0:T(8,128)(2,1)S(1)}, u32[]{:S(2)}, u32[]{:S(2)}) collective-permute-start(bf16[64,1024]{1,0:T(8,128)(2,1)S(1)} %get-tuple-element.314), channel_id=1, source_target_pairs={{0,112},{16,96},{32,16},{48,0},{64,48},{80,32},{96,80},{112,64},{1... | collective-permute-start | bytes 393224 | tf_op jit(solution)/shard_map/ppermute | solution.py:31
  (8 other events, 19.8 us)

commit v4 on v0

v4 whole, which is shorter than its diff:
```python
import jax
import jax.numpy as jnp
from jax import lax
from jax.sharding import Mesh, PartitionSpec as P

F32, BF16, F16 = jnp.float32, jnp.bfloat16, jnp.float16
LIFT = 8.0
AXES = ("x", "z_hi", "y", "z_lo", "core")


def permute(axes, sizes, move):
    def flat(place):
        index = 0
        for size, part in zip(sizes, place):
            index = index * size + part
        return index

    places = [()]
    for size in sizes:
        places = [p + (i,) for p in places for i in range(size)]
    pairs = [(flat(p), flat(move(*p))) for p in places]
    return lambda v: lax.ppermute(v, axes, pairs)


def lifted(v):
    return (v * LIFT).astype(F16)


def lowered(v):
    return v.astype(F32) * (1 / LIFT)


def per_device(tokens, gate_weight, up_weight, down_weight):
    z_hi, y, core = (lax.axis_index(a) for a in ("z_hi", "y", "core"))
    swap_core = permute(("core",), (2,), lambda c: (c ^ 1,))
    swap_z = permute(("z_lo",), (2,), lambda z: (z ^ 1,))
    swap_first = permute(("y", "core"), (4, 2), lambda y, c: (y ^ (3 if c else 1), c))
    swap_second = permute(("y", "core"), (4, 2), lambda y, c: (y ^ (1 if c else 3), c))
    swap_x = {e: permute(("x",), (4,), lambda x, e=e: (x ^ e,)) for e in (1, 2, 3)}
    swap_row = {
        e: permute(("x", "z_hi"), (4, 2), lambda x, z, e=e: (x ^ e, z ^ 1)) for e in range(4)
    }

    features = tokens.shape[1] // 16
    blocks = tokens.reshape(4, 16, features).transpose(1, 0, 2).reshape(1, 64, features)
    blocks = jnp.broadcast_to(blocks, (2, 64, features)).reshape(128, features)
    mine = lax.all_to_all(blocks, AXES[1:], split_axis=0, concat_axis=0, tiled=True)
    mine = mine.reshape(2, 4, 16, features)

    def places(half):
        first = jnp.where(half == 0, 1, 3)
        return (y, y ^ (4 - first), y ^ first, y ^ 2)

    halves = (1 - core, core)
    own = jnp.concatenate(
        [
            lax.dynamic_slice(mine, (half, p, 0, 0), (1, 1, 16, features)).reshape(16, features)
            for half in halves
            for p in places(half)
        ]
    )
    rows = {0: own}
    state = [{} for _ in range(4)]
    arrived = []
    stays = z_hi == core

    def tie(*values):
        values = lax.optimization_barrier(values)
        return values if len(values) > 1 else values[0]

    def product(rows, weight):
        return jnp.dot(rows, weight, preferred_element_type=F32)

    def parted(mixed):
        away, kept = mixed[:64], mixed[64:]
        return jnp.where(stays, kept, away), jnp.where(stays, away, kept)

    def step(e, s):
        st = state[e]
        if s == -1:
            rows[e] = swap_x[e](tie(own))
        elif s == 0:
            both = tie(rows[e])
            terms = [product(both, w) for w in (gate_weight, up_weight)]
            send, *st["total"] = tie(jnp.stack([lifted(v[:64]) for v in terms]), *terms)
            st["flight"] = swap_core(send)
        elif s in (2, 3, 4):
            got = tie(st["flight"])
            part = slice(64, 128) if s == 2 else slice(0, got.shape[1])
            total = [v[part] + lowered(g) for v, g in zip(st["total"], got)]
            part = slice(0 if s == 4 else got.shape[1] // 2, None)
            send, *st["total"] = tie(jnp.stack([lifted(v[part]) for v in total]), *total)
            st["flight"] = (swap_first, swap_second, swap_z)[s - 2](send)
        elif s == 5:
            gate, up = [v + lowered(g) for v, g in zip(st["total"], tie(st["flight"]))]
            st["hidden"] = tie((jax.nn.silu(gate) * up).astype(BF16))
            st["flight"] = swap_second(st["hidden"])
        elif s in (6, 7):
            st["hidden"] = tie(jnp.concatenate((st["hidden"], tie(st["flight"]))))
            st["flight"] = (swap_first if s == 6 else swap_core)(st["hidden"])
        elif s == 8:
            both = jnp.concatenate((tie(st["flight"]), st["hidden"]))
            mixed = product(both, down_weight)
            same, cross = parted(mixed)
            if e == 0:
                same, cross = tie(same, cross.astype(BF16))
                arrived.append(same)
            else:
                same, cross = tie(same.astype(BF16), cross.astype(BF16))
                arrived.append(swap_x[e](same).astype(F32))
            arrived.append(swap_row[e](cross).astype(F32))

    for s in (-1, 0, 2, 3, 4, 5, 6, 7, 8):
        for e in (0, 2, 1, 3):
            if e or s >= 0:
                step(e, s)

    out = sum(arrived).astype(BF16).reshape(4, 16, -1)
    first = jnp.where(z_hi == 0, 1, 3)
    blocks = []
    for p in range(4):
        e = y ^ p
        place = jnp.where(e == 0, 0, jnp.where(e == 2, 3, jnp.where(e == first, 2, 1)))
        blocks.append(lax.dynamic_index_in_dim(out, place, 0, keepdims=False))
    return jnp.concatenate(blocks)


def solution(mesh):
    grid = Mesh(mesh.devices.reshape(4, 2, 4, 2, 2), AXES)
    row, col = AXES[:2], AXES[2:]
    placed = (P(AXES, None), P(col, row), P(col, row), P(row, col))
    return jax.shard_map(
        per_device, mesh=grid, in_specs=placed, out_specs=P(row, col), check_vma=False
    )
```

time: 366 us -> 125 us (0.34)
  waiting for transfers between devices: 306 us -> 48 us
  starting transfers between devices: 0.13 us -> 51.6 us
  blocking collectives: 13.5 us -> 0 us
  between operations: 13.2 us -> 0.85 us
  matrix products: 22.4 us -> 15.8 us
    reduce_scatter x2 -> x0, waiting for transfers between devices: 223 us -> none  [the longest x1 150 us: per_device(): lax.psum_scatter(jnp.concatenate((gate_term, up_term), axis=1), 'col', sc...]
    all_gather x2 -> x0, waiting for transfers between devices: 82.2 us -> none  [the longest x1 46.2 us: per_device(): features = lax.all_gather(split_rows, 'row', axis=0, tiled=True)]
    ppermute x0 -> x38, starting transfers between devices: none -> 42 us  [permute(): return lambda v: lax.ppermute(v, axes, pairs)]
    ppermute x0 -> x38, waiting for transfers between devices: none -> 39.2 us  [permute(): return lambda v: lax.ppermute(v, axes, pairs)]
    all_to_all x1 -> x0, blocking collectives: 13.5 us -> none  [per_device(): lax.all_to_all(tokens, 'col', split_axis=1, concat_axis=0, tiled=True)]
    all_to_all x0 -> x1, starting transfers between devices: none -> 9.6 us  [per_device(): lax.all_to_all(blocks, AXES[1:], split_axis=0, concat_axis=0, tiled=True)]
    all_to_all x0 -> x1, waiting for transfers between devices: none -> 8.8 us  [per_device(): lax.all_to_all(blocks, AXES[1:], split_axis=0, concat_axis=0, tiled=True)]
    dot_general x3 -> x12, matrix products: 22.4 us -> 15.8 us  [product(): return jnp.dot(rows, weight, preferred_element_type=F32)]
  transfers between devices with their start and end apart: 4 -> 39, of which waited for: 4 -> 16; matrix products, arithmetic and copies ran while one was open for 0% -> 17% of each run, Pallas kernels for 0% -> 0%
where the time goes in v4:
time: 125 us; the launch traced here: 124 us
  starting transfers between devices  51.6 us (41%)
  waiting for transfers between devices  48 us (38%)
  matrix products  15.8 us (13%)
  other arithmetic  5.76 us (5%)
  local copies, waits for them, and re-layouts  2 us (2%)
    ppermute x38, starting transfers between devices, permute(): return lambda v: lax.ppermute(v, axes, pairs)  42 us
    ppermute x38, waiting for transfers between devices, permute(): return lambda v: lax.ppermute(v, axes, pairs)  39.2 us
    dot_general x12, matrix products, product(): return jnp.dot(rows, weight, preferred_element_type=F32)  15.8 us
    all_to_all x1, starting transfers between devices, per_device(): lax.all_to_all(blocks, AXES[1:], split_axis=0, concat_axis=0, tiled=True)  9.6 us
    all_to_all x1, waiting for transfers between devices, per_device(): lax.all_to_all(blocks, AXES[1:], split_axis=0, concat_axis=0, tiled=True)  8.8 us
  transfers between devices with their start and end apart: 39, of which 16 were waited for; matrix products, arithmetic and copies ran while one was open for 17% of the time, Pallas kernels for 0%

profile of v4, /device:TPU:1, one launch (start us, length us, event | category | flops | bytes accessed | tf_op | source)
XLA Modules:
  0.0 124.0 jit_solution(4522227177263835433)
XLA Ops:
  0.0 0.9 broadcast_in_dim.7
  1.0 0.8 all_to_all.6
  1.8 9.6 %all-to-all-start = ((bf16[32,4,1024]{2,1,0:T(4,128)(2,1)}), bf16[32,4,1024]{2,1,0:T(4,128)(2,1)S(1)}, u32[]{:S(2)}, u32[]{:S(2)}) async-start(bf16[32,4,1024]{2,1,0:T(4,128)(2,1)} %all_to_all.6), calls=%async_computation | async-start | bytes 524288 | tf_op jit(solution)/shard_map/all_to_all | solution.py:47
  11.4 8.8 %all-to-all-done = bf16[32,4,1024]{2,1,0:T(4,128)(2,1)S(1)} async-done(((bf16[32,4,1024]{2,1,0:T(4,128)(2,1)}), bf16[32,4,1024]{2,1,0:T(4,128)(2,1)S(1)}, u32[]{:S(2)}, u32[]{:S(2)}) %all-to-all-start) | async-done | bytes 262176 | tf_op jit(solution)/shard_map/all_to_all | solution.py:47
  20.5 2.6 %collective-permute-start.28 = (bf16[128,1024]{1,0:T(8,128)(2,1)S(1)}, bf16[128,1024]{1,0:T(8,128)(2,1)S(1)}, u32[]{:S(2)}, u32[]{:S(2)}) collective-permute-start(bf16[128,1024]{1,0:T(8,128)(2,1)S(1)} %bitcast_dynamic-update-slice_fusion), channel_id=1, source_target_pairs={{0,96},{32,64},{64,32},{96,0},{1,97},{33,65},{65,33},{97,1},{2,98}... | collective-permute-start | bytes 786440 | tf_op jit(solution)/shard_map/ppermute | solution.py:22
  23.1 1.4 %collective-permute-start.8 = (bf16[128,1024]{1,0:T(8,128)(2,1)S(1)}, bf16[128,1024]{1,0:T(8,128)(2,1)S(1)}, u32[]{:S(2)}, u32[]{:S(2)}) collective-permute-start(bf16[128,1024]{1,0:T(8,128)(2,1)S(1)} %bitcast_dynamic-update-slice_fusion), channel_id=1, source_target_pairs={{0,64},{32,96},{64,0},{96,32},{1,65},{33,97},{65,1},{97,33},{2,66}... | collective-permute-start | bytes 786440 | tf_op jit(solution)/shard_map/ppermute | solution.py:22
  24.4 4.1 %fusion.84 = f32[128,3328]{1,0:T(8,128)S(1)} fusion(bf16[128,1024]{1,0:T(8,128)(2,1)S(1)} %bitcast_dynamic-update-slice_fusion, bf16[1024,3328]{1,0:T(8,128)(2,1)} %param.5), kind=kOutput, calls=%fused_computation.194 | convolution fusion | flops 872415232 | bytes 8781824 | tf_op jit(solution)/shard_map/dot_general | solution.py:72
  28.6 1.1 fusion.85
  30.1 1.9 %collective-permute-start = (f16[2,64,3328]{2,1,0:T(8,128)(2,1)S(1)}, f16[2,64,3328]{2,1,0:T(8,128)(2,1)S(1)}, u32[]{:S(2)}, u32[]{:S(2)}) collective-permute-start(f16[2,64,3328]{2,1,0:T(8,128)(2,1)S(1)} %pad_maximum_fusion), channel_id=1, source_target_pairs={{0,1},{1,0},{2,3},{3,2},{4,5},{5,4},{6,7},{7,6},{8,9},{9,8},{10,11... | collective-permute-start | bytes 2555912 | tf_op jit(solution)/shard_map/ppermute | solution.py:22
  31.9 1.1 fusion.90
  33.0 1.1 fusion.91
  34.1 1.1 fusion.88
  35.2 1.1 fusion.89
  36.3 1.1 fusion.86
  37.3 1.1 fusion.87
  38.8 1.1 collective-permute-start.29
  41.8 0.8 collective-permute-start.1
  43.1 2.0 %collective-permute-start.30 = (f16[2,32,3328]{2,1,0:T(8,128)(2,1)S(1)}, f16[2,32,3328]{2,1,0:T(8,128)(2,1)S(1)}, u32[]{:S(2)}, u32[]{:S(2)}) collective-permute-start(f16[2,32,3328]{2,1,0:T(8,128)(2,1)S(1)} %pad_maximum_fusion.10), channel_id=1, source_target_pairs={{0,4},{1,13},{4,0},{5,9},{8,12},{9,5},{12,8},{13,1},{2,6},{3,15},{... | collective-permute-start | bytes 1277960 | tf_op jit(solution)/shard_map/ppermute | solution.py:22
  45.5 0.8 collective-permute-start.20
  46.6 3.5 %collective-permute-done.1 = f16[2,32,3328]{2,1,0:T(8,128)(2,1)S(1)} collective-permute-done((f16[2,32,3328]{2,1,0:T(8,128)(2,1)S(1)}, f16[2,32,3328]{2,1,0:T(8,128)(2,1)S(1)}, u32[]{:S(2)}, u32[]{:S(2)}) %collective-permute-start.1) | collective-permute-done | bytes 426016 | tf_op jit(solution)/shard_map/ppermute | solution.py:22
  50.5 0.8 collective-permute-start.10
  51.3 6.4 %collective-permute-done.2 = f16[2,16,3328]{2,1,0:T(8,128)(2,1)S(1)} collective-permute-done((f16[2,16,3328]{2,1,0:T(8,128)(2,1)S(1)}, f16[2,16,3328]{2,1,0:T(8,128)(2,1)S(1)}, u32[]{:S(2)}, u32[]{:S(2)}) %collective-permute-start.2) | collective-permute-done | bytes 213024 | tf_op jit(solution)/shard_map/ppermute | solution.py:22
  58.4 3.1 %collective-permute-done.20 = f16[2,32,3328]{2,1,0:T(8,128)(2,1)S(1)} collective-permute-done((f16[2,32,3328]{2,1,0:T(8,128)(2,1)S(1)}, f16[2,32,3328]{2,1,0:T(8,128)(2,1)S(1)}, u32[]{:S(2)}, u32[]{:S(2)}) %collective-permute-start.20) | collective-permute-done | bytes 426016 | tf_op jit(solution)/shard_map/ppermute | solution.py:22
  61.8 5.8 %collective-permute-done.10 = f16[2,32,3328]{2,1,0:T(8,128)(2,1)S(1)} collective-permute-done((f16[2,32,3328]{2,1,0:T(8,128)(2,1)S(1)}, f16[2,32,3328]{2,1,0:T(8,128)(2,1)S(1)}, u32[]{:S(2)}, u32[]{:S(2)}) %collective-permute-start.10) | collective-permute-done | bytes 426016 | tf_op jit(solution)/shard_map/ppermute | solution.py:22
  68.2 1.4 %collective-permute-start.4 = (bf16[16,3328]{1,0:T(8,128)(2,1)S(1)}, bf16[16,3328]{1,0:T(8,128)(2,1)S(1)}, u32[]{:S(2)}, u32[]{:S(2)}) collective-permute-start(bf16[16,3328]{1,0:T(8,128)(2,1)S(1)} %fusion.63), channel_id=1, source_target_pairs={{0,12},{1,5},{4,8},{5,1},{8,4},{9,13},{12,0},{13,9},{2,14},{3,7},{... | collective-permute-start | bytes 319496 | tf_op jit(solution)/shard_map/ppermute | solution.py:22
  70.4 1.2 collective-permute-start.22
  71.5 1.1 collective-permute-done.11
  72.9 0.9 collective-permute-done.4
  75.1 2.0 %collective-permute-done.22 = f16[2,16,3328]{2,1,0:T(8,128)(2,1)S(1)} collective-permute-done((f16[2,16,3328]{2,1,0:T(8,128)(2,1)S(1)}, f16[2,16,3328]{2,1,0:T(8,128)(2,1)S(1)}, u32[]{:S(2)}, u32[]{:S(2)}) %collective-permute-start.22) | collective-permute-done | bytes 213024 | tf_op jit(solution)/shard_map/ppermute | solution.py:22
  77.9 3.1 %collective-permute-done.12 = f16[2,16,3328]{2,1,0:T(8,128)(2,1)S(1)} collective-permute-done((f16[2,16,3328]{2,1,0:T(8,128)(2,1)S(1)}, f16[2,16,3328]{2,1,0:T(8,128)(2,1)S(1)}, u32[]{:S(2)}, u32[]{:S(2)}) %collective-permute-start.12) | collective-permute-done | bytes 213024 | tf_op jit(solution)/shard_map/ppermute | solution.py:22
  81.1 1.3 %collective-permute-start.13 = (bf16[16,3328]{1,0:T(8,128)(2,1)S(1)}, bf16[16,3328]{1,0:T(8,128)(2,1)S(1)}, u32[]{:S(2)}, u32[]{:S(2)}) collective-permute-start(bf16[16,3328]{1,0:T(8,128)(2,1)S(1)} %fusion.61), channel_id=1, source_target_pairs={{0,12},{1,5},{4,8},{5,1},{8,4},{9,13},{12,0},{13,9},{2,14},{3,7},{... | collective-permute-start | bytes 319496 | tf_op jit(solution)/shard_map/ppermute | solution.py:22
  82.5 5.6 %collective-permute-start.6 = (bf16[64,3328]{1,0:T(8,128)(2,1)S(1)}, bf16[64,3328]{1,0:T(8,128)(2,1)S(1)}, u32[]{:S(2)}, u32[]{:S(2)}) collective-permute-start(bf16[64,3328]{1,0:T(8,128)(2,1)S(1)} %pad_maximum_fusion.5), channel_id=1, source_target_pairs={{0,1},{1,0},{2,3},{3,2},{4,5},{5,4},{6,7},{7,6},{8,9},{9,8},{10,11... | collective-permute-start | bytes 1277960 | tf_op jit(solution)/shard_map/ppermute | solution.py:22
  88.1 1.9 %collective-permute-start.34 = (bf16[32,3328]{1,0:T(8,128)(2,1)S(1)}, bf16[32,3328]{1,0:T(8,128)(2,1)S(1)}, u32[]{:S(2)}, u32[]{:S(2)}) collective-permute-start(bf16[32,3328]{1,0:T(8,128)(2,1)S(1)} %pad_maximum_fusion.23), channel_id=1, source_target_pairs={{0,4},{1,13},{4,0},{5,9},{8,12},{9,5},{12,8},{13,1},{2,6},{3,15},{... | collective-permute-start | bytes 638984 | tf_op jit(solution)/shard_map/ppermute | solution.py:22
  90.0 0.9 collective-permute-start.24
  91.0 1.9 %collective-permute-start.14 = (bf16[32,3328]{1,0:T(8,128)(2,1)S(1)}, bf16[32,3328]{1,0:T(8,128)(2,1)S(1)}, u32[]{:S(2)}, u32[]{:S(2)}) collective-permute-start(bf16[32,3328]{1,0:T(8,128)(2,1)S(1)} %pad_maximum_fusion.17), channel_id=1, source_target_pairs={{0,4},{1,13},{4,0},{5,9},{8,12},{9,5},{12,8},{13,1},{2,6},{3,15},{... | collective-permute-start | bytes 638984 | tf_op jit(solution)/shard_map/ppermute | solution.py:22
  92.9 1.4 %collective-permute-done.34 = bf16[32,3328]{1,0:T(8,128)(2,1)S(1)} collective-permute-done((bf16[32,3328]{1,0:T(8,128)(2,1)S(1)}, bf16[32,3328]{1,0:T(8,128)(2,1)S(1)}, u32[]{:S(2)}, u32[]{:S(2)}) %collective-permute-start.34) | collective-permute-done | bytes 213024 | tf_op jit(solution)/shard_map/ppermute | solution.py:22
  94.4 2.2 %collective-permute-done.24 = bf16[32,3328]{1,0:T(8,128)(2,1)S(1)} collective-permute-done((bf16[32,3328]{1,0:T(8,128)(2,1)S(1)}, bf16[32,3328]{1,0:T(8,128)(2,1)S(1)}, u32[]{:S(2)}, u32[]{:S(2)}) %collective-permute-start.24) | collective-permute-done | bytes 213024 | tf_op jit(solution)/shard_map/ppermute | solution.py:22
  96.7 2.2 %collective-permute-done.14 = bf16[32,3328]{1,0:T(8,128)(2,1)S(1)} collective-permute-done((bf16[32,3328]{1,0:T(8,128)(2,1)S(1)}, bf16[32,3328]{1,0:T(8,128)(2,1)S(1)}, u32[]{:S(2)}, u32[]{:S(2)}) %collective-permute-start.14) | collective-permute-done | bytes 213024 | tf_op jit(solution)/shard_map/ppermute | solution.py:22
  99.0 1.0 fusion.8
  100.7 1.1 fusion.20
  101.8 5.0 %collective-permute-start.37 = (bf16[64,1024]{1,0:T(8,128)(2,1)S(1)}, bf16[64,1024]{1,0:T(8,128)(2,1)S(1)}, u32[]{:S(2)}, u32[]{:S(2)}) collective-permute-start(bf16[64,1024]{1,0:T(8,128)(2,1)S(1)} %get-tuple-element.116), channel_id=1, source_target_pairs={{0,112},{16,96},{32,80},{48,64},{64,48},{80,32},{96,16},{112,0},{1... | collective-permute-start | bytes 393224 | tf_op jit(solution)/shard_map/ppermute | solution.py:22
  107.0 1.1 fusion.16
  108.2 1.4 %collective-permute-start.26 = (bf16[64,1024]{1,0:T(8,128)(2,1)S(1)}, bf16[64,1024]{1,0:T(8,128)(2,1)S(1)}, u32[]{:S(2)}, u32[]{:S(2)}) collective-permute-start(bf16[64,1024]{1,0:T(8,128)(2,1)S(1)} %get-tuple-element.101), channel_id=1, source_target_pairs={{0,32},{32,0},{64,96},{96,64},{1,33},{33,1},{65,97},{97,65},{2,34}... | collective-permute-start | bytes 393224 | tf_op jit(solution)/shard_map/ppermute | solution.py:22
  109.6 1.0 fusion.12
  110.7 4.8 %collective-permute-start.17 = (bf16[64,1024]{1,0:T(8,128)(2,1)S(1)}, bf16[64,1024]{1,0:T(8,128)(2,1)S(1)}, u32[]{:S(2)}, u32[]{:S(2)}) collective-permute-start(bf16[64,1024]{1,0:T(8,128)(2,1)S(1)} %get-tuple-element.88), channel_id=1, source_target_pairs={{0,80},{16,64},{32,112},{48,96},{64,16},{80,0},{96,48},{112,32},{1... | collective-permute-start | bytes 393224 | tf_op jit(solution)/shard_map/ppermute | solution.py:22
  115.4 0.8 collective-permute-start.16
  116.2 5.5 %collective-permute-done.17 = bf16[64,1024]{1,0:T(8,128)(2,1)S(1)} collective-permute-done((bf16[64,1024]{1,0:T(8,128)(2,1)S(1)}, bf16[64,1024]{1,0:T(8,128)(2,1)S(1)}, u32[]{:S(2)}, u32[]{:S(2)}) %collective-permute-start.17) | collective-permute-done | bytes 131104 | tf_op jit(solution)/shard_map/ppermute | solution.py:22
  121.8 1.4 %collective-permute-done.16 = bf16[64,1024]{1,0:T(8,128)(2,1)S(1)} collective-permute-done((bf16[64,1024]{1,0:T(8,128)(2,1)S(1)}, bf16[64,1024]{1,0:T(8,128)(2,1)S(1)}, u32[]{:S(2)}, u32[]{:S(2)}) %collective-permute-start.16) | collective-permute-done | bytes 131104 | tf_op jit(solution)/shard_map/ppermute | solution.py:22
  (137 shorter events, 11.1 us)
Async XLA Ops:
  1.8 18.5 %all-to-all-start = ((bf16[32,4,1024]{2,1,0:T(4,128)(2,1)}), bf16[32,4,1024]{2,1,0:T(4,128)(2,1)S(1)}, u32[]{:S(2)}, u32[]{:S(2)}) async-start(bf16[32,4,1024]{2,1,0:T(4,128)(2,1)} %all_to_all.6), calls=%async_computation | async-start | bytes 524288 | tf_op jit(solution)/shard_map/all_to_all | solution.py:47
  20.4 8.2 %slice-start.2 = ((s8[6815744]{0:T(1024)(128)(4,1)}), s8[4194304]{0:T(1024)(128)(4,1)S(1)}, s32[]{:S(2)}) async-start(s8[6815744]{0:T(1024)(128)(4,1)} %bitcast.210), calls=%async_computation.3 | async-start | bytes 8388608
  20.5 8.1 %slice-start.3 = ((s8[6815744]{0:T(1024)(128)(4,1)}), s8[2621440]{0:T(1024)(128)(4,1)S(1)}, s32[]{:S(2)}) async-start(s8[6815744]{0:T(1024)(128)(4,1)} %bitcast.210), calls=%async_computation.4 | async-start | bytes 5242880
  20.5 11.4 %collective-permute-start.28 = (bf16[128,1024]{1,0:T(8,128)(2,1)S(1)}, bf16[128,1024]{1,0:T(8,128)(2,1)S(1)}, u32[]{:S(2)}, u32[]{:S(2)}) collective-permute-start(bf16[128,1024]{1,0:T(8,128)(2,1)S(1)} %bitcast_dynamic-update-slice_fusion), channel_id=1, source_target_pairs={{0,96},{32,64},{64,32},{96,0},{1,97},{33,65},{65,33},{97,1},{2,98}... | collective-permute-start | bytes 786440 | tf_op jit(solution)/shard_map/ppermute | solution.py:22
  23.1 11.0 %collective-permute-start.18 = (bf16[128,1024]{1,0:T(8,128)(2,1)S(1)}, bf16[128,1024]{1,0:T(8,128)(2,1)S(1)}, u32[]{:S(2)}, u32[]{:S(2)}) collective-permute-start(bf16[128,1024]{1,0:T(8,128)(2,1)S(1)} %bitcast_dynamic-update-slice_fusion), channel_id=1, source_target_pairs={{0,32},{32,0},{64,96},{96,64},{1,33},{33,1},{65,97},{97,65},{2,34}... | collective-permute-start | bytes 786440 | tf_op jit(solution)/shard_map/ppermute | solution.py:22
  23.1 13.2 %collective-permute-start.8 = (bf16[128,1024]{1,0:T(8,128)(2,1)S(1)}, bf16[128,1024]{1,0:T(8,128)(2,1)S(1)}, u32[]{:S(2)}, u32[]{:S(2)}) collective-permute-start(bf16[128,1024]{1,0:T(8,128)(2,1)S(1)} %bitcast_dynamic-update-slice_fusion), channel_id=1, source_target_pairs={{0,64},{32,96},{64,0},{96,32},{1,65},{33,97},{65,1},{97,33},{2,66}... | collective-permute-start | bytes 786440 | tf_op jit(solution)/shard_map/ppermute | solution.py:22
  24.4 7.5 %slice-start = ((s8[6815744]{0:T(1024)(128)(4,1)}), s8[4194304]{0:T(1024)(128)(4,1)S(1)}, s32[]{:S(2)}) async-start(s8[6815744]{0:T(1024)(128)(4,1)} %bitcast.208), calls=%async_computation.1 | async-start | bytes 8388608
  28.6 3.3 %slice-start.1 = ((s8[6815744]{0:T(1024)(128)(4,1)}), s8[2621440]{0:T(1024)(128)(4,1)S(1)}, s32[]{:S(2)}) async-start(s8[6815744]{0:T(1024)(128)(4,1)} %bitcast.208), calls=%async_computation.2 | async-start | bytes 5242880
  30.1 11.4 %collective-permute-start = (f16[2,64,3328]{2,1,0:T(8,128)(2,1)S(1)}, f16[2,64,3328]{2,1,0:T(8,128)(2,1)S(1)}, u32[]{:S(2)}, u32[]{:S(2)}) collective-permute-start(f16[2,64,3328]{2,1,0:T(8,128)(2,1)S(1)} %pad_maximum_fusion), channel_id=1, source_target_pairs={{0,1},{1,0},{2,3},{3,2},{4,5},{5,4},{6,7},{7,6},{8,9},{9,8},{10,11... | collective-permute-start | bytes 2555912 | tf_op jit(solution)/shard_map/ppermute | solution.py:22
  38.8 3.9 %collective-permute-start.29 = (f16[2,64,3328]{2,1,0:T(8,128)(2,1)S(1)}, f16[2,64,3328]{2,1,0:T(8,128)(2,1)S(1)}, u32[]{:S(2)}, u32[]{:S(2)}) collective-permute-start(f16[2,64,3328]{2,1,0:T(8,128)(2,1)S(1)} %pad_maximum_fusion.3), channel_id=1, source_target_pairs={{0,1},{1,0},{2,3},{3,2},{4,5},{5,4},{6,7},{7,6},{8,9},{9,8},{10,11... | collective-permute-start | bytes 2555912 | tf_op jit(solution)/shard_map/ppermute | solution.py:22
  40.2 4.8 %collective-permute-start.19 = (f16[2,64,3328]{2,1,0:T(8,128)(2,1)S(1)}, f16[2,64,3328]{2,1,0:T(8,128)(2,1)S(1)}, u32[]{:S(2)}, u32[]{:S(2)}) collective-permute-start(f16[2,64,3328]{2,1,0:T(8,128)(2,1)S(1)} %pad_maximum_fusion.2), channel_id=1, source_target_pairs={{0,1},{1,0},{2,3},{3,2},{4,5},{5,4},{6,7},{7,6},{8,9},{9,8},{10,11... | collective-permute-start | bytes 2555912 | tf_op jit(solution)/shard_map/ppermute | solution.py:22
  40.7 5.6 %collective-permute-start.9 = (f16[2,64,3328]{2,1,0:T(8,128)(2,1)S(1)}, f16[2,64,3328]{2,1,0:T(8,128)(2,1)S(1)}, u32[]{:S(2)}, u32[]{:S(2)}) collective-permute-start(f16[2,64,3328]{2,1,0:T(8,128)(2,1)S(1)} %pad_maximum_fusion.1), channel_id=1, source_target_pairs={{0,1},{1,0},{2,3},{3,2},{4,5},{5,4},{6,7},{7,6},{8,9},{9,8},{10,11... | collective-permute-start | bytes 2555912 | tf_op jit(solution)/shard_map/ppermute | solution.py:22
  41.8 8.3 %collective-permute-start.1 = (f16[2,32,3328]{2,1,0:T(8,128)(2,1)S(1)}, f16[2,32,3328]{2,1,0:T(8,128)(2,1)S(1)}, u32[]{:S(2)}, u32[]{:S(2)}) collective-permute-start(f16[2,32,3328]{2,1,0:T(8,128)(2,1)S(1)} %pad_maximum_fusion.4), channel_id=1, source_target_pairs={{0,4},{1,13},{4,0},{5,9},{8,12},{9,5},{12,8},{13,1},{2,6},{3,15},{... | collective-permute-start | bytes 1277960 | tf_op jit(solution)/shard_map/ppermute | solution.py:22
  43.1 15.0 %collective-permute-start.30 = (f16[2,32,3328]{2,1,0:T(8,128)(2,1)S(1)}, f16[2,32,3328]{2,1,0:T(8,128)(2,1)S(1)}, u32[]{:S(2)}, u32[]{:S(2)}) collective-permute-start(f16[2,32,3328]{2,1,0:T(8,128)(2,1)S(1)} %pad_maximum_fusion.10), channel_id=1, source_target_pairs={{0,4},{1,13},{4,0},{5,9},{8,12},{9,5},{12,8},{13,1},{2,6},{3,15},{... | collective-permute-start | bytes 1277960 | tf_op jit(solution)/shard_map/ppermute | solution.py:22
  45.5 16.0 %collective-permute-start.20 = (f16[2,32,3328]{2,1,0:T(8,128)(2,1)S(1)}, f16[2,32,3328]{2,1,0:T(8,128)(2,1)S(1)}, u32[]{:S(2)}, u32[]{:S(2)}) collective-permute-start(f16[2,32,3328]{2,1,0:T(8,128)(2,1)S(1)} %pad_maximum_fusion.8), channel_id=1, source_target_pairs={{0,4},{1,13},{4,0},{5,9},{8,12},{9,5},{12,8},{13,1},{2,6},{3,15},{... | collective-permute-start | bytes 1277960 | tf_op jit(solution)/shard_map/ppermute | solution.py:22
  50.3 7.4 %collective-permute-start.2 = (f16[2,16,3328]{2,1,0:T(8,128)(2,1)S(1)}, f16[2,16,3328]{2,1,0:T(8,128)(2,1)S(1)}, u32[]{:S(2)}, u32[]{:S(2)}) collective-permute-start(f16[2,16,3328]{2,1,0:T(8,128)(2,1)S(1)} %pad_maximum_fusion.12), channel_id=1, source_target_pairs={{0,12},{1,5},{4,8},{5,1},{8,4},{9,13},{12,0},{13,9},{2,14},{3,7},{... | collective-permute-start | bytes 638984 | tf_op jit(solution)/shard_map/ppermute | solution.py:22
  50.5 17.1 %collective-permute-start.10 = (f16[2,32,3328]{2,1,0:T(8,128)(2,1)S(1)}, f16[2,32,3328]{2,1,0:T(8,128)(2,1)S(1)}, u32[]{:S(2)}, u32[]{:S(2)}) collective-permute-start(f16[2,32,3328]{2,1,0:T(8,128)(2,1)S(1)} %pad_maximum_fusion.6), channel_id=1, source_target_pairs={{0,4},{1,13},{4,0},{5,9},{8,12},{9,5},{12,8},{13,1},{2,6},{3,15},{... | collective-permute-start | bytes 1277960 | tf_op jit(solution)/shard_map/ppermute | solution.py:22
  57.9 10.2 %collective-permute-start.3 = (f16[2,16,3328]{2,1,0:T(8,128)(2,1)S(1)}, f16[2,16,3328]{2,1,0:T(8,128)(2,1)S(1)}, u32[]{:S(2)}, u32[]{:S(2)}) collective-permute-start(f16[2,16,3328]{2,1,0:T(8,128)(2,1)S(1)} %pad_maximum_fusion.13), channel_id=1, source_target_pairs={{0,2},{2,0},{1,3},{3,1},{4,6},{6,4},{5,7},{7,5},{8,10},{10,8},{9,1... | collective-permute-start | bytes 638984 | tf_op jit(solution)/shard_map/ppermute | solution.py:22
  58.3 11.3 %collective-permute-start.31 = (f16[2,16,3328]{2,1,0:T(8,128)(2,1)S(1)}, f16[2,16,3328]{2,1,0:T(8,128)(2,1)S(1)}, u32[]{:S(2)}, u32[]{:S(2)}) collective-permute-start(f16[2,16,3328]{2,1,0:T(8,128)(2,1)S(1)} %pad_maximum_fusion.21), channel_id=1, source_target_pairs={{0,12},{1,5},{4,8},{5,1},{8,4},{9,13},{12,0},{13,9},{2,14},{3,7},{... | collective-permute-start | bytes 638984 | tf_op jit(solution)/shard_map/ppermute | solution.py:22
  61.7 8.5 %collective-permute-start.21 = (f16[2,16,3328]{2,1,0:T(8,128)(2,1)S(1)}, f16[2,16,3328]{2,1,0:T(8,128)(2,1)S(1)}, u32[]{:S(2)}, u32[]{:S(2)}) collective-permute-start(f16[2,16,3328]{2,1,0:T(8,128)(2,1)S(1)} %pad_maximum_fusion.18), channel_id=1, source_target_pairs={{0,12},{1,5},{4,8},{5,1},{8,4},{9,13},{12,0},{13,9},{2,14},{3,7},{... | collective-permute-start | bytes 638984 | tf_op jit(solution)/shard_map/ppermute | solution.py:22
  67.6 31.4 %slice-start.4 = ((s8[6815744]{0:T(1024)(128)(4,1)}), s8[4194304]{0:T(1024)(128)(4,1)S(1)}, s32[]{:S(2)}) async-start(s8[6815744]{0:T(1024)(128)(4,1)} %bitcast.212), calls=%async_computation.5 | async-start | bytes 8388608
  67.8 4.8 %collective-permute-start.11 = (f16[2,16,3328]{2,1,0:T(8,128)(2,1)S(1)}, f16[2,16,3328]{2,1,0:T(8,128)(2,1)S(1)}, u32[]{:S(2)}, u32[]{:S(2)}) collective-permute-start(f16[2,16,3328]{2,1,0:T(8,128)(2,1)S(1)} %pad_maximum_fusion.15), channel_id=1, source_target_pairs={{0,12},{1,5},{4,8},{5,1},{8,4},{9,13},{12,0},{13,9},{2,14},{3,7},{... | collective-permute-start | bytes 638984 | tf_op jit(solution)/shard_map/ppermute | solution.py:22
  68.2 5.6 %collective-permute-start.4 = (bf16[16,3328]{1,0:T(8,128)(2,1)S(1)}, bf16[16,3328]{1,0:T(8,128)(2,1)S(1)}, u32[]{:S(2)}, u32[]{:S(2)}) collective-permute-start(bf16[16,3328]{1,0:T(8,128)(2,1)S(1)} %fusion.63), channel_id=1, source_target_pairs={{0,12},{1,5},{4,8},{5,1},{8,4},{9,13},{12,0},{13,9},{2,14},{3,7},{... | collective-permute-start | bytes 319496 | tf_op jit(solution)/shard_map/ppermute | solution.py:22
  69.7 4.8 %collective-permute-start.32 = (f16[2,16,3328]{2,1,0:T(8,128)(2,1)S(1)}, f16[2,16,3328]{2,1,0:T(8,128)(2,1)S(1)}, u32[]{:S(2)}, u32[]{:S(2)}) collective-permute-start(f16[2,16,3328]{2,1,0:T(8,128)(2,1)S(1)} %pad_maximum_fusion.22), channel_id=1, source_target_pairs={{0,2},{2,0},{1,3},{3,1},{4,6},{6,4},{5,7},{7,5},{8,10},{10,8},{9,1... | collective-permute-start | bytes 638984 | tf_op jit(solution)/shard_map/ppermute | solution.py:22
  70.4 28.7 %slice-start.5 = ((s8[6815744]{0:T(1024)(128)(4,1)}), s8[2621440]{0:T(1024)(128)(4,1)S(1)}, s32[]{:S(2)}) async-start(s8[6815744]{0:T(1024)(128)(4,1)} %bitcast.212), calls=%async_computation.6 | async-start | bytes 5242880
  70.4 6.7 %collective-permute-start.22 = (f16[2,16,3328]{2,1,0:T(8,128)(2,1)S(1)}, f16[2,16,3328]{2,1,0:T(8,128)(2,1)S(1)}, u32[]{:S(2)}, u32[]{:S(2)}) collective-permute-start(f16[2,16,3328]{2,1,0:T(8,128)(2,1)S(1)} %pad_maximum_fusion.19), channel_id=1, source_target_pairs={{0,2},{2,0},{1,3},{3,1},{4,6},{6,4},{5,7},{7,5},{8,10},{10,8},{9,1... | collective-permute-start | bytes 638984 | tf_op jit(solution)/shard_map/ppermute | solution.py:22
  72.8 8.2 %collective-permute-start.12 = (f16[2,16,3328]{2,1,0:T(8,128)(2,1)S(1)}, f16[2,16,3328]{2,1,0:T(8,128)(2,1)S(1)}, u32[]{:S(2)}, u32[]{:S(2)}) collective-permute-start(f16[2,16,3328]{2,1,0:T(8,128)(2,1)S(1)} %pad_maximum_fusion.16), channel_id=1, source_target_pairs={{0,2},{2,0},{1,3},{3,1},{4,6},{6,4},{5,7},{7,5},{8,10},{10,8},{9,1... | collective-permute-start | bytes 638984 | tf_op jit(solution)/shard_map/ppermute | solution.py:22
  73.8 8.6 %collective-permute-start.5 = (bf16[32,3328]{1,0:T(8,128)(2,1)S(1)}, bf16[32,3328]{1,0:T(8,128)(2,1)S(1)}, u32[]{:S(2)}, u32[]{:S(2)}) collective-permute-start(bf16[32,3328]{1,0:T(8,128)(2,1)S(1)} %pad_maximum_fusion.14), channel_id=1, source_target_pairs={{0,4},{1,13},{4,0},{5,9},{8,12},{9,5},{12,8},{13,1},{2,6},{3,15},{... | collective-permute-start | bytes 638984 | tf_op jit(solution)/shard_map/ppermute | solution.py:22
  74.6 13.4 %collective-permute-start.33 = (bf16[16,3328]{1,0:T(8,128)(2,1)S(1)}, bf16[16,3328]{1,0:T(8,128)(2,1)S(1)}, u32[]{:S(2)}, u32[]{:S(2)}) collective-permute-start(bf16[16,3328]{1,0:T(8,128)(2,1)S(1)} %fusion.57), channel_id=1, source_target_pairs={{0,12},{1,5},{4,8},{5,1},{8,4},{9,13},{12,0},{13,9},{2,14},{3,7},{... | collective-permute-start | bytes 319496 | tf_op jit(solution)/shard_map/ppermute | solution.py:22
  77.2 12.8 %collective-permute-start.23 = (bf16[16,3328]{1,0:T(8,128)(2,1)S(1)}, bf16[16,3328]{1,0:T(8,128)(2,1)S(1)}, u32[]{:S(2)}, u32[]{:S(2)}) collective-permute-start(bf16[16,3328]{1,0:T(8,128)(2,1)S(1)} %fusion.59), channel_id=1, source_target_pairs={{0,12},{1,5},{4,8},{5,1},{8,4},{9,13},{12,0},{13,9},{2,14},{3,7},{... | collective-permute-start | bytes 319496 | tf_op jit(solution)/shard_map/ppermute | solution.py:22
  81.1 9.9 %collective-permute-start.13 = (bf16[16,3328]{1,0:T(8,128)(2,1)S(1)}, bf16[16,3328]{1,0:T(8,128)(2,1)S(1)}, u32[]{:S(2)}, u32[]{:S(2)}) collective-permute-start(bf16[16,3328]{1,0:T(8,128)(2,1)S(1)} %fusion.61), channel_id=1, source_target_pairs={{0,12},{1,5},{4,8},{5,1},{8,4},{9,13},{12,0},{13,9},{2,14},{3,7},{... | collective-permute-start | bytes 319496 | tf_op jit(solution)/shard_map/ppermute | solution.py:22
  82.5 16.6 %collective-permute-start.6 = (bf16[64,3328]{1,0:T(8,128)(2,1)S(1)}, bf16[64,3328]{1,0:T(8,128)(2,1)S(1)}, u32[]{:S(2)}, u32[]{:S(2)}) collective-permute-start(bf16[64,3328]{1,0:T(8,128)(2,1)S(1)} %pad_maximum_fusion.5), channel_id=1, source_target_pairs={{0,1},{1,0},{2,3},{3,2},{4,5},{5,4},{6,7},{7,6},{8,9},{9,8},{10,11... | collective-permute-start | bytes 1277960 | tf_op jit(solution)/shard_map/ppermute | solution.py:22
  88.1 6.2 %collective-permute-start.34 = (bf16[32,3328]{1,0:T(8,128)(2,1)S(1)}, bf16[32,3328]{1,0:T(8,128)(2,1)S(1)}, u32[]{:S(2)}, u32[]{:S(2)}) collective-permute-start(bf16[32,3328]{1,0:T(8,128)(2,1)S(1)} %pad_maximum_fusion.23), channel_id=1, source_target_pairs={{0,4},{1,13},{4,0},{5,9},{8,12},{9,5},{12,8},{13,1},{2,6},{3,15},{... | collective-permute-start | bytes 638984 | tf_op jit(solution)/shard_map/ppermute | solution.py:22
  90.0 6.6 %collective-permute-start.24 = (bf16[32,3328]{1,0:T(8,128)(2,1)S(1)}, bf16[32,3328]{1,0:T(8,128)(2,1)S(1)}, u32[]{:S(2)}, u32[]{:S(2)}) collective-permute-start(bf16[32,3328]{1,0:T(8,128)(2,1)S(1)} %pad_maximum_fusion.20), channel_id=1, source_target_pairs={{0,4},{1,13},{4,0},{5,9},{8,12},{9,5},{12,8},{13,1},{2,6},{3,15},{... | collective-permute-start | bytes 638984 | tf_op jit(solution)/shard_map/ppermute | solution.py:22
  91.0 7.9 %collective-permute-start.14 = (bf16[32,3328]{1,0:T(8,128)(2,1)S(1)}, bf16[32,3328]{1,0:T(8,128)(2,1)S(1)}, u32[]{:S(2)}, u32[]{:S(2)}) collective-permute-start(bf16[32,3328]{1,0:T(8,128)(2,1)S(1)} %pad_maximum_fusion.17), channel_id=1, source_target_pairs={{0,4},{1,13},{4,0},{5,9},{8,12},{9,5},{12,8},{13,1},{2,6},{3,15},{... | collective-permute-start | bytes 638984 | tf_op jit(solution)/shard_map/ppermute | solution.py:22
  94.3 6.3 %collective-permute-start.35 = (bf16[64,3328]{1,0:T(8,128)(2,1)S(1)}, bf16[64,3328]{1,0:T(8,128)(2,1)S(1)}, u32[]{:S(2)}, u32[]{:S(2)}) collective-permute-start(bf16[64,3328]{1,0:T(8,128)(2,1)S(1)} %pad_maximum_fusion.11), channel_id=1, source_target_pairs={{0,1},{1,0},{2,3},{3,2},{4,5},{5,4},{6,7},{7,6},{8,9},{9,8},{10,11... | collective-permute-start | bytes 1277960 | tf_op jit(solution)/shard_map/ppermute | solution.py:22
  96.6 10.4 %collective-permute-start.25 = (bf16[64,3328]{1,0:T(8,128)(2,1)S(1)}, bf16[64,3328]{1,0:T(8,128)(2,1)S(1)}, u32[]{:S(2)}, u32[]{:S(2)}) collective-permute-start(bf16[64,3328]{1,0:T(8,128)(2,1)S(1)} %pad_maximum_fusion.9), channel_id=1, source_target_pairs={{0,1},{1,0},{2,3},{3,2},{4,5},{5,4},{6,7},{7,6},{8,9},{9,8},{10,11... | collective-permute-start | bytes 1277960 | tf_op jit(solution)/shard_map/ppermute | solution.py:22
  98.9 9.3 %collective-permute-start.15 = (bf16[64,3328]{1,0:T(8,128)(2,1)S(1)}, bf16[64,3328]{1,0:T(8,128)(2,1)S(1)}, u32[]{:S(2)}, u32[]{:S(2)}) collective-permute-start(bf16[64,3328]{1,0:T(8,128)(2,1)S(1)} %pad_maximum_fusion.7), channel_id=1, source_target_pairs={{0,1},{1,0},{2,3},{3,2},{4,5},{5,4},{6,7},{7,6},{8,9},{9,8},{10,11... | collective-permute-start | bytes 1277960 | tf_op jit(solution)/shard_map/ppermute | solution.py:22
  100.2 10.5 %collective-permute-start.7 = (bf16[64,1024]{1,0:T(8,128)(2,1)S(1)}, bf16[64,1024]{1,0:T(8,128)(2,1)S(1)}, u32[]{:S(2)}, u32[]{:S(2)}) collective-permute-start(bf16[64,1024]{1,0:T(8,128)(2,1)S(1)} %select_convert_fusion.6), channel_id=1, source_target_pairs={{0,16},{16,0},{32,48},{48,32},{64,80},{80,64},{96,112},{112,96},{1... | collective-permute-start | bytes 393224 | tf_op jit(solution)/shard_map/ppermute | solution.py:22
  101.8 13.7 %collective-permute-start.37 = (bf16[64,1024]{1,0:T(8,128)(2,1)S(1)}, bf16[64,1024]{1,0:T(8,128)(2,1)S(1)}, u32[]{:S(2)}, u32[]{:S(2)}) collective-permute-start(bf16[64,1024]{1,0:T(8,128)(2,1)S(1)} %get-tuple-element.116), channel_id=1, source_target_pairs={{0,112},{16,96},{32,80},{48,64},{64,48},{80,32},{96,16},{112,0},{1... | collective-permute-start | bytes 393224 | tf_op jit(solution)/shard_map/ppermute | solution.py:22
  106.8 9.4 %collective-permute-start.36 = (bf16[64,1024]{1,0:T(8,128)(2,1)S(1)}, bf16[64,1024]{1,0:T(8,128)(2,1)S(1)}, u32[]{:S(2)}, u32[]{:S(2)}) collective-permute-start(bf16[64,1024]{1,0:T(8,128)(2,1)S(1)} %get-tuple-element.115), channel_id=1, source_target_pairs={{0,96},{32,64},{64,32},{96,0},{1,97},{33,65},{65,33},{97,1},{2,98}... | collective-permute-start | bytes 393224 | tf_op jit(solution)/shard_map/ppermute | solution.py:22
  108.1 8.1 %collective-permute-start.27 = (bf16[64,1024]{1,0:T(8,128)(2,1)S(1)}, bf16[64,1024]{1,0:T(8,128)(2,1)S(1)}, u32[]{:S(2)}, u32[]{:S(2)}) collective-permute-start(bf16[64,1024]{1,0:T(8,128)(2,1)S(1)} %get-tuple-element.102), channel_id=1, source_target_pairs={{0,48},{16,32},{32,16},{48,0},{64,112},{80,96},{96,80},{112,64},{1... | collective-permute-start | bytes 393224 | tf_op jit(solution)/shard_map/ppermute | solution.py:22
  108.2 8.0 %collective-permute-start.26 = (bf16[64,1024]{1,0:T(8,128)(2,1)S(1)}, bf16[64,1024]{1,0:T(8,128)(2,1)S(1)}, u32[]{:S(2)}, u32[]{:S(2)}) collective-permute-start(bf16[64,1024]{1,0:T(8,128)(2,1)S(1)} %get-tuple-element.101), channel_id=1, source_target_pairs={{0,32},{32,0},{64,96},{96,64},{1,33},{33,1},{65,97},{97,65},{2,34}... | collective-permute-start | bytes 393224 | tf_op jit(solution)/shard_map/ppermute | solution.py:22
  110.7 11.1 %collective-permute-start.17 = (bf16[64,1024]{1,0:T(8,128)(2,1)S(1)}, bf16[64,1024]{1,0:T(8,128)(2,1)S(1)}, u32[]{:S(2)}, u32[]{:S(2)}) collective-permute-start(bf16[64,1024]{1,0:T(8,128)(2,1)S(1)} %get-tuple-element.88), channel_id=1, source_target_pairs={{0,80},{16,64},{32,112},{48,96},{64,16},{80,0},{96,48},{112,32},{1... | collective-permute-start | bytes 393224 | tf_op jit(solution)/shard_map/ppermute | solution.py:22
  115.4 7.7 %collective-permute-start.16 = (bf16[64,1024]{1,0:T(8,128)(2,1)S(1)}, bf16[64,1024]{1,0:T(8,128)(2,1)S(1)}, u32[]{:S(2)}, u32[]{:S(2)}) collective-permute-start(bf16[64,1024]{1,0:T(8,128)(2,1)S(1)} %get-tuple-element.87), channel_id=1, source_target_pairs={{0,64},{32,96},{64,0},{96,32},{1,65},{33,97},{65,1},{97,33},{2,66}... | collective-permute-start | bytes 393224 | tf_op jit(solution)/shard_map/ppermute | solution.py:22

commit v5 on v4

--- a/solution.py
+++ b/solution.py
@@ -6,6 +6,21 @@
 F32, BF16, F16 = jnp.float32, jnp.bfloat16, jnp.float16
 LIFT = 8.0
 AXES = ("x", "z_hi", "y", "z_lo", "core")
+ORDER = (
+    *((e, -1) for e in (1, 3, 2)),
+    *((e, s) for s in (0, 2, 3) for e in (0, 1)),
+    *((e, s) for s in (0, 2) for e in (2, 3)),
+    *((e, 4) for e in (0, 1)),
+    *((e, 3) for e in (2, 3)),
+    *((e, 5) for e in (0, 1)),
+    *((e, 4) for e in (2, 3)),
+    *((e, 6) for e in (0, 1)),
+    *((e, 5) for e in (2, 3)),
+    *((e, 7) for e in (0, 1)),
+    *((e, 6) for e in (2, 3)),
+    *((e, 8) for e in (0, 1)),
+    *((e, s) for s in (7, 8) for e in (2, 3)),
+)
 
 
 def permute(axes, sizes, move):
@@ -37,9 +52,7 @@
     swap_first = permute(("y", "core"), (4, 2), lambda y, c: (y ^ (3 if c else 1), c))
     swap_second = permute(("y", "core"), (4, 2), lambda y, c: (y ^ (1 if c else 3), c))
     swap_x = {e: permute(("x",), (4,), lambda x, e=e: (x ^ e,)) for e in (1, 2, 3)}
-    swap_row = {
-        e: permute(("x", "z_hi"), (4, 2), lambda x, z, e=e: (x ^ e, z ^ 1)) for e in range(4)
-    }
+    swap_z_hi = permute(("z_hi",), (2,), lambda z: (z ^ 1,))
 
     features = tokens.shape[1] // 16
     blocks = tokens.reshape(4, 16, features).transpose(1, 0, 2).reshape(1, 64, features)
@@ -80,16 +93,21 @@
         if s == -1:
             rows[e] = swap_x[e](tie(own))
         elif s == 0:
-            both = tie(rows[e])
+            both = rows[e]
+            if e > 1:
+                both, _ = tie(both, state[e - 2]["send", 3])
             terms = [product(both, w) for w in (gate_weight, up_weight)]
             send, *st["total"] = tie(jnp.stack([lifted(v[:64]) for v in terms]), *terms)
             st["flight"] = swap_core(send)
         elif s in (2, 3, 4):
             got = tie(st["flight"])
+            if s == 4 and e < 2:
+                got, _ = tie(got, state[e + 2]["send", 2])
             part = slice(64, 128) if s == 2 else slice(0, got.shape[1])
             total = [v[part] + lowered(g) for v, g in zip(st["total"], got)]
             part = slice(0 if s == 4 else got.shape[1] // 2, None)
             send, *st["total"] = tie(jnp.stack([lifted(v[part]) for v in total]), *total)
+            st["send", s] = send
             st["flight"] = (swap_first, swap_second, swap_z)[s - 2](send)
         elif s == 5:
             gate, up = [v + lowered(g) for v, g in zip(st["total"], tie(st["flight"]))]
@@ -101,21 +119,17 @@
         elif s == 8:
             both = jnp.concatenate((tie(st["flight"]), st["hidden"]))
             mixed = product(both, down_weight)
-            same, cross = parted(mixed)
             if e == 0:
-                same, cross = tie(same, cross.astype(BF16))
-                arrived.append(same)
+                arrived.append(tie(mixed))
             else:
-                same, cross = tie(same.astype(BF16), cross.astype(BF16))
-                arrived.append(swap_x[e](same).astype(F32))
-            arrived.append(swap_row[e](cross).astype(F32))
+                arrived.append(swap_x[e](tie(mixed.astype(BF16))).astype(F32))
 
-    for s in (-1, 0, 2, 3, 4, 5, 6, 7, 8):
-        for e in (0, 2, 1, 3):
-            if e or s >= 0:
-                step(e, s)
+    for e, s in ORDER:
+        step(e, s)
+    same, cross = parted(sum(arrived))
+    same, cross = tie(same, cross.astype(BF16))
 
-    out = sum(arrived).astype(BF16).reshape(4, 16, -1)
+    out = (same + swap_z_hi(cross).astype(F32)).astype(BF16).reshape(4, 16, -1)
     first = jnp.where(z_hi == 0, 1, 3)
     blocks = []
     for p in range(4):

time: 125 us -> 132 us (1.056)
  waiting for transfers between devices: 48 us -> 58.1 us
  starting transfers between devices: 51.6 us -> 49.5 us
    ppermute x38 -> x35, waiting for transfers between devices: 39.2 us -> 49.4 us  [permute(): return lambda v: lax.ppermute(v, axes, pairs)]
    ppermute x38 -> x35, starting transfers between devices: 42 us -> 39.9 us  [permute(): return lambda v: lax.ppermute(v, axes, pairs)]
  transfers between devices with their start and end apart: 39 -> 36, of which waited for: 16 -> 16; matrix products, arithmetic and copies ran while one was open for 17% -> 16% of each run, Pallas kernels for 0% -> 0%
where the time goes in v5:
time: 132 us
  waiting for transfers between devices  58.1 us (44%)
  starting transfers between devices  49.5 us (38%)
  matrix products  15.8 us (12%)
  other arithmetic  5.69 us (4%)
  local copies, waits for them, and re-layouts  2.02 us (2%)
    ppermute x35, waiting for transfers between devices, permute(): return lambda v: lax.ppermute(v, axes, pairs)  49.4 us
    ppermute x35, starting transfers between devices, permute(): return lambda v: lax.ppermute(v, axes, pairs)  39.9 us
    dot_general x12, matrix products, product(): return jnp.dot(rows, weight, preferred_element_type=F32)  15.8 us
    all_to_all x1, starting transfers between devices, per_device(): lax.all_to_all(blocks, AXES[1:], split_axis=0, concat_axis=0, tiled=True)  9.6 us
    all_to_all x1, waiting for transfers between devices, per_device(): lax.all_to_all(blocks, AXES[1:], split_axis=0, concat_axis=0, tiled=True)  8.79 us
  transfers between devices with their start and end apart: 36, of which 16 were waited for; matrix products, arithmetic and copies ran while one was open for 16% of the time, Pallas kernels for 0%

profile of v5, /device:TPU:1, one launch (start us, length us, event | category | flops | bytes accessed | tf_op | source)
XLA Modules:
  0.0 132.0 jit_solution(6774792733057023279)
XLA Ops:
  0.0 0.9 broadcast_in_dim.7
  1.0 0.8 all_to_all.6
  1.8 9.6 %all-to-all-start = ((bf16[32,4,1024]{2,1,0:T(4,128)(2,1)}), bf16[32,4,1024]{2,1,0:T(4,128)(2,1)S(1)}, u32[]{:S(2)}, u32[]{:S(2)}) async-start(bf16[32,4,1024]{2,1,0:T(4,128)(2,1)} %all_to_all.6), calls=%async_computation | async-start | bytes 524288 | tf_op jit(solution)/shard_map/all_to_all | solution.py:60
  11.5 8.8 %all-to-all-done = bf16[32,4,1024]{2,1,0:T(4,128)(2,1)S(1)} async-done(((bf16[32,4,1024]{2,1,0:T(4,128)(2,1)}), bf16[32,4,1024]{2,1,0:T(4,128)(2,1)S(1)}, u32[]{:S(2)}, u32[]{:S(2)}) %all-to-all-start) | async-done | bytes 262176 | tf_op jit(solution)/shard_map/all_to_all | solution.py:60
  20.5 2.6 %collective-permute-start.13 = (bf16[128,1024]{1,0:T(8,128)(2,1)S(1)}, bf16[128,1024]{1,0:T(8,128)(2,1)S(1)}, u32[]{:S(2)}, u32[]{:S(2)}) collective-permute-start(bf16[128,1024]{1,0:T(8,128)(2,1)S(1)} %bitcast_dynamic-update-slice_fusion), channel_id=1, source_target_pairs={{0,96},{32,64},{64,32},{96,0},{1,97},{33,65},{65,33},{97,1},{2,98}... | collective-permute-start | bytes 786440 | tf_op jit(solution)/shard_map/ppermute | solution.py:37
  23.1 1.4 %collective-permute-start.3 = (bf16[128,1024]{1,0:T(8,128)(2,1)S(1)}, bf16[128,1024]{1,0:T(8,128)(2,1)S(1)}, u32[]{:S(2)}, u32[]{:S(2)}) collective-permute-start(bf16[128,1024]{1,0:T(8,128)(2,1)S(1)} %bitcast_dynamic-update-slice_fusion), channel_id=1, source_target_pairs={{0,64},{32,96},{64,0},{96,32},{1,65},{33,97},{65,1},{97,33},{2,66}... | collective-permute-start | bytes 786440 | tf_op jit(solution)/shard_map/ppermute | solution.py:37
  24.5 4.1 %fusion.82 = f32[128,3328]{1,0:T(8,128)S(1)} fusion(bf16[128,1024]{1,0:T(8,128)(2,1)S(1)} %bitcast_dynamic-update-slice_fusion, bf16[1024,3328]{1,0:T(8,128)(2,1)} %param.6), kind=kOutput, calls=%fused_computation.190 | convolution fusion | flops 872415232 | bytes 8781824 | tf_op jit(solution)/shard_map/dot_general | solution.py:85
  28.7 1.1 fusion.81
  30.1 1.9 %collective-permute-start = (f16[2,64,3328]{2,1,0:T(8,128)(2,1)S(1)}, f16[2,64,3328]{2,1,0:T(8,128)(2,1)S(1)}, u32[]{:S(2)}, u32[]{:S(2)}) collective-permute-start(f16[2,64,3328]{2,1,0:T(8,128)(2,1)S(1)} %pad_maximum_fusion), channel_id=1, source_target_pairs={{0,1},{1,0},{2,3},{3,2},{4,5},{5,4},{6,7},{7,6},{8,9},{9,8},{10,11... | collective-permute-start | bytes 2555912 | tf_op jit(solution)/shard_map/ppermute | solution.py:37
  32.0 1.1 fusion.86
  33.0 1.1 fusion.85
  34.5 1.7 %collective-permute-start.10 = (f16[2,64,3328]{2,1,0:T(8,128)(2,1)S(1)}, f16[2,64,3328]{2,1,0:T(8,128)(2,1)S(1)}, u32[]{:S(2)}, u32[]{:S(2)}) collective-permute-start(f16[2,64,3328]{2,1,0:T(8,128)(2,1)S(1)} %pad_maximum_fusion.2), channel_id=1, source_target_pairs={{0,1},{1,0},{2,3},{3,2},{4,5},{5,4},{6,7},{7,6},{8,9},{9,8},{10,11... | collective-permute-start | bytes 2555912 | tf_op jit(solution)/shard_map/ppermute | solution.py:37
  36.8 1.4 %collective-permute-done.10 = f16[2,64,3328]{2,1,0:T(8,128)(2,1)S(1)} collective-permute-done((f16[2,64,3328]{2,1,0:T(8,128)(2,1)S(1)}, f16[2,64,3328]{2,1,0:T(8,128)(2,1)S(1)}, u32[]{:S(2)}, u32[]{:S(2)}) %collective-permute-start.10) | collective-permute-done | bytes 852000 | tf_op jit(solution)/shard_map/ppermute | solution.py:37
  38.5 1.2 collective-permute-start.11
  39.8 5.0 %collective-permute-done.1 = f16[2,32,3328]{2,1,0:T(8,128)(2,1)S(1)} collective-permute-done((f16[2,32,3328]{2,1,0:T(8,128)(2,1)S(1)}, f16[2,32,3328]{2,1,0:T(8,128)(2,1)S(1)}, u32[]{:S(2)}, u32[]{:S(2)}) %collective-permute-start.1) | collective-permute-done | bytes 426016 | tf_op jit(solution)/shard_map/ppermute | solution.py:37
  45.1 1.1 fusion.84
  46.2 1.1 fusion.83
  48.1 3.1 %collective-permute-done.2 = f16[2,16,3328]{2,1,0:T(8,128)(2,1)S(1)} collective-permute-done((f16[2,16,3328]{2,1,0:T(8,128)(2,1)S(1)}, f16[2,16,3328]{2,1,0:T(8,128)(2,1)S(1)}, u32[]{:S(2)}, u32[]{:S(2)}) %collective-permute-start.2) | collective-permute-done | bytes 213024 | tf_op jit(solution)/shard_map/ppermute | solution.py:37
  51.8 1.1 fusion.88
  52.9 1.1 fusion.87
  55.3 1.9 %collective-permute-start.14 = (f16[2,64,3328]{2,1,0:T(8,128)(2,1)S(1)}, f16[2,64,3328]{2,1,0:T(8,128)(2,1)S(1)}, u32[]{:S(2)}, u32[]{:S(2)}) collective-permute-start(f16[2,64,3328]{2,1,0:T(8,128)(2,1)S(1)} %pad_maximum_fusion.3), channel_id=1, source_target_pairs={{0,1},{1,0},{2,3},{3,2},{4,5},{5,4},{6,7},{7,6},{8,9},{9,8},{10,11... | collective-permute-start | bytes 2555912 | tf_op jit(solution)/shard_map/ppermute | solution.py:37
  57.2 2.3 %collective-permute-start.20 = (f16[2,32,3328]{2,1,0:T(8,128)(2,1)S(1)}, f16[2,32,3328]{2,1,0:T(8,128)(2,1)S(1)}, u32[]{:S(2)}, u32[]{:S(2)}) collective-permute-start(f16[2,32,3328]{2,1,0:T(8,128)(2,1)S(1)} %pad_maximum_fusion.5), channel_id=1, source_target_pairs={{0,4},{1,13},{4,0},{5,9},{8,12},{9,5},{12,8},{13,1},{2,6},{3,15},{... | collective-permute-start | bytes 1277960 | tf_op jit(solution)/shard_map/ppermute | solution.py:37
  59.5 0.5 collective-permute-done.5
  60.2 3.0 %collective-permute-start.6 = (bf16[16,3328]{1,0:T(8,128)(2,1)S(1)}, bf16[16,3328]{1,0:T(8,128)(2,1)S(1)}, u32[]{:S(2)}, u32[]{:S(2)}) collective-permute-start(bf16[16,3328]{1,0:T(8,128)(2,1)S(1)} %fusion.60), channel_id=1, source_target_pairs={{0,12},{1,5},{4,8},{5,1},{8,4},{9,13},{12,0},{13,9},{2,14},{3,7},{... | collective-permute-start | bytes 319496 | tf_op jit(solution)/shard_map/ppermute | solution.py:37
  64.2 2.6 %collective-permute-done.6 = bf16[16,3328]{1,0:T(8,128)(2,1)S(1)} collective-permute-done((bf16[16,3328]{1,0:T(8,128)(2,1)S(1)}, bf16[16,3328]{1,0:T(8,128)(2,1)S(1)}, u32[]{:S(2)}, u32[]{:S(2)}) %collective-permute-start.6) | collective-permute-done | bytes 106528 | tf_op jit(solution)/shard_map/ppermute | solution.py:37
  67.2 1.5 %collective-permute-start.21 = (f16[2,16,3328]{2,1,0:T(8,128)(2,1)S(1)}, f16[2,16,3328]{2,1,0:T(8,128)(2,1)S(1)}, u32[]{:S(2)}, u32[]{:S(2)}) collective-permute-start(f16[2,16,3328]{2,1,0:T(8,128)(2,1)S(1)} %pad_maximum_fusion.18), channel_id=1, source_target_pairs={{0,12},{1,5},{4,8},{5,1},{8,4},{9,13},{12,0},{13,9},{2,14},{3,7},{... | collective-permute-start | bytes 638984 | tf_op jit(solution)/shard_map/ppermute | solution.py:37
  69.1 6.7 %collective-permute-done.7 = bf16[32,3328]{1,0:T(8,128)(2,1)S(1)} collective-permute-done((bf16[32,3328]{1,0:T(8,128)(2,1)S(1)}, bf16[32,3328]{1,0:T(8,128)(2,1)S(1)}, u32[]{:S(2)}, u32[]{:S(2)}) %collective-permute-start.7) | collective-permute-done | bytes 213024 | tf_op jit(solution)/shard_map/ppermute | solution.py:37
  75.8 3.7 %collective-permute-start.8 = (bf16[64,3328]{1,0:T(8,128)(2,1)S(1)}, bf16[64,3328]{1,0:T(8,128)(2,1)S(1)}, u32[]{:S(2)}, u32[]{:S(2)}) collective-permute-start(bf16[64,3328]{1,0:T(8,128)(2,1)S(1)} %pad_maximum_fusion.6), channel_id=1, source_target_pairs={{0,1},{1,0},{2,3},{3,2},{4,5},{5,4},{6,7},{7,6},{8,9},{9,8},{10,11... | collective-permute-start | bytes 1277960 | tf_op jit(solution)/shard_map/ppermute | solution.py:37
  81.1 5.4 %collective-permute-done.17 = bf16[32,3328]{1,0:T(8,128)(2,1)S(1)} collective-permute-done((bf16[32,3328]{1,0:T(8,128)(2,1)S(1)}, bf16[32,3328]{1,0:T(8,128)(2,1)S(1)}, u32[]{:S(2)}, u32[]{:S(2)}) %collective-permute-start.17) | collective-permute-done | bytes 213024 | tf_op jit(solution)/shard_map/ppermute | solution.py:37
  87.0 0.6 collective-permute-done.22
  88.3 3.0 %collective-permute-done.23 = bf16[16,3328]{1,0:T(8,128)(2,1)S(1)} collective-permute-done((bf16[16,3328]{1,0:T(8,128)(2,1)S(1)}, bf16[16,3328]{1,0:T(8,128)(2,1)S(1)}, u32[]{:S(2)}, u32[]{:S(2)}) %collective-permute-start.23) | collective-permute-done | bytes 106528 | tf_op jit(solution)/shard_map/ppermute | solution.py:37
  91.3 1.6 %collective-permute-start.24 = (bf16[32,3328]{1,0:T(8,128)(2,1)S(1)}, bf16[32,3328]{1,0:T(8,128)(2,1)S(1)}, u32[]{:S(2)}, u32[]{:S(2)}) collective-permute-start(bf16[32,3328]{1,0:T(8,128)(2,1)S(1)} %pad_maximum_fusion.20), channel_id=1, source_target_pairs={{0,4},{1,13},{4,0},{5,9},{8,12},{9,5},{12,8},{13,1},{2,6},{3,15},{... | collective-permute-start | bytes 638984 | tf_op jit(solution)/shard_map/ppermute | solution.py:37
  93.1 3.4 %collective-permute-start.30 = (bf16[16,3328]{1,0:T(8,128)(2,1)S(1)}, bf16[16,3328]{1,0:T(8,128)(2,1)S(1)}, u32[]{:S(2)}, u32[]{:S(2)}) collective-permute-start(bf16[16,3328]{1,0:T(8,128)(2,1)S(1)} %fusion.54), channel_id=1, source_target_pairs={{0,12},{1,5},{4,8},{5,1},{8,4},{9,13},{12,0},{13,9},{2,14},{3,7},{... | collective-permute-start | bytes 319496 | tf_op jit(solution)/shard_map/ppermute | solution.py:37
  96.5 0.8 collective-permute-done.24
  97.3 4.0 %collective-permute-start.25 = (bf16[64,3328]{1,0:T(8,128)(2,1)S(1)}, bf16[64,3328]{1,0:T(8,128)(2,1)S(1)}, u32[]{:S(2)}, u32[]{:S(2)}) collective-permute-start(bf16[64,3328]{1,0:T(8,128)(2,1)S(1)} %pad_maximum_fusion.10), channel_id=1, source_target_pairs={{0,1},{1,0},{2,3},{3,2},{4,5},{5,4},{6,7},{7,6},{8,9},{9,8},{10,11... | collective-permute-start | bytes 1277960 | tf_op jit(solution)/shard_map/ppermute | solution.py:37
  101.3 1.5 %collective-permute-start.31 = (bf16[32,3328]{1,0:T(8,128)(2,1)S(1)}, bf16[32,3328]{1,0:T(8,128)(2,1)S(1)}, u32[]{:S(2)}, u32[]{:S(2)}) collective-permute-start(bf16[32,3328]{1,0:T(8,128)(2,1)S(1)} %pad_maximum_fusion.23), channel_id=1, source_target_pairs={{0,4},{1,13},{4,0},{5,9},{8,12},{9,5},{12,8},{13,1},{2,6},{3,15},{... | collective-permute-start | bytes 638984 | tf_op jit(solution)/shard_map/ppermute | solution.py:37
  102.8 1.1 convolution_convert_fusion.2
  104.0 3.3 %collective-permute-done.31 = bf16[32,3328]{1,0:T(8,128)(2,1)S(1)} collective-permute-done((bf16[32,3328]{1,0:T(8,128)(2,1)S(1)}, bf16[32,3328]{1,0:T(8,128)(2,1)S(1)}, u32[]{:S(2)}, u32[]{:S(2)}) %collective-permute-start.31) | collective-permute-done | bytes 213024 | tf_op jit(solution)/shard_map/ppermute | solution.py:37
  107.4 1.0 collective-permute-start.32
  108.3 1.1 convolution_convert_fusion.1
  109.4 0.6 collective-permute-start.26
  110.0 1.1 convolution_convert_fusion
  111.1 1.9 %collective-permute-start.33 = (bf16[128,1024]{1,0:T(8,128)(2,1)S(1)}, bf16[128,1024]{1,0:T(8,128)(2,1)S(1)}, u32[]{:S(2)}, u32[]{:S(2)}) collective-permute-start(bf16[128,1024]{1,0:T(8,128)(2,1)S(1)} %convolution_convert_fusion), channel_id=1, source_target_pairs={{0,96},{32,64},{64,32},{96,0},{1,97},{33,65},{65,33},{97,1},{2,98}... | collective-permute-start | bytes 786440 | tf_op jit(solution)/shard_map/ppermute | solution.py:37
  112.9 1.0 fusion.8
  114.0 4.9 %collective-permute-done.26 = bf16[128,1024]{1,0:T(8,128)(2,1)S(1)} collective-permute-done((bf16[128,1024]{1,0:T(8,128)(2,1)S(1)}, bf16[128,1024]{1,0:T(8,128)(2,1)S(1)}, u32[]{:S(2)}, u32[]{:S(2)}) %collective-permute-start.26) | collective-permute-done | bytes 262176 | tf_op jit(solution)/shard_map/ppermute | solution.py:37
  118.9 5.9 %collective-permute-done.33 = bf16[128,1024]{1,0:T(8,128)(2,1)S(1)} collective-permute-done((bf16[128,1024]{1,0:T(8,128)(2,1)S(1)}, bf16[128,1024]{1,0:T(8,128)(2,1)S(1)}, u32[]{:S(2)}, u32[]{:S(2)}) %collective-permute-start.33) | collective-permute-done | bytes 262176 | tf_op jit(solution)/shard_map/ppermute | solution.py:37
  125.5 5.8 %collective-permute-done.34 = bf16[64,1024]{1,0:T(8,128)(2,1)S(1)} collective-permute-done((bf16[64,1024]{1,0:T(8,128)(2,1)S(1)}, bf16[64,1024]{1,0:T(8,128)(2,1)S(1)}, u32[]{:S(2)}, u32[]{:S(2)}) %collective-permute-start.34) | collective-permute-done | bytes 131104 | tf_op jit(solution)/shard_map/ppermute | solution.py:37
  131.3 0.7 pad_maximum_fusion.24
  (131 shorter events, 10.3 us)
Async XLA Ops:
  1.8 18.5 %all-to-all-start = ((bf16[32,4,1024]{2,1,0:T(4,128)(2,1)}), bf16[32,4,1024]{2,1,0:T(4,128)(2,1)S(1)}, u32[]{:S(2)}, u32[]{:S(2)}) async-start(bf16[32,4,1024]{2,1,0:T(4,128)(2,1)} %all_to_all.6), calls=%async_computation | async-start | bytes 524288 | tf_op jit(solution)/shard_map/all_to_all | solution.py:60
  20.4 8.2 %slice-start.2 = ((s8[6815744]{0:T(1024)(128)(4,1)}), s8[4194304]{0:T(1024)(128)(4,1)S(1)}, s32[]{:S(2)}) async-start(s8[6815744]{0:T(1024)(128)(4,1)} %bitcast.210), calls=%async_computation.3 | async-start | bytes 8388608
  20.5 8.1 %slice-start.3 = ((s8[6815744]{0:T(1024)(128)(4,1)}), s8[2621440]{0:T(1024)(128)(4,1)S(1)}, s32[]{:S(2)}) async-start(s8[6815744]{0:T(1024)(128)(4,1)} %bitcast.210), calls=%async_computation.4 | async-start | bytes 5242880
  20.5 31.3 %collective-permute-start.13 = (bf16[128,1024]{1,0:T(8,128)(2,1)S(1)}, bf16[128,1024]{1,0:T(8,128)(2,1)S(1)}, u32[]{:S(2)}, u32[]{:S(2)}) collective-permute-start(bf16[128,1024]{1,0:T(8,128)(2,1)S(1)} %bitcast_dynamic-update-slice_fusion), channel_id=1, source_target_pairs={{0,96},{32,64},{64,32},{96,0},{1,97},{33,65},{65,33},{97,1},{2,98}... | collective-permute-start | bytes 786440 | tf_op jit(solution)/shard_map/ppermute | solution.py:37
  23.1 8.9 %collective-permute-start.9 = (bf16[128,1024]{1,0:T(8,128)(2,1)S(1)}, bf16[128,1024]{1,0:T(8,128)(2,1)S(1)}, u32[]{:S(2)}, u32[]{:S(2)}) collective-permute-start(bf16[128,1024]{1,0:T(8,128)(2,1)S(1)} %bitcast_dynamic-update-slice_fusion), channel_id=1, source_target_pairs={{0,32},{32,0},{64,96},{96,64},{1,33},{33,1},{65,97},{97,65},{2,34}... | collective-permute-start | bytes 786440 | tf_op jit(solution)/shard_map/ppermute | solution.py:37
  23.1 22.0 %collective-permute-start.3 = (bf16[128,1024]{1,0:T(8,128)(2,1)S(1)}, bf16[128,1024]{1,0:T(8,128)(2,1)S(1)}, u32[]{:S(2)}, u32[]{:S(2)}) collective-permute-start(bf16[128,1024]{1,0:T(8,128)(2,1)S(1)} %bitcast_dynamic-update-slice_fusion), channel_id=1, source_target_pairs={{0,64},{32,96},{64,0},{96,32},{1,65},{33,97},{65,1},{97,33},{2,66}... | collective-permute-start | bytes 786440 | tf_op jit(solution)/shard_map/ppermute | solution.py:37
  24.5 7.5 %slice-start = ((s8[6815744]{0:T(1024)(128)(4,1)}), s8[4194304]{0:T(1024)(128)(4,1)S(1)}, s32[]{:S(2)}) async-start(s8[6815744]{0:T(1024)(128)(4,1)} %bitcast.208), calls=%async_computation.1 | async-start | bytes 8388608
  28.6 3.3 %slice-start.1 = ((s8[6815744]{0:T(1024)(128)(4,1)}), s8[2621440]{0:T(1024)(128)(4,1)S(1)}, s32[]{:S(2)}) async-start(s8[6815744]{0:T(1024)(128)(4,1)} %bitcast.208), calls=%async_computation.2 | async-start | bytes 5242880
  30.1 6.1 %collective-permute-start = (f16[2,64,3328]{2,1,0:T(8,128)(2,1)S(1)}, f16[2,64,3328]{2,1,0:T(8,128)(2,1)S(1)}, u32[]{:S(2)}, u32[]{:S(2)}) collective-permute-start(f16[2,64,3328]{2,1,0:T(8,128)(2,1)S(1)} %pad_maximum_fusion), channel_id=1, source_target_pairs={{0,1},{1,0},{2,3},{3,2},{4,5},{5,4},{6,7},{7,6},{8,9},{9,8},{10,11... | collective-permute-start | bytes 2555912 | tf_op jit(solution)/shard_map/ppermute | solution.py:37
  34.5 3.7 %collective-permute-start.10 = (f16[2,64,3328]{2,1,0:T(8,128)(2,1)S(1)}, f16[2,64,3328]{2,1,0:T(8,128)(2,1)S(1)}, u32[]{:S(2)}, u32[]{:S(2)}) collective-permute-start(f16[2,64,3328]{2,1,0:T(8,128)(2,1)S(1)} %pad_maximum_fusion.2), channel_id=1, source_target_pairs={{0,1},{1,0},{2,3},{3,2},{4,5},{5,4},{6,7},{7,6},{8,9},{9,8},{10,11... | collective-permute-start | bytes 2555912 | tf_op jit(solution)/shard_map/ppermute | solution.py:37
  36.5 8.3 %collective-permute-start.1 = (f16[2,32,3328]{2,1,0:T(8,128)(2,1)S(1)}, f16[2,32,3328]{2,1,0:T(8,128)(2,1)S(1)}, u32[]{:S(2)}, u32[]{:S(2)}) collective-permute-start(f16[2,32,3328]{2,1,0:T(8,128)(2,1)S(1)} %pad_maximum_fusion.4), channel_id=1, source_target_pairs={{0,4},{1,13},{4,0},{5,9},{8,12},{9,5},{12,8},{13,1},{2,6},{3,15},{... | collective-permute-start | bytes 1277960 | tf_op jit(solution)/shard_map/ppermute | solution.py:37
  38.5 12.7 %collective-permute-start.11 = (f16[2,32,3328]{2,1,0:T(8,128)(2,1)S(1)}, f16[2,32,3328]{2,1,0:T(8,128)(2,1)S(1)}, u32[]{:S(2)}, u32[]{:S(2)}) collective-permute-start(f16[2,32,3328]{2,1,0:T(8,128)(2,1)S(1)} %pad_maximum_fusion.7), channel_id=1, source_target_pairs={{0,4},{1,13},{4,0},{5,9},{8,12},{9,5},{12,8},{13,1},{2,6},{3,15},{... | collective-permute-start | bytes 1277960 | tf_op jit(solution)/shard_map/ppermute | solution.py:37
  45.0 6.2 %collective-permute-start.2 = (f16[2,16,3328]{2,1,0:T(8,128)(2,1)S(1)}, f16[2,16,3328]{2,1,0:T(8,128)(2,1)S(1)}, u32[]{:S(2)}, u32[]{:S(2)}) collective-permute-start(f16[2,16,3328]{2,1,0:T(8,128)(2,1)S(1)} %pad_maximum_fusion.12), channel_id=1, source_target_pairs={{0,12},{1,5},{4,8},{5,1},{8,4},{9,13},{12,0},{13,9},{2,14},{3,7},{... | collective-permute-start | bytes 638984 | tf_op jit(solution)/shard_map/ppermute | solution.py:37
  47.7 6.5 %collective-permute-start.4 = (f16[2,64,3328]{2,1,0:T(8,128)(2,1)S(1)}, f16[2,64,3328]{2,1,0:T(8,128)(2,1)S(1)}, u32[]{:S(2)}, u32[]{:S(2)}) collective-permute-start(f16[2,64,3328]{2,1,0:T(8,128)(2,1)S(1)} %pad_maximum_fusion.1), channel_id=1, source_target_pairs={{0,1},{1,0},{2,3},{3,2},{4,5},{5,4},{6,7},{7,6},{8,9},{9,8},{10,11... | collective-permute-start | bytes 2555912 | tf_op jit(solution)/shard_map/ppermute | solution.py:37
  51.4 5.7 %collective-permute-start.12 = (f16[2,16,3328]{2,1,0:T(8,128)(2,1)S(1)}, f16[2,16,3328]{2,1,0:T(8,128)(2,1)S(1)}, u32[]{:S(2)}, u32[]{:S(2)}) collective-permute-start(f16[2,16,3328]{2,1,0:T(8,128)(2,1)S(1)} %pad_maximum_fusion.15), channel_id=1, source_target_pairs={{0,12},{1,5},{4,8},{5,1},{8,4},{9,13},{12,0},{13,9},{2,14},{3,7},{... | collective-permute-start | bytes 638984 | tf_op jit(solution)/shard_map/ppermute | solution.py:37
  54.7 5.4 %collective-permute-start.5 = (f16[2,16,3328]{2,1,0:T(8,128)(2,1)S(1)}, f16[2,16,3328]{2,1,0:T(8,128)(2,1)S(1)}, u32[]{:S(2)}, u32[]{:S(2)}) collective-permute-start(f16[2,16,3328]{2,1,0:T(8,128)(2,1)S(1)} %pad_maximum_fusion.13), channel_id=1, source_target_pairs={{0,2},{2,0},{1,3},{3,1},{4,6},{6,4},{5,7},{7,5},{8,10},{10,8},{9,1... | collective-permute-start | bytes 638984 | tf_op jit(solution)/shard_map/ppermute | solution.py:37
  55.3 7.9 %collective-permute-start.14 = (f16[2,64,3328]{2,1,0:T(8,128)(2,1)S(1)}, f16[2,64,3328]{2,1,0:T(8,128)(2,1)S(1)}, u32[]{:S(2)}, u32[]{:S(2)}) collective-permute-start(f16[2,64,3328]{2,1,0:T(8,128)(2,1)S(1)} %pad_maximum_fusion.3), channel_id=1, source_target_pairs={{0,1},{1,0},{2,3},{3,2},{4,5},{5,4},{6,7},{7,6},{8,9},{9,8},{10,11... | collective-permute-start | bytes 2555912 | tf_op jit(solution)/shard_map/ppermute | solution.py:37
  57.2 9.8 %collective-permute-start.20 = (f16[2,32,3328]{2,1,0:T(8,128)(2,1)S(1)}, f16[2,32,3328]{2,1,0:T(8,128)(2,1)S(1)}, u32[]{:S(2)}, u32[]{:S(2)}) collective-permute-start(f16[2,32,3328]{2,1,0:T(8,128)(2,1)S(1)} %pad_maximum_fusion.5), channel_id=1, source_target_pairs={{0,4},{1,13},{4,0},{5,9},{8,12},{9,5},{12,8},{13,1},{2,6},{3,15},{... | collective-permute-start | bytes 1277960 | tf_op jit(solution)/shard_map/ppermute | solution.py:37
  60.2 6.6 %collective-permute-start.6 = (bf16[16,3328]{1,0:T(8,128)(2,1)S(1)}, bf16[16,3328]{1,0:T(8,128)(2,1)S(1)}, u32[]{:S(2)}, u32[]{:S(2)}) collective-permute-start(bf16[16,3328]{1,0:T(8,128)(2,1)S(1)} %fusion.60), channel_id=1, source_target_pairs={{0,12},{1,5},{4,8},{5,1},{8,4},{9,13},{12,0},{13,9},{2,14},{3,7},{... | collective-permute-start | bytes 319496 | tf_op jit(solution)/shard_map/ppermute | solution.py:37
  63.6 17.2 %collective-permute-start.27 = (f16[2,32,3328]{2,1,0:T(8,128)(2,1)S(1)}, f16[2,32,3328]{2,1,0:T(8,128)(2,1)S(1)}, u32[]{:S(2)}, u32[]{:S(2)}) collective-permute-start(f16[2,32,3328]{2,1,0:T(8,128)(2,1)S(1)} %pad_maximum_fusion.8), channel_id=1, source_target_pairs={{0,4},{1,13},{4,0},{5,9},{8,12},{9,5},{12,8},{13,1},{2,6},{3,15},{... | collective-permute-start | bytes 1277960 | tf_op jit(solution)/shard_map/ppermute | solution.py:37
  63.8 5.1 %collective-permute-start.15 = (f16[2,16,3328]{2,1,0:T(8,128)(2,1)S(1)}, f16[2,16,3328]{2,1,0:T(8,128)(2,1)S(1)}, u32[]{:S(2)}, u32[]{:S(2)}) collective-permute-start(f16[2,16,3328]{2,1,0:T(8,128)(2,1)S(1)} %pad_maximum_fusion.16), channel_id=1, source_target_pairs={{0,2},{2,0},{1,3},{3,1},{4,6},{6,4},{5,7},{7,5},{8,10},{10,8},{9,1... | collective-permute-start | bytes 638984 | tf_op jit(solution)/shard_map/ppermute | solution.py:37
  66.8 9.0 %collective-permute-start.7 = (bf16[32,3328]{1,0:T(8,128)(2,1)S(1)}, bf16[32,3328]{1,0:T(8,128)(2,1)S(1)}, u32[]{:S(2)}, u32[]{:S(2)}) collective-permute-start(bf16[32,3328]{1,0:T(8,128)(2,1)S(1)} %pad_maximum_fusion.14), channel_id=1, source_target_pairs={{0,4},{1,13},{4,0},{5,9},{8,12},{9,5},{12,8},{13,1},{2,6},{3,15},{... | collective-permute-start | bytes 638984 | tf_op jit(solution)/shard_map/ppermute | solution.py:37
  66.9 35.9 %slice-start.4 = ((s8[6815744]{0:T(1024)(128)(4,1)}), s8[4194304]{0:T(1024)(128)(4,1)S(1)}, s32[]{:S(2)}) async-start(s8[6815744]{0:T(1024)(128)(4,1)} %bitcast.212), calls=%async_computation.5 | async-start | bytes 8388608
  67.2 12.9 %collective-permute-start.21 = (f16[2,16,3328]{2,1,0:T(8,128)(2,1)S(1)}, f16[2,16,3328]{2,1,0:T(8,128)(2,1)S(1)}, u32[]{:S(2)}, u32[]{:S(2)}) collective-permute-start(f16[2,16,3328]{2,1,0:T(8,128)(2,1)S(1)} %pad_maximum_fusion.18), channel_id=1, source_target_pairs={{0,12},{1,5},{4,8},{5,1},{8,4},{9,13},{12,0},{13,9},{2,14},{3,7},{... | collective-permute-start | bytes 638984 | tf_op jit(solution)/shard_map/ppermute | solution.py:37
  69.0 10.6 %collective-permute-start.16 = (bf16[16,3328]{1,0:T(8,128)(2,1)S(1)}, bf16[16,3328]{1,0:T(8,128)(2,1)S(1)}, u32[]{:S(2)}, u32[]{:S(2)}) collective-permute-start(bf16[16,3328]{1,0:T(8,128)(2,1)S(1)} %fusion.58), channel_id=1, source_target_pairs={{0,12},{1,5},{4,8},{5,1},{8,4},{9,13},{12,0},{13,9},{2,14},{3,7},{... | collective-permute-start | bytes 319496 | tf_op jit(solution)/shard_map/ppermute | solution.py:37
  75.8 17.2 %collective-permute-start.8 = (bf16[64,3328]{1,0:T(8,128)(2,1)S(1)}, bf16[64,3328]{1,0:T(8,128)(2,1)S(1)}, u32[]{:S(2)}, u32[]{:S(2)}) collective-permute-start(bf16[64,3328]{1,0:T(8,128)(2,1)S(1)} %pad_maximum_fusion.6), channel_id=1, source_target_pairs={{0,1},{1,0},{2,3},{3,2},{4,5},{5,4},{6,7},{7,6},{8,9},{9,8},{10,11... | collective-permute-start | bytes 1277960 | tf_op jit(solution)/shard_map/ppermute | solution.py:37
  79.6 6.9 %collective-permute-start.17 = (bf16[32,3328]{1,0:T(8,128)(2,1)S(1)}, bf16[32,3328]{1,0:T(8,128)(2,1)S(1)}, u32[]{:S(2)}, u32[]{:S(2)}) collective-permute-start(bf16[32,3328]{1,0:T(8,128)(2,1)S(1)} %pad_maximum_fusion.17), channel_id=1, source_target_pairs={{0,4},{1,13},{4,0},{5,9},{8,12},{9,5},{12,8},{13,1},{2,6},{3,15},{... | collective-permute-start | bytes 638984 | tf_op jit(solution)/shard_map/ppermute | solution.py:37
  80.2 22.6 %slice-start.5 = ((s8[6815744]{0:T(1024)(128)(4,1)}), s8[2621440]{0:T(1024)(128)(4,1)S(1)}, s32[]{:S(2)}) async-start(s8[6815744]{0:T(1024)(128)(4,1)} %bitcast.212), calls=%async_computation.6 | async-start | bytes 5242880
  80.3 7.3 %collective-permute-start.22 = (f16[2,16,3328]{2,1,0:T(8,128)(2,1)S(1)}, f16[2,16,3328]{2,1,0:T(8,128)(2,1)S(1)}, u32[]{:S(2)}, u32[]{:S(2)}) collective-permute-start(f16[2,16,3328]{2,1,0:T(8,128)(2,1)S(1)} %pad_maximum_fusion.19), channel_id=1, source_target_pairs={{0,2},{2,0},{1,3},{3,1},{4,6},{6,4},{5,7},{7,5},{8,10},{10,8},{9,1... | collective-permute-start | bytes 638984 | tf_op jit(solution)/shard_map/ppermute | solution.py:37
  81.0 6.8 %collective-permute-start.28 = (f16[2,16,3328]{2,1,0:T(8,128)(2,1)S(1)}, f16[2,16,3328]{2,1,0:T(8,128)(2,1)S(1)}, u32[]{:S(2)}, u32[]{:S(2)}) collective-permute-start(f16[2,16,3328]{2,1,0:T(8,128)(2,1)S(1)} %pad_maximum_fusion.21), channel_id=1, source_target_pairs={{0,12},{1,5},{4,8},{5,1},{8,4},{9,13},{12,0},{13,9},{2,14},{3,7},{... | collective-permute-start | bytes 638984 | tf_op jit(solution)/shard_map/ppermute | solution.py:37
  86.5 16.3 %collective-permute-start.18 = (bf16[64,3328]{1,0:T(8,128)(2,1)S(1)}, bf16[64,3328]{1,0:T(8,128)(2,1)S(1)}, u32[]{:S(2)}, u32[]{:S(2)}) collective-permute-start(bf16[64,3328]{1,0:T(8,128)(2,1)S(1)} %pad_maximum_fusion.9), channel_id=1, source_target_pairs={{0,1},{1,0},{2,3},{3,2},{4,5},{5,4},{6,7},{7,6},{8,9},{9,8},{10,11... | collective-permute-start | bytes 1277960 | tf_op jit(solution)/shard_map/ppermute | solution.py:37
  87.7 3.6 %collective-permute-start.23 = (bf16[16,3328]{1,0:T(8,128)(2,1)S(1)}, bf16[16,3328]{1,0:T(8,128)(2,1)S(1)}, u32[]{:S(2)}, u32[]{:S(2)}) collective-permute-start(bf16[16,3328]{1,0:T(8,128)(2,1)S(1)} %fusion.56), channel_id=1, source_target_pairs={{0,12},{1,5},{4,8},{5,1},{8,4},{9,13},{12,0},{13,9},{2,14},{3,7},{... | collective-permute-start | bytes 319496 | tf_op jit(solution)/shard_map/ppermute | solution.py:37
  87.9 5.1 %collective-permute-start.29 = (f16[2,16,3328]{2,1,0:T(8,128)(2,1)S(1)}, f16[2,16,3328]{2,1,0:T(8,128)(2,1)S(1)}, u32[]{:S(2)}, u32[]{:S(2)}) collective-permute-start(f16[2,16,3328]{2,1,0:T(8,128)(2,1)S(1)} %pad_maximum_fusion.22), channel_id=1, source_target_pairs={{0,2},{2,0},{1,3},{3,1},{4,6},{6,4},{5,7},{7,5},{8,10},{10,8},{9,1... | collective-permute-start | bytes 638984 | tf_op jit(solution)/shard_map/ppermute | solution.py:37
  91.3 6.0 %collective-permute-start.24 = (bf16[32,3328]{1,0:T(8,128)(2,1)S(1)}, bf16[32,3328]{1,0:T(8,128)(2,1)S(1)}, u32[]{:S(2)}, u32[]{:S(2)}) collective-permute-start(bf16[32,3328]{1,0:T(8,128)(2,1)S(1)} %pad_maximum_fusion.20), channel_id=1, source_target_pairs={{0,4},{1,13},{4,0},{5,9},{8,12},{9,5},{12,8},{13,1},{2,6},{3,15},{... | collective-permute-start | bytes 638984 | tf_op jit(solution)/shard_map/ppermute | solution.py:37
  93.1 8.2 %collective-permute-start.30 = (bf16[16,3328]{1,0:T(8,128)(2,1)S(1)}, bf16[16,3328]{1,0:T(8,128)(2,1)S(1)}, u32[]{:S(2)}, u32[]{:S(2)}) collective-permute-start(bf16[16,3328]{1,0:T(8,128)(2,1)S(1)} %fusion.54), channel_id=1, source_target_pairs={{0,12},{1,5},{4,8},{5,1},{8,4},{9,13},{12,0},{13,9},{2,14},{3,7},{... | collective-permute-start | bytes 319496 | tf_op jit(solution)/shard_map/ppermute | solution.py:37
  97.3 11.0 %collective-permute-start.25 = (bf16[64,3328]{1,0:T(8,128)(2,1)S(1)}, bf16[64,3328]{1,0:T(8,128)(2,1)S(1)}, u32[]{:S(2)}, u32[]{:S(2)}) collective-permute-start(bf16[64,3328]{1,0:T(8,128)(2,1)S(1)} %pad_maximum_fusion.10), channel_id=1, source_target_pairs={{0,1},{1,0},{2,3},{3,2},{4,5},{5,4},{6,7},{7,6},{8,9},{9,8},{10,11... | collective-permute-start | bytes 1277960 | tf_op jit(solution)/shard_map/ppermute | solution.py:37
  101.3 6.0 %collective-permute-start.31 = (bf16[32,3328]{1,0:T(8,128)(2,1)S(1)}, bf16[32,3328]{1,0:T(8,128)(2,1)S(1)}, u32[]{:S(2)}, u32[]{:S(2)}) collective-permute-start(bf16[32,3328]{1,0:T(8,128)(2,1)S(1)} %pad_maximum_fusion.23), channel_id=1, source_target_pairs={{0,4},{1,13},{4,0},{5,9},{8,12},{9,5},{12,8},{13,1},{2,6},{3,15},{... | collective-permute-start | bytes 638984 | tf_op jit(solution)/shard_map/ppermute | solution.py:37
  103.9 10.1 %collective-permute-start.19 = (bf16[128,1024]{1,0:T(8,128)(2,1)S(1)}, bf16[128,1024]{1,0:T(8,128)(2,1)S(1)}, u32[]{:S(2)}, u32[]{:S(2)}) collective-permute-start(bf16[128,1024]{1,0:T(8,128)(2,1)S(1)} %convolution_convert_fusion.2), channel_id=1, source_target_pairs={{0,32},{32,0},{64,96},{96,64},{1,33},{33,1},{65,97},{97,65},{2,34}... | collective-permute-start | bytes 786440 | tf_op jit(solution)/shard_map/ppermute | solution.py:37
  107.4 2.6 %collective-permute-start.32 = (bf16[64,3328]{1,0:T(8,128)(2,1)S(1)}, bf16[64,3328]{1,0:T(8,128)(2,1)S(1)}, u32[]{:S(2)}, u32[]{:S(2)}) collective-permute-start(bf16[64,3328]{1,0:T(8,128)(2,1)S(1)} %pad_maximum_fusion.11), channel_id=1, source_target_pairs={{0,1},{1,0},{2,3},{3,2},{4,5},{5,4},{6,7},{7,6},{8,9},{9,8},{10,11... | collective-permute-start | bytes 1277960 | tf_op jit(solution)/shard_map/ppermute | solution.py:37
  109.4 9.5 %collective-permute-start.26 = (bf16[128,1024]{1,0:T(8,128)(2,1)S(1)}, bf16[128,1024]{1,0:T(8,128)(2,1)S(1)}, u32[]{:S(2)}, u32[]{:S(2)}) collective-permute-start(bf16[128,1024]{1,0:T(8,128)(2,1)S(1)} %convolution_convert_fusion.1), channel_id=1, source_target_pairs={{0,64},{32,96},{64,0},{96,32},{1,65},{33,97},{65,1},{97,33},{2,66}... | collective-permute-start | bytes 786440 | tf_op jit(solution)/shard_map/ppermute | solution.py:37
  111.1 13.8 %collective-permute-start.33 = (bf16[128,1024]{1,0:T(8,128)(2,1)S(1)}, bf16[128,1024]{1,0:T(8,128)(2,1)S(1)}, u32[]{:S(2)}, u32[]{:S(2)}) collective-permute-start(bf16[128,1024]{1,0:T(8,128)(2,1)S(1)} %convolution_convert_fusion), channel_id=1, source_target_pairs={{0,96},{32,64},{64,32},{96,0},{1,97},{33,65},{65,33},{97,1},{2,98}... | collective-permute-start | bytes 786440 | tf_op jit(solution)/shard_map/ppermute | solution.py:37
  125.1 6.2 %collective-permute-start.34 = (bf16[64,1024]{1,0:T(8,128)(2,1)S(1)}, bf16[64,1024]{1,0:T(8,128)(2,1)S(1)}, u32[]{:S(2)}, u32[]{:S(2)}) collective-permute-start(bf16[64,1024]{1,0:T(8,128)(2,1)S(1)} %select_convert_fusion), channel_id=1, source_target_pairs={{0,16},{16,0},{1,17},{17,1},{2,18},{18,2},{3,19},{19,3},{4,20},{20... | collective-permute-start | bytes 393224 | tf_op jit(solution)/shard_map/ppermute | solution.py:37

commit v6 on v4

--- a/solution.py
+++ b/solution.py
@@ -6,6 +6,7 @@
 F32, BF16, F16 = jnp.float32, jnp.bfloat16, jnp.float16
 LIFT = 8.0
 AXES = ("x", "z_hi", "y", "z_lo", "core")
+Z_FIRST = 0
 
 
 def permute(axes, sizes, move):
@@ -31,7 +32,7 @@
 
 
 def per_device(tokens, gate_weight, up_weight, down_weight):
-    z_hi, y, core = (lax.axis_index(a) for a in ("z_hi", "y", "core"))
+    z_hi, y, z_lo, core = (lax.axis_index(a) for a in AXES[1:])
     swap_core = permute(("core",), (2,), lambda c: (c ^ 1,))
     swap_z = permute(("z_lo",), (2,), lambda z: (z ^ 1,))
     swap_first = permute(("y", "core"), (4, 2), lambda y, c: (y ^ (3 if c else 1), c))
@@ -62,6 +63,7 @@
     rows = {0: own}
     state = [{} for _ in range(4)]
     arrived = []
+    half_hidden = gate_weight.shape[1] // 2
     stays = z_hi == core
 
     def tie(*values):
@@ -88,12 +90,26 @@
             got = tie(st["flight"])
             part = slice(64, 128) if s == 2 else slice(0, got.shape[1])
             total = [v[part] + lowered(g) for v, g in zip(st["total"], got)]
-            part = slice(0 if s == 4 else got.shape[1] // 2, None)
-            send, *st["total"] = tie(jnp.stack([lifted(v[part]) for v in total]), *total)
-            st["flight"] = (swap_first, swap_second, swap_z)[s - 2](send)
+            if e == Z_FIRST and s == 2:
+                sides = [(v[:, :half_hidden], v[:, half_hidden:]) for v in total]
+                send = jnp.stack([lifted(jnp.where(z_lo == 0, hi, lo)) for lo, hi in sides])
+                total = [jnp.where(z_lo == 0, lo, hi) for lo, hi in sides]
+                swap = swap_z
+            else:
+                over = s - 1 if e == Z_FIRST else s
+                part = slice(0 if over == 4 else got.shape[1] // 2, None)
+                send = jnp.stack([lifted(v[part]) for v in total])
+                swap = (swap_first, swap_second, swap_z)[over - 2]
+            send, *st["total"] = tie(send, *total)
+            st["flight"] = swap(send)
         elif s == 5:
-            gate, up = [v + lowered(g) for v, g in zip(st["total"], tie(st["flight"]))]
+            got = tie(st["flight"])
+            gate, up = [v[: got.shape[1]] + lowered(g) for v, g in zip(st["total"], got)]
             st["hidden"] = tie((jax.nn.silu(gate) * up).astype(BF16))
+            if e == Z_FIRST:
+                near, far = st["hidden"], tie(swap_z(st["hidden"]))
+                sides = (jnp.where(z_lo == 0, near, far), jnp.where(z_lo == 0, far, near))
+                st["hidden"] = tie(jnp.concatenate(sides, axis=1))
             st["flight"] = swap_second(st["hidden"])
         elif s in (6, 7):
             st["hidden"] = tie(jnp.concatenate((st["hidden"], tie(st["flight"]))))

time: 125 us -> 124 us (level)
  waiting for transfers between devices: 48 us -> 45.2 us
  starting transfers between devices: 51.6 us -> 53.4 us
    ppermute x38 -> x39, waiting for transfers between devices: 39.2 us -> 36.4 us  [permute(): return lambda v: lax.ppermute(v, axes, pairs)]
    ppermute x38 -> x39, starting transfers between devices: 42 us -> 43.8 us  [permute(): return lambda v: lax.ppermute(v, axes, pairs)]
  transfers between devices with their start and end apart: 39 -> 40, of which waited for: 16 -> 16; matrix products, arithmetic and copies ran while one was open for 17% -> 17% of each run, Pallas kernels for 0% -> 0%
where the time goes in v6:
time: 124 us; the launch traced here: 123 us
  starting transfers between devices  53.4 us (43%)
  waiting for transfers between devices  45.2 us (36%)
  matrix products  15.8 us (13%)
  other arithmetic  5.85 us (5%)
  local copies, waits for them, and re-layouts  2 us (2%)
    ppermute x39, starting transfers between devices, permute(): return lambda v: lax.ppermute(v, axes, pairs)  43.8 us
    ppermute x39, waiting for transfers between devices, permute(): return lambda v: lax.ppermute(v, axes, pairs)  36.4 us
    dot_general x12, matrix products, product(): return jnp.dot(rows, weight, preferred_element_type=F32)  15.8 us
    all_to_all x1, starting transfers between devices, per_device(): lax.all_to_all(blocks, AXES[1:], split_axis=0, concat_axis=0, tiled=True)  9.6 us
    all_to_all x1, waiting for transfers between devices, per_device(): lax.all_to_all(blocks, AXES[1:], split_axis=0, concat_axis=0, tiled=True)  8.79 us
  transfers between devices with their start and end apart: 40, of which 16 were waited for; matrix products, arithmetic and copies ran while one was open for 17% of the time, Pallas kernels for 0%

profile of v6, /device:TPU:1, one launch (start us, length us, event | category | flops | bytes accessed | tf_op | source)
XLA Modules:
  0.0 123.2 jit_solution(7426217115604908126)
XLA Ops:
  0.0 0.9 broadcast_in_dim.7
  1.0 0.8 all_to_all.6
  1.8 9.6 %all-to-all-start = ((bf16[32,4,1024]{2,1,0:T(4,128)(2,1)}), bf16[32,4,1024]{2,1,0:T(4,128)(2,1)S(1)}, u32[]{:S(2)}, u32[]{:S(2)}) async-start(bf16[32,4,1024]{2,1,0:T(4,128)(2,1)} %all_to_all.6), calls=%async_computation | async-start | bytes 524288 | tf_op jit(solution)/shard_map/all_to_all | solution.py:48
  11.5 8.8 %all-to-all-done = bf16[32,4,1024]{2,1,0:T(4,128)(2,1)S(1)} async-done(((bf16[32,4,1024]{2,1,0:T(4,128)(2,1)}), bf16[32,4,1024]{2,1,0:T(4,128)(2,1)S(1)}, u32[]{:S(2)}, u32[]{:S(2)}) %all-to-all-start) | async-done | bytes 262176 | tf_op jit(solution)/shard_map/all_to_all | solution.py:48
  20.5 2.6 %collective-permute-start.29 = (bf16[128,1024]{1,0:T(8,128)(2,1)S(1)}, bf16[128,1024]{1,0:T(8,128)(2,1)S(1)}, u32[]{:S(2)}, u32[]{:S(2)}) collective-permute-start(bf16[128,1024]{1,0:T(8,128)(2,1)S(1)} %bitcast_dynamic-update-slice_fusion), channel_id=1, source_target_pairs={{0,96},{32,64},{64,32},{96,0},{1,97},{33,65},{65,33},{97,1},{2,98}... | collective-permute-start | bytes 786440 | tf_op jit(solution)/shard_map/ppermute | solution.py:23
  23.1 1.4 %collective-permute-start.9 = (bf16[128,1024]{1,0:T(8,128)(2,1)S(1)}, bf16[128,1024]{1,0:T(8,128)(2,1)S(1)}, u32[]{:S(2)}, u32[]{:S(2)}) collective-permute-start(bf16[128,1024]{1,0:T(8,128)(2,1)S(1)} %bitcast_dynamic-update-slice_fusion), channel_id=1, source_target_pairs={{0,64},{32,96},{64,0},{96,32},{1,65},{33,97},{65,1},{97,33},{2,66}... | collective-permute-start | bytes 786440 | tf_op jit(solution)/shard_map/ppermute | solution.py:23
  24.5 4.1 %fusion.84 = f32[128,3328]{1,0:T(8,128)S(1)} fusion(bf16[128,1024]{1,0:T(8,128)(2,1)S(1)} %bitcast_dynamic-update-slice_fusion, bf16[1024,3328]{1,0:T(8,128)(2,1)} %param.5), kind=kOutput, calls=%fused_computation.199 | convolution fusion | flops 872415232 | bytes 8781824 | tf_op jit(solution)/shard_map/dot_general | solution.py:74
  28.6 1.1 fusion.85
  30.1 1.9 %collective-permute-start = (f16[2,64,3328]{2,1,0:T(8,128)(2,1)S(1)}, f16[2,64,3328]{2,1,0:T(8,128)(2,1)S(1)}, u32[]{:S(2)}, u32[]{:S(2)}) collective-permute-start(f16[2,64,3328]{2,1,0:T(8,128)(2,1)S(1)} %pad_maximum_fusion), channel_id=1, source_target_pairs={{0,1},{1,0},{2,3},{3,2},{4,5},{5,4},{6,7},{7,6},{8,9},{9,8},{10,11... | collective-permute-start | bytes 2555912 | tf_op jit(solution)/shard_map/ppermute | solution.py:23
  32.0 1.1 fusion.90
  33.0 1.1 fusion.91
  34.1 1.1 fusion.88
  35.2 1.1 fusion.89
  36.3 1.1 fusion.86
  37.3 1.1 fusion.87
  38.8 1.1 collective-permute-start.30
  42.5 1.1 collective-permute-start.31
  44.0 1.7 %collective-permute-start.21 = (f16[2,32,3328]{2,1,0:T(8,128)(2,1)S(1)}, f16[2,32,3328]{2,1,0:T(8,128)(2,1)S(1)}, u32[]{:S(2)}, u32[]{:S(2)}) collective-permute-start(f16[2,32,3328]{2,1,0:T(8,128)(2,1)S(1)} %pad_maximum_fusion.8), channel_id=1, source_target_pairs={{0,4},{1,13},{4,0},{5,9},{8,12},{9,5},{12,8},{13,1},{2,6},{3,15},{... | collective-permute-start | bytes 1277960 | tf_op jit(solution)/shard_map/ppermute | solution.py:23
  46.0 7.4 %collective-permute-done.1 = f16[2,64,1664]{2,1,0:T(8,128)(2,1)S(1)} collective-permute-done((f16[2,64,1664]{2,1,0:T(8,128)(2,1)S(1)}, f16[2,64,1664]{2,1,0:T(8,128)(2,1)S(1)}, u32[]{:S(2)}, u32[]{:S(2)}) %collective-permute-start.1) | collective-permute-done | bytes 426016 | tf_op jit(solution)/shard_map/ppermute | solution.py:23
  53.7 0.8 collective-permute-start.2
  54.6 2.0 %collective-permute-start.11 = (f16[2,32,3328]{2,1,0:T(8,128)(2,1)S(1)}, f16[2,32,3328]{2,1,0:T(8,128)(2,1)S(1)}, u32[]{:S(2)}, u32[]{:S(2)}) collective-permute-start(f16[2,32,3328]{2,1,0:T(8,128)(2,1)S(1)} %pad_maximum_fusion.6), channel_id=1, source_target_pairs={{0,4},{1,13},{4,0},{5,9},{8,12},{9,5},{12,8},{13,1},{2,6},{3,15},{... | collective-permute-start | bytes 1277960 | tf_op jit(solution)/shard_map/ppermute | solution.py:23
  56.6 3.0 %collective-permute-done.2 = f16[2,32,1664]{2,1,0:T(8,128)(2,1)S(1)} collective-permute-done((f16[2,32,1664]{2,1,0:T(8,128)(2,1)S(1)}, f16[2,32,1664]{2,1,0:T(8,128)(2,1)S(1)}, u32[]{:S(2)}, u32[]{:S(2)}) %collective-permute-start.2) | collective-permute-done | bytes 213024 | tf_op jit(solution)/shard_map/ppermute | solution.py:23
  60.1 1.5 %collective-permute-start.32 = (f16[2,16,3328]{2,1,0:T(8,128)(2,1)S(1)}, f16[2,16,3328]{2,1,0:T(8,128)(2,1)S(1)}, u32[]{:S(2)}, u32[]{:S(2)}) collective-permute-start(f16[2,16,3328]{2,1,0:T(8,128)(2,1)S(1)} %pad_maximum_fusion.20), channel_id=1, source_target_pairs={{0,12},{1,5},{4,8},{5,1},{8,4},{9,13},{12,0},{13,9},{2,14},{3,7},{... | collective-permute-start | bytes 638984 | tf_op jit(solution)/shard_map/ppermute | solution.py:23
  62.0 2.2 %collective-permute-done.11 = f16[2,32,3328]{2,1,0:T(8,128)(2,1)S(1)} collective-permute-done((f16[2,32,3328]{2,1,0:T(8,128)(2,1)S(1)}, f16[2,32,3328]{2,1,0:T(8,128)(2,1)S(1)}, u32[]{:S(2)}, u32[]{:S(2)}) %collective-permute-start.11) | collective-permute-done | bytes 426016 | tf_op jit(solution)/shard_map/ppermute | solution.py:23
  65.3 3.1 %collective-permute-done.4 = bf16[16,1664]{1,0:T(8,128)(2,1)S(1)} collective-permute-done((bf16[16,1664]{1,0:T(8,128)(2,1)S(1)}, bf16[16,1664]{1,0:T(8,128)(2,1)S(1)}, u32[]{:S(2)}, u32[]{:S(2)}) %collective-permute-start.4) | collective-permute-done | bytes 53280 | tf_op jit(solution)/shard_map/ppermute | solution.py:23
  68.8 1.5 %collective-permute-done.22 = f16[2,16,3328]{2,1,0:T(8,128)(2,1)S(1)} collective-permute-done((f16[2,16,3328]{2,1,0:T(8,128)(2,1)S(1)}, f16[2,16,3328]{2,1,0:T(8,128)(2,1)S(1)}, u32[]{:S(2)}, u32[]{:S(2)}) %collective-permute-start.22) | collective-permute-done | bytes 213024 | tf_op jit(solution)/shard_map/ppermute | solution.py:23
  70.6 2.0 %collective-permute-done.12 = f16[2,16,3328]{2,1,0:T(8,128)(2,1)S(1)} collective-permute-done((f16[2,16,3328]{2,1,0:T(8,128)(2,1)S(1)}, f16[2,16,3328]{2,1,0:T(8,128)(2,1)S(1)}, u32[]{:S(2)}, u32[]{:S(2)}) %collective-permute-start.12) | collective-permute-done | bytes 213024 | tf_op jit(solution)/shard_map/ppermute | solution.py:23
  72.8 0.9 collective-permute-done.5
  76.2 2.3 %collective-permute-start.24 = (bf16[16,3328]{1,0:T(8,128)(2,1)S(1)}, bf16[16,3328]{1,0:T(8,128)(2,1)S(1)}, u32[]{:S(2)}, u32[]{:S(2)}) collective-permute-start(bf16[16,3328]{1,0:T(8,128)(2,1)S(1)} %fusion.57), channel_id=1, source_target_pairs={{0,12},{1,5},{4,8},{5,1},{8,4},{9,13},{12,0},{13,9},{2,14},{3,7},{... | collective-permute-start | bytes 319496 | tf_op jit(solution)/shard_map/ppermute | solution.py:23
  78.5 2.1 %collective-permute-done.13 = f16[2,16,3328]{2,1,0:T(8,128)(2,1)S(1)} collective-permute-done((f16[2,16,3328]{2,1,0:T(8,128)(2,1)S(1)}, f16[2,16,3328]{2,1,0:T(8,128)(2,1)S(1)}, u32[]{:S(2)}, u32[]{:S(2)}) %collective-permute-start.13) | collective-permute-done | bytes 213024 | tf_op jit(solution)/shard_map/ppermute | solution.py:23
  80.7 2.3 %collective-permute-start.14 = (bf16[16,3328]{1,0:T(8,128)(2,1)S(1)}, bf16[16,3328]{1,0:T(8,128)(2,1)S(1)}, u32[]{:S(2)}, u32[]{:S(2)}) collective-permute-start(bf16[16,3328]{1,0:T(8,128)(2,1)S(1)} %fusion.59), channel_id=1, source_target_pairs={{0,12},{1,5},{4,8},{5,1},{8,4},{9,13},{12,0},{13,9},{2,14},{3,7},{... | collective-permute-start | bytes 319496 | tf_op jit(solution)/shard_map/ppermute | solution.py:23
  83.1 3.9 %collective-permute-start.7 = (bf16[64,3328]{1,0:T(8,128)(2,1)S(1)}, bf16[64,3328]{1,0:T(8,128)(2,1)S(1)}, u32[]{:S(2)}, u32[]{:S(2)}) collective-permute-start(bf16[64,3328]{1,0:T(8,128)(2,1)S(1)} %pad_maximum_fusion.5), channel_id=1, source_target_pairs={{0,1},{1,0},{2,3},{3,2},{4,5},{5,4},{6,7},{7,6},{8,9},{9,8},{10,11... | collective-permute-start | bytes 1277960 | tf_op jit(solution)/shard_map/ppermute | solution.py:23
  87.0 1.9 %collective-permute-start.35 = (bf16[32,3328]{1,0:T(8,128)(2,1)S(1)}, bf16[32,3328]{1,0:T(8,128)(2,1)S(1)}, u32[]{:S(2)}, u32[]{:S(2)}) collective-permute-start(bf16[32,3328]{1,0:T(8,128)(2,1)S(1)} %pad_maximum_fusion.22), channel_id=1, source_target_pairs={{0,4},{1,13},{4,0},{5,9},{8,12},{9,5},{12,8},{13,1},{2,6},{3,15},{... | collective-permute-start | bytes 638984 | tf_op jit(solution)/shard_map/ppermute | solution.py:23
  88.9 0.9 collective-permute-start.25
  89.9 1.9 %collective-permute-start.15 = (bf16[32,3328]{1,0:T(8,128)(2,1)S(1)}, bf16[32,3328]{1,0:T(8,128)(2,1)S(1)}, u32[]{:S(2)}, u32[]{:S(2)}) collective-permute-start(bf16[32,3328]{1,0:T(8,128)(2,1)S(1)} %pad_maximum_fusion.16), channel_id=1, source_target_pairs={{0,4},{1,13},{4,0},{5,9},{8,12},{9,5},{12,8},{13,1},{2,6},{3,15},{... | collective-permute-start | bytes 638984 | tf_op jit(solution)/shard_map/ppermute | solution.py:23
  91.8 1.4 %collective-permute-done.35 = bf16[32,3328]{1,0:T(8,128)(2,1)S(1)} collective-permute-done((bf16[32,3328]{1,0:T(8,128)(2,1)S(1)}, bf16[32,3328]{1,0:T(8,128)(2,1)S(1)}, u32[]{:S(2)}, u32[]{:S(2)}) %collective-permute-start.35) | collective-permute-done | bytes 213024 | tf_op jit(solution)/shard_map/ppermute | solution.py:23
  93.3 2.2 %collective-permute-done.25 = bf16[32,3328]{1,0:T(8,128)(2,1)S(1)} collective-permute-done((bf16[32,3328]{1,0:T(8,128)(2,1)S(1)}, bf16[32,3328]{1,0:T(8,128)(2,1)S(1)}, u32[]{:S(2)}, u32[]{:S(2)}) %collective-permute-start.25) | collective-permute-done | bytes 213024 | tf_op jit(solution)/shard_map/ppermute | solution.py:23
  95.6 2.2 %collective-permute-done.15 = bf16[32,3328]{1,0:T(8,128)(2,1)S(1)} collective-permute-done((bf16[32,3328]{1,0:T(8,128)(2,1)S(1)}, bf16[32,3328]{1,0:T(8,128)(2,1)S(1)}, u32[]{:S(2)}, u32[]{:S(2)}) %collective-permute-start.15) | collective-permute-done | bytes 213024 | tf_op jit(solution)/shard_map/ppermute | solution.py:23
  97.9 1.0 fusion.8
  99.1 1.2 collective-permute-start.8
  100.3 1.1 fusion.20
  101.4 4.4 %collective-permute-start.38 = (bf16[64,1024]{1,0:T(8,128)(2,1)S(1)}, bf16[64,1024]{1,0:T(8,128)(2,1)S(1)}, u32[]{:S(2)}, u32[]{:S(2)}) collective-permute-start(bf16[64,1024]{1,0:T(8,128)(2,1)S(1)} %get-tuple-element.116), channel_id=1, source_target_pairs={{0,112},{16,96},{32,80},{48,64},{64,48},{80,32},{96,16},{112,0},{1... | collective-permute-start | bytes 393224 | tf_op jit(solution)/shard_map/ppermute | solution.py:23
  105.9 1.1 fusion.16
  107.1 2.0 %collective-permute-start.27 = (bf16[64,1024]{1,0:T(8,128)(2,1)S(1)}, bf16[64,1024]{1,0:T(8,128)(2,1)S(1)}, u32[]{:S(2)}, u32[]{:S(2)}) collective-permute-start(bf16[64,1024]{1,0:T(8,128)(2,1)S(1)} %get-tuple-element.101), channel_id=1, source_target_pairs={{0,32},{32,0},{64,96},{96,64},{1,33},{33,1},{65,97},{97,65},{2,34}... | collective-permute-start | bytes 393224 | tf_op jit(solution)/shard_map/ppermute | solution.py:23
  109.2 1.1 fusion.12
  110.3 4.1 %collective-permute-start.18 = (bf16[64,1024]{1,0:T(8,128)(2,1)S(1)}, bf16[64,1024]{1,0:T(8,128)(2,1)S(1)}, u32[]{:S(2)}, u32[]{:S(2)}) collective-permute-start(bf16[64,1024]{1,0:T(8,128)(2,1)S(1)} %get-tuple-element.88), channel_id=1, source_target_pairs={{0,80},{16,64},{32,112},{48,96},{64,16},{80,0},{96,48},{112,32},{1... | collective-permute-start | bytes 393224 | tf_op jit(solution)/shard_map/ppermute | solution.py:23
  115.1 5.6 %collective-permute-done.18 = bf16[64,1024]{1,0:T(8,128)(2,1)S(1)} collective-permute-done((bf16[64,1024]{1,0:T(8,128)(2,1)S(1)}, bf16[64,1024]{1,0:T(8,128)(2,1)S(1)}, u32[]{:S(2)}, u32[]{:S(2)}) %collective-permute-start.18) | collective-permute-done | bytes 131104 | tf_op jit(solution)/shard_map/ppermute | solution.py:23
  120.7 1.6 %collective-permute-done.17 = bf16[64,1024]{1,0:T(8,128)(2,1)S(1)} collective-permute-done((bf16[64,1024]{1,0:T(8,128)(2,1)S(1)}, bf16[64,1024]{1,0:T(8,128)(2,1)S(1)}, u32[]{:S(2)}, u32[]{:S(2)}) %collective-permute-start.17) | collective-permute-done | bytes 131104 | tf_op jit(solution)/shard_map/ppermute | solution.py:23
  (143 shorter events, 12.2 us)
Async XLA Ops:
  1.8 18.5 %all-to-all-start = ((bf16[32,4,1024]{2,1,0:T(4,128)(2,1)}), bf16[32,4,1024]{2,1,0:T(4,128)(2,1)S(1)}, u32[]{:S(2)}, u32[]{:S(2)}) async-start(bf16[32,4,1024]{2,1,0:T(4,128)(2,1)} %all_to_all.6), calls=%async_computation | async-start | bytes 524288 | tf_op jit(solution)/shard_map/all_to_all | solution.py:48
  20.4 8.2 %slice-start.2 = ((s8[6815744]{0:T(1024)(128)(4,1)}), s8[4194304]{0:T(1024)(128)(4,1)S(1)}, s32[]{:S(2)}) async-start(s8[6815744]{0:T(1024)(128)(4,1)} %bitcast.208), calls=%async_computation.3 | async-start | bytes 8388608
  20.5 8.1 %slice-start.3 = ((s8[6815744]{0:T(1024)(128)(4,1)}), s8[2621440]{0:T(1024)(128)(4,1)S(1)}, s32[]{:S(2)}) async-start(s8[6815744]{0:T(1024)(128)(4,1)} %bitcast.208), calls=%async_computation.4 | async-start | bytes 5242880
  20.5 11.4 %collective-permute-start.29 = (bf16[128,1024]{1,0:T(8,128)(2,1)S(1)}, bf16[128,1024]{1,0:T(8,128)(2,1)S(1)}, u32[]{:S(2)}, u32[]{:S(2)}) collective-permute-start(bf16[128,1024]{1,0:T(8,128)(2,1)S(1)} %bitcast_dynamic-update-slice_fusion), channel_id=1, source_target_pairs={{0,96},{32,64},{64,32},{96,0},{1,97},{33,65},{65,33},{97,1},{2,98}... | collective-permute-start | bytes 786440 | tf_op jit(solution)/shard_map/ppermute | solution.py:23
  23.1 11.0 %collective-permute-start.19 = (bf16[128,1024]{1,0:T(8,128)(2,1)S(1)}, bf16[128,1024]{1,0:T(8,128)(2,1)S(1)}, u32[]{:S(2)}, u32[]{:S(2)}) collective-permute-start(bf16[128,1024]{1,0:T(8,128)(2,1)S(1)} %bitcast_dynamic-update-slice_fusion), channel_id=1, source_target_pairs={{0,32},{32,0},{64,96},{96,64},{1,33},{33,1},{65,97},{97,65},{2,34}... | collective-permute-start | bytes 786440 | tf_op jit(solution)/shard_map/ppermute | solution.py:23
  23.1 13.2 %collective-permute-start.9 = (bf16[128,1024]{1,0:T(8,128)(2,1)S(1)}, bf16[128,1024]{1,0:T(8,128)(2,1)S(1)}, u32[]{:S(2)}, u32[]{:S(2)}) collective-permute-start(bf16[128,1024]{1,0:T(8,128)(2,1)S(1)} %bitcast_dynamic-update-slice_fusion), channel_id=1, source_target_pairs={{0,64},{32,96},{64,0},{96,32},{1,65},{33,97},{65,1},{97,33},{2,66}... | collective-permute-start | bytes 786440 | tf_op jit(solution)/shard_map/ppermute | solution.py:23
  24.4 7.5 %slice-start = ((s8[6815744]{0:T(1024)(128)(4,1)}), s8[4194304]{0:T(1024)(128)(4,1)S(1)}, s32[]{:S(2)}) async-start(s8[6815744]{0:T(1024)(128)(4,1)} %bitcast.206), calls=%async_computation.1 | async-start | bytes 8388608
  28.6 3.3 %slice-start.1 = ((s8[6815744]{0:T(1024)(128)(4,1)}), s8[2621440]{0:T(1024)(128)(4,1)S(1)}, s32[]{:S(2)}) async-start(s8[6815744]{0:T(1024)(128)(4,1)} %bitcast.206), calls=%async_computation.2 | async-start | bytes 5242880
  30.1 11.4 %collective-permute-start = (f16[2,64,3328]{2,1,0:T(8,128)(2,1)S(1)}, f16[2,64,3328]{2,1,0:T(8,128)(2,1)S(1)}, u32[]{:S(2)}, u32[]{:S(2)}) collective-permute-start(f16[2,64,3328]{2,1,0:T(8,128)(2,1)S(1)} %pad_maximum_fusion), channel_id=1, source_target_pairs={{0,1},{1,0},{2,3},{3,2},{4,5},{5,4},{6,7},{7,6},{8,9},{9,8},{10,11... | collective-permute-start | bytes 2555912 | tf_op jit(solution)/shard_map/ppermute | solution.py:23
  38.8 3.3 %collective-permute-start.30 = (f16[2,64,3328]{2,1,0:T(8,128)(2,1)S(1)}, f16[2,64,3328]{2,1,0:T(8,128)(2,1)S(1)}, u32[]{:S(2)}, u32[]{:S(2)}) collective-permute-start(f16[2,64,3328]{2,1,0:T(8,128)(2,1)S(1)} %pad_maximum_fusion.3), channel_id=1, source_target_pairs={{0,1},{1,0},{2,3},{3,2},{4,5},{5,4},{6,7},{7,6},{8,9},{9,8},{10,11... | collective-permute-start | bytes 2555912 | tf_op jit(solution)/shard_map/ppermute | solution.py:23
  40.2 3.3 %collective-permute-start.20 = (f16[2,64,3328]{2,1,0:T(8,128)(2,1)S(1)}, f16[2,64,3328]{2,1,0:T(8,128)(2,1)S(1)}, u32[]{:S(2)}, u32[]{:S(2)}) collective-permute-start(f16[2,64,3328]{2,1,0:T(8,128)(2,1)S(1)} %pad_maximum_fusion.2), channel_id=1, source_target_pairs={{0,1},{1,0},{2,3},{3,2},{4,5},{5,4},{6,7},{7,6},{8,9},{9,8},{10,11... | collective-permute-start | bytes 2555912 | tf_op jit(solution)/shard_map/ppermute | solution.py:23
  40.7 5.0 %collective-permute-start.10 = (f16[2,64,3328]{2,1,0:T(8,128)(2,1)S(1)}, f16[2,64,3328]{2,1,0:T(8,128)(2,1)S(1)}, u32[]{:S(2)}, u32[]{:S(2)}) collective-permute-start(f16[2,64,3328]{2,1,0:T(8,128)(2,1)S(1)} %pad_maximum_fusion.1), channel_id=1, source_target_pairs={{0,1},{1,0},{2,3},{3,2},{4,5},{5,4},{6,7},{7,6},{8,9},{9,8},{10,11... | collective-permute-start | bytes 2555912 | tf_op jit(solution)/shard_map/ppermute | solution.py:23
  41.9 11.5 %collective-permute-start.1 = (f16[2,64,1664]{2,1,0:T(8,128)(2,1)S(1)}, f16[2,64,1664]{2,1,0:T(8,128)(2,1)S(1)}, u32[]{:S(2)}, u32[]{:S(2)}) collective-permute-start(f16[2,64,1664]{2,1,0:T(8,128)(2,1)S(1)} %pad_maximum_fusion.4), channel_id=1, source_target_pairs={{0,2},{2,0},{1,3},{3,1},{4,6},{6,4},{5,7},{7,5},{8,10},{10,8},{9,1... | collective-permute-start | bytes 1277960 | tf_op jit(solution)/shard_map/ppermute | solution.py:23
  42.5 17.4 %collective-permute-start.31 = (f16[2,32,3328]{2,1,0:T(8,128)(2,1)S(1)}, f16[2,32,3328]{2,1,0:T(8,128)(2,1)S(1)}, u32[]{:S(2)}, u32[]{:S(2)}) collective-permute-start(f16[2,32,3328]{2,1,0:T(8,128)(2,1)S(1)} %pad_maximum_fusion.10), channel_id=1, source_target_pairs={{0,4},{1,13},{4,0},{5,9},{8,12},{9,5},{12,8},{13,1},{2,6},{3,15},{... | collective-permute-start | bytes 1277960 | tf_op jit(solution)/shard_map/ppermute | solution.py:23
  44.0 17.7 %collective-permute-start.21 = (f16[2,32,3328]{2,1,0:T(8,128)(2,1)S(1)}, f16[2,32,3328]{2,1,0:T(8,128)(2,1)S(1)}, u32[]{:S(2)}, u32[]{:S(2)}) collective-permute-start(f16[2,32,3328]{2,1,0:T(8,128)(2,1)S(1)} %pad_maximum_fusion.8), channel_id=1, source_target_pairs={{0,4},{1,13},{4,0},{5,9},{8,12},{9,5},{12,8},{13,1},{2,6},{3,15},{... | collective-permute-start | bytes 1277960 | tf_op jit(solution)/shard_map/ppermute | solution.py:23
  53.7 6.0 %collective-permute-start.2 = (f16[2,32,1664]{2,1,0:T(8,128)(2,1)S(1)}, f16[2,32,1664]{2,1,0:T(8,128)(2,1)S(1)}, u32[]{:S(2)}, u32[]{:S(2)}) collective-permute-start(f16[2,32,1664]{2,1,0:T(8,128)(2,1)S(1)} %pad_maximum_fusion.12), channel_id=1, source_target_pairs={{0,4},{1,13},{4,0},{5,9},{8,12},{9,5},{12,8},{13,1},{2,6},{3,15},{... | collective-permute-start | bytes 638984 | tf_op jit(solution)/shard_map/ppermute | solution.py:23
  54.6 9.6 %collective-permute-start.11 = (f16[2,32,3328]{2,1,0:T(8,128)(2,1)S(1)}, f16[2,32,3328]{2,1,0:T(8,128)(2,1)S(1)}, u32[]{:S(2)}, u32[]{:S(2)}) collective-permute-start(f16[2,32,3328]{2,1,0:T(8,128)(2,1)S(1)} %pad_maximum_fusion.6), channel_id=1, source_target_pairs={{0,4},{1,13},{4,0},{5,9},{8,12},{9,5},{12,8},{13,1},{2,6},{3,15},{... | collective-permute-start | bytes 1277960 | tf_op jit(solution)/shard_map/ppermute | solution.py:23
  59.8 5.1 %collective-permute-start.3 = (f16[2,16,1664]{2,1,0:T(8,128)(2,1)S(1)}, f16[2,16,1664]{2,1,0:T(8,128)(2,1)S(1)}, u32[]{:S(2)}, u32[]{:S(2)}) collective-permute-start(f16[2,16,1664]{2,1,0:T(8,128)(2,1)S(1)} %pad_maximum_fusion.24), channel_id=1, source_target_pairs={{0,12},{1,5},{4,8},{5,1},{8,4},{9,13},{12,0},{13,9},{2,14},{3,7},{... | collective-permute-start | bytes 319496 | tf_op jit(solution)/shard_map/ppermute | solution.py:23
  60.1 8.3 %collective-permute-start.32 = (f16[2,16,3328]{2,1,0:T(8,128)(2,1)S(1)}, f16[2,16,3328]{2,1,0:T(8,128)(2,1)S(1)}, u32[]{:S(2)}, u32[]{:S(2)}) collective-permute-start(f16[2,16,3328]{2,1,0:T(8,128)(2,1)S(1)} %pad_maximum_fusion.20), channel_id=1, source_target_pairs={{0,12},{1,5},{4,8},{5,1},{8,4},{9,13},{12,0},{13,9},{2,14},{3,7},{... | collective-permute-start | bytes 638984 | tf_op jit(solution)/shard_map/ppermute | solution.py:23
  61.9 8.4 %collective-permute-start.22 = (f16[2,16,3328]{2,1,0:T(8,128)(2,1)S(1)}, f16[2,16,3328]{2,1,0:T(8,128)(2,1)S(1)}, u32[]{:S(2)}, u32[]{:S(2)}) collective-permute-start(f16[2,16,3328]{2,1,0:T(8,128)(2,1)S(1)} %pad_maximum_fusion.17), channel_id=1, source_target_pairs={{0,12},{1,5},{4,8},{5,1},{8,4},{9,13},{12,0},{13,9},{2,14},{3,7},{... | collective-permute-start | bytes 638984 | tf_op jit(solution)/shard_map/ppermute | solution.py:23
  64.2 33.7 %slice-start.4 = ((s8[6815744]{0:T(1024)(128)(4,1)}), s8[4194304]{0:T(1024)(128)(4,1)S(1)}, s32[]{:S(2)}) async-start(s8[6815744]{0:T(1024)(128)(4,1)} %bitcast.210), calls=%async_computation.5 | async-start | bytes 8388608
  65.0 3.4 %collective-permute-start.4 = (bf16[16,1664]{1,0:T(8,128)(2,1)S(1)}, bf16[16,1664]{1,0:T(8,128)(2,1)S(1)}, u32[]{:S(2)}, u32[]{:S(2)}) collective-permute-start(bf16[16,1664]{1,0:T(8,128)(2,1)S(1)} %fusion.77), channel_id=1, source_target_pairs={{0,2},{2,0},{1,3},{3,1},{4,6},{6,4},{5,7},{7,5},{8,10},{10,8},{9,1... | collective-permute-start | bytes 159752 | tf_op jit(solution)/shard_map/ppermute | solution.py:23
  65.2 7.4 %collective-permute-start.12 = (f16[2,16,3328]{2,1,0:T(8,128)(2,1)S(1)}, f16[2,16,3328]{2,1,0:T(8,128)(2,1)S(1)}, u32[]{:S(2)}, u32[]{:S(2)}) collective-permute-start(f16[2,16,3328]{2,1,0:T(8,128)(2,1)S(1)} %pad_maximum_fusion.14), channel_id=1, source_target_pairs={{0,12},{1,5},{4,8},{5,1},{8,4},{9,13},{12,0},{13,9},{2,14},{3,7},{... | collective-permute-start | bytes 638984 | tf_op jit(solution)/shard_map/ppermute | solution.py:23
  68.4 5.3 %collective-permute-start.5 = (bf16[16,3328]{1,0:T(8,128)(2,1)S(1)}, bf16[16,3328]{1,0:T(8,128)(2,1)S(1)}, u32[]{:S(2)}, u32[]{:S(2)}) collective-permute-start(bf16[16,3328]{1,0:T(8,128)(2,1)S(1)} %pad_maximum_fusion.25), channel_id=1, source_target_pairs={{0,12},{1,5},{4,8},{5,1},{8,4},{9,13},{12,0},{13,9},{2,14},{3,7},{... | collective-permute-start | bytes 319496 | tf_op jit(solution)/shard_map/ppermute | solution.py:23
  68.6 5.9 %collective-permute-start.33 = (f16[2,16,3328]{2,1,0:T(8,128)(2,1)S(1)}, f16[2,16,3328]{2,1,0:T(8,128)(2,1)S(1)}, u32[]{:S(2)}, u32[]{:S(2)}) collective-permute-start(f16[2,16,3328]{2,1,0:T(8,128)(2,1)S(1)} %pad_maximum_fusion.21), channel_id=1, source_target_pairs={{0,2},{2,0},{1,3},{3,1},{4,6},{6,4},{5,7},{7,5},{8,10},{10,8},{9,1... | collective-permute-start | bytes 638984 | tf_op jit(solution)/shard_map/ppermute | solution.py:23
  70.4 27.5 %slice-start.5 = ((s8[6815744]{0:T(1024)(128)(4,1)}), s8[2621440]{0:T(1024)(128)(4,1)S(1)}, s32[]{:S(2)}) async-start(s8[6815744]{0:T(1024)(128)(4,1)} %bitcast.210), calls=%async_computation.6 | async-start | bytes 5242880
  70.4 5.6 %collective-permute-start.23 = (f16[2,16,3328]{2,1,0:T(8,128)(2,1)S(1)}, f16[2,16,3328]{2,1,0:T(8,128)(2,1)S(1)}, u32[]{:S(2)}, u32[]{:S(2)}) collective-permute-start(f16[2,16,3328]{2,1,0:T(8,128)(2,1)S(1)} %pad_maximum_fusion.18), channel_id=1, source_target_pairs={{0,2},{2,0},{1,3},{3,1},{4,6},{6,4},{5,7},{7,5},{8,10},{10,8},{9,1... | collective-permute-start | bytes 638984 | tf_op jit(solution)/shard_map/ppermute | solution.py:23
  72.7 7.9 %collective-permute-start.13 = (f16[2,16,3328]{2,1,0:T(8,128)(2,1)S(1)}, f16[2,16,3328]{2,1,0:T(8,128)(2,1)S(1)}, u32[]{:S(2)}, u32[]{:S(2)}) collective-permute-start(f16[2,16,3328]{2,1,0:T(8,128)(2,1)S(1)} %pad_maximum_fusion.15), channel_id=1, source_target_pairs={{0,2},{2,0},{1,3},{3,1},{4,6},{6,4},{5,7},{7,5},{8,10},{10,8},{9,1... | collective-permute-start | bytes 638984 | tf_op jit(solution)/shard_map/ppermute | solution.py:23
  73.7 9.3 %collective-permute-start.6 = (bf16[32,3328]{1,0:T(8,128)(2,1)S(1)}, bf16[32,3328]{1,0:T(8,128)(2,1)S(1)}, u32[]{:S(2)}, u32[]{:S(2)}) collective-permute-start(bf16[32,3328]{1,0:T(8,128)(2,1)S(1)} %pad_maximum_fusion.13), channel_id=1, source_target_pairs={{0,4},{1,13},{4,0},{5,9},{8,12},{9,5},{12,8},{13,1},{2,6},{3,15},{... | collective-permute-start | bytes 638984 | tf_op jit(solution)/shard_map/ppermute | solution.py:23
  74.6 12.3 %collective-permute-start.34 = (bf16[16,3328]{1,0:T(8,128)(2,1)S(1)}, bf16[16,3328]{1,0:T(8,128)(2,1)S(1)}, u32[]{:S(2)}, u32[]{:S(2)}) collective-permute-start(bf16[16,3328]{1,0:T(8,128)(2,1)S(1)} %fusion.55), channel_id=1, source_target_pairs={{0,12},{1,5},{4,8},{5,1},{8,4},{9,13},{12,0},{13,9},{2,14},{3,7},{... | collective-permute-start | bytes 319496 | tf_op jit(solution)/shard_map/ppermute | solution.py:23
  76.2 12.7 %collective-permute-start.24 = (bf16[16,3328]{1,0:T(8,128)(2,1)S(1)}, bf16[16,3328]{1,0:T(8,128)(2,1)S(1)}, u32[]{:S(2)}, u32[]{:S(2)}) collective-permute-start(bf16[16,3328]{1,0:T(8,128)(2,1)S(1)} %fusion.57), channel_id=1, source_target_pairs={{0,12},{1,5},{4,8},{5,1},{8,4},{9,13},{12,0},{13,9},{2,14},{3,7},{... | collective-permute-start | bytes 319496 | tf_op jit(solution)/shard_map/ppermute | solution.py:23
  80.7 9.1 %collective-permute-start.14 = (bf16[16,3328]{1,0:T(8,128)(2,1)S(1)}, bf16[16,3328]{1,0:T(8,128)(2,1)S(1)}, u32[]{:S(2)}, u32[]{:S(2)}) collective-permute-start(bf16[16,3328]{1,0:T(8,128)(2,1)S(1)} %fusion.59), channel_id=1, source_target_pairs={{0,12},{1,5},{4,8},{5,1},{8,4},{9,13},{12,0},{13,9},{2,14},{3,7},{... | collective-permute-start | bytes 319496 | tf_op jit(solution)/shard_map/ppermute | solution.py:23
  83.1 14.8 %collective-permute-start.7 = (bf16[64,3328]{1,0:T(8,128)(2,1)S(1)}, bf16[64,3328]{1,0:T(8,128)(2,1)S(1)}, u32[]{:S(2)}, u32[]{:S(2)}) collective-permute-start(bf16[64,3328]{1,0:T(8,128)(2,1)S(1)} %pad_maximum_fusion.5), channel_id=1, source_target_pairs={{0,1},{1,0},{2,3},{3,2},{4,5},{5,4},{6,7},{7,6},{8,9},{9,8},{10,11... | collective-permute-start | bytes 1277960 | tf_op jit(solution)/shard_map/ppermute | solution.py:23
  87.0 6.2 %collective-permute-start.35 = (bf16[32,3328]{1,0:T(8,128)(2,1)S(1)}, bf16[32,3328]{1,0:T(8,128)(2,1)S(1)}, u32[]{:S(2)}, u32[]{:S(2)}) collective-permute-start(bf16[32,3328]{1,0:T(8,128)(2,1)S(1)} %pad_maximum_fusion.22), channel_id=1, source_target_pairs={{0,4},{1,13},{4,0},{5,9},{8,12},{9,5},{12,8},{13,1},{2,6},{3,15},{... | collective-permute-start | bytes 638984 | tf_op jit(solution)/shard_map/ppermute | solution.py:23
  88.9 6.6 %collective-permute-start.25 = (bf16[32,3328]{1,0:T(8,128)(2,1)S(1)}, bf16[32,3328]{1,0:T(8,128)(2,1)S(1)}, u32[]{:S(2)}, u32[]{:S(2)}) collective-permute-start(bf16[32,3328]{1,0:T(8,128)(2,1)S(1)} %pad_maximum_fusion.19), channel_id=1, source_target_pairs={{0,4},{1,13},{4,0},{5,9},{8,12},{9,5},{12,8},{13,1},{2,6},{3,15},{... | collective-permute-start | bytes 638984 | tf_op jit(solution)/shard_map/ppermute | solution.py:23
  89.9 7.9 %collective-permute-start.15 = (bf16[32,3328]{1,0:T(8,128)(2,1)S(1)}, bf16[32,3328]{1,0:T(8,128)(2,1)S(1)}, u32[]{:S(2)}, u32[]{:S(2)}) collective-permute-start(bf16[32,3328]{1,0:T(8,128)(2,1)S(1)} %pad_maximum_fusion.16), channel_id=1, source_target_pairs={{0,4},{1,13},{4,0},{5,9},{8,12},{9,5},{12,8},{13,1},{2,6},{3,15},{... | collective-permute-start | bytes 638984 | tf_op jit(solution)/shard_map/ppermute | solution.py:23
  93.2 7.0 %collective-permute-start.36 = (bf16[64,3328]{1,0:T(8,128)(2,1)S(1)}, bf16[64,3328]{1,0:T(8,128)(2,1)S(1)}, u32[]{:S(2)}, u32[]{:S(2)}) collective-permute-start(bf16[64,3328]{1,0:T(8,128)(2,1)S(1)} %pad_maximum_fusion.11), channel_id=1, source_target_pairs={{0,1},{1,0},{2,3},{3,2},{4,5},{5,4},{6,7},{7,6},{8,9},{9,8},{10,11... | collective-permute-start | bytes 1277960 | tf_op jit(solution)/shard_map/ppermute | solution.py:23
  95.5 10.4 %collective-permute-start.26 = (bf16[64,3328]{1,0:T(8,128)(2,1)S(1)}, bf16[64,3328]{1,0:T(8,128)(2,1)S(1)}, u32[]{:S(2)}, u32[]{:S(2)}) collective-permute-start(bf16[64,3328]{1,0:T(8,128)(2,1)S(1)} %pad_maximum_fusion.9), channel_id=1, source_target_pairs={{0,1},{1,0},{2,3},{3,2},{4,5},{5,4},{6,7},{7,6},{8,9},{9,8},{10,11... | collective-permute-start | bytes 1277960 | tf_op jit(solution)/shard_map/ppermute | solution.py:23
  97.8 9.3 %collective-permute-start.16 = (bf16[64,3328]{1,0:T(8,128)(2,1)S(1)}, bf16[64,3328]{1,0:T(8,128)(2,1)S(1)}, u32[]{:S(2)}, u32[]{:S(2)}) collective-permute-start(bf16[64,3328]{1,0:T(8,128)(2,1)S(1)} %pad_maximum_fusion.7), channel_id=1, source_target_pairs={{0,1},{1,0},{2,3},{3,2},{4,5},{5,4},{6,7},{7,6},{8,9},{9,8},{10,11... | collective-permute-start | bytes 1277960 | tf_op jit(solution)/shard_map/ppermute | solution.py:23
  99.1 11.2 %collective-permute-start.8 = (bf16[64,1024]{1,0:T(8,128)(2,1)S(1)}, bf16[64,1024]{1,0:T(8,128)(2,1)S(1)}, u32[]{:S(2)}, u32[]{:S(2)}) collective-permute-start(bf16[64,1024]{1,0:T(8,128)(2,1)S(1)} %select_convert_fusion.6), channel_id=1, source_target_pairs={{0,16},{16,0},{32,48},{48,32},{64,80},{80,64},{96,112},{112,96},{1... | collective-permute-start | bytes 393224 | tf_op jit(solution)/shard_map/ppermute | solution.py:23
  101.4 13.0 %collective-permute-start.38 = (bf16[64,1024]{1,0:T(8,128)(2,1)S(1)}, bf16[64,1024]{1,0:T(8,128)(2,1)S(1)}, u32[]{:S(2)}, u32[]{:S(2)}) collective-permute-start(bf16[64,1024]{1,0:T(8,128)(2,1)S(1)} %get-tuple-element.116), channel_id=1, source_target_pairs={{0,112},{16,96},{32,80},{48,64},{64,48},{80,32},{96,16},{112,0},{1... | collective-permute-start | bytes 393224 | tf_op jit(solution)/shard_map/ppermute | solution.py:23
  105.7 9.4 %collective-permute-start.37 = (bf16[64,1024]{1,0:T(8,128)(2,1)S(1)}, bf16[64,1024]{1,0:T(8,128)(2,1)S(1)}, u32[]{:S(2)}, u32[]{:S(2)}) collective-permute-start(bf16[64,1024]{1,0:T(8,128)(2,1)S(1)} %get-tuple-element.115), channel_id=1, source_target_pairs={{0,96},{32,64},{64,32},{96,0},{1,97},{33,65},{65,33},{97,1},{2,98}... | collective-permute-start | bytes 393224 | tf_op jit(solution)/shard_map/ppermute | solution.py:23
  107.0 8.1 %collective-permute-start.28 = (bf16[64,1024]{1,0:T(8,128)(2,1)S(1)}, bf16[64,1024]{1,0:T(8,128)(2,1)S(1)}, u32[]{:S(2)}, u32[]{:S(2)}) collective-permute-start(bf16[64,1024]{1,0:T(8,128)(2,1)S(1)} %get-tuple-element.102), channel_id=1, source_target_pairs={{0,48},{16,32},{32,16},{48,0},{64,112},{80,96},{96,80},{112,64},{1... | collective-permute-start | bytes 393224 | tf_op jit(solution)/shard_map/ppermute | solution.py:23
  107.1 8.0 %collective-permute-start.27 = (bf16[64,1024]{1,0:T(8,128)(2,1)S(1)}, bf16[64,1024]{1,0:T(8,128)(2,1)S(1)}, u32[]{:S(2)}, u32[]{:S(2)}) collective-permute-start(bf16[64,1024]{1,0:T(8,128)(2,1)S(1)} %get-tuple-element.101), channel_id=1, source_target_pairs={{0,32},{32,0},{64,96},{96,64},{1,33},{33,1},{65,97},{97,65},{2,34}... | collective-permute-start | bytes 393224 | tf_op jit(solution)/shard_map/ppermute | solution.py:23
  110.3 10.4 %collective-permute-start.18 = (bf16[64,1024]{1,0:T(8,128)(2,1)S(1)}, bf16[64,1024]{1,0:T(8,128)(2,1)S(1)}, u32[]{:S(2)}, u32[]{:S(2)}) collective-permute-start(bf16[64,1024]{1,0:T(8,128)(2,1)S(1)} %get-tuple-element.88), channel_id=1, source_target_pairs={{0,80},{16,64},{32,112},{48,96},{64,16},{80,0},{96,48},{112,32},{1... | collective-permute-start | bytes 393224 | tf_op jit(solution)/shard_map/ppermute | solution.py:23
  114.3 8.0 %collective-permute-start.17 = (bf16[64,1024]{1,0:T(8,128)(2,1)S(1)}, bf16[64,1024]{1,0:T(8,128)(2,1)S(1)}, u32[]{:S(2)}, u32[]{:S(2)}) collective-permute-start(bf16[64,1024]{1,0:T(8,128)(2,1)S(1)} %get-tuple-element.87), channel_id=1, source_target_pairs={{0,64},{32,96},{64,0},{96,32},{1,65},{33,97},{65,1},{97,33},{2,66}... | collective-permute-start | bytes 393224 | tf_op jit(solution)/shard_map/ppermute | solution.py:23

commit v7 on v6

--- a/solution.py
+++ b/solution.py
@@ -6,7 +6,7 @@
 F32, BF16, F16 = jnp.float32, jnp.bfloat16, jnp.float16
 LIFT = 8.0
 AXES = ("x", "z_hi", "y", "z_lo", "core")
-Z_FIRST = 0
+Z_FIRST = 3
 
 
 def permute(axes, sizes, move):

time: 124 us -> 124 us (level)
  starting transfers between devices: 53.4 us -> 62.7 us
  waiting for transfers between devices: 45.2 us -> 36.7 us
    ppermute x39, starting transfers between devices: 43.8 us -> 53.1 us  [permute(): return lambda v: lax.ppermute(v, axes, pairs)]
    ppermute x39, waiting for transfers between devices: 36.4 us -> 27.9 us  [permute(): return lambda v: lax.ppermute(v, axes, pairs)]
  transfers between devices with their start and end apart: 40 -> 40, of which waited for: 16 -> 15; matrix products, arithmetic and copies ran while one was open for 17% -> 17% of each run, Pallas kernels for 0% -> 0%
where the time goes in v7:
time: 124 us
  starting transfers between devices  62.7 us (51%)
  waiting for transfers between devices  36.7 us (30%)
  matrix products  15.8 us (13%)
  other arithmetic  5.82 us (5%)
  local copies, waits for them, and re-layouts  2 us (2%)
    ppermute x39, starting transfers between devices, permute(): return lambda v: lax.ppermute(v, axes, pairs)  53.1 us
    ppermute x39, waiting for transfers between devices, permute(): return lambda v: lax.ppermute(v, axes, pairs)  27.9 us
    dot_general x12, matrix products, product(): return jnp.dot(rows, weight, preferred_element_type=F32)  15.8 us
    all_to_all x1, starting transfers between devices, per_device(): lax.all_to_all(blocks, AXES[1:], split_axis=0, concat_axis=0, tiled=True)  9.6 us
    all_to_all x1, waiting for transfers between devices, per_device(): lax.all_to_all(blocks, AXES[1:], split_axis=0, concat_axis=0, tiled=True)  8.79 us
  transfers between devices with their start and end apart: 40, of which 15 were waited for; matrix products, arithmetic and copies ran while one was open for 17% of the time, Pallas kernels for 0%

profile of v7, /device:TPU:1, one launch (start us, length us, event | category | flops | bytes accessed | tf_op | source)
XLA Modules:
  0.0 123.9 jit_solution(11208589935547532972)
XLA Ops:
  0.0 0.9 broadcast_in_dim.7
  1.0 0.8 all_to_all.6
  1.8 9.6 %all-to-all-start = ((bf16[32,4,1024]{2,1,0:T(4,128)(2,1)}), bf16[32,4,1024]{2,1,0:T(4,128)(2,1)S(1)}, u32[]{:S(2)}, u32[]{:S(2)}) async-start(bf16[32,4,1024]{2,1,0:T(4,128)(2,1)} %all_to_all.6), calls=%async_computation | async-start | bytes 524288 | tf_op jit(solution)/shard_map/all_to_all | solution.py:48
  11.5 8.8 %all-to-all-done = bf16[32,4,1024]{2,1,0:T(4,128)(2,1)S(1)} async-done(((bf16[32,4,1024]{2,1,0:T(4,128)(2,1)}), bf16[32,4,1024]{2,1,0:T(4,128)(2,1)S(1)}, u32[]{:S(2)}, u32[]{:S(2)}) %all-to-all-start) | async-done | bytes 262176 | tf_op jit(solution)/shard_map/all_to_all | solution.py:48
  20.5 2.6 %collective-permute-start.28 = (bf16[128,1024]{1,0:T(8,128)(2,1)S(1)}, bf16[128,1024]{1,0:T(8,128)(2,1)S(1)}, u32[]{:S(2)}, u32[]{:S(2)}) collective-permute-start(bf16[128,1024]{1,0:T(8,128)(2,1)S(1)} %bitcast_dynamic-update-slice_fusion), channel_id=1, source_target_pairs={{0,96},{32,64},{64,32},{96,0},{1,97},{33,65},{65,33},{97,1},{2,98}... | collective-permute-start | bytes 786440 | tf_op jit(solution)/shard_map/ppermute | solution.py:23
  23.1 1.4 %collective-permute-start.8 = (bf16[128,1024]{1,0:T(8,128)(2,1)S(1)}, bf16[128,1024]{1,0:T(8,128)(2,1)S(1)}, u32[]{:S(2)}, u32[]{:S(2)}) collective-permute-start(bf16[128,1024]{1,0:T(8,128)(2,1)S(1)} %bitcast_dynamic-update-slice_fusion), channel_id=1, source_target_pairs={{0,64},{32,96},{64,0},{96,32},{1,65},{33,97},{65,1},{97,33},{2,66}... | collective-permute-start | bytes 786440 | tf_op jit(solution)/shard_map/ppermute | solution.py:23
  24.5 4.1 %fusion.84 = f32[128,3328]{1,0:T(8,128)S(1)} fusion(bf16[128,1024]{1,0:T(8,128)(2,1)S(1)} %bitcast_dynamic-update-slice_fusion, bf16[1024,3328]{1,0:T(8,128)(2,1)} %param.5), kind=kOutput, calls=%fused_computation.199 | convolution fusion | flops 872415232 | bytes 8781824 | tf_op jit(solution)/shard_map/dot_general | solution.py:74
  28.6 1.1 fusion.85
  30.1 1.9 %collective-permute-start = (f16[2,64,3328]{2,1,0:T(8,128)(2,1)S(1)}, f16[2,64,3328]{2,1,0:T(8,128)(2,1)S(1)}, u32[]{:S(2)}, u32[]{:S(2)}) collective-permute-start(f16[2,64,3328]{2,1,0:T(8,128)(2,1)S(1)} %pad_maximum_fusion), channel_id=1, source_target_pairs={{0,1},{1,0},{2,3},{3,2},{4,5},{5,4},{6,7},{7,6},{8,9},{9,8},{10,11... | collective-permute-start | bytes 2555912 | tf_op jit(solution)/shard_map/ppermute | solution.py:23
  32.0 1.1 fusion.90
  33.0 1.1 fusion.91
  34.1 1.1 fusion.88
  35.2 1.1 fusion.89
  36.3 1.1 fusion.86
  37.3 1.1 fusion.87
  38.8 1.1 collective-permute-start.29
  41.8 0.8 collective-permute-start.1
  43.9 1.7 %collective-permute-start.20 = (f16[2,32,3328]{2,1,0:T(8,128)(2,1)S(1)}, f16[2,32,3328]{2,1,0:T(8,128)(2,1)S(1)}, u32[]{:S(2)}, u32[]{:S(2)}) collective-permute-start(f16[2,32,3328]{2,1,0:T(8,128)(2,1)S(1)} %pad_maximum_fusion.8), channel_id=1, source_target_pairs={{0,4},{1,13},{4,0},{5,9},{8,12},{9,5},{12,8},{13,1},{2,6},{3,15},{... | collective-permute-start | bytes 1277960 | tf_op jit(solution)/shard_map/ppermute | solution.py:23
  46.0 4.1 %collective-permute-done.1 = f16[2,32,3328]{2,1,0:T(8,128)(2,1)S(1)} collective-permute-done((f16[2,32,3328]{2,1,0:T(8,128)(2,1)S(1)}, f16[2,32,3328]{2,1,0:T(8,128)(2,1)S(1)}, u32[]{:S(2)}, u32[]{:S(2)}) %collective-permute-start.1) | collective-permute-done | bytes 426016 | tf_op jit(solution)/shard_map/ppermute | solution.py:23
  51.4 6.4 %collective-permute-done.2 = f16[2,16,3328]{2,1,0:T(8,128)(2,1)S(1)} collective-permute-done((f16[2,16,3328]{2,1,0:T(8,128)(2,1)S(1)}, f16[2,16,3328]{2,1,0:T(8,128)(2,1)S(1)}, u32[]{:S(2)}, u32[]{:S(2)}) %collective-permute-start.2) | collective-permute-done | bytes 213024 | tf_op jit(solution)/shard_map/ppermute | solution.py:23
  59.3 2.2 %collective-permute-done.10 = f16[2,32,3328]{2,1,0:T(8,128)(2,1)S(1)} collective-permute-done((f16[2,32,3328]{2,1,0:T(8,128)(2,1)S(1)}, f16[2,32,3328]{2,1,0:T(8,128)(2,1)S(1)}, u32[]{:S(2)}, u32[]{:S(2)}) %collective-permute-start.10) | collective-permute-done | bytes 426016 | tf_op jit(solution)/shard_map/ppermute | solution.py:23
  62.8 2.0 %collective-permute-start.4 = (bf16[16,3328]{1,0:T(8,128)(2,1)S(1)}, bf16[16,3328]{1,0:T(8,128)(2,1)S(1)}, u32[]{:S(2)}, u32[]{:S(2)}) collective-permute-start(bf16[16,3328]{1,0:T(8,128)(2,1)S(1)} %fusion.59), channel_id=1, source_target_pairs={{0,12},{1,5},{4,8},{5,1},{8,4},{9,13},{12,0},{13,9},{2,14},{3,7},{... | collective-permute-start | bytes 319496 | tf_op jit(solution)/shard_map/ppermute | solution.py:23
  65.2 1.0 collective-permute-start.22
  66.2 2.6 %collective-permute-done.11 = f16[2,16,3328]{2,1,0:T(8,128)(2,1)S(1)} collective-permute-done((f16[2,16,3328]{2,1,0:T(8,128)(2,1)S(1)}, f16[2,16,3328]{2,1,0:T(8,128)(2,1)S(1)}, u32[]{:S(2)}, u32[]{:S(2)}) %collective-permute-start.11) | collective-permute-done | bytes 213024 | tf_op jit(solution)/shard_map/ppermute | solution.py:23
  70.0 1.1 collective-permute-done.32
  71.2 0.9 collective-permute-start.33
  72.1 2.4 %collective-permute-start.5 = (bf16[32,3328]{1,0:T(8,128)(2,1)S(1)}, bf16[32,3328]{1,0:T(8,128)(2,1)S(1)}, u32[]{:S(2)}, u32[]{:S(2)}) collective-permute-start(bf16[32,3328]{1,0:T(8,128)(2,1)S(1)} %pad_maximum_fusion.14), channel_id=1, source_target_pairs={{0,4},{1,13},{4,0},{5,9},{8,12},{9,5},{12,8},{13,1},{2,6},{3,15},{... | collective-permute-start | bytes 638984 | tf_op jit(solution)/shard_map/ppermute | solution.py:23
  74.6 0.9 collective-permute-done.33
  75.5 1.1 collective-permute-start.34
  77.4 1.1 collective-permute-start.13
  78.4 1.0 collective-permute-done.34
  79.5 3.7 %collective-permute-start.35 = (bf16[32,3328]{1,0:T(8,128)(2,1)S(1)}, bf16[32,3328]{1,0:T(8,128)(2,1)S(1)}, u32[]{:S(2)}, u32[]{:S(2)}) collective-permute-start(bf16[32,3328]{1,0:T(8,128)(2,1)S(1)} %pad_maximum_fusion.22), channel_id=1, source_target_pairs={{0,4},{1,13},{4,0},{5,9},{8,12},{9,5},{12,8},{13,1},{2,6},{3,15},{... | collective-permute-start | bytes 638984 | tf_op jit(solution)/shard_map/ppermute | solution.py:23
  83.2 4.4 %collective-permute-start.6 = (bf16[64,3328]{1,0:T(8,128)(2,1)S(1)}, bf16[64,3328]{1,0:T(8,128)(2,1)S(1)}, u32[]{:S(2)}, u32[]{:S(2)}) collective-permute-start(bf16[64,3328]{1,0:T(8,128)(2,1)S(1)} %pad_maximum_fusion.5), channel_id=1, source_target_pairs={{0,1},{1,0},{2,3},{3,2},{4,5},{5,4},{6,7},{7,6},{8,9},{9,8},{10,11... | collective-permute-start | bytes 1277960 | tf_op jit(solution)/shard_map/ppermute | solution.py:23
  87.6 1.9 %collective-permute-start.24 = (bf16[32,3328]{1,0:T(8,128)(2,1)S(1)}, bf16[32,3328]{1,0:T(8,128)(2,1)S(1)}, u32[]{:S(2)}, u32[]{:S(2)}) collective-permute-start(bf16[32,3328]{1,0:T(8,128)(2,1)S(1)} %pad_maximum_fusion.20), channel_id=1, source_target_pairs={{0,4},{1,13},{4,0},{5,9},{8,12},{9,5},{12,8},{13,1},{2,6},{3,15},{... | collective-permute-start | bytes 638984 | tf_op jit(solution)/shard_map/ppermute | solution.py:23
  89.5 0.9 collective-permute-start.14
  90.5 2.9 %collective-permute-start.36 = (bf16[64,3328]{1,0:T(8,128)(2,1)S(1)}, bf16[64,3328]{1,0:T(8,128)(2,1)S(1)}, u32[]{:S(2)}, u32[]{:S(2)}) collective-permute-start(bf16[64,3328]{1,0:T(8,128)(2,1)S(1)} %pad_maximum_fusion.11), channel_id=1, source_target_pairs={{0,1},{1,0},{2,3},{3,2},{4,5},{5,4},{6,7},{7,6},{8,9},{9,8},{10,11... | collective-permute-start | bytes 1277960 | tf_op jit(solution)/shard_map/ppermute | solution.py:23
  93.6 2.1 %collective-permute-start.25 = (bf16[64,3328]{1,0:T(8,128)(2,1)S(1)}, bf16[64,3328]{1,0:T(8,128)(2,1)S(1)}, u32[]{:S(2)}, u32[]{:S(2)}) collective-permute-start(bf16[64,3328]{1,0:T(8,128)(2,1)S(1)} %pad_maximum_fusion.9), channel_id=1, source_target_pairs={{0,1},{1,0},{2,3},{3,2},{4,5},{5,4},{6,7},{7,6},{8,9},{9,8},{10,11... | collective-permute-start | bytes 1277960 | tf_op jit(solution)/shard_map/ppermute | solution.py:23
  95.9 2.1 %collective-permute-start.15 = (bf16[64,3328]{1,0:T(8,128)(2,1)S(1)}, bf16[64,3328]{1,0:T(8,128)(2,1)S(1)}, u32[]{:S(2)}, u32[]{:S(2)}) collective-permute-start(bf16[64,3328]{1,0:T(8,128)(2,1)S(1)} %pad_maximum_fusion.7), channel_id=1, source_target_pairs={{0,1},{1,0},{2,3},{3,2},{4,5},{5,4},{6,7},{7,6},{8,9},{9,8},{10,11... | collective-permute-start | bytes 1277960 | tf_op jit(solution)/shard_map/ppermute | solution.py:23
  98.0 1.0 fusion.8
  99.1 1.8 %collective-permute-start.7 = (bf16[64,1024]{1,0:T(8,128)(2,1)S(1)}, bf16[64,1024]{1,0:T(8,128)(2,1)S(1)}, u32[]{:S(2)}, u32[]{:S(2)}) collective-permute-start(bf16[64,1024]{1,0:T(8,128)(2,1)S(1)} %select_convert_fusion.6), channel_id=1, source_target_pairs={{0,16},{16,0},{32,48},{48,32},{64,80},{80,64},{96,112},{112,96},{1... | collective-permute-start | bytes 393224 | tf_op jit(solution)/shard_map/ppermute | solution.py:23
  100.9 1.1 fusion.20
  102.0 3.8 %collective-permute-start.38 = (bf16[64,1024]{1,0:T(8,128)(2,1)S(1)}, bf16[64,1024]{1,0:T(8,128)(2,1)S(1)}, u32[]{:S(2)}, u32[]{:S(2)}) collective-permute-start(bf16[64,1024]{1,0:T(8,128)(2,1)S(1)} %get-tuple-element.116), channel_id=1, source_target_pairs={{0,112},{16,96},{32,80},{48,64},{64,48},{80,32},{96,16},{112,0},{1... | collective-permute-start | bytes 393224 | tf_op jit(solution)/shard_map/ppermute | solution.py:23
  105.9 1.1 fusion.16
  107.1 2.6 %collective-permute-start.26 = (bf16[64,1024]{1,0:T(8,128)(2,1)S(1)}, bf16[64,1024]{1,0:T(8,128)(2,1)S(1)}, u32[]{:S(2)}, u32[]{:S(2)}) collective-permute-start(bf16[64,1024]{1,0:T(8,128)(2,1)S(1)} %get-tuple-element.101), channel_id=1, source_target_pairs={{0,32},{32,0},{64,96},{96,64},{1,33},{33,1},{65,97},{97,65},{2,34}... | collective-permute-start | bytes 393224 | tf_op jit(solution)/shard_map/ppermute | solution.py:23
  109.8 1.0 fusion.12
  110.9 3.5 %collective-permute-start.17 = (bf16[64,1024]{1,0:T(8,128)(2,1)S(1)}, bf16[64,1024]{1,0:T(8,128)(2,1)S(1)}, u32[]{:S(2)}, u32[]{:S(2)}) collective-permute-start(bf16[64,1024]{1,0:T(8,128)(2,1)S(1)} %get-tuple-element.88), channel_id=1, source_target_pairs={{0,80},{16,64},{32,112},{48,96},{64,16},{80,0},{96,48},{112,32},{1... | collective-permute-start | bytes 393224 | tf_op jit(solution)/shard_map/ppermute | solution.py:23
  115.2 6.2 %collective-permute-done.17 = bf16[64,1024]{1,0:T(8,128)(2,1)S(1)} collective-permute-done((bf16[64,1024]{1,0:T(8,128)(2,1)S(1)}, bf16[64,1024]{1,0:T(8,128)(2,1)S(1)}, u32[]{:S(2)}, u32[]{:S(2)}) %collective-permute-start.17) | collective-permute-done | bytes 131104 | tf_op jit(solution)/shard_map/ppermute | solution.py:23
  121.5 1.6 %collective-permute-done.16 = bf16[64,1024]{1,0:T(8,128)(2,1)S(1)} collective-permute-done((bf16[64,1024]{1,0:T(8,128)(2,1)S(1)}, bf16[64,1024]{1,0:T(8,128)(2,1)S(1)}, u32[]{:S(2)}, u32[]{:S(2)}) %collective-permute-start.16) | collective-permute-done | bytes 131104 | tf_op jit(solution)/shard_map/ppermute | solution.py:23
  (143 shorter events, 13.3 us)
Async XLA Ops:
  1.8 18.5 %all-to-all-start = ((bf16[32,4,1024]{2,1,0:T(4,128)(2,1)}), bf16[32,4,1024]{2,1,0:T(4,128)(2,1)S(1)}, u32[]{:S(2)}, u32[]{:S(2)}) async-start(bf16[32,4,1024]{2,1,0:T(4,128)(2,1)} %all_to_all.6), calls=%async_computation | async-start | bytes 524288 | tf_op jit(solution)/shard_map/all_to_all | solution.py:48
  20.4 8.2 %slice-start.2 = ((s8[6815744]{0:T(1024)(128)(4,1)}), s8[4194304]{0:T(1024)(128)(4,1)S(1)}, s32[]{:S(2)}) async-start(s8[6815744]{0:T(1024)(128)(4,1)} %bitcast.208), calls=%async_computation.3 | async-start | bytes 8388608
  20.5 8.1 %slice-start.3 = ((s8[6815744]{0:T(1024)(128)(4,1)}), s8[2621440]{0:T(1024)(128)(4,1)S(1)}, s32[]{:S(2)}) async-start(s8[6815744]{0:T(1024)(128)(4,1)} %bitcast.208), calls=%async_computation.4 | async-start | bytes 5242880
  20.5 11.4 %collective-permute-start.28 = (bf16[128,1024]{1,0:T(8,128)(2,1)S(1)}, bf16[128,1024]{1,0:T(8,128)(2,1)S(1)}, u32[]{:S(2)}, u32[]{:S(2)}) collective-permute-start(bf16[128,1024]{1,0:T(8,128)(2,1)S(1)} %bitcast_dynamic-update-slice_fusion), channel_id=1, source_target_pairs={{0,96},{32,64},{64,32},{96,0},{1,97},{33,65},{65,33},{97,1},{2,98}... | collective-permute-start | bytes 786440 | tf_op jit(solution)/shard_map/ppermute | solution.py:23
  23.1 11.0 %collective-permute-start.18 = (bf16[128,1024]{1,0:T(8,128)(2,1)S(1)}, bf16[128,1024]{1,0:T(8,128)(2,1)S(1)}, u32[]{:S(2)}, u32[]{:S(2)}) collective-permute-start(bf16[128,1024]{1,0:T(8,128)(2,1)S(1)} %bitcast_dynamic-update-slice_fusion), channel_id=1, source_target_pairs={{0,32},{32,0},{64,96},{96,64},{1,33},{33,1},{65,97},{97,65},{2,34}... | collective-permute-start | bytes 786440 | tf_op jit(solution)/shard_map/ppermute | solution.py:23
  23.1 13.2 %collective-permute-start.8 = (bf16[128,1024]{1,0:T(8,128)(2,1)S(1)}, bf16[128,1024]{1,0:T(8,128)(2,1)S(1)}, u32[]{:S(2)}, u32[]{:S(2)}) collective-permute-start(bf16[128,1024]{1,0:T(8,128)(2,1)S(1)} %bitcast_dynamic-update-slice_fusion), channel_id=1, source_target_pairs={{0,64},{32,96},{64,0},{96,32},{1,65},{33,97},{65,1},{97,33},{2,66}... | collective-permute-start | bytes 786440 | tf_op jit(solution)/shard_map/ppermute | solution.py:23
  24.4 7.5 %slice-start = ((s8[6815744]{0:T(1024)(128)(4,1)}), s8[4194304]{0:T(1024)(128)(4,1)S(1)}, s32[]{:S(2)}) async-start(s8[6815744]{0:T(1024)(128)(4,1)} %bitcast.206), calls=%async_computation.1 | async-start | bytes 8388608
  28.6 3.3 %slice-start.1 = ((s8[6815744]{0:T(1024)(128)(4,1)}), s8[2621440]{0:T(1024)(128)(4,1)S(1)}, s32[]{:S(2)}) async-start(s8[6815744]{0:T(1024)(128)(4,1)} %bitcast.206), calls=%async_computation.2 | async-start | bytes 5242880
  30.1 11.4 %collective-permute-start = (f16[2,64,3328]{2,1,0:T(8,128)(2,1)S(1)}, f16[2,64,3328]{2,1,0:T(8,128)(2,1)S(1)}, u32[]{:S(2)}, u32[]{:S(2)}) collective-permute-start(f16[2,64,3328]{2,1,0:T(8,128)(2,1)S(1)} %pad_maximum_fusion), channel_id=1, source_target_pairs={{0,1},{1,0},{2,3},{3,2},{4,5},{5,4},{6,7},{7,6},{8,9},{9,8},{10,11... | collective-permute-start | bytes 2555912 | tf_op jit(solution)/shard_map/ppermute | solution.py:23
  38.8 3.9 %collective-permute-start.29 = (f16[2,64,3328]{2,1,0:T(8,128)(2,1)S(1)}, f16[2,64,3328]{2,1,0:T(8,128)(2,1)S(1)}, u32[]{:S(2)}, u32[]{:S(2)}) collective-permute-start(f16[2,64,3328]{2,1,0:T(8,128)(2,1)S(1)} %pad_maximum_fusion.3), channel_id=1, source_target_pairs={{0,1},{1,0},{2,3},{3,2},{4,5},{5,4},{6,7},{7,6},{8,9},{9,8},{10,11... | collective-permute-start | bytes 2555912 | tf_op jit(solution)/shard_map/ppermute | solution.py:23
  40.2 3.3 %collective-permute-start.19 = (f16[2,64,3328]{2,1,0:T(8,128)(2,1)S(1)}, f16[2,64,3328]{2,1,0:T(8,128)(2,1)S(1)}, u32[]{:S(2)}, u32[]{:S(2)}) collective-permute-start(f16[2,64,3328]{2,1,0:T(8,128)(2,1)S(1)} %pad_maximum_fusion.2), channel_id=1, source_target_pairs={{0,1},{1,0},{2,3},{3,2},{4,5},{5,4},{6,7},{7,6},{8,9},{9,8},{10,11... | collective-permute-start | bytes 2555912 | tf_op jit(solution)/shard_map/ppermute | solution.py:23
  40.7 5.0 %collective-permute-start.9 = (f16[2,64,3328]{2,1,0:T(8,128)(2,1)S(1)}, f16[2,64,3328]{2,1,0:T(8,128)(2,1)S(1)}, u32[]{:S(2)}, u32[]{:S(2)}) collective-permute-start(f16[2,64,3328]{2,1,0:T(8,128)(2,1)S(1)} %pad_maximum_fusion.1), channel_id=1, source_target_pairs={{0,1},{1,0},{2,3},{3,2},{4,5},{5,4},{6,7},{7,6},{8,9},{9,8},{10,11... | collective-permute-start | bytes 2555912 | tf_op jit(solution)/shard_map/ppermute | solution.py:23
  41.8 8.3 %collective-permute-start.1 = (f16[2,32,3328]{2,1,0:T(8,128)(2,1)S(1)}, f16[2,32,3328]{2,1,0:T(8,128)(2,1)S(1)}, u32[]{:S(2)}, u32[]{:S(2)}) collective-permute-start(f16[2,32,3328]{2,1,0:T(8,128)(2,1)S(1)} %pad_maximum_fusion.4), channel_id=1, source_target_pairs={{0,4},{1,13},{4,0},{5,9},{8,12},{9,5},{12,8},{13,1},{2,6},{3,15},{... | collective-permute-start | bytes 1277960 | tf_op jit(solution)/shard_map/ppermute | solution.py:23
  43.1 14.9 %collective-permute-start.30 = (f16[2,64,1664]{2,1,0:T(8,128)(2,1)S(1)}, f16[2,64,1664]{2,1,0:T(8,128)(2,1)S(1)}, u32[]{:S(2)}, u32[]{:S(2)}) collective-permute-start(f16[2,64,1664]{2,1,0:T(8,128)(2,1)S(1)} %pad_maximum_fusion.10), channel_id=1, source_target_pairs={{0,2},{2,0},{1,3},{3,1},{4,6},{6,4},{5,7},{7,5},{8,10},{10,8},{9,1... | collective-permute-start | bytes 1277960 | tf_op jit(solution)/shard_map/ppermute | solution.py:23
  43.9 15.0 %collective-permute-start.20 = (f16[2,32,3328]{2,1,0:T(8,128)(2,1)S(1)}, f16[2,32,3328]{2,1,0:T(8,128)(2,1)S(1)}, u32[]{:S(2)}, u32[]{:S(2)}) collective-permute-start(f16[2,32,3328]{2,1,0:T(8,128)(2,1)S(1)} %pad_maximum_fusion.8), channel_id=1, source_target_pairs={{0,4},{1,13},{4,0},{5,9},{8,12},{9,5},{12,8},{13,1},{2,6},{3,15},{... | collective-permute-start | bytes 1277960 | tf_op jit(solution)/shard_map/ppermute | solution.py:23
  50.3 7.4 %collective-permute-start.2 = (f16[2,16,3328]{2,1,0:T(8,128)(2,1)S(1)}, f16[2,16,3328]{2,1,0:T(8,128)(2,1)S(1)}, u32[]{:S(2)}, u32[]{:S(2)}) collective-permute-start(f16[2,16,3328]{2,1,0:T(8,128)(2,1)S(1)} %pad_maximum_fusion.12), channel_id=1, source_target_pairs={{0,12},{1,5},{4,8},{5,1},{8,4},{9,13},{12,0},{13,9},{2,14},{3,7},{... | collective-permute-start | bytes 638984 | tf_op jit(solution)/shard_map/ppermute | solution.py:23
  50.5 11.0 %collective-permute-start.10 = (f16[2,32,3328]{2,1,0:T(8,128)(2,1)S(1)}, f16[2,32,3328]{2,1,0:T(8,128)(2,1)S(1)}, u32[]{:S(2)}, u32[]{:S(2)}) collective-permute-start(f16[2,32,3328]{2,1,0:T(8,128)(2,1)S(1)} %pad_maximum_fusion.6), channel_id=1, source_target_pairs={{0,4},{1,13},{4,0},{5,9},{8,12},{9,5},{12,8},{13,1},{2,6},{3,15},{... | collective-permute-start | bytes 1277960 | tf_op jit(solution)/shard_map/ppermute | solution.py:23
  57.9 4.8 %collective-permute-start.3 = (f16[2,16,3328]{2,1,0:T(8,128)(2,1)S(1)}, f16[2,16,3328]{2,1,0:T(8,128)(2,1)S(1)}, u32[]{:S(2)}, u32[]{:S(2)}) collective-permute-start(f16[2,16,3328]{2,1,0:T(8,128)(2,1)S(1)} %pad_maximum_fusion.13), channel_id=1, source_target_pairs={{0,2},{2,0},{1,3},{3,1},{4,6},{6,4},{5,7},{7,5},{8,10},{10,8},{9,1... | collective-permute-start | bytes 638984 | tf_op jit(solution)/shard_map/ppermute | solution.py:23
  58.3 6.4 %collective-permute-start.31 = (f16[2,32,1664]{2,1,0:T(8,128)(2,1)S(1)}, f16[2,32,1664]{2,1,0:T(8,128)(2,1)S(1)}, u32[]{:S(2)}, u32[]{:S(2)}) collective-permute-start(f16[2,32,1664]{2,1,0:T(8,128)(2,1)S(1)} %pad_maximum_fusion.21), channel_id=1, source_target_pairs={{0,4},{1,13},{4,0},{5,9},{8,12},{9,5},{12,8},{13,1},{2,6},{3,15},{... | collective-permute-start | bytes 638984 | tf_op jit(solution)/shard_map/ppermute | solution.py:23
  59.2 5.8 %collective-permute-start.21 = (f16[2,16,3328]{2,1,0:T(8,128)(2,1)S(1)}, f16[2,16,3328]{2,1,0:T(8,128)(2,1)S(1)}, u32[]{:S(2)}, u32[]{:S(2)}) collective-permute-start(f16[2,16,3328]{2,1,0:T(8,128)(2,1)S(1)} %pad_maximum_fusion.18), channel_id=1, source_target_pairs={{0,12},{1,5},{4,8},{5,1},{8,4},{9,13},{12,0},{13,9},{2,14},{3,7},{... | collective-permute-start | bytes 638984 | tf_op jit(solution)/shard_map/ppermute | solution.py:23
  61.5 36.4 %slice-start.4 = ((s8[6815744]{0:T(1024)(128)(4,1)}), s8[4194304]{0:T(1024)(128)(4,1)S(1)}, s32[]{:S(2)}) async-start(s8[6815744]{0:T(1024)(128)(4,1)} %bitcast.210), calls=%async_computation.5 | async-start | bytes 8388608
  61.8 7.0 %collective-permute-start.11 = (f16[2,16,3328]{2,1,0:T(8,128)(2,1)S(1)}, f16[2,16,3328]{2,1,0:T(8,128)(2,1)S(1)}, u32[]{:S(2)}, u32[]{:S(2)}) collective-permute-start(f16[2,16,3328]{2,1,0:T(8,128)(2,1)S(1)} %pad_maximum_fusion.15), channel_id=1, source_target_pairs={{0,12},{1,5},{4,8},{5,1},{8,4},{9,13},{12,0},{13,9},{2,14},{3,7},{... | collective-permute-start | bytes 638984 | tf_op jit(solution)/shard_map/ppermute | solution.py:23
  62.8 7.2 %collective-permute-start.4 = (bf16[16,3328]{1,0:T(8,128)(2,1)S(1)}, bf16[16,3328]{1,0:T(8,128)(2,1)S(1)}, u32[]{:S(2)}, u32[]{:S(2)}) collective-permute-start(bf16[16,3328]{1,0:T(8,128)(2,1)S(1)} %fusion.59), channel_id=1, source_target_pairs={{0,12},{1,5},{4,8},{5,1},{8,4},{9,13},{12,0},{13,9},{2,14},{3,7},{... | collective-permute-start | bytes 319496 | tf_op jit(solution)/shard_map/ppermute | solution.py:23
  64.9 6.2 %collective-permute-start.32 = (f16[2,16,1664]{2,1,0:T(8,128)(2,1)S(1)}, f16[2,16,1664]{2,1,0:T(8,128)(2,1)S(1)}, u32[]{:S(2)}, u32[]{:S(2)}) collective-permute-start(f16[2,16,1664]{2,1,0:T(8,128)(2,1)S(1)} %pad_maximum_fusion.24), channel_id=1, source_target_pairs={{0,12},{1,5},{4,8},{5,1},{8,4},{9,13},{12,0},{13,9},{2,14},{3,7},{... | collective-permute-start | bytes 319496 | tf_op jit(solution)/shard_map/ppermute | solution.py:23
  65.2 32.8 %slice-start.5 = ((s8[6815744]{0:T(1024)(128)(4,1)}), s8[2621440]{0:T(1024)(128)(4,1)S(1)}, s32[]{:S(2)}) async-start(s8[6815744]{0:T(1024)(128)(4,1)} %bitcast.210), calls=%async_computation.6 | async-start | bytes 5242880
  65.2 11.4 %collective-permute-start.22 = (f16[2,16,3328]{2,1,0:T(8,128)(2,1)S(1)}, f16[2,16,3328]{2,1,0:T(8,128)(2,1)S(1)}, u32[]{:S(2)}, u32[]{:S(2)}) collective-permute-start(f16[2,16,3328]{2,1,0:T(8,128)(2,1)S(1)} %pad_maximum_fusion.19), channel_id=1, source_target_pairs={{0,2},{2,0},{1,3},{3,1},{4,6},{6,4},{5,7},{7,5},{8,10},{10,8},{9,1... | collective-permute-start | bytes 638984 | tf_op jit(solution)/shard_map/ppermute | solution.py:23
  69.0 8.3 %collective-permute-start.12 = (f16[2,16,3328]{2,1,0:T(8,128)(2,1)S(1)}, f16[2,16,3328]{2,1,0:T(8,128)(2,1)S(1)}, u32[]{:S(2)}, u32[]{:S(2)}) collective-permute-start(f16[2,16,3328]{2,1,0:T(8,128)(2,1)S(1)} %pad_maximum_fusion.16), channel_id=1, source_target_pairs={{0,2},{2,0},{1,3},{3,1},{4,6},{6,4},{5,7},{7,5},{8,10},{10,8},{9,1... | collective-permute-start | bytes 638984 | tf_op jit(solution)/shard_map/ppermute | solution.py:23
  71.2 4.3 %collective-permute-start.33 = (bf16[16,1664]{1,0:T(8,128)(2,1)S(1)}, bf16[16,1664]{1,0:T(8,128)(2,1)S(1)}, u32[]{:S(2)}, u32[]{:S(2)}) collective-permute-start(bf16[16,1664]{1,0:T(8,128)(2,1)S(1)} %fusion.77), channel_id=1, source_target_pairs={{0,2},{2,0},{1,3},{3,1},{4,6},{6,4},{5,7},{7,5},{8,10},{10,8},{9,1... | collective-permute-start | bytes 159752 | tf_op jit(solution)/shard_map/ppermute | solution.py:23
  72.1 11.0 %collective-permute-start.5 = (bf16[32,3328]{1,0:T(8,128)(2,1)S(1)}, bf16[32,3328]{1,0:T(8,128)(2,1)S(1)}, u32[]{:S(2)}, u32[]{:S(2)}) collective-permute-start(bf16[32,3328]{1,0:T(8,128)(2,1)S(1)} %pad_maximum_fusion.14), channel_id=1, source_target_pairs={{0,4},{1,13},{4,0},{5,9},{8,12},{9,5},{12,8},{13,1},{2,6},{3,15},{... | collective-permute-start | bytes 638984 | tf_op jit(solution)/shard_map/ppermute | solution.py:23
  75.5 3.9 %collective-permute-start.34 = (bf16[16,3328]{1,0:T(8,128)(2,1)S(1)}, bf16[16,3328]{1,0:T(8,128)(2,1)S(1)}, u32[]{:S(2)}, u32[]{:S(2)}) collective-permute-start(bf16[16,3328]{1,0:T(8,128)(2,1)S(1)} %pad_maximum_fusion.25), channel_id=1, source_target_pairs={{0,12},{1,5},{4,8},{5,1},{8,4},{9,13},{12,0},{13,9},{2,14},{3,7},{... | collective-permute-start | bytes 319496 | tf_op jit(solution)/shard_map/ppermute | solution.py:23
  76.7 10.9 %collective-permute-start.23 = (bf16[16,3328]{1,0:T(8,128)(2,1)S(1)}, bf16[16,3328]{1,0:T(8,128)(2,1)S(1)}, u32[]{:S(2)}, u32[]{:S(2)}) collective-permute-start(bf16[16,3328]{1,0:T(8,128)(2,1)S(1)} %fusion.55), channel_id=1, source_target_pairs={{0,12},{1,5},{4,8},{5,1},{8,4},{9,13},{12,0},{13,9},{2,14},{3,7},{... | collective-permute-start | bytes 319496 | tf_op jit(solution)/shard_map/ppermute | solution.py:23
  77.4 12.2 %collective-permute-start.13 = (bf16[16,3328]{1,0:T(8,128)(2,1)S(1)}, bf16[16,3328]{1,0:T(8,128)(2,1)S(1)}, u32[]{:S(2)}, u32[]{:S(2)}) collective-permute-start(bf16[16,3328]{1,0:T(8,128)(2,1)S(1)} %fusion.57), channel_id=1, source_target_pairs={{0,12},{1,5},{4,8},{5,1},{8,4},{9,13},{12,0},{13,9},{2,14},{3,7},{... | collective-permute-start | bytes 319496 | tf_op jit(solution)/shard_map/ppermute | solution.py:23
  79.5 11.0 %collective-permute-start.35 = (bf16[32,3328]{1,0:T(8,128)(2,1)S(1)}, bf16[32,3328]{1,0:T(8,128)(2,1)S(1)}, u32[]{:S(2)}, u32[]{:S(2)}) collective-permute-start(bf16[32,3328]{1,0:T(8,128)(2,1)S(1)} %pad_maximum_fusion.22), channel_id=1, source_target_pairs={{0,4},{1,13},{4,0},{5,9},{8,12},{9,5},{12,8},{13,1},{2,6},{3,15},{... | collective-permute-start | bytes 638984 | tf_op jit(solution)/shard_map/ppermute | solution.py:23
  83.2 14.8 %collective-permute-start.6 = (bf16[64,3328]{1,0:T(8,128)(2,1)S(1)}, bf16[64,3328]{1,0:T(8,128)(2,1)S(1)}, u32[]{:S(2)}, u32[]{:S(2)}) collective-permute-start(bf16[64,3328]{1,0:T(8,128)(2,1)S(1)} %pad_maximum_fusion.5), channel_id=1, source_target_pairs={{0,1},{1,0},{2,3},{3,2},{4,5},{5,4},{6,7},{7,6},{8,9},{9,8},{10,11... | collective-permute-start | bytes 1277960 | tf_op jit(solution)/shard_map/ppermute | solution.py:23
  87.6 6.0 %collective-permute-start.24 = (bf16[32,3328]{1,0:T(8,128)(2,1)S(1)}, bf16[32,3328]{1,0:T(8,128)(2,1)S(1)}, u32[]{:S(2)}, u32[]{:S(2)}) collective-permute-start(bf16[32,3328]{1,0:T(8,128)(2,1)S(1)} %pad_maximum_fusion.20), channel_id=1, source_target_pairs={{0,4},{1,13},{4,0},{5,9},{8,12},{9,5},{12,8},{13,1},{2,6},{3,15},{... | collective-permute-start | bytes 638984 | tf_op jit(solution)/shard_map/ppermute | solution.py:23
  89.5 6.3 %collective-permute-start.14 = (bf16[32,3328]{1,0:T(8,128)(2,1)S(1)}, bf16[32,3328]{1,0:T(8,128)(2,1)S(1)}, u32[]{:S(2)}, u32[]{:S(2)}) collective-permute-start(bf16[32,3328]{1,0:T(8,128)(2,1)S(1)} %pad_maximum_fusion.17), channel_id=1, source_target_pairs={{0,4},{1,13},{4,0},{5,9},{8,12},{9,5},{12,8},{13,1},{2,6},{3,15},{... | collective-permute-start | bytes 638984 | tf_op jit(solution)/shard_map/ppermute | solution.py:23
  90.5 10.4 %collective-permute-start.36 = (bf16[64,3328]{1,0:T(8,128)(2,1)S(1)}, bf16[64,3328]{1,0:T(8,128)(2,1)S(1)}, u32[]{:S(2)}, u32[]{:S(2)}) collective-permute-start(bf16[64,3328]{1,0:T(8,128)(2,1)S(1)} %pad_maximum_fusion.11), channel_id=1, source_target_pairs={{0,1},{1,0},{2,3},{3,2},{4,5},{5,4},{6,7},{7,6},{8,9},{9,8},{10,11... | collective-permute-start | bytes 1277960 | tf_op jit(solution)/shard_map/ppermute | solution.py:23
  93.6 12.3 %collective-permute-start.25 = (bf16[64,3328]{1,0:T(8,128)(2,1)S(1)}, bf16[64,3328]{1,0:T(8,128)(2,1)S(1)}, u32[]{:S(2)}, u32[]{:S(2)}) collective-permute-start(bf16[64,3328]{1,0:T(8,128)(2,1)S(1)} %pad_maximum_fusion.9), channel_id=1, source_target_pairs={{0,1},{1,0},{2,3},{3,2},{4,5},{5,4},{6,7},{7,6},{8,9},{9,8},{10,11... | collective-permute-start | bytes 1277960 | tf_op jit(solution)/shard_map/ppermute | solution.py:23
  95.9 11.2 %collective-permute-start.15 = (bf16[64,3328]{1,0:T(8,128)(2,1)S(1)}, bf16[64,3328]{1,0:T(8,128)(2,1)S(1)}, u32[]{:S(2)}, u32[]{:S(2)}) collective-permute-start(bf16[64,3328]{1,0:T(8,128)(2,1)S(1)} %pad_maximum_fusion.7), channel_id=1, source_target_pairs={{0,1},{1,0},{2,3},{3,2},{4,5},{5,4},{6,7},{7,6},{8,9},{9,8},{10,11... | collective-permute-start | bytes 1277960 | tf_op jit(solution)/shard_map/ppermute | solution.py:23
  99.1 11.8 %collective-permute-start.7 = (bf16[64,1024]{1,0:T(8,128)(2,1)S(1)}, bf16[64,1024]{1,0:T(8,128)(2,1)S(1)}, u32[]{:S(2)}, u32[]{:S(2)}) collective-permute-start(bf16[64,1024]{1,0:T(8,128)(2,1)S(1)} %select_convert_fusion.6), channel_id=1, source_target_pairs={{0,16},{16,0},{32,48},{48,32},{64,80},{80,64},{96,112},{112,96},{1... | collective-permute-start | bytes 393224 | tf_op jit(solution)/shard_map/ppermute | solution.py:23
  102.0 12.4 %collective-permute-start.38 = (bf16[64,1024]{1,0:T(8,128)(2,1)S(1)}, bf16[64,1024]{1,0:T(8,128)(2,1)S(1)}, u32[]{:S(2)}, u32[]{:S(2)}) collective-permute-start(bf16[64,1024]{1,0:T(8,128)(2,1)S(1)} %get-tuple-element.116), channel_id=1, source_target_pairs={{0,112},{16,96},{32,80},{48,64},{64,48},{80,32},{96,16},{112,0},{1... | collective-permute-start | bytes 393224 | tf_op jit(solution)/shard_map/ppermute | solution.py:23
  105.7 9.4 %collective-permute-start.37 = (bf16[64,1024]{1,0:T(8,128)(2,1)S(1)}, bf16[64,1024]{1,0:T(8,128)(2,1)S(1)}, u32[]{:S(2)}, u32[]{:S(2)}) collective-permute-start(bf16[64,1024]{1,0:T(8,128)(2,1)S(1)} %get-tuple-element.115), channel_id=1, source_target_pairs={{0,96},{32,64},{64,32},{96,0},{1,97},{33,65},{65,33},{97,1},{2,98}... | collective-permute-start | bytes 393224 | tf_op jit(solution)/shard_map/ppermute | solution.py:23
  107.0 8.1 %collective-permute-start.27 = (bf16[64,1024]{1,0:T(8,128)(2,1)S(1)}, bf16[64,1024]{1,0:T(8,128)(2,1)S(1)}, u32[]{:S(2)}, u32[]{:S(2)}) collective-permute-start(bf16[64,1024]{1,0:T(8,128)(2,1)S(1)} %get-tuple-element.102), channel_id=1, source_target_pairs={{0,48},{16,32},{32,16},{48,0},{64,112},{80,96},{96,80},{112,64},{1... | collective-permute-start | bytes 393224 | tf_op jit(solution)/shard_map/ppermute | solution.py:23
  107.1 8.1 %collective-permute-start.26 = (bf16[64,1024]{1,0:T(8,128)(2,1)S(1)}, bf16[64,1024]{1,0:T(8,128)(2,1)S(1)}, u32[]{:S(2)}, u32[]{:S(2)}) collective-permute-start(bf16[64,1024]{1,0:T(8,128)(2,1)S(1)} %get-tuple-element.101), channel_id=1, source_target_pairs={{0,32},{32,0},{64,96},{96,64},{1,33},{33,1},{65,97},{97,65},{2,34}... | collective-permute-start | bytes 393224 | tf_op jit(solution)/shard_map/ppermute | solution.py:23
  110.9 10.6 %collective-permute-start.17 = (bf16[64,1024]{1,0:T(8,128)(2,1)S(1)}, bf16[64,1024]{1,0:T(8,128)(2,1)S(1)}, u32[]{:S(2)}, u32[]{:S(2)}) collective-permute-start(bf16[64,1024]{1,0:T(8,128)(2,1)S(1)} %get-tuple-element.88), channel_id=1, source_target_pairs={{0,80},{16,64},{32,112},{48,96},{64,16},{80,0},{96,48},{112,32},{1... | collective-permute-start | bytes 393224 | tf_op jit(solution)/shard_map/ppermute | solution.py:23
  114.4 8.7 %collective-permute-start.16 = (bf16[64,1024]{1,0:T(8,128)(2,1)S(1)}, bf16[64,1024]{1,0:T(8,128)(2,1)S(1)}, u32[]{:S(2)}, u32[]{:S(2)}) collective-permute-start(bf16[64,1024]{1,0:T(8,128)(2,1)S(1)} %get-tuple-element.87), channel_id=1, source_target_pairs={{0,64},{32,96},{64,0},{96,32},{1,65},{33,97},{65,1},{97,33},{2,66}... | collective-permute-start | bytes 393224 | tf_op jit(solution)/shard_map/ppermute | solution.py:23

commit v8 on v6

--- a/solution.py
+++ b/solution.py
@@ -43,28 +43,27 @@
     }
 
     features = tokens.shape[1] // 16
-    blocks = tokens.reshape(4, 16, features).transpose(1, 0, 2).reshape(1, 64, features)
-    blocks = jnp.broadcast_to(blocks, (2, 64, features)).reshape(128, features)
-    mine = lax.all_to_all(blocks, AXES[1:], split_axis=0, concat_axis=0, tiled=True)
-    mine = mine.reshape(2, 4, 16, features)
+    blocks = tokens.reshape(4, 16, features).transpose(1, 0, 2)
+    mine = lax.all_to_all(blocks, AXES[2:], split_axis=0, concat_axis=0, tiled=True)
+    mine = mine.reshape(4, 16, features)
 
     def places(half):
         first = jnp.where(half == 0, 1, 3)
         return (y, y ^ (4 - first), y ^ first, y ^ 2)
 
-    halves = (1 - core, core)
-    own = jnp.concatenate(
-        [
-            lax.dynamic_slice(mine, (half, p, 0, 0), (1, 1, 16, features)).reshape(16, features)
-            for half in halves
-            for p in places(half)
-        ]
+    near = jnp.concatenate(
+        [lax.dynamic_index_in_dim(mine, p, 0, keepdims=False) for p in places(z_hi)]
     )
-    rows = {0: own}
+    pairs = {0: (near, swap_row[0](near))}
+    for e in (2, 1, 3):
+        pairs[e] = (swap_x[e](near), swap_row[e](near))
+    stays = z_hi == core
+    rows = {
+        e: jnp.concatenate((jnp.where(stays, b, a), jnp.where(stays, a, b)))
+        for e, (a, b) in pairs.items()
+    }
     state = [{} for _ in range(4)]
-    arrived = []
     half_hidden = gate_weight.shape[1] // 2
-    stays = z_hi == core
 
     def tie(*values):
         values = lax.optimization_barrier(values)
@@ -79,9 +78,7 @@
 
     def step(e, s):
         st = state[e]
-        if s == -1:
-            rows[e] = swap_x[e](tie(own))
-        elif s == 0:
+        if s == 0:
             both = tie(rows[e])
             terms = [product(both, w) for w in (gate_weight, up_weight)]
             send, *st["total"] = tie(jnp.stack([lifted(v[:64]) for v in terms]), *terms)
@@ -116,21 +113,21 @@
             st["flight"] = (swap_first if s == 6 else swap_core)(st["hidden"])
         elif s == 8:
             both = jnp.concatenate((tie(st["flight"]), st["hidden"]))
-            mixed = product(both, down_weight)
-            same, cross = parted(mixed)
-            if e == 0:
-                same, cross = tie(same, cross.astype(BF16))
-                arrived.append(same)
-            else:
-                same, cross = tie(same.astype(BF16), cross.astype(BF16))
-                arrived.append(swap_x[e](same).astype(F32))
-            arrived.append(swap_row[e](cross).astype(F32))
+            st["mixed"] = product(both, down_weight)
 
-    for s in (-1, 0, 2, 3, 4, 5, 6, 7, 8):
+    for s in (0, 2, 3, 4, 5, 6, 7, 8):
         for e in (0, 2, 1, 3):
-            if e or s >= 0:
-                step(e, s)
+            step(e, s)
 
+    mixed = tie(*[st["mixed"] for st in state])
+    arrived = []
+    for e in (2, 3, 1, 0):
+        same, cross = parted(mixed[e])
+        if e == 0:
+            arrived.append(same)
+        else:
+            arrived.append(swap_x[e](same.astype(BF16)).astype(F32))
+        arrived.append(swap_row[e](cross.astype(BF16)).astype(F32))
     out = sum(arrived).astype(BF16).reshape(4, 16, -1)
     first = jnp.where(z_hi == 0, 1, 3)
     blocks = []

time: 124 us -> 140 us (1.13)
  starting transfers between devices: 53.4 us -> 70.6 us
    ppermute x39 -> x43, starting transfers between devices: 43.8 us -> 63.2 us  [permute(): return lambda v: lax.ppermute(v, axes, pairs)]
    all_to_all x1, waiting for transfers between devices: 8.79 us -> 6.17 us  [per_device(): lax.all_to_all(blocks, AXES[2:], split_axis=0, concat_axis=0, tiled=True)]
    ppermute x39 -> x43, waiting for transfers between devices: 36.4 us -> 38.9 us  [permute(): return lambda v: lax.ppermute(v, axes, pairs)]
    all_to_all x1, starting transfers between devices: 9.6 us -> 7.34 us  [per_device(): lax.all_to_all(blocks, AXES[2:], split_axis=0, concat_axis=0, tiled=True)]
    unnamed x19 -> x10, local copies, waits for them, and re-layouts: 0.13 us -> 1.76 us
  transfers between devices with their start and end apart: 40 -> 44, of which waited for: 16 -> 14; matrix products, arithmetic and copies ran while one was open for 17% -> 12% of each run, Pallas kernels for 0% -> 0%
where the time goes in v8:
time: 140 us
  starting transfers between devices  70.6 us (50%)
  waiting for transfers between devices  45.1 us (32%)
  matrix products  15.8 us (11%)
  other arithmetic  5.96 us (4%)
  local copies, waits for them, and re-layouts  1.83 us (1%)
    ppermute x43, starting transfers between devices, permute(): return lambda v: lax.ppermute(v, axes, pairs)  63.2 us
    ppermute x43, waiting for transfers between devices, permute(): return lambda v: lax.ppermute(v, axes, pairs)  38.9 us
    dot_general x12, matrix products, product(): return jnp.dot(rows, weight, preferred_element_type=F32)  15.8 us
    all_to_all x1, starting transfers between devices, per_device(): lax.all_to_all(blocks, AXES[2:], split_axis=0, concat_axis=0, tiled=True)  7.34 us
    all_to_all x1, waiting for transfers between devices, per_device(): lax.all_to_all(blocks, AXES[2:], split_axis=0, concat_axis=0, tiled=True)  6.17 us
  transfers between devices with their start and end apart: 44, of which 14 were waited for; matrix products, arithmetic and copies ran while one was open for 12% of the time, Pallas kernels for 0%

profile of v8, /device:TPU:1, one launch (start us, length us, event | category | flops | bytes accessed | tf_op | source)
XLA Modules:
  0.0 140.1 jit_solution(11958395062856439650)
XLA Ops:
  0.0 7.3 %all-to-all-start = ((bf16[16,4,1024]{2,1,0:T(4,128)(2,1)}), bf16[16,4,1024]{2,1,0:T(4,128)(2,1)S(1)}, u32[]{:S(2)}, u32[]{:S(2)}) async-start(bf16[16,4,1024]{2,1,0:T(4,128)(2,1)} %bitcast.203), calls=%async_computation | async-start | bytes 262144 | tf_op jit(solution)/shard_map/all_to_all | solution.py:47
  7.3 6.2 %all-to-all-done = bf16[16,4,1024]{2,1,0:T(4,128)(2,1)S(1)} async-done(((bf16[16,4,1024]{2,1,0:T(4,128)(2,1)}), bf16[16,4,1024]{2,1,0:T(4,128)(2,1)S(1)}, u32[]{:S(2)}, u32[]{:S(2)}) %all-to-all-start) | async-done | bytes 131104 | tf_op jit(solution)/shard_map/all_to_all | solution.py:47
  13.6 5.6 %collective-permute-start.27 = (bf16[64,1024]{1,0:T(8,128)(2,1)S(1)}, bf16[64,1024]{1,0:T(8,128)(2,1)S(1)}, u32[]{:S(2)}, u32[]{:S(2)}) collective-permute-start(bf16[64,1024]{1,0:T(8,128)(2,1)S(1)} %pad_maximum_fusion.27), channel_id=1, source_target_pairs={{0,112},{16,96},{32,80},{48,64},{64,48},{80,32},{96,16},{112,0},{1... | collective-permute-start | bytes 393224 | tf_op jit(solution)/shard_map/ppermute | solution.py:23
  19.4 0.9 collective-permute-start.18
  20.3 1.9 %collective-permute-start.19 = (bf16[64,1024]{1,0:T(8,128)(2,1)S(1)}, bf16[64,1024]{1,0:T(8,128)(2,1)S(1)}, u32[]{:S(2)}, u32[]{:S(2)}) collective-permute-start(bf16[64,1024]{1,0:T(8,128)(2,1)S(1)} %pad_maximum_fusion.27), channel_id=1, source_target_pairs={{0,64},{32,96},{64,0},{96,32},{1,65},{33,97},{65,1},{97,33},{2,66}... | collective-permute-start | bytes 393224 | tf_op jit(solution)/shard_map/ppermute | solution.py:23
  22.7 3.5 %collective-permute-start.9 = (bf16[64,1024]{1,0:T(8,128)(2,1)S(1)}, bf16[64,1024]{1,0:T(8,128)(2,1)S(1)}, u32[]{:S(2)}, u32[]{:S(2)}) collective-permute-start(bf16[64,1024]{1,0:T(8,128)(2,1)S(1)} %pad_maximum_fusion.27), channel_id=1, source_target_pairs={{0,48},{16,32},{32,16},{48,0},{64,112},{80,96},{96,80},{112,64},{1... | collective-permute-start | bytes 393224 | tf_op jit(solution)/shard_map/ppermute | solution.py:23
  26.2 5.4 %collective-permute-done.28 = bf16[64,1024]{1,0:T(8,128)(2,1)S(1)} collective-permute-done((bf16[64,1024]{1,0:T(8,128)(2,1)S(1)}, bf16[64,1024]{1,0:T(8,128)(2,1)S(1)}, u32[]{:S(2)}, u32[]{:S(2)}) %collective-permute-start.28) | collective-permute-done | bytes 131104 | tf_op jit(solution)/shard_map/ppermute | solution.py:23
  31.7 4.1 %fusion.90 = f32[128,3328]{1,0:T(8,128)S(1)} fusion(bf16[128,1024]{1,0:T(8,128)(2,1)S(1)} %pad_maximum_fusion.15, bf16[1024,3328]{1,0:T(8,128)(2,1)} %param.5), kind=kOutput, calls=%fused_computation.213 | convolution fusion | flops 872415232 | bytes 8781824 | tf_op jit(solution)/shard_map/dot_general | solution.py:73
  36.5 1.1 fusion.91
  37.7 1.0 slice-done.1
  38.7 1.1 fusion.88
  39.8 1.1 fusion.89
  40.9 1.1 fusion.86
  42.0 1.1 fusion.87
  43.2 1.1 fusion.84
  44.2 1.1 fusion.85
  50.1 2.0 %collective-permute-start.21 = (f16[2,32,3328]{2,1,0:T(8,128)(2,1)S(1)}, f16[2,32,3328]{2,1,0:T(8,128)(2,1)S(1)}, u32[]{:S(2)}, u32[]{:S(2)}) collective-permute-start(f16[2,32,3328]{2,1,0:T(8,128)(2,1)S(1)} %pad_maximum_fusion.8), channel_id=1, source_target_pairs={{0,4},{1,13},{4,0},{5,9},{8,12},{9,5},{12,8},{13,1},{2,6},{3,15},{... | collective-permute-start | bytes 1277960 | tf_op jit(solution)/shard_map/ppermute | solution.py:23
  53.9 3.2 %collective-permute-done.30 = f16[2,32,3328]{2,1,0:T(8,128)(2,1)S(1)} collective-permute-done((f16[2,32,3328]{2,1,0:T(8,128)(2,1)S(1)}, f16[2,32,3328]{2,1,0:T(8,128)(2,1)S(1)}, u32[]{:S(2)}, u32[]{:S(2)}) %collective-permute-start.30) | collective-permute-done | bytes 426016 | tf_op jit(solution)/shard_map/ppermute | solution.py:23
  57.4 4.2 %collective-permute-done.21 = f16[2,32,3328]{2,1,0:T(8,128)(2,1)S(1)} collective-permute-done((f16[2,32,3328]{2,1,0:T(8,128)(2,1)S(1)}, f16[2,32,3328]{2,1,0:T(8,128)(2,1)S(1)}, u32[]{:S(2)}, u32[]{:S(2)}) %collective-permute-start.21) | collective-permute-done | bytes 426016 | tf_op jit(solution)/shard_map/ppermute | solution.py:23
  62.0 7.3 %collective-permute-done.12 = f16[2,32,3328]{2,1,0:T(8,128)(2,1)S(1)} collective-permute-done((f16[2,32,3328]{2,1,0:T(8,128)(2,1)S(1)}, f16[2,32,3328]{2,1,0:T(8,128)(2,1)S(1)}, u32[]{:S(2)}, u32[]{:S(2)}) %collective-permute-start.12) | collective-permute-done | bytes 426016 | tf_op jit(solution)/shard_map/ppermute | solution.py:23
  71.1 1.5 %collective-permute-start.23 = (f16[2,16,3328]{2,1,0:T(8,128)(2,1)S(1)}, f16[2,16,3328]{2,1,0:T(8,128)(2,1)S(1)}, u32[]{:S(2)}, u32[]{:S(2)}) collective-permute-start(f16[2,16,3328]{2,1,0:T(8,128)(2,1)S(1)} %pad_maximum_fusion.22), channel_id=1, source_target_pairs={{0,2},{2,0},{1,3},{3,1},{4,6},{6,4},{5,7},{7,5},{8,10},{10,8},{9,1... | collective-permute-start | bytes 638984 | tf_op jit(solution)/shard_map/ppermute | solution.py:23
  72.7 3.7 %collective-permute-done.3 = f16[2,32,1664]{2,1,0:T(8,128)(2,1)S(1)} collective-permute-done((f16[2,32,1664]{2,1,0:T(8,128)(2,1)S(1)}, f16[2,32,1664]{2,1,0:T(8,128)(2,1)S(1)}, u32[]{:S(2)}, u32[]{:S(2)}) %collective-permute-start.3) | collective-permute-done | bytes 213024 | tf_op jit(solution)/shard_map/ppermute | solution.py:23
  76.5 1.7 %collective-permute-start.4 = (f16[2,16,1664]{2,1,0:T(8,128)(2,1)S(1)}, f16[2,16,1664]{2,1,0:T(8,128)(2,1)S(1)}, u32[]{:S(2)}, u32[]{:S(2)}) collective-permute-start(f16[2,16,1664]{2,1,0:T(8,128)(2,1)S(1)} %pad_maximum_fusion.29), channel_id=1, source_target_pairs={{0,12},{1,5},{4,8},{5,1},{8,4},{9,13},{12,0},{13,9},{2,14},{3,7},{... | collective-permute-start | bytes 319496 | tf_op jit(solution)/shard_map/ppermute | solution.py:23
  78.2 2.3 %collective-permute-done.4 = f16[2,16,1664]{2,1,0:T(8,128)(2,1)S(1)} collective-permute-done((f16[2,16,1664]{2,1,0:T(8,128)(2,1)S(1)}, f16[2,16,1664]{2,1,0:T(8,128)(2,1)S(1)}, u32[]{:S(2)}, u32[]{:S(2)}) %collective-permute-start.4) | collective-permute-done | bytes 106528 | tf_op jit(solution)/shard_map/ppermute | solution.py:23
  80.8 1.5 %collective-permute-start.14 = (f16[2,16,3328]{2,1,0:T(8,128)(2,1)S(1)}, f16[2,16,3328]{2,1,0:T(8,128)(2,1)S(1)}, u32[]{:S(2)}, u32[]{:S(2)}) collective-permute-start(f16[2,16,3328]{2,1,0:T(8,128)(2,1)S(1)} %pad_maximum_fusion.19), channel_id=1, source_target_pairs={{0,2},{2,0},{1,3},{3,1},{4,6},{6,4},{5,7},{7,5},{8,10},{10,8},{9,1... | collective-permute-start | bytes 638984 | tf_op jit(solution)/shard_map/ppermute | solution.py:23
  82.3 1.7 %collective-permute-done.5 = bf16[16,1664]{1,0:T(8,128)(2,1)S(1)} collective-permute-done((bf16[16,1664]{1,0:T(8,128)(2,1)S(1)}, bf16[16,1664]{1,0:T(8,128)(2,1)S(1)}, u32[]{:S(2)}, u32[]{:S(2)}) %collective-permute-start.5) | collective-permute-done | bytes 53280 | tf_op jit(solution)/shard_map/ppermute | solution.py:23
  84.0 1.2 collective-permute-start.6
  85.8 1.2 collective-permute-start.24
  87.2 1.5 %collective-permute-start.15 = (bf16[16,3328]{1,0:T(8,128)(2,1)S(1)}, bf16[16,3328]{1,0:T(8,128)(2,1)S(1)}, u32[]{:S(2)}, u32[]{:S(2)}) collective-permute-start(bf16[16,3328]{1,0:T(8,128)(2,1)S(1)} %fusion.59), channel_id=1, source_target_pairs={{0,12},{1,5},{4,8},{5,1},{8,4},{9,13},{12,0},{13,9},{2,14},{3,7},{... | collective-permute-start | bytes 319496 | tf_op jit(solution)/shard_map/ppermute | solution.py:23
  89.3 2.3 %collective-permute-start.34 = (bf16[32,3328]{1,0:T(8,128)(2,1)S(1)}, bf16[32,3328]{1,0:T(8,128)(2,1)S(1)}, u32[]{:S(2)}, u32[]{:S(2)}) collective-permute-start(bf16[32,3328]{1,0:T(8,128)(2,1)S(1)} %pad_maximum_fusion.26), channel_id=1, source_target_pairs={{0,4},{1,13},{4,0},{5,9},{8,12},{9,5},{12,8},{13,1},{2,6},{3,15},{... | collective-permute-start | bytes 638984 | tf_op jit(solution)/shard_map/ppermute | solution.py:23
  92.2 2.3 %collective-permute-start.16 = (bf16[32,3328]{1,0:T(8,128)(2,1)S(1)}, bf16[32,3328]{1,0:T(8,128)(2,1)S(1)}, u32[]{:S(2)}, u32[]{:S(2)}) collective-permute-start(bf16[32,3328]{1,0:T(8,128)(2,1)S(1)} %pad_maximum_fusion.20), channel_id=1, source_target_pairs={{0,4},{1,13},{4,0},{5,9},{8,12},{9,5},{12,8},{13,1},{2,6},{3,15},{... | collective-permute-start | bytes 638984 | tf_op jit(solution)/shard_map/ppermute | solution.py:23
  94.4 1.5 %collective-permute-done.7 = bf16[32,3328]{1,0:T(8,128)(2,1)S(1)} collective-permute-done((bf16[32,3328]{1,0:T(8,128)(2,1)S(1)}, bf16[32,3328]{1,0:T(8,128)(2,1)S(1)}, u32[]{:S(2)}, u32[]{:S(2)}) %collective-permute-start.7) | collective-permute-done | bytes 213024 | tf_op jit(solution)/shard_map/ppermute | solution.py:23
  96.0 7.8 %collective-permute-start.8 = (bf16[64,3328]{1,0:T(8,128)(2,1)S(1)}, bf16[64,3328]{1,0:T(8,128)(2,1)S(1)}, u32[]{:S(2)}, u32[]{:S(2)}) collective-permute-start(bf16[64,3328]{1,0:T(8,128)(2,1)S(1)} %pad_maximum_fusion.5), channel_id=1, source_target_pairs={{0,1},{1,0},{2,3},{3,2},{4,5},{5,4},{6,7},{7,6},{8,9},{9,8},{10,11... | collective-permute-start | bytes 1277960 | tf_op jit(solution)/shard_map/ppermute | solution.py:23
  103.8 1.2 collective-permute-start.35
  105.1 2.2 %collective-permute-start.26 = (bf16[64,3328]{1,0:T(8,128)(2,1)S(1)}, bf16[64,3328]{1,0:T(8,128)(2,1)S(1)}, u32[]{:S(2)}, u32[]{:S(2)}) collective-permute-start(bf16[64,3328]{1,0:T(8,128)(2,1)S(1)} %pad_maximum_fusion.9), channel_id=1, source_target_pairs={{0,1},{1,0},{2,3},{3,2},{4,5},{5,4},{6,7},{7,6},{8,9},{9,8},{10,11... | collective-permute-start | bytes 1277960 | tf_op jit(solution)/shard_map/ppermute | solution.py:23
  107.3 2.5 %collective-permute-start.17 = (bf16[64,3328]{1,0:T(8,128)(2,1)S(1)}, bf16[64,3328]{1,0:T(8,128)(2,1)S(1)}, u32[]{:S(2)}, u32[]{:S(2)}) collective-permute-start(bf16[64,3328]{1,0:T(8,128)(2,1)S(1)} %pad_maximum_fusion.7), channel_id=1, source_target_pairs={{0,1},{1,0},{2,3},{3,2},{4,5},{5,4},{6,7},{7,6},{8,9},{9,8},{10,11... | collective-permute-start | bytes 1277960 | tf_op jit(solution)/shard_map/ppermute | solution.py:23
  109.8 1.1 fusion.8
  110.9 1.1 fusion.20
  112.0 1.1 fusion.16
  113.0 1.1 fusion.12
  114.1 4.2 %collective-permute-start.36 = (bf16[64,1024]{1,0:T(8,128)(2,1)S(1)}, bf16[64,1024]{1,0:T(8,128)(2,1)S(1)}, u32[]{:S(2)}, u32[]{:S(2)}) collective-permute-start(bf16[64,1024]{1,0:T(8,128)(2,1)S(1)} %get-tuple-element.141), channel_id=1, source_target_pairs={{0,64},{32,96},{64,0},{96,32},{1,65},{33,97},{65,1},{97,33},{2,66}... | collective-permute-start | bytes 393224 | tf_op jit(solution)/shard_map/ppermute | solution.py:23
  118.4 3.1 %collective-permute-start.37 = (bf16[64,1024]{1,0:T(8,128)(2,1)S(1)}, bf16[64,1024]{1,0:T(8,128)(2,1)S(1)}, u32[]{:S(2)}, u32[]{:S(2)}) collective-permute-start(bf16[64,1024]{1,0:T(8,128)(2,1)S(1)} %get-tuple-element.142), channel_id=1, source_target_pairs={{0,80},{16,64},{32,112},{48,96},{64,16},{80,0},{96,48},{112,32},{1... | collective-permute-start | bytes 393224 | tf_op jit(solution)/shard_map/ppermute | solution.py:23
  121.4 1.3 collective-permute-start.38
  122.7 1.4 collective-permute-start.39
  124.3 4.0 %collective-permute-start.41 = (bf16[64,1024]{1,0:T(8,128)(2,1)S(1)}, bf16[64,1024]{1,0:T(8,128)(2,1)S(1)}, u32[]{:S(2)}, u32[]{:S(2)}) collective-permute-start(bf16[64,1024]{1,0:T(8,128)(2,1)S(1)} %get-tuple-element.146), channel_id=1, source_target_pairs={{0,48},{16,32},{32,16},{48,0},{64,112},{80,96},{96,80},{112,64},{1... | collective-permute-start | bytes 393224 | tf_op jit(solution)/shard_map/ppermute | solution.py:23
  128.3 2.0 %collective-permute-start.42 = (bf16[64,1024]{1,0:T(8,128)(2,1)S(1)}, bf16[64,1024]{1,0:T(8,128)(2,1)S(1)}, u32[]{:S(2)}, u32[]{:S(2)}) collective-permute-start(bf16[64,1024]{1,0:T(8,128)(2,1)S(1)} %select_convert_fusion), channel_id=1, source_target_pairs={{0,16},{16,0},{32,48},{48,32},{64,80},{80,64},{96,112},{112,96},{1... | collective-permute-start | bytes 393224 | tf_op jit(solution)/shard_map/ppermute | solution.py:23
  130.9 4.3 %collective-permute-done.39 = bf16[64,1024]{1,0:T(8,128)(2,1)S(1)} collective-permute-done((bf16[64,1024]{1,0:T(8,128)(2,1)S(1)}, bf16[64,1024]{1,0:T(8,128)(2,1)S(1)}, u32[]{:S(2)}, u32[]{:S(2)}) %collective-permute-start.39) | collective-permute-done | bytes 131104 | tf_op jit(solution)/shard_map/ppermute | solution.py:23
  135.1 4.1 %collective-permute-done.42 = bf16[64,1024]{1,0:T(8,128)(2,1)S(1)} collective-permute-done((bf16[64,1024]{1,0:T(8,128)(2,1)S(1)}, bf16[64,1024]{1,0:T(8,128)(2,1)S(1)}, u32[]{:S(2)}, u32[]{:S(2)}) %collective-permute-start.42) | collective-permute-done | bytes 131104 | tf_op jit(solution)/shard_map/ppermute | solution.py:23
  (146 shorter events, 14.5 us)
Async XLA Ops:
  0.0 13.5 %all-to-all-start = ((bf16[16,4,1024]{2,1,0:T(4,128)(2,1)}), bf16[16,4,1024]{2,1,0:T(4,128)(2,1)S(1)}, u32[]{:S(2)}, u32[]{:S(2)}) async-start(bf16[16,4,1024]{2,1,0:T(4,128)(2,1)} %bitcast.203), calls=%async_computation | async-start | bytes 262144 | tf_op jit(solution)/shard_map/all_to_all | solution.py:47
  13.6 9.1 %collective-permute-start.27 = (bf16[64,1024]{1,0:T(8,128)(2,1)S(1)}, bf16[64,1024]{1,0:T(8,128)(2,1)S(1)}, u32[]{:S(2)}, u32[]{:S(2)}) collective-permute-start(bf16[64,1024]{1,0:T(8,128)(2,1)S(1)} %pad_maximum_fusion.27), channel_id=1, source_target_pairs={{0,112},{16,96},{32,80},{48,64},{64,48},{80,32},{96,16},{112,0},{1... | collective-permute-start | bytes 393224 | tf_op jit(solution)/shard_map/ppermute | solution.py:23
  19.2 12.4 %collective-permute-start.28 = (bf16[64,1024]{1,0:T(8,128)(2,1)S(1)}, bf16[64,1024]{1,0:T(8,128)(2,1)S(1)}, u32[]{:S(2)}, u32[]{:S(2)}) collective-permute-start(bf16[64,1024]{1,0:T(8,128)(2,1)S(1)} %pad_maximum_fusion.27), channel_id=1, source_target_pairs={{0,96},{32,64},{64,32},{96,0},{1,97},{33,65},{65,33},{97,1},{2,98}... | collective-permute-start | bytes 393224 | tf_op jit(solution)/shard_map/ppermute | solution.py:23
  19.4 18.2 %collective-permute-start.18 = (bf16[64,1024]{1,0:T(8,128)(2,1)S(1)}, bf16[64,1024]{1,0:T(8,128)(2,1)S(1)}, u32[]{:S(2)}, u32[]{:S(2)}) collective-permute-start(bf16[64,1024]{1,0:T(8,128)(2,1)S(1)} %pad_maximum_fusion.27), channel_id=1, source_target_pairs={{0,80},{16,64},{32,112},{48,96},{64,16},{80,0},{96,48},{112,32},{1... | collective-permute-start | bytes 393224 | tf_op jit(solution)/shard_map/ppermute | solution.py:23
  20.3 17.3 %collective-permute-start.19 = (bf16[64,1024]{1,0:T(8,128)(2,1)S(1)}, bf16[64,1024]{1,0:T(8,128)(2,1)S(1)}, u32[]{:S(2)}, u32[]{:S(2)}) collective-permute-start(bf16[64,1024]{1,0:T(8,128)(2,1)S(1)} %pad_maximum_fusion.27), channel_id=1, source_target_pairs={{0,64},{32,96},{64,0},{96,32},{1,65},{33,97},{65,1},{97,33},{2,66}... | collective-permute-start | bytes 393224 | tf_op jit(solution)/shard_map/ppermute | solution.py:23
  22.2 18.6 %collective-permute-start.10 = (bf16[64,1024]{1,0:T(8,128)(2,1)S(1)}, bf16[64,1024]{1,0:T(8,128)(2,1)S(1)}, u32[]{:S(2)}, u32[]{:S(2)}) collective-permute-start(bf16[64,1024]{1,0:T(8,128)(2,1)S(1)} %pad_maximum_fusion.27), channel_id=1, source_target_pairs={{0,32},{32,0},{64,96},{96,64},{1,33},{33,1},{65,97},{97,65},{2,34}... | collective-permute-start | bytes 393224 | tf_op jit(solution)/shard_map/ppermute | solution.py:23
  22.7 18.1 %collective-permute-start.9 = (bf16[64,1024]{1,0:T(8,128)(2,1)S(1)}, bf16[64,1024]{1,0:T(8,128)(2,1)S(1)}, u32[]{:S(2)}, u32[]{:S(2)}) collective-permute-start(bf16[64,1024]{1,0:T(8,128)(2,1)S(1)} %pad_maximum_fusion.27), channel_id=1, source_target_pairs={{0,48},{16,32},{32,16},{48,0},{64,112},{80,96},{96,80},{112,64},{1... | collective-permute-start | bytes 393224 | tf_op jit(solution)/shard_map/ppermute | solution.py:23
  31.6 11.5 %collective-permute-start = (bf16[64,1024]{1,0:T(8,128)(2,1)S(1)}, bf16[64,1024]{1,0:T(8,128)(2,1)S(1)}, u32[]{:S(2)}, u32[]{:S(2)}) collective-permute-start(bf16[64,1024]{1,0:T(8,128)(2,1)S(1)} %pad_maximum_fusion.27), channel_id=1, source_target_pairs={{0,16},{16,0},{32,48},{48,32},{64,80},{80,64},{96,112},{112,96},{1... | collective-permute-start | bytes 393224 | tf_op jit(solution)/shard_map/ppermute | solution.py:23
  31.6 4.9 %copy-start = (bf16[1024,3328]{1,0:T(8,128)(2,1)S(1)}, bf16[1024,3328]{1,0:T(8,128)(2,1)}, u32[]{:S(2)}) copy-start(bf16[1024,3328]{1,0:T(8,128)(2,1)} %param.6) | copy-start | bytes 20447236
  31.7 6.1 %slice-start = ((s8[6815744]{0:T(1024)(128)(4,1)}), s8[4194304]{0:T(1024)(128)(4,1)S(1)}, s32[]{:S(2)}) async-start(s8[6815744]{0:T(1024)(128)(4,1)} %bitcast.198), calls=%async_computation.1 | async-start | bytes 8388608
  45.7 2.8 %collective-permute-start.29 = (f16[2,64,3328]{2,1,0:T(8,128)(2,1)S(1)}, f16[2,64,3328]{2,1,0:T(8,128)(2,1)S(1)}, u32[]{:S(2)}, u32[]{:S(2)}) collective-permute-start(f16[2,64,3328]{2,1,0:T(8,128)(2,1)S(1)} %pad_maximum_fusion.3), channel_id=1, source_target_pairs={{0,1},{1,0},{2,3},{3,2},{4,5},{5,4},{6,7},{7,6},{8,9},{9,8},{10,11... | collective-permute-start | bytes 2555912 | tf_op jit(solution)/shard_map/ppermute | solution.py:23
  46.8 2.9 %collective-permute-start.20 = (f16[2,64,3328]{2,1,0:T(8,128)(2,1)S(1)}, f16[2,64,3328]{2,1,0:T(8,128)(2,1)S(1)}, u32[]{:S(2)}, u32[]{:S(2)}) collective-permute-start(f16[2,64,3328]{2,1,0:T(8,128)(2,1)S(1)} %pad_maximum_fusion.2), channel_id=1, source_target_pairs={{0,1},{1,0},{2,3},{3,2},{4,5},{5,4},{6,7},{7,6},{8,9},{9,8},{10,11... | collective-permute-start | bytes 2555912 | tf_op jit(solution)/shard_map/ppermute | solution.py:23
  47.2 4.8 %collective-permute-start.11 = (f16[2,64,3328]{2,1,0:T(8,128)(2,1)S(1)}, f16[2,64,3328]{2,1,0:T(8,128)(2,1)S(1)}, u32[]{:S(2)}, u32[]{:S(2)}) collective-permute-start(f16[2,64,3328]{2,1,0:T(8,128)(2,1)S(1)} %pad_maximum_fusion.1), channel_id=1, source_target_pairs={{0,1},{1,0},{2,3},{3,2},{4,5},{5,4},{6,7},{7,6},{8,9},{9,8},{10,11... | collective-permute-start | bytes 2555912 | tf_op jit(solution)/shard_map/ppermute | solution.py:23
  48.3 5.0 %collective-permute-start.1 = (f16[2,64,3328]{2,1,0:T(8,128)(2,1)S(1)}, f16[2,64,3328]{2,1,0:T(8,128)(2,1)S(1)}, u32[]{:S(2)}, u32[]{:S(2)}) collective-permute-start(f16[2,64,3328]{2,1,0:T(8,128)(2,1)S(1)} %pad_maximum_fusion), channel_id=1, source_target_pairs={{0,1},{1,0},{2,3},{3,2},{4,5},{5,4},{6,7},{7,6},{8,9},{9,8},{10,11... | collective-permute-start | bytes 2555912 | tf_op jit(solution)/shard_map/ppermute | solution.py:23
  48.8 8.3 %collective-permute-start.30 = (f16[2,32,3328]{2,1,0:T(8,128)(2,1)S(1)}, f16[2,32,3328]{2,1,0:T(8,128)(2,1)S(1)}, u32[]{:S(2)}, u32[]{:S(2)}) collective-permute-start(f16[2,32,3328]{2,1,0:T(8,128)(2,1)S(1)} %pad_maximum_fusion.10), channel_id=1, source_target_pairs={{0,4},{1,13},{4,0},{5,9},{8,12},{9,5},{12,8},{13,1},{2,6},{3,15},{... | collective-permute-start | bytes 1277960 | tf_op jit(solution)/shard_map/ppermute | solution.py:23
  50.1 11.6 %collective-permute-start.21 = (f16[2,32,3328]{2,1,0:T(8,128)(2,1)S(1)}, f16[2,32,3328]{2,1,0:T(8,128)(2,1)S(1)}, u32[]{:S(2)}, u32[]{:S(2)}) collective-permute-start(f16[2,32,3328]{2,1,0:T(8,128)(2,1)S(1)} %pad_maximum_fusion.8), channel_id=1, source_target_pairs={{0,4},{1,13},{4,0},{5,9},{8,12},{9,5},{12,8},{13,1},{2,6},{3,15},{... | collective-permute-start | bytes 1277960 | tf_op jit(solution)/shard_map/ppermute | solution.py:23
  52.5 16.8 %collective-permute-start.12 = (f16[2,32,3328]{2,1,0:T(8,128)(2,1)S(1)}, f16[2,32,3328]{2,1,0:T(8,128)(2,1)S(1)}, u32[]{:S(2)}, u32[]{:S(2)}) collective-permute-start(f16[2,32,3328]{2,1,0:T(8,128)(2,1)S(1)} %pad_maximum_fusion.6), channel_id=1, source_target_pairs={{0,4},{1,13},{4,0},{5,9},{8,12},{9,5},{12,8},{13,1},{2,6},{3,15},{... | collective-permute-start | bytes 1277960 | tf_op jit(solution)/shard_map/ppermute | solution.py:23
  53.8 15.8 %collective-permute-start.2 = (f16[2,64,1664]{2,1,0:T(8,128)(2,1)S(1)}, f16[2,64,1664]{2,1,0:T(8,128)(2,1)S(1)}, u32[]{:S(2)}, u32[]{:S(2)}) collective-permute-start(f16[2,64,1664]{2,1,0:T(8,128)(2,1)S(1)} %pad_maximum_fusion.4), channel_id=1, source_target_pairs={{0,2},{2,0},{1,3},{3,1},{4,6},{6,4},{5,7},{7,5},{8,10},{10,8},{9,1... | collective-permute-start | bytes 1277960 | tf_op jit(solution)/shard_map/ppermute | solution.py:23
  57.3 13.4 %collective-permute-start.31 = (f16[2,16,3328]{2,1,0:T(8,128)(2,1)S(1)}, f16[2,16,3328]{2,1,0:T(8,128)(2,1)S(1)}, u32[]{:S(2)}, u32[]{:S(2)}) collective-permute-start(f16[2,16,3328]{2,1,0:T(8,128)(2,1)S(1)} %pad_maximum_fusion.24), channel_id=1, source_target_pairs={{0,12},{1,5},{4,8},{5,1},{8,4},{9,13},{12,0},{13,9},{2,14},{3,7},{... | collective-permute-start | bytes 638984 | tf_op jit(solution)/shard_map/ppermute | solution.py:23
  61.9 9.1 %collective-permute-start.22 = (f16[2,16,3328]{2,1,0:T(8,128)(2,1)S(1)}, f16[2,16,3328]{2,1,0:T(8,128)(2,1)S(1)}, u32[]{:S(2)}, u32[]{:S(2)}) collective-permute-start(f16[2,16,3328]{2,1,0:T(8,128)(2,1)S(1)} %pad_maximum_fusion.21), channel_id=1, source_target_pairs={{0,12},{1,5},{4,8},{5,1},{8,4},{9,13},{12,0},{13,9},{2,14},{3,7},{... | collective-permute-start | bytes 638984 | tf_op jit(solution)/shard_map/ppermute | solution.py:23
  69.5 8.7 %collective-permute-start.13 = (f16[2,16,3328]{2,1,0:T(8,128)(2,1)S(1)}, f16[2,16,3328]{2,1,0:T(8,128)(2,1)S(1)}, u32[]{:S(2)}, u32[]{:S(2)}) collective-permute-start(f16[2,16,3328]{2,1,0:T(8,128)(2,1)S(1)} %pad_maximum_fusion.18), channel_id=1, source_target_pairs={{0,12},{1,5},{4,8},{5,1},{8,4},{9,13},{12,0},{13,9},{2,14},{3,7},{... | collective-permute-start | bytes 638984 | tf_op jit(solution)/shard_map/ppermute | solution.py:23
  69.8 40.0 %slice-start.2 = ((s8[6815744]{0:T(1024)(128)(4,1)}), s8[4194304]{0:T(1024)(128)(4,1)S(1)}, s32[]{:S(2)}) async-start(s8[6815744]{0:T(1024)(128)(4,1)} %bitcast.200), calls=%async_computation.3 | async-start | bytes 8388608
  69.9 6.5 %collective-permute-start.3 = (f16[2,32,1664]{2,1,0:T(8,128)(2,1)S(1)}, f16[2,32,1664]{2,1,0:T(8,128)(2,1)S(1)}, u32[]{:S(2)}, u32[]{:S(2)}) collective-permute-start(f16[2,32,1664]{2,1,0:T(8,128)(2,1)S(1)} %pad_maximum_fusion.16), channel_id=1, source_target_pairs={{0,4},{1,13},{4,0},{5,9},{8,12},{9,5},{12,8},{13,1},{2,6},{3,15},{... | collective-permute-start | bytes 638984 | tf_op jit(solution)/shard_map/ppermute | solution.py:23
  70.9 14.4 %collective-permute-start.32 = (f16[2,16,3328]{2,1,0:T(8,128)(2,1)S(1)}, f16[2,16,3328]{2,1,0:T(8,128)(2,1)S(1)}, u32[]{:S(2)}, u32[]{:S(2)}) collective-permute-start(f16[2,16,3328]{2,1,0:T(8,128)(2,1)S(1)} %pad_maximum_fusion.25), channel_id=1, source_target_pairs={{0,2},{2,0},{1,3},{3,1},{4,6},{6,4},{5,7},{7,5},{8,10},{10,8},{9,1... | collective-permute-start | bytes 638984 | tf_op jit(solution)/shard_map/ppermute | solution.py:23
  71.1 14.6 %collective-permute-start.23 = (f16[2,16,3328]{2,1,0:T(8,128)(2,1)S(1)}, f16[2,16,3328]{2,1,0:T(8,128)(2,1)S(1)}, u32[]{:S(2)}, u32[]{:S(2)}) collective-permute-start(f16[2,16,3328]{2,1,0:T(8,128)(2,1)S(1)} %pad_maximum_fusion.22), channel_id=1, source_target_pairs={{0,2},{2,0},{1,3},{3,1},{4,6},{6,4},{5,7},{7,5},{8,10},{10,8},{9,1... | collective-permute-start | bytes 638984 | tf_op jit(solution)/shard_map/ppermute | solution.py:23
  76.5 4.1 %collective-permute-start.4 = (f16[2,16,1664]{2,1,0:T(8,128)(2,1)S(1)}, f16[2,16,1664]{2,1,0:T(8,128)(2,1)S(1)}, u32[]{:S(2)}, u32[]{:S(2)}) collective-permute-start(f16[2,16,1664]{2,1,0:T(8,128)(2,1)S(1)} %pad_maximum_fusion.29), channel_id=1, source_target_pairs={{0,12},{1,5},{4,8},{5,1},{8,4},{9,13},{12,0},{13,9},{2,14},{3,7},{... | collective-permute-start | bytes 319496 | tf_op jit(solution)/shard_map/ppermute | solution.py:23
  80.6 3.4 %collective-permute-start.5 = (bf16[16,1664]{1,0:T(8,128)(2,1)S(1)}, bf16[16,1664]{1,0:T(8,128)(2,1)S(1)}, u32[]{:S(2)}, u32[]{:S(2)}) collective-permute-start(bf16[16,1664]{1,0:T(8,128)(2,1)S(1)} %fusion.77), channel_id=1, source_target_pairs={{0,2},{2,0},{1,3},{3,1},{4,6},{6,4},{5,7},{7,5},{8,10},{10,8},{9,1... | collective-permute-start | bytes 159752 | tf_op jit(solution)/shard_map/ppermute | solution.py:23
  80.7 29.1 %slice-start.3 = ((s8[6815744]{0:T(1024)(128)(4,1)}), s8[2621440]{0:T(1024)(128)(4,1)S(1)}, s32[]{:S(2)}) async-start(s8[6815744]{0:T(1024)(128)(4,1)} %bitcast.200), calls=%async_computation.4 | async-start | bytes 5242880
  80.8 6.3 %collective-permute-start.14 = (f16[2,16,3328]{2,1,0:T(8,128)(2,1)S(1)}, f16[2,16,3328]{2,1,0:T(8,128)(2,1)S(1)}, u32[]{:S(2)}, u32[]{:S(2)}) collective-permute-start(f16[2,16,3328]{2,1,0:T(8,128)(2,1)S(1)} %pad_maximum_fusion.19), channel_id=1, source_target_pairs={{0,2},{2,0},{1,3},{3,1},{4,6},{6,4},{5,7},{7,5},{8,10},{10,8},{9,1... | collective-permute-start | bytes 638984 | tf_op jit(solution)/shard_map/ppermute | solution.py:23
  84.0 4.7 %collective-permute-start.6 = (bf16[16,3328]{1,0:T(8,128)(2,1)S(1)}, bf16[16,3328]{1,0:T(8,128)(2,1)S(1)}, u32[]{:S(2)}, u32[]{:S(2)}) collective-permute-start(bf16[16,3328]{1,0:T(8,128)(2,1)S(1)} %pad_maximum_fusion.30), channel_id=1, source_target_pairs={{0,12},{1,5},{4,8},{5,1},{8,4},{9,13},{12,0},{13,9},{2,14},{3,7},{... | collective-permute-start | bytes 319496 | tf_op jit(solution)/shard_map/ppermute | solution.py:23
  85.4 3.9 %collective-permute-start.33 = (bf16[16,3328]{1,0:T(8,128)(2,1)S(1)}, bf16[16,3328]{1,0:T(8,128)(2,1)S(1)}, u32[]{:S(2)}, u32[]{:S(2)}) collective-permute-start(bf16[16,3328]{1,0:T(8,128)(2,1)S(1)} %fusion.55), channel_id=1, source_target_pairs={{0,12},{1,5},{4,8},{5,1},{8,4},{9,13},{12,0},{13,9},{2,14},{3,7},{... | collective-permute-start | bytes 319496 | tf_op jit(solution)/shard_map/ppermute | solution.py:23
  85.8 5.7 %collective-permute-start.24 = (bf16[16,3328]{1,0:T(8,128)(2,1)S(1)}, bf16[16,3328]{1,0:T(8,128)(2,1)S(1)}, u32[]{:S(2)}, u32[]{:S(2)}) collective-permute-start(bf16[16,3328]{1,0:T(8,128)(2,1)S(1)} %fusion.57), channel_id=1, source_target_pairs={{0,12},{1,5},{4,8},{5,1},{8,4},{9,13},{12,0},{13,9},{2,14},{3,7},{... | collective-permute-start | bytes 319496 | tf_op jit(solution)/shard_map/ppermute | solution.py:23
  87.2 5.0 %collective-permute-start.15 = (bf16[16,3328]{1,0:T(8,128)(2,1)S(1)}, bf16[16,3328]{1,0:T(8,128)(2,1)S(1)}, u32[]{:S(2)}, u32[]{:S(2)}) collective-permute-start(bf16[16,3328]{1,0:T(8,128)(2,1)S(1)} %fusion.59), channel_id=1, source_target_pairs={{0,12},{1,5},{4,8},{5,1},{8,4},{9,13},{12,0},{13,9},{2,14},{3,7},{... | collective-permute-start | bytes 319496 | tf_op jit(solution)/shard_map/ppermute | solution.py:23
  88.7 7.2 %collective-permute-start.7 = (bf16[32,3328]{1,0:T(8,128)(2,1)S(1)}, bf16[32,3328]{1,0:T(8,128)(2,1)S(1)}, u32[]{:S(2)}, u32[]{:S(2)}) collective-permute-start(bf16[32,3328]{1,0:T(8,128)(2,1)S(1)} %pad_maximum_fusion.17), channel_id=1, source_target_pairs={{0,4},{1,13},{4,0},{5,9},{8,12},{9,5},{12,8},{13,1},{2,6},{3,15},{... | collective-permute-start | bytes 638984 | tf_op jit(solution)/shard_map/ppermute | solution.py:23
  89.3 14.5 %collective-permute-start.34 = (bf16[32,3328]{1,0:T(8,128)(2,1)S(1)}, bf16[32,3328]{1,0:T(8,128)(2,1)S(1)}, u32[]{:S(2)}, u32[]{:S(2)}) collective-permute-start(bf16[32,3328]{1,0:T(8,128)(2,1)S(1)} %pad_maximum_fusion.26), channel_id=1, source_target_pairs={{0,4},{1,13},{4,0},{5,9},{8,12},{9,5},{12,8},{13,1},{2,6},{3,15},{... | collective-permute-start | bytes 638984 | tf_op jit(solution)/shard_map/ppermute | solution.py:23
  91.6 13.4 %collective-permute-start.25 = (bf16[32,3328]{1,0:T(8,128)(2,1)S(1)}, bf16[32,3328]{1,0:T(8,128)(2,1)S(1)}, u32[]{:S(2)}, u32[]{:S(2)}) collective-permute-start(bf16[32,3328]{1,0:T(8,128)(2,1)S(1)} %pad_maximum_fusion.23), channel_id=1, source_target_pairs={{0,4},{1,13},{4,0},{5,9},{8,12},{9,5},{12,8},{13,1},{2,6},{3,15},{... | collective-permute-start | bytes 638984 | tf_op jit(solution)/shard_map/ppermute | solution.py:23
  92.2 15.1 %collective-permute-start.16 = (bf16[32,3328]{1,0:T(8,128)(2,1)S(1)}, bf16[32,3328]{1,0:T(8,128)(2,1)S(1)}, u32[]{:S(2)}, u32[]{:S(2)}) collective-permute-start(bf16[32,3328]{1,0:T(8,128)(2,1)S(1)} %pad_maximum_fusion.20), channel_id=1, source_target_pairs={{0,4},{1,13},{4,0},{5,9},{8,12},{9,5},{12,8},{13,1},{2,6},{3,15},{... | collective-permute-start | bytes 638984 | tf_op jit(solution)/shard_map/ppermute | solution.py:23
  96.0 13.8 %collective-permute-start.8 = (bf16[64,3328]{1,0:T(8,128)(2,1)S(1)}, bf16[64,3328]{1,0:T(8,128)(2,1)S(1)}, u32[]{:S(2)}, u32[]{:S(2)}) collective-permute-start(bf16[64,3328]{1,0:T(8,128)(2,1)S(1)} %pad_maximum_fusion.5), channel_id=1, source_target_pairs={{0,1},{1,0},{2,3},{3,2},{4,5},{5,4},{6,7},{7,6},{8,9},{9,8},{10,11... | collective-permute-start | bytes 1277960 | tf_op jit(solution)/shard_map/ppermute | solution.py:23
  103.8 7.1 %collective-permute-start.35 = (bf16[64,3328]{1,0:T(8,128)(2,1)S(1)}, bf16[64,3328]{1,0:T(8,128)(2,1)S(1)}, u32[]{:S(2)}, u32[]{:S(2)}) collective-permute-start(bf16[64,3328]{1,0:T(8,128)(2,1)S(1)} %pad_maximum_fusion.11), channel_id=1, source_target_pairs={{0,1},{1,0},{2,3},{3,2},{4,5},{5,4},{6,7},{7,6},{8,9},{9,8},{10,11... | collective-permute-start | bytes 1277960 | tf_op jit(solution)/shard_map/ppermute | solution.py:23
  105.1 6.9 %collective-permute-start.26 = (bf16[64,3328]{1,0:T(8,128)(2,1)S(1)}, bf16[64,3328]{1,0:T(8,128)(2,1)S(1)}, u32[]{:S(2)}, u32[]{:S(2)}) collective-permute-start(bf16[64,3328]{1,0:T(8,128)(2,1)S(1)} %pad_maximum_fusion.9), channel_id=1, source_target_pairs={{0,1},{1,0},{2,3},{3,2},{4,5},{5,4},{6,7},{7,6},{8,9},{9,8},{10,11... | collective-permute-start | bytes 1277960 | tf_op jit(solution)/shard_map/ppermute | solution.py:23
  107.3 5.7 %collective-permute-start.17 = (bf16[64,3328]{1,0:T(8,128)(2,1)S(1)}, bf16[64,3328]{1,0:T(8,128)(2,1)S(1)}, u32[]{:S(2)}, u32[]{:S(2)}) collective-permute-start(bf16[64,3328]{1,0:T(8,128)(2,1)S(1)} %pad_maximum_fusion.7), channel_id=1, source_target_pairs={{0,1},{1,0},{2,3},{3,2},{4,5},{5,4},{6,7},{7,6},{8,9},{9,8},{10,11... | collective-permute-start | bytes 1277960 | tf_op jit(solution)/shard_map/ppermute | solution.py:23
  114.1 10.1 %collective-permute-start.36 = (bf16[64,1024]{1,0:T(8,128)(2,1)S(1)}, bf16[64,1024]{1,0:T(8,128)(2,1)S(1)}, u32[]{:S(2)}, u32[]{:S(2)}) collective-permute-start(bf16[64,1024]{1,0:T(8,128)(2,1)S(1)} %get-tuple-element.141), channel_id=1, source_target_pairs={{0,64},{32,96},{64,0},{96,32},{1,65},{33,97},{65,1},{97,33},{2,66}... | collective-permute-start | bytes 393224 | tf_op jit(solution)/shard_map/ppermute | solution.py:23
  118.4 9.9 %collective-permute-start.37 = (bf16[64,1024]{1,0:T(8,128)(2,1)S(1)}, bf16[64,1024]{1,0:T(8,128)(2,1)S(1)}, u32[]{:S(2)}, u32[]{:S(2)}) collective-permute-start(bf16[64,1024]{1,0:T(8,128)(2,1)S(1)} %get-tuple-element.142), channel_id=1, source_target_pairs={{0,80},{16,64},{32,112},{48,96},{64,16},{80,0},{96,48},{112,32},{1... | collective-permute-start | bytes 393224 | tf_op jit(solution)/shard_map/ppermute | solution.py:23
  121.4 9.4 %collective-permute-start.38 = (bf16[64,1024]{1,0:T(8,128)(2,1)S(1)}, bf16[64,1024]{1,0:T(8,128)(2,1)S(1)}, u32[]{:S(2)}, u32[]{:S(2)}) collective-permute-start(bf16[64,1024]{1,0:T(8,128)(2,1)S(1)} %get-tuple-element.143), channel_id=1, source_target_pairs={{0,96},{32,64},{64,32},{96,0},{1,97},{33,65},{65,33},{97,1},{2,98}... | collective-permute-start | bytes 393224 | tf_op jit(solution)/shard_map/ppermute | solution.py:23
  122.7 12.4 %collective-permute-start.39 = (bf16[64,1024]{1,0:T(8,128)(2,1)S(1)}, bf16[64,1024]{1,0:T(8,128)(2,1)S(1)}, u32[]{:S(2)}, u32[]{:S(2)}) collective-permute-start(bf16[64,1024]{1,0:T(8,128)(2,1)S(1)} %get-tuple-element.144), channel_id=1, source_target_pairs={{0,112},{16,96},{32,80},{48,64},{64,48},{80,32},{96,16},{112,0},{1... | collective-permute-start | bytes 393224 | tf_op jit(solution)/shard_map/ppermute | solution.py:23
  124.1 11.0 %collective-permute-start.40 = (bf16[64,1024]{1,0:T(8,128)(2,1)S(1)}, bf16[64,1024]{1,0:T(8,128)(2,1)S(1)}, u32[]{:S(2)}, u32[]{:S(2)}) collective-permute-start(bf16[64,1024]{1,0:T(8,128)(2,1)S(1)} %get-tuple-element.145), channel_id=1, source_target_pairs={{0,32},{32,0},{64,96},{96,64},{1,33},{33,1},{65,97},{97,65},{2,34}... | collective-permute-start | bytes 393224 | tf_op jit(solution)/shard_map/ppermute | solution.py:23
  124.3 10.9 %collective-permute-start.41 = (bf16[64,1024]{1,0:T(8,128)(2,1)S(1)}, bf16[64,1024]{1,0:T(8,128)(2,1)S(1)}, u32[]{:S(2)}, u32[]{:S(2)}) collective-permute-start(bf16[64,1024]{1,0:T(8,128)(2,1)S(1)} %get-tuple-element.146), channel_id=1, source_target_pairs={{0,48},{16,32},{32,16},{48,0},{64,112},{80,96},{96,80},{112,64},{1... | collective-permute-start | bytes 393224 | tf_op jit(solution)/shard_map/ppermute | solution.py:23
  128.3 10.9 %collective-permute-start.42 = (bf16[64,1024]{1,0:T(8,128)(2,1)S(1)}, bf16[64,1024]{1,0:T(8,128)(2,1)S(1)}, u32[]{:S(2)}, u32[]{:S(2)}) collective-permute-start(bf16[64,1024]{1,0:T(8,128)(2,1)S(1)} %select_convert_fusion), channel_id=1, source_target_pairs={{0,16},{16,0},{32,48},{48,32},{64,80},{80,64},{96,112},{112,96},{1... | collective-permute-start | bytes 393224 | tf_op jit(solution)/shard_map/ppermute | solution.py:23
  (1 other events, 2.2 us)

commit v9 on v7

--- a/solution.py
+++ b/solution.py
@@ -88,6 +88,8 @@
             st["flight"] = swap_core(send)
         elif s in (2, 3, 4):
             got = tie(st["flight"])
+            if s == 4 and e == 0:
+                got, *_ = tie(got, *[other["send"] for other in state[1:]])
             part = slice(64, 128) if s == 2 else slice(0, got.shape[1])
             total = [v[part] + lowered(g) for v, g in zip(st["total"], got)]
             if e == Z_FIRST and s == 2:
@@ -101,6 +103,7 @@
                 send = jnp.stack([lifted(v[part]) for v in total])
                 swap = (swap_first, swap_second, swap_z)[over - 2]
             send, *st["total"] = tie(send, *total)
+            st["send"] = send
             st["flight"] = swap(send)
         elif s == 5:
             got = tie(st["flight"])
@@ -127,7 +130,7 @@
             arrived.append(swap_row[e](cross).astype(F32))
 
     for s in (-1, 0, 2, 3, 4, 5, 6, 7, 8):
-        for e in (0, 2, 1, 3):
+        for e in range(4):
             if e or s >= 0:
                 step(e, s)
 

time: 124 us -> 127 us (1.024)
  waiting for transfers between devices: 36.7 us -> 43 us
  starting transfers between devices: 62.7 us -> 58.4 us
    ppermute x39, waiting for transfers between devices: 27.9 us -> 34.3 us  [permute(): return lambda v: lax.ppermute(v, axes, pairs)]
    ppermute x39, starting transfers between devices: 53.1 us -> 48.8 us  [permute(): return lambda v: lax.ppermute(v, axes, pairs)]
  transfers between devices with their start and end apart: 40 -> 40, of which waited for: 15 -> 16; matrix products, arithmetic and copies ran while one was open for 17% -> 16% of each run, Pallas kernels for 0% -> 0%
where the time goes in v9:
time: 127 us; the launch traced here: 126 us
  starting transfers between devices  58.4 us (46%)
  waiting for transfers between devices  43 us (34%)
  matrix products  15.8 us (12%)
  other arithmetic  5.79 us (5%)
  local copies, waits for them, and re-layouts  2.01 us (2%)
    ppermute x39, starting transfers between devices, permute(): return lambda v: lax.ppermute(v, axes, pairs)  48.8 us
    ppermute x39, waiting for transfers between devices, permute(): return lambda v: lax.ppermute(v, axes, pairs)  34.3 us
    dot_general x12, matrix products, product(): return jnp.dot(rows, weight, preferred_element_type=F32)  15.8 us
    all_to_all x1, starting transfers between devices, per_device(): lax.all_to_all(blocks, AXES[1:], split_axis=0, concat_axis=0, tiled=True)  9.6 us
    all_to_all x1, waiting for transfers between devices, per_device(): lax.all_to_all(blocks, AXES[1:], split_axis=0, concat_axis=0, tiled=True)  8.79 us
  transfers between devices with their start and end apart: 40, of which 16 were waited for; matrix products, arithmetic and copies ran while one was open for 16% of the time, Pallas kernels for 0%

profile of v9, /device:TPU:1, one launch (start us, length us, event | category | flops | bytes accessed | tf_op | source)
XLA Modules:
  0.0 125.9 jit_solution(2345805463873551996)
XLA Ops:
  0.0 0.9 broadcast_in_dim.7
  1.8 9.6 %all-to-all-start = ((bf16[32,4,1024]{2,1,0:T(4,128)(2,1)}), bf16[32,4,1024]{2,1,0:T(4,128)(2,1)S(1)}, u32[]{:S(2)}, u32[]{:S(2)}) async-start(bf16[32,4,1024]{2,1,0:T(4,128)(2,1)} %all_to_all.6), calls=%async_computation | async-start | bytes 524288 | tf_op jit(solution)/shard_map/all_to_all | solution.py:48
  11.5 8.8 %all-to-all-done = bf16[32,4,1024]{2,1,0:T(4,128)(2,1)S(1)} async-done(((bf16[32,4,1024]{2,1,0:T(4,128)(2,1)}), bf16[32,4,1024]{2,1,0:T(4,128)(2,1)S(1)}, u32[]{:S(2)}, u32[]{:S(2)}) %all-to-all-start) | async-done | bytes 262176 | tf_op jit(solution)/shard_map/all_to_all | solution.py:48
  20.5 2.6 %collective-permute-start.9 = (bf16[128,1024]{1,0:T(8,128)(2,1)S(1)}, bf16[128,1024]{1,0:T(8,128)(2,1)S(1)}, u32[]{:S(2)}, u32[]{:S(2)}) collective-permute-start(bf16[128,1024]{1,0:T(8,128)(2,1)S(1)} %bitcast_dynamic-update-slice_fusion), channel_id=1, source_target_pairs={{0,96},{32,64},{64,32},{96,0},{1,97},{33,65},{65,33},{97,1},{2,98}... | collective-permute-start | bytes 786440 | tf_op jit(solution)/shard_map/ppermute | solution.py:23
  23.8 4.1 %fusion.84 = f32[128,3328]{1,0:T(8,128)S(1)} fusion(bf16[128,1024]{1,0:T(8,128)(2,1)S(1)} %bitcast_dynamic-update-slice_fusion, bf16[1024,3328]{1,0:T(8,128)(2,1)} %param.5), kind=kOutput, calls=%fused_computation.199 | convolution fusion | flops 872415232 | bytes 8781824 | tf_op jit(solution)/shard_map/dot_general | solution.py:74
  28.0 1.1 fusion.85
  29.5 1.9 %collective-permute-start = (f16[2,64,3328]{2,1,0:T(8,128)(2,1)S(1)}, f16[2,64,3328]{2,1,0:T(8,128)(2,1)S(1)}, u32[]{:S(2)}, u32[]{:S(2)}) collective-permute-start(f16[2,64,3328]{2,1,0:T(8,128)(2,1)S(1)} %pad_maximum_fusion), channel_id=1, source_target_pairs={{0,1},{1,0},{2,3},{3,2},{4,5},{5,4},{6,7},{7,6},{8,9},{9,8},{10,11... | collective-permute-start | bytes 2555912 | tf_op jit(solution)/shard_map/ppermute | solution.py:23
  31.3 2.8 %collective-permute-done.9 = bf16[128,1024]{1,0:T(8,128)(2,1)S(1)} collective-permute-done((bf16[128,1024]{1,0:T(8,128)(2,1)S(1)}, bf16[128,1024]{1,0:T(8,128)(2,1)S(1)}, u32[]{:S(2)}, u32[]{:S(2)}) %collective-permute-start.9) | collective-permute-done | bytes 262176 | tf_op jit(solution)/shard_map/ppermute | solution.py:23
  34.2 1.1 fusion.90
  35.2 1.1 fusion.91
  36.3 1.1 fusion.88
  37.4 1.1 fusion.89
  38.5 1.1 fusion.86
  39.6 1.1 fusion.87
  41.0 2.1 %collective-permute-start.10 = (f16[2,64,3328]{2,1,0:T(8,128)(2,1)S(1)}, f16[2,64,3328]{2,1,0:T(8,128)(2,1)S(1)}, u32[]{:S(2)}, u32[]{:S(2)}) collective-permute-start(f16[2,64,3328]{2,1,0:T(8,128)(2,1)S(1)} %pad_maximum_fusion.3), channel_id=1, source_target_pairs={{0,1},{1,0},{2,3},{3,2},{4,5},{5,4},{6,7},{7,6},{8,9},{9,8},{10,11... | collective-permute-start | bytes 2555912 | tf_op jit(solution)/shard_map/ppermute | solution.py:23
  47.1 1.8 %collective-permute-start.8 = (f16[2,32,3328]{2,1,0:T(8,128)(2,1)S(1)}, f16[2,32,3328]{2,1,0:T(8,128)(2,1)S(1)}, u32[]{:S(2)}, u32[]{:S(2)}) collective-permute-start(f16[2,32,3328]{2,1,0:T(8,128)(2,1)S(1)} %pad_maximum_fusion.6), channel_id=1, source_target_pairs={{0,4},{1,13},{4,0},{5,9},{8,12},{9,5},{12,8},{13,1},{2,6},{3,15},{... | collective-permute-start | bytes 1277960 | tf_op jit(solution)/shard_map/ppermute | solution.py:23
  49.1 4.1 %collective-permute-done.1 = f16[2,32,3328]{2,1,0:T(8,128)(2,1)S(1)} collective-permute-done((f16[2,32,3328]{2,1,0:T(8,128)(2,1)S(1)}, f16[2,32,3328]{2,1,0:T(8,128)(2,1)S(1)}, u32[]{:S(2)}, u32[]{:S(2)}) %collective-permute-start.1) | collective-permute-done | bytes 426016 | tf_op jit(solution)/shard_map/ppermute | solution.py:23
  54.5 6.4 %collective-permute-done.2 = f16[2,16,3328]{2,1,0:T(8,128)(2,1)S(1)} collective-permute-done((f16[2,16,3328]{2,1,0:T(8,128)(2,1)S(1)}, f16[2,16,3328]{2,1,0:T(8,128)(2,1)S(1)}, u32[]{:S(2)}, u32[]{:S(2)}) %collective-permute-start.2) | collective-permute-done | bytes 213024 | tf_op jit(solution)/shard_map/ppermute | solution.py:23
  61.6 3.0 %collective-permute-done.5 = f16[2,32,3328]{2,1,0:T(8,128)(2,1)S(1)} collective-permute-done((f16[2,32,3328]{2,1,0:T(8,128)(2,1)S(1)}, f16[2,32,3328]{2,1,0:T(8,128)(2,1)S(1)}, u32[]{:S(2)}, u32[]{:S(2)}) %collective-permute-start.5) | collective-permute-done | bytes 426016 | tf_op jit(solution)/shard_map/ppermute | solution.py:23
  65.3 1.8 %collective-permute-done.31 = f16[2,32,1664]{2,1,0:T(8,128)(2,1)S(1)} collective-permute-done((f16[2,32,1664]{2,1,0:T(8,128)(2,1)S(1)}, f16[2,32,1664]{2,1,0:T(8,128)(2,1)S(1)}, u32[]{:S(2)}, u32[]{:S(2)}) %collective-permute-start.31) | collective-permute-done | bytes 213024 | tf_op jit(solution)/shard_map/ppermute | solution.py:23
  67.5 1.1 collective-permute-start.25
  68.6 2.5 %collective-permute-done.17 = f16[2,16,3328]{2,1,0:T(8,128)(2,1)S(1)} collective-permute-done((f16[2,16,3328]{2,1,0:T(8,128)(2,1)S(1)}, f16[2,16,3328]{2,1,0:T(8,128)(2,1)S(1)}, u32[]{:S(2)}, u32[]{:S(2)}) %collective-permute-start.17) | collective-permute-done | bytes 213024 | tf_op jit(solution)/shard_map/ppermute | solution.py:23
  73.3 2.7 %collective-permute-done.13 = bf16[16,3328]{1,0:T(8,128)(2,1)S(1)} collective-permute-done((bf16[16,3328]{1,0:T(8,128)(2,1)S(1)}, bf16[16,3328]{1,0:T(8,128)(2,1)S(1)}, u32[]{:S(2)}, u32[]{:S(2)}) %collective-permute-start.13) | collective-permute-done | bytes 106528 | tf_op jit(solution)/shard_map/ppermute | solution.py:23
  76.0 2.2 %collective-permute-start.14 = (bf16[32,3328]{1,0:T(8,128)(2,1)S(1)}, bf16[32,3328]{1,0:T(8,128)(2,1)S(1)}, u32[]{:S(2)}, u32[]{:S(2)}) collective-permute-start(bf16[32,3328]{1,0:T(8,128)(2,1)S(1)} %pad_maximum_fusion.17), channel_id=1, source_target_pairs={{0,4},{1,13},{4,0},{5,9},{8,12},{9,5},{12,8},{13,1},{2,6},{3,15},{... | collective-permute-start | bytes 638984 | tf_op jit(solution)/shard_map/ppermute | solution.py:23
  78.2 1.1 collective-permute-done.33
  79.4 3.2 %collective-permute-start.34 = (bf16[16,3328]{1,0:T(8,128)(2,1)S(1)}, bf16[16,3328]{1,0:T(8,128)(2,1)S(1)}, u32[]{:S(2)}, u32[]{:S(2)}) collective-permute-start(bf16[16,3328]{1,0:T(8,128)(2,1)S(1)} %pad_maximum_fusion.25), channel_id=1, source_target_pairs={{0,12},{1,5},{4,8},{5,1},{8,4},{9,13},{12,0},{13,9},{2,14},{3,7},{... | collective-permute-start | bytes 319496 | tf_op jit(solution)/shard_map/ppermute | solution.py:23
  82.9 1.5 %collective-permute-start.19 = (bf16[16,3328]{1,0:T(8,128)(2,1)S(1)}, bf16[16,3328]{1,0:T(8,128)(2,1)S(1)}, u32[]{:S(2)}, u32[]{:S(2)}) collective-permute-start(bf16[16,3328]{1,0:T(8,128)(2,1)S(1)} %fusion.57), channel_id=1, source_target_pairs={{0,12},{1,5},{4,8},{5,1},{8,4},{9,13},{12,0},{13,9},{2,14},{3,7},{... | collective-permute-start | bytes 319496 | tf_op jit(solution)/shard_map/ppermute | solution.py:23
  85.1 1.4 %collective-permute-start.35 = (bf16[32,3328]{1,0:T(8,128)(2,1)S(1)}, bf16[32,3328]{1,0:T(8,128)(2,1)S(1)}, u32[]{:S(2)}, u32[]{:S(2)}) collective-permute-start(bf16[32,3328]{1,0:T(8,128)(2,1)S(1)} %pad_maximum_fusion.22), channel_id=1, source_target_pairs={{0,4},{1,13},{4,0},{5,9},{8,12},{9,5},{12,8},{13,1},{2,6},{3,15},{... | collective-permute-start | bytes 638984 | tf_op jit(solution)/shard_map/ppermute | solution.py:23
  86.5 0.9 collective-permute-done.26
  87.4 1.4 %collective-permute-start.27 = (bf16[32,3328]{1,0:T(8,128)(2,1)S(1)}, bf16[32,3328]{1,0:T(8,128)(2,1)S(1)}, u32[]{:S(2)}, u32[]{:S(2)}) collective-permute-start(bf16[32,3328]{1,0:T(8,128)(2,1)S(1)} %pad_maximum_fusion.21), channel_id=1, source_target_pairs={{0,4},{1,13},{4,0},{5,9},{8,12},{9,5},{12,8},{13,1},{2,6},{3,15},{... | collective-permute-start | bytes 638984 | tf_op jit(solution)/shard_map/ppermute | solution.py:23
  88.8 0.9 collective-permute-done.19
  89.7 0.8 collective-permute-start.20
  90.6 4.5 %collective-permute-start.15 = (bf16[64,3328]{1,0:T(8,128)(2,1)S(1)}, bf16[64,3328]{1,0:T(8,128)(2,1)S(1)}, u32[]{:S(2)}, u32[]{:S(2)}) collective-permute-start(bf16[64,3328]{1,0:T(8,128)(2,1)S(1)} %pad_maximum_fusion.8), channel_id=1, source_target_pairs={{0,1},{1,0},{2,3},{3,2},{4,5},{5,4},{6,7},{7,6},{8,9},{9,8},{10,11... | collective-permute-start | bytes 1277960 | tf_op jit(solution)/shard_map/ppermute | solution.py:23
  95.7 2.9 %collective-permute-start.28 = (bf16[64,3328]{1,0:T(8,128)(2,1)S(1)}, bf16[64,3328]{1,0:T(8,128)(2,1)S(1)}, u32[]{:S(2)}, u32[]{:S(2)}) collective-permute-start(bf16[64,3328]{1,0:T(8,128)(2,1)S(1)} %pad_maximum_fusion.10), channel_id=1, source_target_pairs={{0,1},{1,0},{2,3},{3,2},{4,5},{5,4},{6,7},{7,6},{8,9},{9,8},{10,11... | collective-permute-start | bytes 1277960 | tf_op jit(solution)/shard_map/ppermute | solution.py:23
  98.6 2.2 %collective-permute-start.21 = (bf16[64,3328]{1,0:T(8,128)(2,1)S(1)}, bf16[64,3328]{1,0:T(8,128)(2,1)S(1)}, u32[]{:S(2)}, u32[]{:S(2)}) collective-permute-start(bf16[64,3328]{1,0:T(8,128)(2,1)S(1)} %pad_maximum_fusion.9), channel_id=1, source_target_pairs={{0,1},{1,0},{2,3},{3,2},{4,5},{5,4},{6,7},{7,6},{8,9},{9,8},{10,11... | collective-permute-start | bytes 1277960 | tf_op jit(solution)/shard_map/ppermute | solution.py:23
  100.9 1.0 fusion.8
  102.0 1.3 %collective-permute-start.16 = (bf16[64,1024]{1,0:T(8,128)(2,1)S(1)}, bf16[64,1024]{1,0:T(8,128)(2,1)S(1)}, u32[]{:S(2)}, u32[]{:S(2)}) collective-permute-start(bf16[64,1024]{1,0:T(8,128)(2,1)S(1)} %select_convert_fusion.6), channel_id=1, source_target_pairs={{0,16},{16,0},{32,48},{48,32},{64,80},{80,64},{96,112},{112,96},{1... | collective-permute-start | bytes 393224 | tf_op jit(solution)/shard_map/ppermute | solution.py:23
  103.3 1.1 fusion.20
  104.4 4.2 %collective-permute-start.38 = (bf16[64,1024]{1,0:T(8,128)(2,1)S(1)}, bf16[64,1024]{1,0:T(8,128)(2,1)S(1)}, u32[]{:S(2)}, u32[]{:S(2)}) collective-permute-start(bf16[64,1024]{1,0:T(8,128)(2,1)S(1)} %get-tuple-element.118), channel_id=1, source_target_pairs={{0,112},{16,96},{32,80},{48,64},{64,48},{80,32},{96,16},{112,0},{1... | collective-permute-start | bytes 393224 | tf_op jit(solution)/shard_map/ppermute | solution.py:23
  108.9 1.1 fusion.16
  110.0 1.1 collective-permute-start.30
  111.1 2.6 %collective-permute-start.29 = (bf16[64,1024]{1,0:T(8,128)(2,1)S(1)}, bf16[64,1024]{1,0:T(8,128)(2,1)S(1)}, u32[]{:S(2)}, u32[]{:S(2)}) collective-permute-start(bf16[64,1024]{1,0:T(8,128)(2,1)S(1)} %get-tuple-element.110), channel_id=1, source_target_pairs={{0,64},{32,96},{64,0},{96,32},{1,65},{33,97},{65,1},{97,33},{2,66}... | collective-permute-start | bytes 393224 | tf_op jit(solution)/shard_map/ppermute | solution.py:23
  113.7 1.0 fusion.12
  114.8 1.9 %collective-permute-start.23 = (bf16[64,1024]{1,0:T(8,128)(2,1)S(1)}, bf16[64,1024]{1,0:T(8,128)(2,1)S(1)}, u32[]{:S(2)}, u32[]{:S(2)}) collective-permute-start(bf16[64,1024]{1,0:T(8,128)(2,1)S(1)} %get-tuple-element.104), channel_id=1, source_target_pairs={{0,48},{16,32},{32,16},{48,0},{64,112},{80,96},{96,80},{112,64},{1... | collective-permute-start | bytes 393224 | tf_op jit(solution)/shard_map/ppermute | solution.py:23
  116.7 1.4 %collective-permute-start.22 = (bf16[64,1024]{1,0:T(8,128)(2,1)S(1)}, bf16[64,1024]{1,0:T(8,128)(2,1)S(1)}, u32[]{:S(2)}, u32[]{:S(2)}) collective-permute-start(bf16[64,1024]{1,0:T(8,128)(2,1)S(1)} %get-tuple-element.103), channel_id=1, source_target_pairs={{0,32},{32,0},{64,96},{96,64},{1,33},{33,1},{65,97},{97,65},{2,34}... | collective-permute-start | bytes 393224 | tf_op jit(solution)/shard_map/ppermute | solution.py:23
  118.1 1.2 collective-permute-done.29
  119.3 4.5 %collective-permute-done.23 = bf16[64,1024]{1,0:T(8,128)(2,1)S(1)} collective-permute-done((bf16[64,1024]{1,0:T(8,128)(2,1)S(1)}, bf16[64,1024]{1,0:T(8,128)(2,1)S(1)}, u32[]{:S(2)}, u32[]{:S(2)}) %collective-permute-start.23) | collective-permute-done | bytes 131104 | tf_op jit(solution)/shard_map/ppermute | solution.py:23
  123.8 1.2 collective-permute-done.22
  (143 shorter events, 14.7 us)
Async XLA Ops:
  1.8 18.5 %all-to-all-start = ((bf16[32,4,1024]{2,1,0:T(4,128)(2,1)}), bf16[32,4,1024]{2,1,0:T(4,128)(2,1)S(1)}, u32[]{:S(2)}, u32[]{:S(2)}) async-start(bf16[32,4,1024]{2,1,0:T(4,128)(2,1)} %all_to_all.6), calls=%async_computation | async-start | bytes 524288 | tf_op jit(solution)/shard_map/all_to_all | solution.py:48
  20.4 7.6 %slice-start.2 = ((s8[6815744]{0:T(1024)(128)(4,1)}), s8[4194304]{0:T(1024)(128)(4,1)S(1)}, s32[]{:S(2)}) async-start(s8[6815744]{0:T(1024)(128)(4,1)} %bitcast.208), calls=%async_computation.3 | async-start | bytes 8388608
  20.5 7.5 %slice-start.3 = ((s8[6815744]{0:T(1024)(128)(4,1)}), s8[2621440]{0:T(1024)(128)(4,1)S(1)}, s32[]{:S(2)}) async-start(s8[6815744]{0:T(1024)(128)(4,1)} %bitcast.208), calls=%async_computation.4 | async-start | bytes 5242880
  20.5 13.7 %collective-permute-start.9 = (bf16[128,1024]{1,0:T(8,128)(2,1)S(1)}, bf16[128,1024]{1,0:T(8,128)(2,1)S(1)}, u32[]{:S(2)}, u32[]{:S(2)}) collective-permute-start(bf16[128,1024]{1,0:T(8,128)(2,1)S(1)} %bitcast_dynamic-update-slice_fusion), channel_id=1, source_target_pairs={{0,96},{32,64},{64,32},{96,0},{1,97},{33,65},{65,33},{97,1},{2,98}... | collective-permute-start | bytes 786440 | tf_op jit(solution)/shard_map/ppermute | solution.py:23
  23.1 13.2 %collective-permute-start.6 = (bf16[128,1024]{1,0:T(8,128)(2,1)S(1)}, bf16[128,1024]{1,0:T(8,128)(2,1)S(1)}, u32[]{:S(2)}, u32[]{:S(2)}) collective-permute-start(bf16[128,1024]{1,0:T(8,128)(2,1)S(1)} %bitcast_dynamic-update-slice_fusion), channel_id=1, source_target_pairs={{0,64},{32,96},{64,0},{96,32},{1,65},{33,97},{65,1},{97,33},{2,66}... | collective-permute-start | bytes 786440 | tf_op jit(solution)/shard_map/ppermute | solution.py:23
  23.6 14.9 %collective-permute-start.3 = (bf16[128,1024]{1,0:T(8,128)(2,1)S(1)}, bf16[128,1024]{1,0:T(8,128)(2,1)S(1)}, u32[]{:S(2)}, u32[]{:S(2)}) collective-permute-start(bf16[128,1024]{1,0:T(8,128)(2,1)S(1)} %bitcast_dynamic-update-slice_fusion), channel_id=1, source_target_pairs={{0,32},{32,0},{64,96},{96,64},{1,33},{33,1},{65,97},{97,65},{2,34}... | collective-permute-start | bytes 786440 | tf_op jit(solution)/shard_map/ppermute | solution.py:23
  23.8 10.3 %slice-start = ((s8[6815744]{0:T(1024)(128)(4,1)}), s8[4194304]{0:T(1024)(128)(4,1)S(1)}, s32[]{:S(2)}) async-start(s8[6815744]{0:T(1024)(128)(4,1)} %bitcast.206), calls=%async_computation.1 | async-start | bytes 8388608
  28.0 6.1 %slice-start.1 = ((s8[6815744]{0:T(1024)(128)(4,1)}), s8[2621440]{0:T(1024)(128)(4,1)S(1)}, s32[]{:S(2)}) async-start(s8[6815744]{0:T(1024)(128)(4,1)} %bitcast.206), calls=%async_computation.2 | async-start | bytes 5242880
  29.5 15.1 %collective-permute-start = (f16[2,64,3328]{2,1,0:T(8,128)(2,1)S(1)}, f16[2,64,3328]{2,1,0:T(8,128)(2,1)S(1)}, u32[]{:S(2)}, u32[]{:S(2)}) collective-permute-start(f16[2,64,3328]{2,1,0:T(8,128)(2,1)S(1)} %pad_maximum_fusion), channel_id=1, source_target_pairs={{0,1},{1,0},{2,3},{3,2},{4,5},{5,4},{6,7},{7,6},{8,9},{9,8},{10,11... | collective-permute-start | bytes 2555912 | tf_op jit(solution)/shard_map/ppermute | solution.py:23
  41.0 4.8 %collective-permute-start.10 = (f16[2,64,3328]{2,1,0:T(8,128)(2,1)S(1)}, f16[2,64,3328]{2,1,0:T(8,128)(2,1)S(1)}, u32[]{:S(2)}, u32[]{:S(2)}) collective-permute-start(f16[2,64,3328]{2,1,0:T(8,128)(2,1)S(1)} %pad_maximum_fusion.3), channel_id=1, source_target_pairs={{0,1},{1,0},{2,3},{3,2},{4,5},{5,4},{6,7},{7,6},{8,9},{9,8},{10,11... | collective-permute-start | bytes 2555912 | tf_op jit(solution)/shard_map/ppermute | solution.py:23
  43.4 3.3 %collective-permute-start.7 = (f16[2,64,3328]{2,1,0:T(8,128)(2,1)S(1)}, f16[2,64,3328]{2,1,0:T(8,128)(2,1)S(1)}, u32[]{:S(2)}, u32[]{:S(2)}) collective-permute-start(f16[2,64,3328]{2,1,0:T(8,128)(2,1)S(1)} %pad_maximum_fusion.2), channel_id=1, source_target_pairs={{0,1},{1,0},{2,3},{3,2},{4,5},{5,4},{6,7},{7,6},{8,9},{9,8},{10,11... | collective-permute-start | bytes 2555912 | tf_op jit(solution)/shard_map/ppermute | solution.py:23
  43.8 5.0 %collective-permute-start.4 = (f16[2,64,3328]{2,1,0:T(8,128)(2,1)S(1)}, f16[2,64,3328]{2,1,0:T(8,128)(2,1)S(1)}, u32[]{:S(2)}, u32[]{:S(2)}) collective-permute-start(f16[2,64,3328]{2,1,0:T(8,128)(2,1)S(1)} %pad_maximum_fusion.1), channel_id=1, source_target_pairs={{0,1},{1,0},{2,3},{3,2},{4,5},{5,4},{6,7},{7,6},{8,9},{9,8},{10,11... | collective-permute-start | bytes 2555912 | tf_op jit(solution)/shard_map/ppermute | solution.py:23
  45.0 8.3 %collective-permute-start.1 = (f16[2,32,3328]{2,1,0:T(8,128)(2,1)S(1)}, f16[2,32,3328]{2,1,0:T(8,128)(2,1)S(1)}, u32[]{:S(2)}, u32[]{:S(2)}) collective-permute-start(f16[2,32,3328]{2,1,0:T(8,128)(2,1)S(1)} %pad_maximum_fusion.4), channel_id=1, source_target_pairs={{0,4},{1,13},{4,0},{5,9},{8,12},{9,5},{12,8},{13,1},{2,6},{3,15},{... | collective-permute-start | bytes 1277960 | tf_op jit(solution)/shard_map/ppermute | solution.py:23
  46.3 14.6 %collective-permute-start.11 = (f16[2,64,1664]{2,1,0:T(8,128)(2,1)S(1)}, f16[2,64,1664]{2,1,0:T(8,128)(2,1)S(1)}, u32[]{:S(2)}, u32[]{:S(2)}) collective-permute-start(f16[2,64,1664]{2,1,0:T(8,128)(2,1)S(1)} %pad_maximum_fusion.7), channel_id=1, source_target_pairs={{0,2},{2,0},{1,3},{3,1},{4,6},{6,4},{5,7},{7,5},{8,10},{10,8},{9,1... | collective-permute-start | bytes 1277960 | tf_op jit(solution)/shard_map/ppermute | solution.py:23
  47.1 14.1 %collective-permute-start.8 = (f16[2,32,3328]{2,1,0:T(8,128)(2,1)S(1)}, f16[2,32,3328]{2,1,0:T(8,128)(2,1)S(1)}, u32[]{:S(2)}, u32[]{:S(2)}) collective-permute-start(f16[2,32,3328]{2,1,0:T(8,128)(2,1)S(1)} %pad_maximum_fusion.6), channel_id=1, source_target_pairs={{0,4},{1,13},{4,0},{5,9},{8,12},{9,5},{12,8},{13,1},{2,6},{3,15},{... | collective-permute-start | bytes 1277960 | tf_op jit(solution)/shard_map/ppermute | solution.py:23
  53.5 7.4 %collective-permute-start.2 = (f16[2,16,3328]{2,1,0:T(8,128)(2,1)S(1)}, f16[2,16,3328]{2,1,0:T(8,128)(2,1)S(1)}, u32[]{:S(2)}, u32[]{:S(2)}) collective-permute-start(f16[2,16,3328]{2,1,0:T(8,128)(2,1)S(1)} %pad_maximum_fusion.12), channel_id=1, source_target_pairs={{0,12},{1,5},{4,8},{5,1},{8,4},{9,13},{12,0},{13,9},{2,14},{3,7},{... | collective-permute-start | bytes 638984 | tf_op jit(solution)/shard_map/ppermute | solution.py:23
  53.7 11.0 %collective-permute-start.5 = (f16[2,32,3328]{2,1,0:T(8,128)(2,1)S(1)}, f16[2,32,3328]{2,1,0:T(8,128)(2,1)S(1)}, u32[]{:S(2)}, u32[]{:S(2)}) collective-permute-start(f16[2,32,3328]{2,1,0:T(8,128)(2,1)S(1)} %pad_maximum_fusion.5), channel_id=1, source_target_pairs={{0,4},{1,13},{4,0},{5,9},{8,12},{9,5},{12,8},{13,1},{2,6},{3,15},{... | collective-permute-start | bytes 1277960 | tf_op jit(solution)/shard_map/ppermute | solution.py:23
  61.1 6.0 %collective-permute-start.31 = (f16[2,32,1664]{2,1,0:T(8,128)(2,1)S(1)}, f16[2,32,1664]{2,1,0:T(8,128)(2,1)S(1)}, u32[]{:S(2)}, u32[]{:S(2)}) collective-permute-start(f16[2,32,1664]{2,1,0:T(8,128)(2,1)S(1)} %pad_maximum_fusion.15), channel_id=1, source_target_pairs={{0,4},{1,13},{4,0},{5,9},{8,12},{9,5},{12,8},{13,1},{2,6},{3,15},{... | collective-permute-start | bytes 638984 | tf_op jit(solution)/shard_map/ppermute | solution.py:23
  61.5 5.9 %collective-permute-start.24 = (f16[2,16,3328]{2,1,0:T(8,128)(2,1)S(1)}, f16[2,16,3328]{2,1,0:T(8,128)(2,1)S(1)}, u32[]{:S(2)}, u32[]{:S(2)}) collective-permute-start(f16[2,16,3328]{2,1,0:T(8,128)(2,1)S(1)} %pad_maximum_fusion.14), channel_id=1, source_target_pairs={{0,12},{1,5},{4,8},{5,1},{8,4},{9,13},{12,0},{13,9},{2,14},{3,7},{... | collective-permute-start | bytes 638984 | tf_op jit(solution)/shard_map/ppermute | solution.py:23
  64.8 36.1 %slice-start.4 = ((s8[6815744]{0:T(1024)(128)(4,1)}), s8[4194304]{0:T(1024)(128)(4,1)S(1)}, s32[]{:S(2)}) async-start(s8[6815744]{0:T(1024)(128)(4,1)} %bitcast.210), calls=%async_computation.5 | async-start | bytes 8388608
  64.9 6.2 %collective-permute-start.17 = (f16[2,16,3328]{2,1,0:T(8,128)(2,1)S(1)}, f16[2,16,3328]{2,1,0:T(8,128)(2,1)S(1)}, u32[]{:S(2)}, u32[]{:S(2)}) collective-permute-start(f16[2,16,3328]{2,1,0:T(8,128)(2,1)S(1)} %pad_maximum_fusion.13), channel_id=1, source_target_pairs={{0,12},{1,5},{4,8},{5,1},{8,4},{9,13},{12,0},{13,9},{2,14},{3,7},{... | collective-permute-start | bytes 638984 | tf_op jit(solution)/shard_map/ppermute | solution.py:23
  65.1 6.8 %collective-permute-start.12 = (f16[2,16,3328]{2,1,0:T(8,128)(2,1)S(1)}, f16[2,16,3328]{2,1,0:T(8,128)(2,1)S(1)}, u32[]{:S(2)}, u32[]{:S(2)}) collective-permute-start(f16[2,16,3328]{2,1,0:T(8,128)(2,1)S(1)} %pad_maximum_fusion.16), channel_id=1, source_target_pairs={{0,2},{2,0},{1,3},{3,1},{4,6},{6,4},{5,7},{7,5},{8,10},{10,8},{9,1... | collective-permute-start | bytes 638984 | tf_op jit(solution)/shard_map/ppermute | solution.py:23
  67.2 5.2 %collective-permute-start.32 = (f16[2,16,1664]{2,1,0:T(8,128)(2,1)S(1)}, f16[2,16,1664]{2,1,0:T(8,128)(2,1)S(1)}, u32[]{:S(2)}, u32[]{:S(2)}) collective-permute-start(f16[2,16,1664]{2,1,0:T(8,128)(2,1)S(1)} %pad_maximum_fusion.24), channel_id=1, source_target_pairs={{0,12},{1,5},{4,8},{5,1},{8,4},{9,13},{12,0},{13,9},{2,14},{3,7},{... | collective-permute-start | bytes 319496 | tf_op jit(solution)/shard_map/ppermute | solution.py:23
  67.5 15.1 %collective-permute-start.25 = (f16[2,16,3328]{2,1,0:T(8,128)(2,1)S(1)}, f16[2,16,3328]{2,1,0:T(8,128)(2,1)S(1)}, u32[]{:S(2)}, u32[]{:S(2)}) collective-permute-start(f16[2,16,3328]{2,1,0:T(8,128)(2,1)S(1)} %pad_maximum_fusion.20), channel_id=1, source_target_pairs={{0,2},{2,0},{1,3},{3,1},{4,6},{6,4},{5,7},{7,5},{8,10},{10,8},{9,1... | collective-permute-start | bytes 638984 | tf_op jit(solution)/shard_map/ppermute | solution.py:23
  71.2 29.6 %slice-start.5 = ((s8[6815744]{0:T(1024)(128)(4,1)}), s8[2621440]{0:T(1024)(128)(4,1)S(1)}, s32[]{:S(2)}) async-start(s8[6815744]{0:T(1024)(128)(4,1)} %bitcast.210), calls=%async_computation.6 | async-start | bytes 5242880
  71.3 11.6 %collective-permute-start.18 = (f16[2,16,3328]{2,1,0:T(8,128)(2,1)S(1)}, f16[2,16,3328]{2,1,0:T(8,128)(2,1)S(1)}, u32[]{:S(2)}, u32[]{:S(2)}) collective-permute-start(f16[2,16,3328]{2,1,0:T(8,128)(2,1)S(1)} %pad_maximum_fusion.18), channel_id=1, source_target_pairs={{0,2},{2,0},{1,3},{3,1},{4,6},{6,4},{5,7},{7,5},{8,10},{10,8},{9,1... | collective-permute-start | bytes 638984 | tf_op jit(solution)/shard_map/ppermute | solution.py:23
  72.1 3.9 %collective-permute-start.13 = (bf16[16,3328]{1,0:T(8,128)(2,1)S(1)}, bf16[16,3328]{1,0:T(8,128)(2,1)S(1)}, u32[]{:S(2)}, u32[]{:S(2)}) collective-permute-start(bf16[16,3328]{1,0:T(8,128)(2,1)S(1)} %fusion.59), channel_id=1, source_target_pairs={{0,12},{1,5},{4,8},{5,1},{8,4},{9,13},{12,0},{13,9},{2,14},{3,7},{... | collective-permute-start | bytes 319496 | tf_op jit(solution)/shard_map/ppermute | solution.py:23
  72.5 6.9 %collective-permute-start.33 = (bf16[16,1664]{1,0:T(8,128)(2,1)S(1)}, bf16[16,1664]{1,0:T(8,128)(2,1)S(1)}, u32[]{:S(2)}, u32[]{:S(2)}) collective-permute-start(bf16[16,1664]{1,0:T(8,128)(2,1)S(1)} %fusion.77), channel_id=1, source_target_pairs={{0,2},{2,0},{1,3},{3,1},{4,6},{6,4},{5,7},{7,5},{8,10},{10,8},{9,1... | collective-permute-start | bytes 159752 | tf_op jit(solution)/shard_map/ppermute | solution.py:23
  76.0 14.5 %collective-permute-start.14 = (bf16[32,3328]{1,0:T(8,128)(2,1)S(1)}, bf16[32,3328]{1,0:T(8,128)(2,1)S(1)}, u32[]{:S(2)}, u32[]{:S(2)}) collective-permute-start(bf16[32,3328]{1,0:T(8,128)(2,1)S(1)} %pad_maximum_fusion.17), channel_id=1, source_target_pairs={{0,4},{1,13},{4,0},{5,9},{8,12},{9,5},{12,8},{13,1},{2,6},{3,15},{... | collective-permute-start | bytes 638984 | tf_op jit(solution)/shard_map/ppermute | solution.py:23
  79.4 5.7 %collective-permute-start.34 = (bf16[16,3328]{1,0:T(8,128)(2,1)S(1)}, bf16[16,3328]{1,0:T(8,128)(2,1)S(1)}, u32[]{:S(2)}, u32[]{:S(2)}) collective-permute-start(bf16[16,3328]{1,0:T(8,128)(2,1)S(1)} %pad_maximum_fusion.25), channel_id=1, source_target_pairs={{0,12},{1,5},{4,8},{5,1},{8,4},{9,13},{12,0},{13,9},{2,14},{3,7},{... | collective-permute-start | bytes 319496 | tf_op jit(solution)/shard_map/ppermute | solution.py:23
  82.7 4.7 %collective-permute-start.26 = (bf16[16,3328]{1,0:T(8,128)(2,1)S(1)}, bf16[16,3328]{1,0:T(8,128)(2,1)S(1)}, u32[]{:S(2)}, u32[]{:S(2)}) collective-permute-start(bf16[16,3328]{1,0:T(8,128)(2,1)S(1)} %fusion.55), channel_id=1, source_target_pairs={{0,12},{1,5},{4,8},{5,1},{8,4},{9,13},{12,0},{13,9},{2,14},{3,7},{... | collective-permute-start | bytes 319496 | tf_op jit(solution)/shard_map/ppermute | solution.py:23
  82.9 6.7 %collective-permute-start.19 = (bf16[16,3328]{1,0:T(8,128)(2,1)S(1)}, bf16[16,3328]{1,0:T(8,128)(2,1)S(1)}, u32[]{:S(2)}, u32[]{:S(2)}) collective-permute-start(bf16[16,3328]{1,0:T(8,128)(2,1)S(1)} %fusion.57), channel_id=1, source_target_pairs={{0,12},{1,5},{4,8},{5,1},{8,4},{9,13},{12,0},{13,9},{2,14},{3,7},{... | collective-permute-start | bytes 319496 | tf_op jit(solution)/shard_map/ppermute | solution.py:23
  85.1 9.9 %collective-permute-start.35 = (bf16[32,3328]{1,0:T(8,128)(2,1)S(1)}, bf16[32,3328]{1,0:T(8,128)(2,1)S(1)}, u32[]{:S(2)}, u32[]{:S(2)}) collective-permute-start(bf16[32,3328]{1,0:T(8,128)(2,1)S(1)} %pad_maximum_fusion.22), channel_id=1, source_target_pairs={{0,4},{1,13},{4,0},{5,9},{8,12},{9,5},{12,8},{13,1},{2,6},{3,15},{... | collective-permute-start | bytes 638984 | tf_op jit(solution)/shard_map/ppermute | solution.py:23
  87.4 8.2 %collective-permute-start.27 = (bf16[32,3328]{1,0:T(8,128)(2,1)S(1)}, bf16[32,3328]{1,0:T(8,128)(2,1)S(1)}, u32[]{:S(2)}, u32[]{:S(2)}) collective-permute-start(bf16[32,3328]{1,0:T(8,128)(2,1)S(1)} %pad_maximum_fusion.21), channel_id=1, source_target_pairs={{0,4},{1,13},{4,0},{5,9},{8,12},{9,5},{12,8},{13,1},{2,6},{3,15},{... | collective-permute-start | bytes 638984 | tf_op jit(solution)/shard_map/ppermute | solution.py:23
  89.7 8.9 %collective-permute-start.20 = (bf16[32,3328]{1,0:T(8,128)(2,1)S(1)}, bf16[32,3328]{1,0:T(8,128)(2,1)S(1)}, u32[]{:S(2)}, u32[]{:S(2)}) collective-permute-start(bf16[32,3328]{1,0:T(8,128)(2,1)S(1)} %pad_maximum_fusion.19), channel_id=1, source_target_pairs={{0,4},{1,13},{4,0},{5,9},{8,12},{9,5},{12,8},{13,1},{2,6},{3,15},{... | collective-permute-start | bytes 638984 | tf_op jit(solution)/shard_map/ppermute | solution.py:23
  90.6 10.3 %collective-permute-start.15 = (bf16[64,3328]{1,0:T(8,128)(2,1)S(1)}, bf16[64,3328]{1,0:T(8,128)(2,1)S(1)}, u32[]{:S(2)}, u32[]{:S(2)}) collective-permute-start(bf16[64,3328]{1,0:T(8,128)(2,1)S(1)} %pad_maximum_fusion.8), channel_id=1, source_target_pairs={{0,1},{1,0},{2,3},{3,2},{4,5},{5,4},{6,7},{7,6},{8,9},{9,8},{10,11... | collective-permute-start | bytes 1277960 | tf_op jit(solution)/shard_map/ppermute | solution.py:23
  95.1 8.2 %collective-permute-start.36 = (bf16[64,3328]{1,0:T(8,128)(2,1)S(1)}, bf16[64,3328]{1,0:T(8,128)(2,1)S(1)}, u32[]{:S(2)}, u32[]{:S(2)}) collective-permute-start(bf16[64,3328]{1,0:T(8,128)(2,1)S(1)} %pad_maximum_fusion.11), channel_id=1, source_target_pairs={{0,1},{1,0},{2,3},{3,2},{4,5},{5,4},{6,7},{7,6},{8,9},{9,8},{10,11... | collective-permute-start | bytes 1277960 | tf_op jit(solution)/shard_map/ppermute | solution.py:23
  95.7 13.2 %collective-permute-start.28 = (bf16[64,3328]{1,0:T(8,128)(2,1)S(1)}, bf16[64,3328]{1,0:T(8,128)(2,1)S(1)}, u32[]{:S(2)}, u32[]{:S(2)}) collective-permute-start(bf16[64,3328]{1,0:T(8,128)(2,1)S(1)} %pad_maximum_fusion.10), channel_id=1, source_target_pairs={{0,1},{1,0},{2,3},{3,2},{4,5},{5,4},{6,7},{7,6},{8,9},{9,8},{10,11... | collective-permute-start | bytes 1277960 | tf_op jit(solution)/shard_map/ppermute | solution.py:23
  98.6 12.5 %collective-permute-start.21 = (bf16[64,3328]{1,0:T(8,128)(2,1)S(1)}, bf16[64,3328]{1,0:T(8,128)(2,1)S(1)}, u32[]{:S(2)}, u32[]{:S(2)}) collective-permute-start(bf16[64,3328]{1,0:T(8,128)(2,1)S(1)} %pad_maximum_fusion.9), channel_id=1, source_target_pairs={{0,1},{1,0},{2,3},{3,2},{4,5},{5,4},{6,7},{7,6},{8,9},{9,8},{10,11... | collective-permute-start | bytes 1277960 | tf_op jit(solution)/shard_map/ppermute | solution.py:23
  102.0 12.8 %collective-permute-start.16 = (bf16[64,1024]{1,0:T(8,128)(2,1)S(1)}, bf16[64,1024]{1,0:T(8,128)(2,1)S(1)}, u32[]{:S(2)}, u32[]{:S(2)}) collective-permute-start(bf16[64,1024]{1,0:T(8,128)(2,1)S(1)} %select_convert_fusion.6), channel_id=1, source_target_pairs={{0,16},{16,0},{32,48},{48,32},{64,80},{80,64},{96,112},{112,96},{1... | collective-permute-start | bytes 393224 | tf_op jit(solution)/shard_map/ppermute | solution.py:23
  104.4 12.3 %collective-permute-start.38 = (bf16[64,1024]{1,0:T(8,128)(2,1)S(1)}, bf16[64,1024]{1,0:T(8,128)(2,1)S(1)}, u32[]{:S(2)}, u32[]{:S(2)}) collective-permute-start(bf16[64,1024]{1,0:T(8,128)(2,1)S(1)} %get-tuple-element.118), channel_id=1, source_target_pairs={{0,112},{16,96},{32,80},{48,64},{64,48},{80,32},{96,16},{112,0},{1... | collective-permute-start | bytes 393224 | tf_op jit(solution)/shard_map/ppermute | solution.py:23
  108.7 9.4 %collective-permute-start.37 = (bf16[64,1024]{1,0:T(8,128)(2,1)S(1)}, bf16[64,1024]{1,0:T(8,128)(2,1)S(1)}, u32[]{:S(2)}, u32[]{:S(2)}) collective-permute-start(bf16[64,1024]{1,0:T(8,128)(2,1)S(1)} %get-tuple-element.117), channel_id=1, source_target_pairs={{0,96},{32,64},{64,32},{96,0},{1,97},{33,65},{65,33},{97,1},{2,98}... | collective-permute-start | bytes 393224 | tf_op jit(solution)/shard_map/ppermute | solution.py:23
  110.0 8.1 %collective-permute-start.30 = (bf16[64,1024]{1,0:T(8,128)(2,1)S(1)}, bf16[64,1024]{1,0:T(8,128)(2,1)S(1)}, u32[]{:S(2)}, u32[]{:S(2)}) collective-permute-start(bf16[64,1024]{1,0:T(8,128)(2,1)S(1)} %get-tuple-element.111), channel_id=1, source_target_pairs={{0,80},{16,64},{32,112},{48,96},{64,16},{80,0},{96,48},{112,32},{1... | collective-permute-start | bytes 393224 | tf_op jit(solution)/shard_map/ppermute | solution.py:23
  111.1 8.2 %collective-permute-start.29 = (bf16[64,1024]{1,0:T(8,128)(2,1)S(1)}, bf16[64,1024]{1,0:T(8,128)(2,1)S(1)}, u32[]{:S(2)}, u32[]{:S(2)}) collective-permute-start(bf16[64,1024]{1,0:T(8,128)(2,1)S(1)} %get-tuple-element.110), channel_id=1, source_target_pairs={{0,64},{32,96},{64,0},{96,32},{1,65},{33,97},{65,1},{97,33},{2,66}... | collective-permute-start | bytes 393224 | tf_op jit(solution)/shard_map/ppermute | solution.py:23
  114.8 9.0 %collective-permute-start.23 = (bf16[64,1024]{1,0:T(8,128)(2,1)S(1)}, bf16[64,1024]{1,0:T(8,128)(2,1)S(1)}, u32[]{:S(2)}, u32[]{:S(2)}) collective-permute-start(bf16[64,1024]{1,0:T(8,128)(2,1)S(1)} %get-tuple-element.104), channel_id=1, source_target_pairs={{0,48},{16,32},{32,16},{48,0},{64,112},{80,96},{96,80},{112,64},{1... | collective-permute-start | bytes 393224 | tf_op jit(solution)/shard_map/ppermute | solution.py:23
  116.7 8.3 %collective-permute-start.22 = (bf16[64,1024]{1,0:T(8,128)(2,1)S(1)}, bf16[64,1024]{1,0:T(8,128)(2,1)S(1)}, u32[]{:S(2)}, u32[]{:S(2)}) collective-permute-start(bf16[64,1024]{1,0:T(8,128)(2,1)S(1)} %get-tuple-element.103), channel_id=1, source_target_pairs={{0,32},{32,0},{64,96},{96,64},{1,33},{33,1},{65,97},{97,65},{2,34}... | collective-permute-start | bytes 393224 | tf_op jit(solution)/shard_map/ppermute | solution.py:23

commit v10 on v7

--- a/solution.py
+++ b/solution.py
@@ -39,7 +39,7 @@
     swap_second = permute(("y", "core"), (4, 2), lambda y, c: (y ^ (1 if c else 3), c))
     swap_x = {e: permute(("x",), (4,), lambda x, e=e: (x ^ e,)) for e in (1, 2, 3)}
     swap_row = {
-        e: permute(("x", "z_hi"), (4, 2), lambda x, z, e=e: (x ^ e, z ^ 1)) for e in range(4)
+        e: permute(("x", "z_hi"), (4, 2), lambda x, z, e=e: (x ^ e, z ^ 1)) for e in range(3)
     }
 
     features = tokens.shape[1] // 16
@@ -117,20 +117,25 @@
         elif s == 8:
             both = jnp.concatenate((tie(st["flight"]), st["hidden"]))
             mixed = product(both, down_weight)
-            same, cross = parted(mixed)
             if e == 0:
-                same, cross = tie(same, cross.astype(BF16))
-                arrived.append(same)
+                whole.append(tie(mixed))
+            elif e == 3:
+                whole.append(swap_x[e](tie(mixed.astype(BF16))).astype(F32))
             else:
+                same, cross = parted(mixed)
                 same, cross = tie(same.astype(BF16), cross.astype(BF16))
                 arrived.append(swap_x[e](same).astype(F32))
-            arrived.append(swap_row[e](cross).astype(F32))
+                arrived.append(swap_row[e](cross).astype(F32))
 
+    whole = []
     for s in (-1, 0, 2, 3, 4, 5, 6, 7, 8):
         for e in (0, 2, 1, 3):
             if e or s >= 0:
                 step(e, s)
 
+    same, cross = parted(sum(whole))
+    same, cross = tie(same, cross.astype(BF16))
+    arrived += [same, swap_row[0](cross).astype(F32)]
     out = sum(arrived).astype(BF16).reshape(4, 16, -1)
     first = jnp.where(z_hi == 0, 1, 3)
     blocks = []

time: 124 us -> 120 us (0.968)
  waiting for transfers between devices: 36.7 us -> 34.4 us
  starting transfers between devices: 62.7 us -> 61.3 us
    ppermute x39 -> x38, waiting for transfers between devices: 27.9 us -> 25.6 us  [permute(): return lambda v: lax.ppermute(v, axes, pairs)]
    ppermute x39 -> x38, starting transfers between devices: 53.1 us -> 51.7 us  [permute(): return lambda v: lax.ppermute(v, axes, pairs)]
  transfers between devices with their start and end apart: 40 -> 39, of which waited for: 15 -> 15; matrix products, arithmetic and copies ran while one was open for 17% -> 17% of each run, Pallas kernels for 0% -> 0%
where the time goes in v10:
time: 120 us
  starting transfers between devices  61.3 us (51%)
  waiting for transfers between devices  34.4 us (29%)
  matrix products  15.8 us (13%)
  other arithmetic  5.8 us (5%)
  local copies, waits for them, and re-layouts  2.01 us (2%)
    ppermute x38, starting transfers between devices, permute(): return lambda v: lax.ppermute(v, axes, pairs)  51.7 us
    ppermute x38, waiting for transfers between devices, permute(): return lambda v: lax.ppermute(v, axes, pairs)  25.6 us
    dot_general x12, matrix products, product(): return jnp.dot(rows, weight, preferred_element_type=F32)  15.8 us
    all_to_all x1, starting transfers between devices, per_device(): lax.all_to_all(blocks, AXES[1:], split_axis=0, concat_axis=0, tiled=True)  9.6 us
    all_to_all x1, waiting for transfers between devices, per_device(): lax.all_to_all(blocks, AXES[1:], split_axis=0, concat_axis=0, tiled=True)  8.79 us
  transfers between devices with their start and end apart: 39, of which 15 were waited for; matrix products, arithmetic and copies ran while one was open for 17% of the time, Pallas kernels for 0%

profile of v10, /device:TPU:1, one launch (start us, length us, event | category | flops | bytes accessed | tf_op | source)
XLA Modules:
  0.0 120.2 jit_solution(9181348742865400259)
XLA Ops:
  0.0 0.9 broadcast_in_dim.7
  1.8 9.6 %all-to-all-start = ((bf16[32,4,1024]{2,1,0:T(4,128)(2,1)}), bf16[32,4,1024]{2,1,0:T(4,128)(2,1)S(1)}, u32[]{:S(2)}, u32[]{:S(2)}) async-start(bf16[32,4,1024]{2,1,0:T(4,128)(2,1)} %all_to_all.6), calls=%async_computation | async-start | bytes 524288 | tf_op jit(solution)/shard_map/all_to_all | solution.py:48
  11.5 8.8 %all-to-all-done = bf16[32,4,1024]{2,1,0:T(4,128)(2,1)S(1)} async-done(((bf16[32,4,1024]{2,1,0:T(4,128)(2,1)}), bf16[32,4,1024]{2,1,0:T(4,128)(2,1)S(1)}, u32[]{:S(2)}, u32[]{:S(2)}) %all-to-all-start) | async-done | bytes 262176 | tf_op jit(solution)/shard_map/all_to_all | solution.py:48
  20.5 2.6 %collective-permute-start.27 = (bf16[128,1024]{1,0:T(8,128)(2,1)S(1)}, bf16[128,1024]{1,0:T(8,128)(2,1)S(1)}, u32[]{:S(2)}, u32[]{:S(2)}) collective-permute-start(bf16[128,1024]{1,0:T(8,128)(2,1)S(1)} %bitcast_dynamic-update-slice_fusion), channel_id=1, source_target_pairs={{0,96},{32,64},{64,32},{96,0},{1,97},{33,65},{65,33},{97,1},{2,98}... | collective-permute-start | bytes 786440 | tf_op jit(solution)/shard_map/ppermute | solution.py:23
  23.1 1.4 %collective-permute-start = (bf16[128,1024]{1,0:T(8,128)(2,1)S(1)}, bf16[128,1024]{1,0:T(8,128)(2,1)S(1)}, u32[]{:S(2)}, u32[]{:S(2)}) collective-permute-start(bf16[128,1024]{1,0:T(8,128)(2,1)S(1)} %bitcast_dynamic-update-slice_fusion), channel_id=1, source_target_pairs={{0,64},{32,96},{64,0},{96,32},{1,65},{33,97},{65,1},{97,33},{2,66}... | collective-permute-start | bytes 786440 | tf_op jit(solution)/shard_map/ppermute | solution.py:23
  24.5 4.1 %fusion.87 = f32[128,3328]{1,0:T(8,128)S(1)} fusion(bf16[128,1024]{1,0:T(8,128)(2,1)S(1)} %bitcast_dynamic-update-slice_fusion, bf16[1024,3328]{1,0:T(8,128)(2,1)} %param.5), kind=kOutput, calls=%fused_computation.202 | convolution fusion | flops 872415232 | bytes 8781824 | tf_op jit(solution)/shard_map/dot_general | solution.py:74
  28.6 1.1 fusion.88
  30.1 1.9 %collective-permute-start.20 = (f16[2,64,3328]{2,1,0:T(8,128)(2,1)S(1)}, f16[2,64,3328]{2,1,0:T(8,128)(2,1)S(1)}, u32[]{:S(2)}, u32[]{:S(2)}) collective-permute-start(f16[2,64,3328]{2,1,0:T(8,128)(2,1)S(1)} %pad_maximum_fusion.2), channel_id=1, source_target_pairs={{0,1},{1,0},{2,3},{3,2},{4,5},{5,4},{6,7},{7,6},{8,9},{9,8},{10,11... | collective-permute-start | bytes 2555912 | tf_op jit(solution)/shard_map/ppermute | solution.py:23
  32.0 1.1 fusion.89
  33.0 1.1 fusion.90
  34.1 1.1 fusion.85
  35.2 1.1 fusion.86
  36.3 1.1 fusion.83
  37.3 1.1 fusion.84
  38.8 1.1 collective-permute-start.28
  44.0 1.8 %collective-permute-start.12 = (f16[2,32,3328]{2,1,0:T(8,128)(2,1)S(1)}, f16[2,32,3328]{2,1,0:T(8,128)(2,1)S(1)}, u32[]{:S(2)}, u32[]{:S(2)}) collective-permute-start(f16[2,32,3328]{2,1,0:T(8,128)(2,1)S(1)} %pad_maximum_fusion.6), channel_id=1, source_target_pairs={{0,4},{1,13},{4,0},{5,9},{8,12},{9,5},{12,8},{13,1},{2,6},{3,15},{... | collective-permute-start | bytes 1277960 | tf_op jit(solution)/shard_map/ppermute | solution.py:23
  46.0 4.1 %collective-permute-done.21 = f16[2,32,3328]{2,1,0:T(8,128)(2,1)S(1)} collective-permute-done((f16[2,32,3328]{2,1,0:T(8,128)(2,1)S(1)}, f16[2,32,3328]{2,1,0:T(8,128)(2,1)S(1)}, u32[]{:S(2)}, u32[]{:S(2)}) %collective-permute-start.21) | collective-permute-done | bytes 426016 | tf_op jit(solution)/shard_map/ppermute | solution.py:23
  51.4 6.4 %collective-permute-done.22 = f16[2,16,3328]{2,1,0:T(8,128)(2,1)S(1)} collective-permute-done((f16[2,16,3328]{2,1,0:T(8,128)(2,1)S(1)}, f16[2,16,3328]{2,1,0:T(8,128)(2,1)S(1)}, u32[]{:S(2)}, u32[]{:S(2)}) %collective-permute-start.22) | collective-permute-done | bytes 213024 | tf_op jit(solution)/shard_map/ppermute | solution.py:23
  59.3 2.2 %collective-permute-done.2 = f16[2,32,3328]{2,1,0:T(8,128)(2,1)S(1)} collective-permute-done((f16[2,32,3328]{2,1,0:T(8,128)(2,1)S(1)}, f16[2,32,3328]{2,1,0:T(8,128)(2,1)S(1)}, u32[]{:S(2)}, u32[]{:S(2)}) %collective-permute-start.2) | collective-permute-done | bytes 426016 | tf_op jit(solution)/shard_map/ppermute | solution.py:23
  62.8 1.9 %collective-permute-start.24 = (bf16[16,3328]{1,0:T(8,128)(2,1)S(1)}, bf16[16,3328]{1,0:T(8,128)(2,1)S(1)}, u32[]{:S(2)}, u32[]{:S(2)}) collective-permute-start(bf16[16,3328]{1,0:T(8,128)(2,1)S(1)} %fusion.54), channel_id=1, source_target_pairs={{0,12},{1,5},{4,8},{5,1},{8,4},{9,13},{12,0},{13,9},{2,14},{3,7},{... | collective-permute-start | bytes 319496 | tf_op jit(solution)/shard_map/ppermute | solution.py:23
  65.2 1.0 collective-permute-start.14
  66.2 2.7 %collective-permute-done.3 = f16[2,16,3328]{2,1,0:T(8,128)(2,1)S(1)} collective-permute-done((f16[2,16,3328]{2,1,0:T(8,128)(2,1)S(1)}, f16[2,16,3328]{2,1,0:T(8,128)(2,1)S(1)}, u32[]{:S(2)}, u32[]{:S(2)}) %collective-permute-start.3) | collective-permute-done | bytes 213024 | tf_op jit(solution)/shard_map/ppermute | solution.py:23
  70.0 1.1 collective-permute-done.31
  71.2 0.9 collective-permute-start.32
  72.1 2.4 %collective-permute-start.25 = (bf16[32,3328]{1,0:T(8,128)(2,1)S(1)}, bf16[32,3328]{1,0:T(8,128)(2,1)S(1)}, u32[]{:S(2)}, u32[]{:S(2)}) collective-permute-start(bf16[32,3328]{1,0:T(8,128)(2,1)S(1)} %pad_maximum_fusion.20), channel_id=1, source_target_pairs={{0,4},{1,13},{4,0},{5,9},{8,12},{9,5},{12,8},{13,1},{2,6},{3,15},{... | collective-permute-start | bytes 638984 | tf_op jit(solution)/shard_map/ppermute | solution.py:23
  74.6 0.9 collective-permute-done.32
  75.5 1.1 collective-permute-start.33
  77.4 1.1 collective-permute-start.5
  78.4 1.0 collective-permute-done.33
  79.5 3.7 %collective-permute-start.34 = (bf16[32,3328]{1,0:T(8,128)(2,1)S(1)}, bf16[32,3328]{1,0:T(8,128)(2,1)S(1)}, u32[]{:S(2)}, u32[]{:S(2)}) collective-permute-start(bf16[32,3328]{1,0:T(8,128)(2,1)S(1)} %pad_maximum_fusion.22), channel_id=1, source_target_pairs={{0,4},{1,13},{4,0},{5,9},{8,12},{9,5},{12,8},{13,1},{2,6},{3,15},{... | collective-permute-start | bytes 638984 | tf_op jit(solution)/shard_map/ppermute | solution.py:23
  83.2 4.4 %collective-permute-start.26 = (bf16[64,3328]{1,0:T(8,128)(2,1)S(1)}, bf16[64,3328]{1,0:T(8,128)(2,1)S(1)}, u32[]{:S(2)}, u32[]{:S(2)}) collective-permute-start(bf16[64,3328]{1,0:T(8,128)(2,1)S(1)} %pad_maximum_fusion.9), channel_id=1, source_target_pairs={{0,1},{1,0},{2,3},{3,2},{4,5},{5,4},{6,7},{7,6},{8,9},{9,8},{10,11... | collective-permute-start | bytes 1277960 | tf_op jit(solution)/shard_map/ppermute | solution.py:23
  87.6 1.9 %collective-permute-start.16 = (bf16[32,3328]{1,0:T(8,128)(2,1)S(1)}, bf16[32,3328]{1,0:T(8,128)(2,1)S(1)}, u32[]{:S(2)}, u32[]{:S(2)}) collective-permute-start(bf16[32,3328]{1,0:T(8,128)(2,1)S(1)} %pad_maximum_fusion.17), channel_id=1, source_target_pairs={{0,4},{1,13},{4,0},{5,9},{8,12},{9,5},{12,8},{13,1},{2,6},{3,15},{... | collective-permute-start | bytes 638984 | tf_op jit(solution)/shard_map/ppermute | solution.py:23
  89.5 0.9 collective-permute-start.6
  90.5 2.9 %collective-permute-start.35 = (bf16[64,3328]{1,0:T(8,128)(2,1)S(1)}, bf16[64,3328]{1,0:T(8,128)(2,1)S(1)}, u32[]{:S(2)}, u32[]{:S(2)}) collective-permute-start(bf16[64,3328]{1,0:T(8,128)(2,1)S(1)} %pad_maximum_fusion.11), channel_id=1, source_target_pairs={{0,1},{1,0},{2,3},{3,2},{4,5},{5,4},{6,7},{7,6},{8,9},{9,8},{10,11... | collective-permute-start | bytes 1277960 | tf_op jit(solution)/shard_map/ppermute | solution.py:23
  93.6 2.1 %collective-permute-start.17 = (bf16[64,3328]{1,0:T(8,128)(2,1)S(1)}, bf16[64,3328]{1,0:T(8,128)(2,1)S(1)}, u32[]{:S(2)}, u32[]{:S(2)}) collective-permute-start(bf16[64,3328]{1,0:T(8,128)(2,1)S(1)} %pad_maximum_fusion.7), channel_id=1, source_target_pairs={{0,1},{1,0},{2,3},{3,2},{4,5},{5,4},{6,7},{7,6},{8,9},{9,8},{10,11... | collective-permute-start | bytes 1277960 | tf_op jit(solution)/shard_map/ppermute | solution.py:23
  95.9 2.3 %collective-permute-start.7 = (bf16[64,3328]{1,0:T(8,128)(2,1)S(1)}, bf16[64,3328]{1,0:T(8,128)(2,1)S(1)}, u32[]{:S(2)}, u32[]{:S(2)}) collective-permute-start(bf16[64,3328]{1,0:T(8,128)(2,1)S(1)} %pad_maximum_fusion.5), channel_id=1, source_target_pairs={{0,1},{1,0},{2,3},{3,2},{4,5},{5,4},{6,7},{7,6},{8,9},{9,8},{10,11... | collective-permute-start | bytes 1277960 | tf_op jit(solution)/shard_map/ppermute | solution.py:23
  98.2 1.0 fusion.16
  99.3 1.1 convolution_convert_fusion
  100.3 2.6 %collective-permute-start.36 = (bf16[128,1024]{1,0:T(8,128)(2,1)S(1)}, bf16[128,1024]{1,0:T(8,128)(2,1)S(1)}, u32[]{:S(2)}, u32[]{:S(2)}) collective-permute-start(bf16[128,1024]{1,0:T(8,128)(2,1)S(1)} %convolution_convert_fusion), channel_id=1, source_target_pairs={{0,96},{32,64},{64,32},{96,0},{1,97},{33,65},{65,33},{97,1},{2,98}... | collective-permute-start | bytes 786440 | tf_op jit(solution)/shard_map/ppermute | solution.py:23
  102.9 1.1 fusion.12
  104.1 2.6 %collective-permute-start.18 = (bf16[64,1024]{1,0:T(8,128)(2,1)S(1)}, bf16[64,1024]{1,0:T(8,128)(2,1)S(1)}, u32[]{:S(2)}, u32[]{:S(2)}) collective-permute-start(bf16[64,1024]{1,0:T(8,128)(2,1)S(1)} %get-tuple-element.85), channel_id=1, source_target_pairs={{0,32},{32,0},{64,96},{96,64},{1,33},{33,1},{65,97},{97,65},{2,34}... | collective-permute-start | bytes 393224 | tf_op jit(solution)/shard_map/ppermute | solution.py:23
  106.7 1.1 fusion.8
  107.8 1.2 %collective-permute-start.9 = (bf16[64,1024]{1,0:T(8,128)(2,1)S(1)}, bf16[64,1024]{1,0:T(8,128)(2,1)S(1)}, u32[]{:S(2)}, u32[]{:S(2)}) collective-permute-start(bf16[64,1024]{1,0:T(8,128)(2,1)S(1)} %get-tuple-element.72), channel_id=1, source_target_pairs={{0,80},{16,64},{32,112},{48,96},{64,16},{80,0},{96,48},{112,32},{1... | collective-permute-start | bytes 393224 | tf_op jit(solution)/shard_map/ppermute | solution.py:23
  109.0 3.1 %collective-permute-start.8 = (bf16[64,1024]{1,0:T(8,128)(2,1)S(1)}, bf16[64,1024]{1,0:T(8,128)(2,1)S(1)}, u32[]{:S(2)}, u32[]{:S(2)}) collective-permute-start(bf16[64,1024]{1,0:T(8,128)(2,1)S(1)} %get-tuple-element.71), channel_id=1, source_target_pairs={{0,64},{32,96},{64,0},{96,32},{1,65},{33,97},{65,1},{97,33},{2,66}... | collective-permute-start | bytes 393224 | tf_op jit(solution)/shard_map/ppermute | solution.py:23
  112.2 1.6 %collective-permute-start.37 = (bf16[64,1024]{1,0:T(8,128)(2,1)S(1)}, bf16[64,1024]{1,0:T(8,128)(2,1)S(1)}, u32[]{:S(2)}, u32[]{:S(2)}) collective-permute-start(bf16[64,1024]{1,0:T(8,128)(2,1)S(1)} %select_convert_fusion), channel_id=1, source_target_pairs={{0,16},{16,0},{32,48},{48,32},{64,80},{80,64},{96,112},{112,96},{1... | collective-permute-start | bytes 393224 | tf_op jit(solution)/shard_map/ppermute | solution.py:23
  113.8 2.6 %collective-permute-done.9 = bf16[64,1024]{1,0:T(8,128)(2,1)S(1)} collective-permute-done((bf16[64,1024]{1,0:T(8,128)(2,1)S(1)}, bf16[64,1024]{1,0:T(8,128)(2,1)S(1)}, u32[]{:S(2)}, u32[]{:S(2)}) %collective-permute-start.9) | collective-permute-done | bytes 131104 | tf_op jit(solution)/shard_map/ppermute | solution.py:23
  116.3 1.6 %collective-permute-done.8 = bf16[64,1024]{1,0:T(8,128)(2,1)S(1)} collective-permute-done((bf16[64,1024]{1,0:T(8,128)(2,1)S(1)}, bf16[64,1024]{1,0:T(8,128)(2,1)S(1)}, u32[]{:S(2)}, u32[]{:S(2)}) %collective-permute-start.8) | collective-permute-done | bytes 131104 | tf_op jit(solution)/shard_map/ppermute | solution.py:23
  117.9 1.5 %collective-permute-done.37 = bf16[64,1024]{1,0:T(8,128)(2,1)S(1)} collective-permute-done((bf16[64,1024]{1,0:T(8,128)(2,1)S(1)}, bf16[64,1024]{1,0:T(8,128)(2,1)S(1)}, u32[]{:S(2)}, u32[]{:S(2)}) %collective-permute-start.37) | collective-permute-done | bytes 131104 | tf_op jit(solution)/shard_map/ppermute | solution.py:23
  (141 shorter events, 13.8 us)
Async XLA Ops:
  1.8 18.5 %all-to-all-start = ((bf16[32,4,1024]{2,1,0:T(4,128)(2,1)}), bf16[32,4,1024]{2,1,0:T(4,128)(2,1)S(1)}, u32[]{:S(2)}, u32[]{:S(2)}) async-start(bf16[32,4,1024]{2,1,0:T(4,128)(2,1)} %all_to_all.6), calls=%async_computation | async-start | bytes 524288 | tf_op jit(solution)/shard_map/all_to_all | solution.py:48
  20.4 8.2 %slice-start.2 = ((s8[6815744]{0:T(1024)(128)(4,1)}), s8[4194304]{0:T(1024)(128)(4,1)S(1)}, s32[]{:S(2)}) async-start(s8[6815744]{0:T(1024)(128)(4,1)} %bitcast.208), calls=%async_computation.3 | async-start | bytes 8388608
  20.5 8.1 %slice-start.3 = ((s8[6815744]{0:T(1024)(128)(4,1)}), s8[2621440]{0:T(1024)(128)(4,1)S(1)}, s32[]{:S(2)}) async-start(s8[6815744]{0:T(1024)(128)(4,1)} %bitcast.208), calls=%async_computation.4 | async-start | bytes 5242880
  20.5 11.4 %collective-permute-start.27 = (bf16[128,1024]{1,0:T(8,128)(2,1)S(1)}, bf16[128,1024]{1,0:T(8,128)(2,1)S(1)}, u32[]{:S(2)}, u32[]{:S(2)}) collective-permute-start(bf16[128,1024]{1,0:T(8,128)(2,1)S(1)} %bitcast_dynamic-update-slice_fusion), channel_id=1, source_target_pairs={{0,96},{32,64},{64,32},{96,0},{1,97},{33,65},{65,33},{97,1},{2,98}... | collective-permute-start | bytes 786440 | tf_op jit(solution)/shard_map/ppermute | solution.py:23
  23.1 11.0 %collective-permute-start.10 = (bf16[128,1024]{1,0:T(8,128)(2,1)S(1)}, bf16[128,1024]{1,0:T(8,128)(2,1)S(1)}, u32[]{:S(2)}, u32[]{:S(2)}) collective-permute-start(bf16[128,1024]{1,0:T(8,128)(2,1)S(1)} %bitcast_dynamic-update-slice_fusion), channel_id=1, source_target_pairs={{0,32},{32,0},{64,96},{96,64},{1,33},{33,1},{65,97},{97,65},{2,34}... | collective-permute-start | bytes 786440 | tf_op jit(solution)/shard_map/ppermute | solution.py:23
  23.1 13.2 %collective-permute-start = (bf16[128,1024]{1,0:T(8,128)(2,1)S(1)}, bf16[128,1024]{1,0:T(8,128)(2,1)S(1)}, u32[]{:S(2)}, u32[]{:S(2)}) collective-permute-start(bf16[128,1024]{1,0:T(8,128)(2,1)S(1)} %bitcast_dynamic-update-slice_fusion), channel_id=1, source_target_pairs={{0,64},{32,96},{64,0},{96,32},{1,65},{33,97},{65,1},{97,33},{2,66}... | collective-permute-start | bytes 786440 | tf_op jit(solution)/shard_map/ppermute | solution.py:23
  24.5 7.5 %slice-start = ((s8[6815744]{0:T(1024)(128)(4,1)}), s8[4194304]{0:T(1024)(128)(4,1)S(1)}, s32[]{:S(2)}) async-start(s8[6815744]{0:T(1024)(128)(4,1)} %bitcast.206), calls=%async_computation.1 | async-start | bytes 8388608
  28.6 3.3 %slice-start.1 = ((s8[6815744]{0:T(1024)(128)(4,1)}), s8[2621440]{0:T(1024)(128)(4,1)S(1)}, s32[]{:S(2)}) async-start(s8[6815744]{0:T(1024)(128)(4,1)} %bitcast.206), calls=%async_computation.2 | async-start | bytes 5242880
  30.1 11.4 %collective-permute-start.20 = (f16[2,64,3328]{2,1,0:T(8,128)(2,1)S(1)}, f16[2,64,3328]{2,1,0:T(8,128)(2,1)S(1)}, u32[]{:S(2)}, u32[]{:S(2)}) collective-permute-start(f16[2,64,3328]{2,1,0:T(8,128)(2,1)S(1)} %pad_maximum_fusion.2), channel_id=1, source_target_pairs={{0,1},{1,0},{2,3},{3,2},{4,5},{5,4},{6,7},{7,6},{8,9},{9,8},{10,11... | collective-permute-start | bytes 2555912 | tf_op jit(solution)/shard_map/ppermute | solution.py:23
  38.8 3.9 %collective-permute-start.28 = (f16[2,64,3328]{2,1,0:T(8,128)(2,1)S(1)}, f16[2,64,3328]{2,1,0:T(8,128)(2,1)S(1)}, u32[]{:S(2)}, u32[]{:S(2)}) collective-permute-start(f16[2,64,3328]{2,1,0:T(8,128)(2,1)S(1)} %pad_maximum_fusion.3), channel_id=1, source_target_pairs={{0,1},{1,0},{2,3},{3,2},{4,5},{5,4},{6,7},{7,6},{8,9},{9,8},{10,11... | collective-permute-start | bytes 2555912 | tf_op jit(solution)/shard_map/ppermute | solution.py:23
  40.2 3.3 %collective-permute-start.11 = (f16[2,64,3328]{2,1,0:T(8,128)(2,1)S(1)}, f16[2,64,3328]{2,1,0:T(8,128)(2,1)S(1)}, u32[]{:S(2)}, u32[]{:S(2)}) collective-permute-start(f16[2,64,3328]{2,1,0:T(8,128)(2,1)S(1)} %pad_maximum_fusion.1), channel_id=1, source_target_pairs={{0,1},{1,0},{2,3},{3,2},{4,5},{5,4},{6,7},{7,6},{8,9},{9,8},{10,11... | collective-permute-start | bytes 2555912 | tf_op jit(solution)/shard_map/ppermute | solution.py:23
  40.7 5.0 %collective-permute-start.1 = (f16[2,64,3328]{2,1,0:T(8,128)(2,1)S(1)}, f16[2,64,3328]{2,1,0:T(8,128)(2,1)S(1)}, u32[]{:S(2)}, u32[]{:S(2)}) collective-permute-start(f16[2,64,3328]{2,1,0:T(8,128)(2,1)S(1)} %pad_maximum_fusion), channel_id=1, source_target_pairs={{0,1},{1,0},{2,3},{3,2},{4,5},{5,4},{6,7},{7,6},{8,9},{9,8},{10,11... | collective-permute-start | bytes 2555912 | tf_op jit(solution)/shard_map/ppermute | solution.py:23
  41.8 8.3 %collective-permute-start.21 = (f16[2,32,3328]{2,1,0:T(8,128)(2,1)S(1)}, f16[2,32,3328]{2,1,0:T(8,128)(2,1)S(1)}, u32[]{:S(2)}, u32[]{:S(2)}) collective-permute-start(f16[2,32,3328]{2,1,0:T(8,128)(2,1)S(1)} %pad_maximum_fusion.8), channel_id=1, source_target_pairs={{0,4},{1,13},{4,0},{5,9},{8,12},{9,5},{12,8},{13,1},{2,6},{3,15},{... | collective-permute-start | bytes 1277960 | tf_op jit(solution)/shard_map/ppermute | solution.py:23
  43.1 14.9 %collective-permute-start.29 = (f16[2,64,1664]{2,1,0:T(8,128)(2,1)S(1)}, f16[2,64,1664]{2,1,0:T(8,128)(2,1)S(1)}, u32[]{:S(2)}, u32[]{:S(2)}) collective-permute-start(f16[2,64,1664]{2,1,0:T(8,128)(2,1)S(1)} %pad_maximum_fusion.10), channel_id=1, source_target_pairs={{0,2},{2,0},{1,3},{3,1},{4,6},{6,4},{5,7},{7,5},{8,10},{10,8},{9,1... | collective-permute-start | bytes 1277960 | tf_op jit(solution)/shard_map/ppermute | solution.py:23
  44.0 15.0 %collective-permute-start.12 = (f16[2,32,3328]{2,1,0:T(8,128)(2,1)S(1)}, f16[2,32,3328]{2,1,0:T(8,128)(2,1)S(1)}, u32[]{:S(2)}, u32[]{:S(2)}) collective-permute-start(f16[2,32,3328]{2,1,0:T(8,128)(2,1)S(1)} %pad_maximum_fusion.6), channel_id=1, source_target_pairs={{0,4},{1,13},{4,0},{5,9},{8,12},{9,5},{12,8},{13,1},{2,6},{3,15},{... | collective-permute-start | bytes 1277960 | tf_op jit(solution)/shard_map/ppermute | solution.py:23
  50.3 7.4 %collective-permute-start.22 = (f16[2,16,3328]{2,1,0:T(8,128)(2,1)S(1)}, f16[2,16,3328]{2,1,0:T(8,128)(2,1)S(1)}, u32[]{:S(2)}, u32[]{:S(2)}) collective-permute-start(f16[2,16,3328]{2,1,0:T(8,128)(2,1)S(1)} %pad_maximum_fusion.18), channel_id=1, source_target_pairs={{0,12},{1,5},{4,8},{5,1},{8,4},{9,13},{12,0},{13,9},{2,14},{3,7},{... | collective-permute-start | bytes 638984 | tf_op jit(solution)/shard_map/ppermute | solution.py:23
  50.5 11.0 %collective-permute-start.2 = (f16[2,32,3328]{2,1,0:T(8,128)(2,1)S(1)}, f16[2,32,3328]{2,1,0:T(8,128)(2,1)S(1)}, u32[]{:S(2)}, u32[]{:S(2)}) collective-permute-start(f16[2,32,3328]{2,1,0:T(8,128)(2,1)S(1)} %pad_maximum_fusion.4), channel_id=1, source_target_pairs={{0,4},{1,13},{4,0},{5,9},{8,12},{9,5},{12,8},{13,1},{2,6},{3,15},{... | collective-permute-start | bytes 1277960 | tf_op jit(solution)/shard_map/ppermute | solution.py:23
  57.9 4.8 %collective-permute-start.23 = (f16[2,16,3328]{2,1,0:T(8,128)(2,1)S(1)}, f16[2,16,3328]{2,1,0:T(8,128)(2,1)S(1)}, u32[]{:S(2)}, u32[]{:S(2)}) collective-permute-start(f16[2,16,3328]{2,1,0:T(8,128)(2,1)S(1)} %pad_maximum_fusion.19), channel_id=1, source_target_pairs={{0,2},{2,0},{1,3},{3,1},{4,6},{6,4},{5,7},{7,5},{8,10},{10,8},{9,1... | collective-permute-start | bytes 638984 | tf_op jit(solution)/shard_map/ppermute | solution.py:23
  58.3 6.4 %collective-permute-start.30 = (f16[2,32,1664]{2,1,0:T(8,128)(2,1)S(1)}, f16[2,32,1664]{2,1,0:T(8,128)(2,1)S(1)}, u32[]{:S(2)}, u32[]{:S(2)}) collective-permute-start(f16[2,32,1664]{2,1,0:T(8,128)(2,1)S(1)} %pad_maximum_fusion.21), channel_id=1, source_target_pairs={{0,4},{1,13},{4,0},{5,9},{8,12},{9,5},{12,8},{13,1},{2,6},{3,15},{... | collective-permute-start | bytes 638984 | tf_op jit(solution)/shard_map/ppermute | solution.py:23
  59.2 5.8 %collective-permute-start.13 = (f16[2,16,3328]{2,1,0:T(8,128)(2,1)S(1)}, f16[2,16,3328]{2,1,0:T(8,128)(2,1)S(1)}, u32[]{:S(2)}, u32[]{:S(2)}) collective-permute-start(f16[2,16,3328]{2,1,0:T(8,128)(2,1)S(1)} %pad_maximum_fusion.15), channel_id=1, source_target_pairs={{0,12},{1,5},{4,8},{5,1},{8,4},{9,13},{12,0},{13,9},{2,14},{3,7},{... | collective-permute-start | bytes 638984 | tf_op jit(solution)/shard_map/ppermute | solution.py:23
  61.5 36.6 %slice-start.4 = ((s8[6815744]{0:T(1024)(128)(4,1)}), s8[4194304]{0:T(1024)(128)(4,1)S(1)}, s32[]{:S(2)}) async-start(s8[6815744]{0:T(1024)(128)(4,1)} %bitcast.210), calls=%async_computation.5 | async-start | bytes 8388608
  61.8 7.1 %collective-permute-start.3 = (f16[2,16,3328]{2,1,0:T(8,128)(2,1)S(1)}, f16[2,16,3328]{2,1,0:T(8,128)(2,1)S(1)}, u32[]{:S(2)}, u32[]{:S(2)}) collective-permute-start(f16[2,16,3328]{2,1,0:T(8,128)(2,1)S(1)} %pad_maximum_fusion.12), channel_id=1, source_target_pairs={{0,12},{1,5},{4,8},{5,1},{8,4},{9,13},{12,0},{13,9},{2,14},{3,7},{... | collective-permute-start | bytes 638984 | tf_op jit(solution)/shard_map/ppermute | solution.py:23
  62.8 7.2 %collective-permute-start.24 = (bf16[16,3328]{1,0:T(8,128)(2,1)S(1)}, bf16[16,3328]{1,0:T(8,128)(2,1)S(1)}, u32[]{:S(2)}, u32[]{:S(2)}) collective-permute-start(bf16[16,3328]{1,0:T(8,128)(2,1)S(1)} %fusion.54), channel_id=1, source_target_pairs={{0,12},{1,5},{4,8},{5,1},{8,4},{9,13},{12,0},{13,9},{2,14},{3,7},{... | collective-permute-start | bytes 319496 | tf_op jit(solution)/shard_map/ppermute | solution.py:23
  64.9 6.2 %collective-permute-start.31 = (f16[2,16,1664]{2,1,0:T(8,128)(2,1)S(1)}, f16[2,16,1664]{2,1,0:T(8,128)(2,1)S(1)}, u32[]{:S(2)}, u32[]{:S(2)}) collective-permute-start(f16[2,16,1664]{2,1,0:T(8,128)(2,1)S(1)} %pad_maximum_fusion.24), channel_id=1, source_target_pairs={{0,12},{1,5},{4,8},{5,1},{8,4},{9,13},{12,0},{13,9},{2,14},{3,7},{... | collective-permute-start | bytes 319496 | tf_op jit(solution)/shard_map/ppermute | solution.py:23
  65.1 33.0 %slice-start.5 = ((s8[6815744]{0:T(1024)(128)(4,1)}), s8[2621440]{0:T(1024)(128)(4,1)S(1)}, s32[]{:S(2)}) async-start(s8[6815744]{0:T(1024)(128)(4,1)} %bitcast.210), calls=%async_computation.6 | async-start | bytes 5242880
  65.2 11.4 %collective-permute-start.14 = (f16[2,16,3328]{2,1,0:T(8,128)(2,1)S(1)}, f16[2,16,3328]{2,1,0:T(8,128)(2,1)S(1)}, u32[]{:S(2)}, u32[]{:S(2)}) collective-permute-start(f16[2,16,3328]{2,1,0:T(8,128)(2,1)S(1)} %pad_maximum_fusion.16), channel_id=1, source_target_pairs={{0,2},{2,0},{1,3},{3,1},{4,6},{6,4},{5,7},{7,5},{8,10},{10,8},{9,1... | collective-permute-start | bytes 638984 | tf_op jit(solution)/shard_map/ppermute | solution.py:23
  69.0 8.3 %collective-permute-start.4 = (f16[2,16,3328]{2,1,0:T(8,128)(2,1)S(1)}, f16[2,16,3328]{2,1,0:T(8,128)(2,1)S(1)}, u32[]{:S(2)}, u32[]{:S(2)}) collective-permute-start(f16[2,16,3328]{2,1,0:T(8,128)(2,1)S(1)} %pad_maximum_fusion.13), channel_id=1, source_target_pairs={{0,2},{2,0},{1,3},{3,1},{4,6},{6,4},{5,7},{7,5},{8,10},{10,8},{9,1... | collective-permute-start | bytes 638984 | tf_op jit(solution)/shard_map/ppermute | solution.py:23
  71.2 4.3 %collective-permute-start.32 = (bf16[16,1664]{1,0:T(8,128)(2,1)S(1)}, bf16[16,1664]{1,0:T(8,128)(2,1)S(1)}, u32[]{:S(2)}, u32[]{:S(2)}) collective-permute-start(bf16[16,1664]{1,0:T(8,128)(2,1)S(1)} %fusion.76), channel_id=1, source_target_pairs={{0,2},{2,0},{1,3},{3,1},{4,6},{6,4},{5,7},{7,5},{8,10},{10,8},{9,1... | collective-permute-start | bytes 159752 | tf_op jit(solution)/shard_map/ppermute | solution.py:23
  72.1 11.0 %collective-permute-start.25 = (bf16[32,3328]{1,0:T(8,128)(2,1)S(1)}, bf16[32,3328]{1,0:T(8,128)(2,1)S(1)}, u32[]{:S(2)}, u32[]{:S(2)}) collective-permute-start(bf16[32,3328]{1,0:T(8,128)(2,1)S(1)} %pad_maximum_fusion.20), channel_id=1, source_target_pairs={{0,4},{1,13},{4,0},{5,9},{8,12},{9,5},{12,8},{13,1},{2,6},{3,15},{... | collective-permute-start | bytes 638984 | tf_op jit(solution)/shard_map/ppermute | solution.py:23
  75.5 3.9 %collective-permute-start.33 = (bf16[16,3328]{1,0:T(8,128)(2,1)S(1)}, bf16[16,3328]{1,0:T(8,128)(2,1)S(1)}, u32[]{:S(2)}, u32[]{:S(2)}) collective-permute-start(bf16[16,3328]{1,0:T(8,128)(2,1)S(1)} %pad_maximum_fusion.25), channel_id=1, source_target_pairs={{0,12},{1,5},{4,8},{5,1},{8,4},{9,13},{12,0},{13,9},{2,14},{3,7},{... | collective-permute-start | bytes 319496 | tf_op jit(solution)/shard_map/ppermute | solution.py:23
  76.7 10.9 %collective-permute-start.15 = (bf16[16,3328]{1,0:T(8,128)(2,1)S(1)}, bf16[16,3328]{1,0:T(8,128)(2,1)S(1)}, u32[]{:S(2)}, u32[]{:S(2)}) collective-permute-start(bf16[16,3328]{1,0:T(8,128)(2,1)S(1)} %fusion.56), channel_id=1, source_target_pairs={{0,12},{1,5},{4,8},{5,1},{8,4},{9,13},{12,0},{13,9},{2,14},{3,7},{... | collective-permute-start | bytes 319496 | tf_op jit(solution)/shard_map/ppermute | solution.py:23
  77.4 12.2 %collective-permute-start.5 = (bf16[16,3328]{1,0:T(8,128)(2,1)S(1)}, bf16[16,3328]{1,0:T(8,128)(2,1)S(1)}, u32[]{:S(2)}, u32[]{:S(2)}) collective-permute-start(bf16[16,3328]{1,0:T(8,128)(2,1)S(1)} %fusion.58), channel_id=1, source_target_pairs={{0,12},{1,5},{4,8},{5,1},{8,4},{9,13},{12,0},{13,9},{2,14},{3,7},{... | collective-permute-start | bytes 319496 | tf_op jit(solution)/shard_map/ppermute | solution.py:23
  79.5 11.0 %collective-permute-start.34 = (bf16[32,3328]{1,0:T(8,128)(2,1)S(1)}, bf16[32,3328]{1,0:T(8,128)(2,1)S(1)}, u32[]{:S(2)}, u32[]{:S(2)}) collective-permute-start(bf16[32,3328]{1,0:T(8,128)(2,1)S(1)} %pad_maximum_fusion.22), channel_id=1, source_target_pairs={{0,4},{1,13},{4,0},{5,9},{8,12},{9,5},{12,8},{13,1},{2,6},{3,15},{... | collective-permute-start | bytes 638984 | tf_op jit(solution)/shard_map/ppermute | solution.py:23
  83.2 15.0 %collective-permute-start.26 = (bf16[64,3328]{1,0:T(8,128)(2,1)S(1)}, bf16[64,3328]{1,0:T(8,128)(2,1)S(1)}, u32[]{:S(2)}, u32[]{:S(2)}) collective-permute-start(bf16[64,3328]{1,0:T(8,128)(2,1)S(1)} %pad_maximum_fusion.9), channel_id=1, source_target_pairs={{0,1},{1,0},{2,3},{3,2},{4,5},{5,4},{6,7},{7,6},{8,9},{9,8},{10,11... | collective-permute-start | bytes 1277960 | tf_op jit(solution)/shard_map/ppermute | solution.py:23
  87.6 6.0 %collective-permute-start.16 = (bf16[32,3328]{1,0:T(8,128)(2,1)S(1)}, bf16[32,3328]{1,0:T(8,128)(2,1)S(1)}, u32[]{:S(2)}, u32[]{:S(2)}) collective-permute-start(bf16[32,3328]{1,0:T(8,128)(2,1)S(1)} %pad_maximum_fusion.17), channel_id=1, source_target_pairs={{0,4},{1,13},{4,0},{5,9},{8,12},{9,5},{12,8},{13,1},{2,6},{3,15},{... | collective-permute-start | bytes 638984 | tf_op jit(solution)/shard_map/ppermute | solution.py:23
  89.5 6.3 %collective-permute-start.6 = (bf16[32,3328]{1,0:T(8,128)(2,1)S(1)}, bf16[32,3328]{1,0:T(8,128)(2,1)S(1)}, u32[]{:S(2)}, u32[]{:S(2)}) collective-permute-start(bf16[32,3328]{1,0:T(8,128)(2,1)S(1)} %pad_maximum_fusion.14), channel_id=1, source_target_pairs={{0,4},{1,13},{4,0},{5,9},{8,12},{9,5},{12,8},{13,1},{2,6},{3,15},{... | collective-permute-start | bytes 638984 | tf_op jit(solution)/shard_map/ppermute | solution.py:23
  90.5 8.8 %collective-permute-start.35 = (bf16[64,3328]{1,0:T(8,128)(2,1)S(1)}, bf16[64,3328]{1,0:T(8,128)(2,1)S(1)}, u32[]{:S(2)}, u32[]{:S(2)}) collective-permute-start(bf16[64,3328]{1,0:T(8,128)(2,1)S(1)} %pad_maximum_fusion.11), channel_id=1, source_target_pairs={{0,1},{1,0},{2,3},{3,2},{4,5},{5,4},{6,7},{7,6},{8,9},{9,8},{10,11... | collective-permute-start | bytes 1277960 | tf_op jit(solution)/shard_map/ppermute | solution.py:23
  93.6 9.3 %collective-permute-start.17 = (bf16[64,3328]{1,0:T(8,128)(2,1)S(1)}, bf16[64,3328]{1,0:T(8,128)(2,1)S(1)}, u32[]{:S(2)}, u32[]{:S(2)}) collective-permute-start(bf16[64,3328]{1,0:T(8,128)(2,1)S(1)} %pad_maximum_fusion.7), channel_id=1, source_target_pairs={{0,1},{1,0},{2,3},{3,2},{4,5},{5,4},{6,7},{7,6},{8,9},{9,8},{10,11... | collective-permute-start | bytes 1277960 | tf_op jit(solution)/shard_map/ppermute | solution.py:23
  95.9 10.8 %collective-permute-start.7 = (bf16[64,3328]{1,0:T(8,128)(2,1)S(1)}, bf16[64,3328]{1,0:T(8,128)(2,1)S(1)}, u32[]{:S(2)}, u32[]{:S(2)}) collective-permute-start(bf16[64,3328]{1,0:T(8,128)(2,1)S(1)} %pad_maximum_fusion.5), channel_id=1, source_target_pairs={{0,1},{1,0},{2,3},{3,2},{4,5},{5,4},{6,7},{7,6},{8,9},{9,8},{10,11... | collective-permute-start | bytes 1277960 | tf_op jit(solution)/shard_map/ppermute | solution.py:23
  100.3 11.8 %collective-permute-start.36 = (bf16[128,1024]{1,0:T(8,128)(2,1)S(1)}, bf16[128,1024]{1,0:T(8,128)(2,1)S(1)}, u32[]{:S(2)}, u32[]{:S(2)}) collective-permute-start(bf16[128,1024]{1,0:T(8,128)(2,1)S(1)} %convolution_convert_fusion), channel_id=1, source_target_pairs={{0,96},{32,64},{64,32},{96,0},{1,97},{33,65},{65,33},{97,1},{2,98}... | collective-permute-start | bytes 786440 | tf_op jit(solution)/shard_map/ppermute | solution.py:23
  104.0 9.8 %collective-permute-start.19 = (bf16[64,1024]{1,0:T(8,128)(2,1)S(1)}, bf16[64,1024]{1,0:T(8,128)(2,1)S(1)}, u32[]{:S(2)}, u32[]{:S(2)}) collective-permute-start(bf16[64,1024]{1,0:T(8,128)(2,1)S(1)} %get-tuple-element.86), channel_id=1, source_target_pairs={{0,48},{16,32},{32,16},{48,0},{64,112},{80,96},{96,80},{112,64},{1... | collective-permute-start | bytes 393224 | tf_op jit(solution)/shard_map/ppermute | solution.py:23
  104.1 9.7 %collective-permute-start.18 = (bf16[64,1024]{1,0:T(8,128)(2,1)S(1)}, bf16[64,1024]{1,0:T(8,128)(2,1)S(1)}, u32[]{:S(2)}, u32[]{:S(2)}) collective-permute-start(bf16[64,1024]{1,0:T(8,128)(2,1)S(1)} %get-tuple-element.85), channel_id=1, source_target_pairs={{0,32},{32,0},{64,96},{96,64},{1,33},{33,1},{65,97},{97,65},{2,34}... | collective-permute-start | bytes 393224 | tf_op jit(solution)/shard_map/ppermute | solution.py:23
  107.8 8.5 %collective-permute-start.9 = (bf16[64,1024]{1,0:T(8,128)(2,1)S(1)}, bf16[64,1024]{1,0:T(8,128)(2,1)S(1)}, u32[]{:S(2)}, u32[]{:S(2)}) collective-permute-start(bf16[64,1024]{1,0:T(8,128)(2,1)S(1)} %get-tuple-element.72), channel_id=1, source_target_pairs={{0,80},{16,64},{32,112},{48,96},{64,16},{80,0},{96,48},{112,32},{1... | collective-permute-start | bytes 393224 | tf_op jit(solution)/shard_map/ppermute | solution.py:23
  109.0 8.9 %collective-permute-start.8 = (bf16[64,1024]{1,0:T(8,128)(2,1)S(1)}, bf16[64,1024]{1,0:T(8,128)(2,1)S(1)}, u32[]{:S(2)}, u32[]{:S(2)}) collective-permute-start(bf16[64,1024]{1,0:T(8,128)(2,1)S(1)} %get-tuple-element.71), channel_id=1, source_target_pairs={{0,64},{32,96},{64,0},{96,32},{1,65},{33,97},{65,1},{97,33},{2,66}... | collective-permute-start | bytes 393224 | tf_op jit(solution)/shard_map/ppermute | solution.py:23
  112.2 7.2 %collective-permute-start.37 = (bf16[64,1024]{1,0:T(8,128)(2,1)S(1)}, bf16[64,1024]{1,0:T(8,128)(2,1)S(1)}, u32[]{:S(2)}, u32[]{:S(2)}) collective-permute-start(bf16[64,1024]{1,0:T(8,128)(2,1)S(1)} %select_convert_fusion), channel_id=1, source_target_pairs={{0,16},{16,0},{32,48},{48,32},{64,80},{80,64},{96,112},{112,96},{1... | collective-permute-start | bytes 393224 | tf_op jit(solution)/shard_map/ppermute | solution.py:23

commit v11 on v10

--- a/solution.py
+++ b/solution.py
@@ -43,8 +43,8 @@
     }
 
     features = tokens.shape[1] // 16
-    blocks = tokens.reshape(4, 16, features).transpose(1, 0, 2).reshape(1, 64, features)
-    blocks = jnp.broadcast_to(blocks, (2, 64, features)).reshape(128, features)
+    blocks = tokens.reshape(4, 16, features).transpose(1, 0, 2)
+    blocks = jnp.concatenate((blocks, blocks))
     mine = lax.all_to_all(blocks, AXES[1:], split_axis=0, concat_axis=0, tiled=True)
     mine = mine.reshape(2, 4, 16, features)
 

time: 120 us -> 120 us (level)
  other arithmetic: 5.8 us -> 7.67 us
  local copies, waits for them, and re-layouts: 2.01 us -> 0.23 us
    concatenate x0 -> x1, other arithmetic: none -> 1.86 us  [per_device(): blocks = jnp.concatenate((blocks, blocks))]
where the time goes in v11:
time: 120 us
  starting transfers between devices  61.4 us (51%)
  waiting for transfers between devices  34.4 us (29%)
  matrix products  15.8 us (13%)
  other arithmetic  7.67 us (6%)
    ppermute x38, starting transfers between devices, permute(): return lambda v: lax.ppermute(v, axes, pairs)  51.8 us
    ppermute x38, waiting for transfers between devices, permute(): return lambda v: lax.ppermute(v, axes, pairs)  25.6 us
    dot_general x12, matrix products, product(): return jnp.dot(rows, weight, preferred_element_type=F32)  15.8 us
    all_to_all x1, starting transfers between devices, per_device(): lax.all_to_all(blocks, AXES[1:], split_axis=0, concat_axis=0, tiled=True)  9.6 us
    all_to_all x1, waiting for transfers between devices, per_device(): lax.all_to_all(blocks, AXES[1:], split_axis=0, concat_axis=0, tiled=True)  8.79 us
  transfers between devices with their start and end apart: 39, of which 15 were waited for; matrix products, arithmetic and copies ran while one was open for 17% of the time, Pallas kernels for 0%

profile of v11, /device:TPU:1, one launch (start us, length us, event | category | flops | bytes accessed | tf_op | source)
XLA Modules:
  0.0 120.3 jit_solution(6614490949460999923)
XLA Ops:
  0.0 1.9 %pad_maximum_fusion.12 = bf16[32,4,1024]{2,1,0:T(4,128)(2,1)} fusion(bf16[16,4,1024]{2,1,0:T(4,128)(2,1)} %bitcast.213), kind=kLoop, calls=%fused_computation.85 | loop fusion | flops 131072 | bytes 393216 | tf_op jit(solution)/shard_map/concatenate | solution.py:47
  1.9 9.6 %all-to-all-start = ((bf16[32,4,1024]{2,1,0:T(4,128)(2,1)}), bf16[32,4,1024]{2,1,0:T(4,128)(2,1)S(1)}, u32[]{:S(2)}, u32[]{:S(2)}) async-start(bf16[32,4,1024]{2,1,0:T(4,128)(2,1)} %pad_maximum_fusion.12), calls=%async_computation | async-start | bytes 524288 | tf_op jit(solution)/shard_map/all_to_all | solution.py:48
  11.5 8.8 %all-to-all-done = bf16[32,4,1024]{2,1,0:T(4,128)(2,1)S(1)} async-done(((bf16[32,4,1024]{2,1,0:T(4,128)(2,1)}), bf16[32,4,1024]{2,1,0:T(4,128)(2,1)S(1)}, u32[]{:S(2)}, u32[]{:S(2)}) %all-to-all-start) | async-done | bytes 262176 | tf_op jit(solution)/shard_map/all_to_all | solution.py:48
  20.6 2.6 %collective-permute-start.27 = (bf16[128,1024]{1,0:T(8,128)(2,1)S(1)}, bf16[128,1024]{1,0:T(8,128)(2,1)S(1)}, u32[]{:S(2)}, u32[]{:S(2)}) collective-permute-start(bf16[128,1024]{1,0:T(8,128)(2,1)S(1)} %bitcast_dynamic-update-slice_fusion), channel_id=1, source_target_pairs={{0,96},{32,64},{64,32},{96,0},{1,97},{33,65},{65,33},{97,1},{2,98}... | collective-permute-start | bytes 786440 | tf_op jit(solution)/shard_map/ppermute | solution.py:23
  23.2 1.4 %collective-permute-start = (bf16[128,1024]{1,0:T(8,128)(2,1)S(1)}, bf16[128,1024]{1,0:T(8,128)(2,1)S(1)}, u32[]{:S(2)}, u32[]{:S(2)}) collective-permute-start(bf16[128,1024]{1,0:T(8,128)(2,1)S(1)} %bitcast_dynamic-update-slice_fusion), channel_id=1, source_target_pairs={{0,64},{32,96},{64,0},{96,32},{1,65},{33,97},{65,1},{97,33},{2,66}... | collective-permute-start | bytes 786440 | tf_op jit(solution)/shard_map/ppermute | solution.py:23
  24.5 4.1 %fusion.87 = f32[128,3328]{1,0:T(8,128)S(1)} fusion(bf16[128,1024]{1,0:T(8,128)(2,1)S(1)} %bitcast_dynamic-update-slice_fusion, bf16[1024,3328]{1,0:T(8,128)(2,1)} %param.5), kind=kOutput, calls=%fused_computation.203 | convolution fusion | flops 872415232 | bytes 8781824 | tf_op jit(solution)/shard_map/dot_general | solution.py:74
  28.7 1.1 fusion.88
  30.2 1.9 %collective-permute-start.20 = (f16[2,64,3328]{2,1,0:T(8,128)(2,1)S(1)}, f16[2,64,3328]{2,1,0:T(8,128)(2,1)S(1)}, u32[]{:S(2)}, u32[]{:S(2)}) collective-permute-start(f16[2,64,3328]{2,1,0:T(8,128)(2,1)S(1)} %pad_maximum_fusion.2), channel_id=1, source_target_pairs={{0,1},{1,0},{2,3},{3,2},{4,5},{5,4},{6,7},{7,6},{8,9},{9,8},{10,11... | collective-permute-start | bytes 2555912 | tf_op jit(solution)/shard_map/ppermute | solution.py:23
  32.0 1.1 fusion.89
  33.1 1.1 fusion.90
  34.2 1.1 fusion.85
  35.3 1.1 fusion.86
  36.3 1.1 fusion.83
  37.4 1.1 fusion.84
  38.8 1.1 collective-permute-start.28
  44.0 1.8 %collective-permute-start.12 = (f16[2,32,3328]{2,1,0:T(8,128)(2,1)S(1)}, f16[2,32,3328]{2,1,0:T(8,128)(2,1)S(1)}, u32[]{:S(2)}, u32[]{:S(2)}) collective-permute-start(f16[2,32,3328]{2,1,0:T(8,128)(2,1)S(1)} %pad_maximum_fusion.6), channel_id=1, source_target_pairs={{0,4},{1,13},{4,0},{5,9},{8,12},{9,5},{12,8},{13,1},{2,6},{3,15},{... | collective-permute-start | bytes 1277960 | tf_op jit(solution)/shard_map/ppermute | solution.py:23
  46.1 4.1 %collective-permute-done.21 = f16[2,32,3328]{2,1,0:T(8,128)(2,1)S(1)} collective-permute-done((f16[2,32,3328]{2,1,0:T(8,128)(2,1)S(1)}, f16[2,32,3328]{2,1,0:T(8,128)(2,1)S(1)}, u32[]{:S(2)}, u32[]{:S(2)}) %collective-permute-start.21) | collective-permute-done | bytes 426016 | tf_op jit(solution)/shard_map/ppermute | solution.py:23
  51.4 6.4 %collective-permute-done.22 = f16[2,16,3328]{2,1,0:T(8,128)(2,1)S(1)} collective-permute-done((f16[2,16,3328]{2,1,0:T(8,128)(2,1)S(1)}, f16[2,16,3328]{2,1,0:T(8,128)(2,1)S(1)}, u32[]{:S(2)}, u32[]{:S(2)}) %collective-permute-start.22) | collective-permute-done | bytes 213024 | tf_op jit(solution)/shard_map/ppermute | solution.py:23
  59.4 2.2 %collective-permute-done.2 = f16[2,32,3328]{2,1,0:T(8,128)(2,1)S(1)} collective-permute-done((f16[2,32,3328]{2,1,0:T(8,128)(2,1)S(1)}, f16[2,32,3328]{2,1,0:T(8,128)(2,1)S(1)}, u32[]{:S(2)}, u32[]{:S(2)}) %collective-permute-start.2) | collective-permute-done | bytes 426016 | tf_op jit(solution)/shard_map/ppermute | solution.py:23
  62.9 2.0 %collective-permute-start.24 = (bf16[16,3328]{1,0:T(8,128)(2,1)S(1)}, bf16[16,3328]{1,0:T(8,128)(2,1)S(1)}, u32[]{:S(2)}, u32[]{:S(2)}) collective-permute-start(bf16[16,3328]{1,0:T(8,128)(2,1)S(1)} %fusion.54), channel_id=1, source_target_pairs={{0,12},{1,5},{4,8},{5,1},{8,4},{9,13},{12,0},{13,9},{2,14},{3,7},{... | collective-permute-start | bytes 319496 | tf_op jit(solution)/shard_map/ppermute | solution.py:23
  65.2 1.0 collective-permute-start.14
  66.3 2.6 %collective-permute-done.3 = f16[2,16,3328]{2,1,0:T(8,128)(2,1)S(1)} collective-permute-done((f16[2,16,3328]{2,1,0:T(8,128)(2,1)S(1)}, f16[2,16,3328]{2,1,0:T(8,128)(2,1)S(1)}, u32[]{:S(2)}, u32[]{:S(2)}) %collective-permute-start.3) | collective-permute-done | bytes 213024 | tf_op jit(solution)/shard_map/ppermute | solution.py:23
  70.0 1.1 collective-permute-done.31
  71.2 0.9 collective-permute-start.32
  72.2 2.4 %collective-permute-start.25 = (bf16[32,3328]{1,0:T(8,128)(2,1)S(1)}, bf16[32,3328]{1,0:T(8,128)(2,1)S(1)}, u32[]{:S(2)}, u32[]{:S(2)}) collective-permute-start(bf16[32,3328]{1,0:T(8,128)(2,1)S(1)} %pad_maximum_fusion.21), channel_id=1, source_target_pairs={{0,4},{1,13},{4,0},{5,9},{8,12},{9,5},{12,8},{13,1},{2,6},{3,15},{... | collective-permute-start | bytes 638984 | tf_op jit(solution)/shard_map/ppermute | solution.py:23
  74.6 0.9 collective-permute-done.32
  75.6 1.1 collective-permute-start.33
  77.4 1.1 collective-permute-start.5
  78.5 1.0 collective-permute-done.33
  79.5 3.7 %collective-permute-start.34 = (bf16[32,3328]{1,0:T(8,128)(2,1)S(1)}, bf16[32,3328]{1,0:T(8,128)(2,1)S(1)}, u32[]{:S(2)}, u32[]{:S(2)}) collective-permute-start(bf16[32,3328]{1,0:T(8,128)(2,1)S(1)} %pad_maximum_fusion.23), channel_id=1, source_target_pairs={{0,4},{1,13},{4,0},{5,9},{8,12},{9,5},{12,8},{13,1},{2,6},{3,15},{... | collective-permute-start | bytes 638984 | tf_op jit(solution)/shard_map/ppermute | solution.py:23
  83.2 4.4 %collective-permute-start.26 = (bf16[64,3328]{1,0:T(8,128)(2,1)S(1)}, bf16[64,3328]{1,0:T(8,128)(2,1)S(1)}, u32[]{:S(2)}, u32[]{:S(2)}) collective-permute-start(bf16[64,3328]{1,0:T(8,128)(2,1)S(1)} %pad_maximum_fusion.9), channel_id=1, source_target_pairs={{0,1},{1,0},{2,3},{3,2},{4,5},{5,4},{6,7},{7,6},{8,9},{9,8},{10,11... | collective-permute-start | bytes 1277960 | tf_op jit(solution)/shard_map/ppermute | solution.py:23
  87.7 1.9 %collective-permute-start.16 = (bf16[32,3328]{1,0:T(8,128)(2,1)S(1)}, bf16[32,3328]{1,0:T(8,128)(2,1)S(1)}, u32[]{:S(2)}, u32[]{:S(2)}) collective-permute-start(bf16[32,3328]{1,0:T(8,128)(2,1)S(1)} %pad_maximum_fusion.18), channel_id=1, source_target_pairs={{0,4},{1,13},{4,0},{5,9},{8,12},{9,5},{12,8},{13,1},{2,6},{3,15},{... | collective-permute-start | bytes 638984 | tf_op jit(solution)/shard_map/ppermute | solution.py:23
  89.6 0.9 collective-permute-start.6
  90.6 2.9 %collective-permute-start.35 = (bf16[64,3328]{1,0:T(8,128)(2,1)S(1)}, bf16[64,3328]{1,0:T(8,128)(2,1)S(1)}, u32[]{:S(2)}, u32[]{:S(2)}) collective-permute-start(bf16[64,3328]{1,0:T(8,128)(2,1)S(1)} %pad_maximum_fusion.11), channel_id=1, source_target_pairs={{0,1},{1,0},{2,3},{3,2},{4,5},{5,4},{6,7},{7,6},{8,9},{9,8},{10,11... | collective-permute-start | bytes 1277960 | tf_op jit(solution)/shard_map/ppermute | solution.py:23
  93.7 2.1 %collective-permute-start.17 = (bf16[64,3328]{1,0:T(8,128)(2,1)S(1)}, bf16[64,3328]{1,0:T(8,128)(2,1)S(1)}, u32[]{:S(2)}, u32[]{:S(2)}) collective-permute-start(bf16[64,3328]{1,0:T(8,128)(2,1)S(1)} %pad_maximum_fusion.7), channel_id=1, source_target_pairs={{0,1},{1,0},{2,3},{3,2},{4,5},{5,4},{6,7},{7,6},{8,9},{9,8},{10,11... | collective-permute-start | bytes 1277960 | tf_op jit(solution)/shard_map/ppermute | solution.py:23
  96.0 2.3 %collective-permute-start.7 = (bf16[64,3328]{1,0:T(8,128)(2,1)S(1)}, bf16[64,3328]{1,0:T(8,128)(2,1)S(1)}, u32[]{:S(2)}, u32[]{:S(2)}) collective-permute-start(bf16[64,3328]{1,0:T(8,128)(2,1)S(1)} %pad_maximum_fusion.5), channel_id=1, source_target_pairs={{0,1},{1,0},{2,3},{3,2},{4,5},{5,4},{6,7},{7,6},{8,9},{9,8},{10,11... | collective-permute-start | bytes 1277960 | tf_op jit(solution)/shard_map/ppermute | solution.py:23
  98.3 1.0 fusion.16
  99.3 1.1 convolution_convert_fusion
  100.4 2.6 %collective-permute-start.36 = (bf16[128,1024]{1,0:T(8,128)(2,1)S(1)}, bf16[128,1024]{1,0:T(8,128)(2,1)S(1)}, u32[]{:S(2)}, u32[]{:S(2)}) collective-permute-start(bf16[128,1024]{1,0:T(8,128)(2,1)S(1)} %convolution_convert_fusion), channel_id=1, source_target_pairs={{0,96},{32,64},{64,32},{96,0},{1,97},{33,65},{65,33},{97,1},{2,98}... | collective-permute-start | bytes 786440 | tf_op jit(solution)/shard_map/ppermute | solution.py:23
  103.0 1.1 fusion.12
  104.1 2.6 %collective-permute-start.18 = (bf16[64,1024]{1,0:T(8,128)(2,1)S(1)}, bf16[64,1024]{1,0:T(8,128)(2,1)S(1)}, u32[]{:S(2)}, u32[]{:S(2)}) collective-permute-start(bf16[64,1024]{1,0:T(8,128)(2,1)S(1)} %get-tuple-element.85), channel_id=1, source_target_pairs={{0,32},{32,0},{64,96},{96,64},{1,33},{33,1},{65,97},{97,65},{2,34}... | collective-permute-start | bytes 393224 | tf_op jit(solution)/shard_map/ppermute | solution.py:23
  106.8 1.1 fusion.8
  107.9 1.2 %collective-permute-start.9 = (bf16[64,1024]{1,0:T(8,128)(2,1)S(1)}, bf16[64,1024]{1,0:T(8,128)(2,1)S(1)}, u32[]{:S(2)}, u32[]{:S(2)}) collective-permute-start(bf16[64,1024]{1,0:T(8,128)(2,1)S(1)} %get-tuple-element.72), channel_id=1, source_target_pairs={{0,80},{16,64},{32,112},{48,96},{64,16},{80,0},{96,48},{112,32},{1... | collective-permute-start | bytes 393224 | tf_op jit(solution)/shard_map/ppermute | solution.py:23
  109.1 3.1 %collective-permute-start.8 = (bf16[64,1024]{1,0:T(8,128)(2,1)S(1)}, bf16[64,1024]{1,0:T(8,128)(2,1)S(1)}, u32[]{:S(2)}, u32[]{:S(2)}) collective-permute-start(bf16[64,1024]{1,0:T(8,128)(2,1)S(1)} %get-tuple-element.71), channel_id=1, source_target_pairs={{0,64},{32,96},{64,0},{96,32},{1,65},{33,97},{65,1},{97,33},{2,66}... | collective-permute-start | bytes 393224 | tf_op jit(solution)/shard_map/ppermute | solution.py:23
  112.3 1.5 %collective-permute-start.37 = (bf16[64,1024]{1,0:T(8,128)(2,1)S(1)}, bf16[64,1024]{1,0:T(8,128)(2,1)S(1)}, u32[]{:S(2)}, u32[]{:S(2)}) collective-permute-start(bf16[64,1024]{1,0:T(8,128)(2,1)S(1)} %select_convert_fusion), channel_id=1, source_target_pairs={{0,16},{16,0},{32,48},{48,32},{64,80},{80,64},{96,112},{112,96},{1... | collective-permute-start | bytes 393224 | tf_op jit(solution)/shard_map/ppermute | solution.py:23
  113.8 2.6 %collective-permute-done.9 = bf16[64,1024]{1,0:T(8,128)(2,1)S(1)} collective-permute-done((bf16[64,1024]{1,0:T(8,128)(2,1)S(1)}, bf16[64,1024]{1,0:T(8,128)(2,1)S(1)}, u32[]{:S(2)}, u32[]{:S(2)}) %collective-permute-start.9) | collective-permute-done | bytes 131104 | tf_op jit(solution)/shard_map/ppermute | solution.py:23
  116.4 1.6 %collective-permute-done.8 = bf16[64,1024]{1,0:T(8,128)(2,1)S(1)} collective-permute-done((bf16[64,1024]{1,0:T(8,128)(2,1)S(1)}, bf16[64,1024]{1,0:T(8,128)(2,1)S(1)}, u32[]{:S(2)}, u32[]{:S(2)}) %collective-permute-start.8) | collective-permute-done | bytes 131104 | tf_op jit(solution)/shard_map/ppermute | solution.py:23
  118.0 1.5 %collective-permute-done.37 = bf16[64,1024]{1,0:T(8,128)(2,1)S(1)} collective-permute-done((bf16[64,1024]{1,0:T(8,128)(2,1)S(1)}, bf16[64,1024]{1,0:T(8,128)(2,1)S(1)}, u32[]{:S(2)}, u32[]{:S(2)}) %collective-permute-start.37) | collective-permute-done | bytes 131104 | tf_op jit(solution)/shard_map/ppermute | solution.py:23
  (139 shorter events, 13.0 us)
Async XLA Ops:
  1.9 18.5 %all-to-all-start = ((bf16[32,4,1024]{2,1,0:T(4,128)(2,1)}), bf16[32,4,1024]{2,1,0:T(4,128)(2,1)S(1)}, u32[]{:S(2)}, u32[]{:S(2)}) async-start(bf16[32,4,1024]{2,1,0:T(4,128)(2,1)} %pad_maximum_fusion.12), calls=%async_computation | async-start | bytes 524288 | tf_op jit(solution)/shard_map/all_to_all | solution.py:48
  20.5 8.2 %slice-start.2 = ((s8[6815744]{0:T(1024)(128)(4,1)}), s8[4194304]{0:T(1024)(128)(4,1)S(1)}, s32[]{:S(2)}) async-start(s8[6815744]{0:T(1024)(128)(4,1)} %bitcast.208), calls=%async_computation.3 | async-start | bytes 8388608
  20.6 8.1 %slice-start.3 = ((s8[6815744]{0:T(1024)(128)(4,1)}), s8[2621440]{0:T(1024)(128)(4,1)S(1)}, s32[]{:S(2)}) async-start(s8[6815744]{0:T(1024)(128)(4,1)} %bitcast.208), calls=%async_computation.4 | async-start | bytes 5242880
  20.6 11.4 %collective-permute-start.27 = (bf16[128,1024]{1,0:T(8,128)(2,1)S(1)}, bf16[128,1024]{1,0:T(8,128)(2,1)S(1)}, u32[]{:S(2)}, u32[]{:S(2)}) collective-permute-start(bf16[128,1024]{1,0:T(8,128)(2,1)S(1)} %bitcast_dynamic-update-slice_fusion), channel_id=1, source_target_pairs={{0,96},{32,64},{64,32},{96,0},{1,97},{33,65},{65,33},{97,1},{2,98}... | collective-permute-start | bytes 786440 | tf_op jit(solution)/shard_map/ppermute | solution.py:23
  23.1 11.0 %collective-permute-start.10 = (bf16[128,1024]{1,0:T(8,128)(2,1)S(1)}, bf16[128,1024]{1,0:T(8,128)(2,1)S(1)}, u32[]{:S(2)}, u32[]{:S(2)}) collective-permute-start(bf16[128,1024]{1,0:T(8,128)(2,1)S(1)} %bitcast_dynamic-update-slice_fusion), channel_id=1, source_target_pairs={{0,32},{32,0},{64,96},{96,64},{1,33},{33,1},{65,97},{97,65},{2,34}... | collective-permute-start | bytes 786440 | tf_op jit(solution)/shard_map/ppermute | solution.py:23
  23.2 13.2 %collective-permute-start = (bf16[128,1024]{1,0:T(8,128)(2,1)S(1)}, bf16[128,1024]{1,0:T(8,128)(2,1)S(1)}, u32[]{:S(2)}, u32[]{:S(2)}) collective-permute-start(bf16[128,1024]{1,0:T(8,128)(2,1)S(1)} %bitcast_dynamic-update-slice_fusion), channel_id=1, source_target_pairs={{0,64},{32,96},{64,0},{96,32},{1,65},{33,97},{65,1},{97,33},{2,66}... | collective-permute-start | bytes 786440 | tf_op jit(solution)/shard_map/ppermute | solution.py:23
  24.5 7.5 %slice-start = ((s8[6815744]{0:T(1024)(128)(4,1)}), s8[4194304]{0:T(1024)(128)(4,1)S(1)}, s32[]{:S(2)}) async-start(s8[6815744]{0:T(1024)(128)(4,1)} %bitcast.206), calls=%async_computation.1 | async-start | bytes 8388608
  28.7 3.3 %slice-start.1 = ((s8[6815744]{0:T(1024)(128)(4,1)}), s8[2621440]{0:T(1024)(128)(4,1)S(1)}, s32[]{:S(2)}) async-start(s8[6815744]{0:T(1024)(128)(4,1)} %bitcast.206), calls=%async_computation.2 | async-start | bytes 5242880
  30.2 11.4 %collective-permute-start.20 = (f16[2,64,3328]{2,1,0:T(8,128)(2,1)S(1)}, f16[2,64,3328]{2,1,0:T(8,128)(2,1)S(1)}, u32[]{:S(2)}, u32[]{:S(2)}) collective-permute-start(f16[2,64,3328]{2,1,0:T(8,128)(2,1)S(1)} %pad_maximum_fusion.2), channel_id=1, source_target_pairs={{0,1},{1,0},{2,3},{3,2},{4,5},{5,4},{6,7},{7,6},{8,9},{9,8},{10,11... | collective-permute-start | bytes 2555912 | tf_op jit(solution)/shard_map/ppermute | solution.py:23
  38.8 3.9 %collective-permute-start.28 = (f16[2,64,3328]{2,1,0:T(8,128)(2,1)S(1)}, f16[2,64,3328]{2,1,0:T(8,128)(2,1)S(1)}, u32[]{:S(2)}, u32[]{:S(2)}) collective-permute-start(f16[2,64,3328]{2,1,0:T(8,128)(2,1)S(1)} %pad_maximum_fusion.3), channel_id=1, source_target_pairs={{0,1},{1,0},{2,3},{3,2},{4,5},{5,4},{6,7},{7,6},{8,9},{9,8},{10,11... | collective-permute-start | bytes 2555912 | tf_op jit(solution)/shard_map/ppermute | solution.py:23
  40.3 3.3 %collective-permute-start.11 = (f16[2,64,3328]{2,1,0:T(8,128)(2,1)S(1)}, f16[2,64,3328]{2,1,0:T(8,128)(2,1)S(1)}, u32[]{:S(2)}, u32[]{:S(2)}) collective-permute-start(f16[2,64,3328]{2,1,0:T(8,128)(2,1)S(1)} %pad_maximum_fusion.1), channel_id=1, source_target_pairs={{0,1},{1,0},{2,3},{3,2},{4,5},{5,4},{6,7},{7,6},{8,9},{9,8},{10,11... | collective-permute-start | bytes 2555912 | tf_op jit(solution)/shard_map/ppermute | solution.py:23
  40.8 5.0 %collective-permute-start.1 = (f16[2,64,3328]{2,1,0:T(8,128)(2,1)S(1)}, f16[2,64,3328]{2,1,0:T(8,128)(2,1)S(1)}, u32[]{:S(2)}, u32[]{:S(2)}) collective-permute-start(f16[2,64,3328]{2,1,0:T(8,128)(2,1)S(1)} %pad_maximum_fusion), channel_id=1, source_target_pairs={{0,1},{1,0},{2,3},{3,2},{4,5},{5,4},{6,7},{7,6},{8,9},{9,8},{10,11... | collective-permute-start | bytes 2555912 | tf_op jit(solution)/shard_map/ppermute | solution.py:23
  41.9 8.3 %collective-permute-start.21 = (f16[2,32,3328]{2,1,0:T(8,128)(2,1)S(1)}, f16[2,32,3328]{2,1,0:T(8,128)(2,1)S(1)}, u32[]{:S(2)}, u32[]{:S(2)}) collective-permute-start(f16[2,32,3328]{2,1,0:T(8,128)(2,1)S(1)} %pad_maximum_fusion.8), channel_id=1, source_target_pairs={{0,4},{1,13},{4,0},{5,9},{8,12},{9,5},{12,8},{13,1},{2,6},{3,15},{... | collective-permute-start | bytes 1277960 | tf_op jit(solution)/shard_map/ppermute | solution.py:23
  43.2 14.9 %collective-permute-start.29 = (f16[2,64,1664]{2,1,0:T(8,128)(2,1)S(1)}, f16[2,64,1664]{2,1,0:T(8,128)(2,1)S(1)}, u32[]{:S(2)}, u32[]{:S(2)}) collective-permute-start(f16[2,64,1664]{2,1,0:T(8,128)(2,1)S(1)} %pad_maximum_fusion.10), channel_id=1, source_target_pairs={{0,2},{2,0},{1,3},{3,1},{4,6},{6,4},{5,7},{7,5},{8,10},{10,8},{9,1... | collective-permute-start | bytes 1277960 | tf_op jit(solution)/shard_map/ppermute | solution.py:23
  44.0 15.0 %collective-permute-start.12 = (f16[2,32,3328]{2,1,0:T(8,128)(2,1)S(1)}, f16[2,32,3328]{2,1,0:T(8,128)(2,1)S(1)}, u32[]{:S(2)}, u32[]{:S(2)}) collective-permute-start(f16[2,32,3328]{2,1,0:T(8,128)(2,1)S(1)} %pad_maximum_fusion.6), channel_id=1, source_target_pairs={{0,4},{1,13},{4,0},{5,9},{8,12},{9,5},{12,8},{13,1},{2,6},{3,15},{... | collective-permute-start | bytes 1277960 | tf_op jit(solution)/shard_map/ppermute | solution.py:23
  50.4 7.4 %collective-permute-start.22 = (f16[2,16,3328]{2,1,0:T(8,128)(2,1)S(1)}, f16[2,16,3328]{2,1,0:T(8,128)(2,1)S(1)}, u32[]{:S(2)}, u32[]{:S(2)}) collective-permute-start(f16[2,16,3328]{2,1,0:T(8,128)(2,1)S(1)} %pad_maximum_fusion.19), channel_id=1, source_target_pairs={{0,12},{1,5},{4,8},{5,1},{8,4},{9,13},{12,0},{13,9},{2,14},{3,7},{... | collective-permute-start | bytes 638984 | tf_op jit(solution)/shard_map/ppermute | solution.py:23
  50.6 11.0 %collective-permute-start.2 = (f16[2,32,3328]{2,1,0:T(8,128)(2,1)S(1)}, f16[2,32,3328]{2,1,0:T(8,128)(2,1)S(1)}, u32[]{:S(2)}, u32[]{:S(2)}) collective-permute-start(f16[2,32,3328]{2,1,0:T(8,128)(2,1)S(1)} %pad_maximum_fusion.4), channel_id=1, source_target_pairs={{0,4},{1,13},{4,0},{5,9},{8,12},{9,5},{12,8},{13,1},{2,6},{3,15},{... | collective-permute-start | bytes 1277960 | tf_op jit(solution)/shard_map/ppermute | solution.py:23
  58.0 4.8 %collective-permute-start.23 = (f16[2,16,3328]{2,1,0:T(8,128)(2,1)S(1)}, f16[2,16,3328]{2,1,0:T(8,128)(2,1)S(1)}, u32[]{:S(2)}, u32[]{:S(2)}) collective-permute-start(f16[2,16,3328]{2,1,0:T(8,128)(2,1)S(1)} %pad_maximum_fusion.20), channel_id=1, source_target_pairs={{0,2},{2,0},{1,3},{3,1},{4,6},{6,4},{5,7},{7,5},{8,10},{10,8},{9,1... | collective-permute-start | bytes 638984 | tf_op jit(solution)/shard_map/ppermute | solution.py:23
  58.4 6.4 %collective-permute-start.30 = (f16[2,32,1664]{2,1,0:T(8,128)(2,1)S(1)}, f16[2,32,1664]{2,1,0:T(8,128)(2,1)S(1)}, u32[]{:S(2)}, u32[]{:S(2)}) collective-permute-start(f16[2,32,1664]{2,1,0:T(8,128)(2,1)S(1)} %pad_maximum_fusion.22), channel_id=1, source_target_pairs={{0,4},{1,13},{4,0},{5,9},{8,12},{9,5},{12,8},{13,1},{2,6},{3,15},{... | collective-permute-start | bytes 638984 | tf_op jit(solution)/shard_map/ppermute | solution.py:23
  59.3 5.8 %collective-permute-start.13 = (f16[2,16,3328]{2,1,0:T(8,128)(2,1)S(1)}, f16[2,16,3328]{2,1,0:T(8,128)(2,1)S(1)}, u32[]{:S(2)}, u32[]{:S(2)}) collective-permute-start(f16[2,16,3328]{2,1,0:T(8,128)(2,1)S(1)} %pad_maximum_fusion.16), channel_id=1, source_target_pairs={{0,12},{1,5},{4,8},{5,1},{8,4},{9,13},{12,0},{13,9},{2,14},{3,7},{... | collective-permute-start | bytes 638984 | tf_op jit(solution)/shard_map/ppermute | solution.py:23
  61.6 36.6 %slice-start.4 = ((s8[6815744]{0:T(1024)(128)(4,1)}), s8[4194304]{0:T(1024)(128)(4,1)S(1)}, s32[]{:S(2)}) async-start(s8[6815744]{0:T(1024)(128)(4,1)} %bitcast.210), calls=%async_computation.5 | async-start | bytes 8388608
  61.9 7.0 %collective-permute-start.3 = (f16[2,16,3328]{2,1,0:T(8,128)(2,1)S(1)}, f16[2,16,3328]{2,1,0:T(8,128)(2,1)S(1)}, u32[]{:S(2)}, u32[]{:S(2)}) collective-permute-start(f16[2,16,3328]{2,1,0:T(8,128)(2,1)S(1)} %pad_maximum_fusion.13), channel_id=1, source_target_pairs={{0,12},{1,5},{4,8},{5,1},{8,4},{9,13},{12,0},{13,9},{2,14},{3,7},{... | collective-permute-start | bytes 638984 | tf_op jit(solution)/shard_map/ppermute | solution.py:23
  62.9 7.2 %collective-permute-start.24 = (bf16[16,3328]{1,0:T(8,128)(2,1)S(1)}, bf16[16,3328]{1,0:T(8,128)(2,1)S(1)}, u32[]{:S(2)}, u32[]{:S(2)}) collective-permute-start(bf16[16,3328]{1,0:T(8,128)(2,1)S(1)} %fusion.54), channel_id=1, source_target_pairs={{0,12},{1,5},{4,8},{5,1},{8,4},{9,13},{12,0},{13,9},{2,14},{3,7},{... | collective-permute-start | bytes 319496 | tf_op jit(solution)/shard_map/ppermute | solution.py:23
  65.0 6.2 %collective-permute-start.31 = (f16[2,16,1664]{2,1,0:T(8,128)(2,1)S(1)}, f16[2,16,1664]{2,1,0:T(8,128)(2,1)S(1)}, u32[]{:S(2)}, u32[]{:S(2)}) collective-permute-start(f16[2,16,1664]{2,1,0:T(8,128)(2,1)S(1)} %pad_maximum_fusion.25), channel_id=1, source_target_pairs={{0,12},{1,5},{4,8},{5,1},{8,4},{9,13},{12,0},{13,9},{2,14},{3,7},{... | collective-permute-start | bytes 319496 | tf_op jit(solution)/shard_map/ppermute | solution.py:23
  65.2 33.0 %slice-start.5 = ((s8[6815744]{0:T(1024)(128)(4,1)}), s8[2621440]{0:T(1024)(128)(4,1)S(1)}, s32[]{:S(2)}) async-start(s8[6815744]{0:T(1024)(128)(4,1)} %bitcast.210), calls=%async_computation.6 | async-start | bytes 5242880
  65.2 11.4 %collective-permute-start.14 = (f16[2,16,3328]{2,1,0:T(8,128)(2,1)S(1)}, f16[2,16,3328]{2,1,0:T(8,128)(2,1)S(1)}, u32[]{:S(2)}, u32[]{:S(2)}) collective-permute-start(f16[2,16,3328]{2,1,0:T(8,128)(2,1)S(1)} %pad_maximum_fusion.17), channel_id=1, source_target_pairs={{0,2},{2,0},{1,3},{3,1},{4,6},{6,4},{5,7},{7,5},{8,10},{10,8},{9,1... | collective-permute-start | bytes 638984 | tf_op jit(solution)/shard_map/ppermute | solution.py:23
  69.1 8.3 %collective-permute-start.4 = (f16[2,16,3328]{2,1,0:T(8,128)(2,1)S(1)}, f16[2,16,3328]{2,1,0:T(8,128)(2,1)S(1)}, u32[]{:S(2)}, u32[]{:S(2)}) collective-permute-start(f16[2,16,3328]{2,1,0:T(8,128)(2,1)S(1)} %pad_maximum_fusion.14), channel_id=1, source_target_pairs={{0,2},{2,0},{1,3},{3,1},{4,6},{6,4},{5,7},{7,5},{8,10},{10,8},{9,1... | collective-permute-start | bytes 638984 | tf_op jit(solution)/shard_map/ppermute | solution.py:23
  71.2 4.3 %collective-permute-start.32 = (bf16[16,1664]{1,0:T(8,128)(2,1)S(1)}, bf16[16,1664]{1,0:T(8,128)(2,1)S(1)}, u32[]{:S(2)}, u32[]{:S(2)}) collective-permute-start(bf16[16,1664]{1,0:T(8,128)(2,1)S(1)} %fusion.76), channel_id=1, source_target_pairs={{0,2},{2,0},{1,3},{3,1},{4,6},{6,4},{5,7},{7,5},{8,10},{10,8},{9,1... | collective-permute-start | bytes 159752 | tf_op jit(solution)/shard_map/ppermute | solution.py:23
  72.2 11.0 %collective-permute-start.25 = (bf16[32,3328]{1,0:T(8,128)(2,1)S(1)}, bf16[32,3328]{1,0:T(8,128)(2,1)S(1)}, u32[]{:S(2)}, u32[]{:S(2)}) collective-permute-start(bf16[32,3328]{1,0:T(8,128)(2,1)S(1)} %pad_maximum_fusion.21), channel_id=1, source_target_pairs={{0,4},{1,13},{4,0},{5,9},{8,12},{9,5},{12,8},{13,1},{2,6},{3,15},{... | collective-permute-start | bytes 638984 | tf_op jit(solution)/shard_map/ppermute | solution.py:23
  75.6 3.9 %collective-permute-start.33 = (bf16[16,3328]{1,0:T(8,128)(2,1)S(1)}, bf16[16,3328]{1,0:T(8,128)(2,1)S(1)}, u32[]{:S(2)}, u32[]{:S(2)}) collective-permute-start(bf16[16,3328]{1,0:T(8,128)(2,1)S(1)} %pad_maximum_fusion.26), channel_id=1, source_target_pairs={{0,12},{1,5},{4,8},{5,1},{8,4},{9,13},{12,0},{13,9},{2,14},{3,7},{... | collective-permute-start | bytes 319496 | tf_op jit(solution)/shard_map/ppermute | solution.py:23
  76.8 10.9 %collective-permute-start.15 = (bf16[16,3328]{1,0:T(8,128)(2,1)S(1)}, bf16[16,3328]{1,0:T(8,128)(2,1)S(1)}, u32[]{:S(2)}, u32[]{:S(2)}) collective-permute-start(bf16[16,3328]{1,0:T(8,128)(2,1)S(1)} %fusion.56), channel_id=1, source_target_pairs={{0,12},{1,5},{4,8},{5,1},{8,4},{9,13},{12,0},{13,9},{2,14},{3,7},{... | collective-permute-start | bytes 319496 | tf_op jit(solution)/shard_map/ppermute | solution.py:23
  77.4 12.2 %collective-permute-start.5 = (bf16[16,3328]{1,0:T(8,128)(2,1)S(1)}, bf16[16,3328]{1,0:T(8,128)(2,1)S(1)}, u32[]{:S(2)}, u32[]{:S(2)}) collective-permute-start(bf16[16,3328]{1,0:T(8,128)(2,1)S(1)} %fusion.58), channel_id=1, source_target_pairs={{0,12},{1,5},{4,8},{5,1},{8,4},{9,13},{12,0},{13,9},{2,14},{3,7},{... | collective-permute-start | bytes 319496 | tf_op jit(solution)/shard_map/ppermute | solution.py:23
  79.5 11.0 %collective-permute-start.34 = (bf16[32,3328]{1,0:T(8,128)(2,1)S(1)}, bf16[32,3328]{1,0:T(8,128)(2,1)S(1)}, u32[]{:S(2)}, u32[]{:S(2)}) collective-permute-start(bf16[32,3328]{1,0:T(8,128)(2,1)S(1)} %pad_maximum_fusion.23), channel_id=1, source_target_pairs={{0,4},{1,13},{4,0},{5,9},{8,12},{9,5},{12,8},{13,1},{2,6},{3,15},{... | collective-permute-start | bytes 638984 | tf_op jit(solution)/shard_map/ppermute | solution.py:23
  83.2 15.0 %collective-permute-start.26 = (bf16[64,3328]{1,0:T(8,128)(2,1)S(1)}, bf16[64,3328]{1,0:T(8,128)(2,1)S(1)}, u32[]{:S(2)}, u32[]{:S(2)}) collective-permute-start(bf16[64,3328]{1,0:T(8,128)(2,1)S(1)} %pad_maximum_fusion.9), channel_id=1, source_target_pairs={{0,1},{1,0},{2,3},{3,2},{4,5},{5,4},{6,7},{7,6},{8,9},{9,8},{10,11... | collective-permute-start | bytes 1277960 | tf_op jit(solution)/shard_map/ppermute | solution.py:23
  87.7 6.0 %collective-permute-start.16 = (bf16[32,3328]{1,0:T(8,128)(2,1)S(1)}, bf16[32,3328]{1,0:T(8,128)(2,1)S(1)}, u32[]{:S(2)}, u32[]{:S(2)}) collective-permute-start(bf16[32,3328]{1,0:T(8,128)(2,1)S(1)} %pad_maximum_fusion.18), channel_id=1, source_target_pairs={{0,4},{1,13},{4,0},{5,9},{8,12},{9,5},{12,8},{13,1},{2,6},{3,15},{... | collective-permute-start | bytes 638984 | tf_op jit(solution)/shard_map/ppermute | solution.py:23
  89.6 6.3 %collective-permute-start.6 = (bf16[32,3328]{1,0:T(8,128)(2,1)S(1)}, bf16[32,3328]{1,0:T(8,128)(2,1)S(1)}, u32[]{:S(2)}, u32[]{:S(2)}) collective-permute-start(bf16[32,3328]{1,0:T(8,128)(2,1)S(1)} %pad_maximum_fusion.15), channel_id=1, source_target_pairs={{0,4},{1,13},{4,0},{5,9},{8,12},{9,5},{12,8},{13,1},{2,6},{3,15},{... | collective-permute-start | bytes 638984 | tf_op jit(solution)/shard_map/ppermute | solution.py:23
  90.6 8.8 %collective-permute-start.35 = (bf16[64,3328]{1,0:T(8,128)(2,1)S(1)}, bf16[64,3328]{1,0:T(8,128)(2,1)S(1)}, u32[]{:S(2)}, u32[]{:S(2)}) collective-permute-start(bf16[64,3328]{1,0:T(8,128)(2,1)S(1)} %pad_maximum_fusion.11), channel_id=1, source_target_pairs={{0,1},{1,0},{2,3},{3,2},{4,5},{5,4},{6,7},{7,6},{8,9},{9,8},{10,11... | collective-permute-start | bytes 1277960 | tf_op jit(solution)/shard_map/ppermute | solution.py:23
  93.7 9.3 %collective-permute-start.17 = (bf16[64,3328]{1,0:T(8,128)(2,1)S(1)}, bf16[64,3328]{1,0:T(8,128)(2,1)S(1)}, u32[]{:S(2)}, u32[]{:S(2)}) collective-permute-start(bf16[64,3328]{1,0:T(8,128)(2,1)S(1)} %pad_maximum_fusion.7), channel_id=1, source_target_pairs={{0,1},{1,0},{2,3},{3,2},{4,5},{5,4},{6,7},{7,6},{8,9},{9,8},{10,11... | collective-permute-start | bytes 1277960 | tf_op jit(solution)/shard_map/ppermute | solution.py:23
  96.0 10.8 %collective-permute-start.7 = (bf16[64,3328]{1,0:T(8,128)(2,1)S(1)}, bf16[64,3328]{1,0:T(8,128)(2,1)S(1)}, u32[]{:S(2)}, u32[]{:S(2)}) collective-permute-start(bf16[64,3328]{1,0:T(8,128)(2,1)S(1)} %pad_maximum_fusion.5), channel_id=1, source_target_pairs={{0,1},{1,0},{2,3},{3,2},{4,5},{5,4},{6,7},{7,6},{8,9},{9,8},{10,11... | collective-permute-start | bytes 1277960 | tf_op jit(solution)/shard_map/ppermute | solution.py:23
  100.4 11.8 %collective-permute-start.36 = (bf16[128,1024]{1,0:T(8,128)(2,1)S(1)}, bf16[128,1024]{1,0:T(8,128)(2,1)S(1)}, u32[]{:S(2)}, u32[]{:S(2)}) collective-permute-start(bf16[128,1024]{1,0:T(8,128)(2,1)S(1)} %convolution_convert_fusion), channel_id=1, source_target_pairs={{0,96},{32,64},{64,32},{96,0},{1,97},{33,65},{65,33},{97,1},{2,98}... | collective-permute-start | bytes 786440 | tf_op jit(solution)/shard_map/ppermute | solution.py:23
  104.0 9.8 %collective-permute-start.19 = (bf16[64,1024]{1,0:T(8,128)(2,1)S(1)}, bf16[64,1024]{1,0:T(8,128)(2,1)S(1)}, u32[]{:S(2)}, u32[]{:S(2)}) collective-permute-start(bf16[64,1024]{1,0:T(8,128)(2,1)S(1)} %get-tuple-element.86), channel_id=1, source_target_pairs={{0,48},{16,32},{32,16},{48,0},{64,112},{80,96},{96,80},{112,64},{1... | collective-permute-start | bytes 393224 | tf_op jit(solution)/shard_map/ppermute | solution.py:23
  104.1 9.7 %collective-permute-start.18 = (bf16[64,1024]{1,0:T(8,128)(2,1)S(1)}, bf16[64,1024]{1,0:T(8,128)(2,1)S(1)}, u32[]{:S(2)}, u32[]{:S(2)}) collective-permute-start(bf16[64,1024]{1,0:T(8,128)(2,1)S(1)} %get-tuple-element.85), channel_id=1, source_target_pairs={{0,32},{32,0},{64,96},{96,64},{1,33},{33,1},{65,97},{97,65},{2,34}... | collective-permute-start | bytes 393224 | tf_op jit(solution)/shard_map/ppermute | solution.py:23
  107.9 8.5 %collective-permute-start.9 = (bf16[64,1024]{1,0:T(8,128)(2,1)S(1)}, bf16[64,1024]{1,0:T(8,128)(2,1)S(1)}, u32[]{:S(2)}, u32[]{:S(2)}) collective-permute-start(bf16[64,1024]{1,0:T(8,128)(2,1)S(1)} %get-tuple-element.72), channel_id=1, source_target_pairs={{0,80},{16,64},{32,112},{48,96},{64,16},{80,0},{96,48},{112,32},{1... | collective-permute-start | bytes 393224 | tf_op jit(solution)/shard_map/ppermute | solution.py:23
  109.1 8.9 %collective-permute-start.8 = (bf16[64,1024]{1,0:T(8,128)(2,1)S(1)}, bf16[64,1024]{1,0:T(8,128)(2,1)S(1)}, u32[]{:S(2)}, u32[]{:S(2)}) collective-permute-start(bf16[64,1024]{1,0:T(8,128)(2,1)S(1)} %get-tuple-element.71), channel_id=1, source_target_pairs={{0,64},{32,96},{64,0},{96,32},{1,65},{33,97},{65,1},{97,33},{2,66}... | collective-permute-start | bytes 393224 | tf_op jit(solution)/shard_map/ppermute | solution.py:23
  112.3 7.2 %collective-permute-start.37 = (bf16[64,1024]{1,0:T(8,128)(2,1)S(1)}, bf16[64,1024]{1,0:T(8,128)(2,1)S(1)}, u32[]{:S(2)}, u32[]{:S(2)}) collective-permute-start(bf16[64,1024]{1,0:T(8,128)(2,1)S(1)} %select_convert_fusion), channel_id=1, source_target_pairs={{0,16},{16,0},{32,48},{48,32},{64,80},{80,64},{96,112},{112,96},{1... | collective-permute-start | bytes 393224 | tf_op jit(solution)/shard_map/ppermute | solution.py:23

commit v12 on v10

--- a/solution.py
+++ b/solution.py
@@ -6,7 +6,7 @@
 F32, BF16, F16 = jnp.float32, jnp.bfloat16, jnp.float16
 LIFT = 8.0
 AXES = ("x", "z_hi", "y", "z_lo", "core")
-Z_FIRST = 3
+Z_FIRST = 1
 
 
 def permute(axes, sizes, move):
@@ -39,7 +39,7 @@
     swap_second = permute(("y", "core"), (4, 2), lambda y, c: (y ^ (1 if c else 3), c))
     swap_x = {e: permute(("x",), (4,), lambda x, e=e: (x ^ e,)) for e in (1, 2, 3)}
     swap_row = {
-        e: permute(("x", "z_hi"), (4, 2), lambda x, z, e=e: (x ^ e, z ^ 1)) for e in range(3)
+        e: permute(("x", "z_hi"), (4, 2), lambda x, z, e=e: (x ^ e, z ^ 1)) for e in (0, 2, 3)
     }
 
     features = tokens.shape[1] // 16
@@ -119,7 +119,7 @@
             mixed = product(both, down_weight)
             if e == 0:
                 whole.append(tie(mixed))
-            elif e == 3:
+            elif e == 1:
                 whole.append(swap_x[e](tie(mixed.astype(BF16))).astype(F32))
             else:
                 same, cross = parted(mixed)
@@ -129,7 +129,7 @@
 
     whole = []
     for s in (-1, 0, 2, 3, 4, 5, 6, 7, 8):
-        for e in (0, 2, 1, 3):
+        for e in (0, 2, 3, 1):
             if e or s >= 0:
                 step(e, s)
 

time: 120 us -> 121 us (level)
  no operation moved by 1% of the time
where the time goes in v12:
time: 121 us
  starting transfers between devices  62.3 us (51%)
  waiting for transfers between devices  34.4 us (28%)
  matrix products  15.8 us (13%)
  other arithmetic  5.8 us (5%)
  local copies, waits for them, and re-layouts  2.01 us (2%)
    ppermute x38, starting transfers between devices, permute(): return lambda v: lax.ppermute(v, axes, pairs)  52.7 us
    ppermute x38, waiting for transfers between devices, permute(): return lambda v: lax.ppermute(v, axes, pairs)  25.6 us
    dot_general x12, matrix products, product(): return jnp.dot(rows, weight, preferred_element_type=F32)  15.8 us
    all_to_all x1, starting transfers between devices, per_device(): lax.all_to_all(blocks, AXES[1:], split_axis=0, concat_axis=0, tiled=True)  9.6 us
    all_to_all x1, waiting for transfers between devices, per_device(): lax.all_to_all(blocks, AXES[1:], split_axis=0, concat_axis=0, tiled=True)  8.79 us
  transfers between devices with their start and end apart: 39, of which 15 were waited for; matrix products, arithmetic and copies ran while one was open for 17% of the time, Pallas kernels for 0%

profile of v12, /device:TPU:1, one launch (start us, length us, event | category | flops | bytes accessed | tf_op | source)
XLA Modules:
  0.0 121.1 jit_solution(17165223350672564217)
XLA Ops:
  0.0 0.9 broadcast_in_dim.7
  1.8 9.6 %all-to-all-start = ((bf16[32,4,1024]{2,1,0:T(4,128)(2,1)}), bf16[32,4,1024]{2,1,0:T(4,128)(2,1)S(1)}, u32[]{:S(2)}, u32[]{:S(2)}) async-start(bf16[32,4,1024]{2,1,0:T(4,128)(2,1)} %all_to_all.6), calls=%async_computation | async-start | bytes 524288 | tf_op jit(solution)/shard_map/all_to_all | solution.py:48
  11.5 8.8 %all-to-all-done = bf16[32,4,1024]{2,1,0:T(4,128)(2,1)S(1)} async-done(((bf16[32,4,1024]{2,1,0:T(4,128)(2,1)}), bf16[32,4,1024]{2,1,0:T(4,128)(2,1)S(1)}, u32[]{:S(2)}, u32[]{:S(2)}) %all-to-all-start) | async-done | bytes 262176 | tf_op jit(solution)/shard_map/all_to_all | solution.py:48
  20.5 1.3 %collective-permute-start.27 = (bf16[128,1024]{1,0:T(8,128)(2,1)S(1)}, bf16[128,1024]{1,0:T(8,128)(2,1)S(1)}, u32[]{:S(2)}, u32[]{:S(2)}) collective-permute-start(bf16[128,1024]{1,0:T(8,128)(2,1)S(1)} %bitcast_dynamic-update-slice_fusion), channel_id=1, source_target_pairs={{0,32},{32,0},{64,96},{96,64},{1,33},{33,1},{65,97},{97,65},{2,34}... | collective-permute-start | bytes 786440 | tf_op jit(solution)/shard_map/ppermute | solution.py:23
  21.8 1.8 %collective-permute-start.10 = (bf16[128,1024]{1,0:T(8,128)(2,1)S(1)}, bf16[128,1024]{1,0:T(8,128)(2,1)S(1)}, u32[]{:S(2)}, u32[]{:S(2)}) collective-permute-start(bf16[128,1024]{1,0:T(8,128)(2,1)S(1)} %bitcast_dynamic-update-slice_fusion), channel_id=1, source_target_pairs={{0,96},{32,64},{64,32},{96,0},{1,97},{33,65},{65,33},{97,1},{2,98}... | collective-permute-start | bytes 786440 | tf_op jit(solution)/shard_map/ppermute | solution.py:23
  24.3 4.1 %fusion.87 = f32[128,3328]{1,0:T(8,128)S(1)} fusion(bf16[128,1024]{1,0:T(8,128)(2,1)S(1)} %bitcast_dynamic-update-slice_fusion, bf16[1024,3328]{1,0:T(8,128)(2,1)} %param.5), kind=kOutput, calls=%fused_computation.202 | convolution fusion | flops 872415232 | bytes 8781824 | tf_op jit(solution)/shard_map/dot_general | solution.py:74
  28.5 1.1 fusion.88
  29.9 1.6 %collective-permute-start.20 = (f16[2,64,3328]{2,1,0:T(8,128)(2,1)S(1)}, f16[2,64,3328]{2,1,0:T(8,128)(2,1)S(1)}, u32[]{:S(2)}, u32[]{:S(2)}) collective-permute-start(f16[2,64,3328]{2,1,0:T(8,128)(2,1)S(1)} %pad_maximum_fusion.2), channel_id=1, source_target_pairs={{0,1},{1,0},{2,3},{3,2},{4,5},{5,4},{6,7},{7,6},{8,9},{9,8},{10,11... | collective-permute-start | bytes 2555912 | tf_op jit(solution)/shard_map/ppermute | solution.py:23
  31.5 1.1 fusion.89
  32.5 1.1 fusion.90
  33.6 1.1 fusion.85
  34.7 1.1 fusion.86
  35.8 1.1 fusion.83
  36.9 1.1 fusion.84
  38.3 3.8 %collective-permute-start.28 = (f16[2,64,3328]{2,1,0:T(8,128)(2,1)S(1)}, f16[2,64,3328]{2,1,0:T(8,128)(2,1)S(1)}, u32[]{:S(2)}, u32[]{:S(2)}) collective-permute-start(f16[2,64,3328]{2,1,0:T(8,128)(2,1)S(1)} %pad_maximum_fusion.3), channel_id=1, source_target_pairs={{0,1},{1,0},{2,3},{3,2},{4,5},{5,4},{6,7},{7,6},{8,9},{9,8},{10,11... | collective-permute-start | bytes 2555912 | tf_op jit(solution)/shard_map/ppermute | solution.py:23
  46.1 1.8 %collective-permute-start.12 = (f16[2,32,3328]{2,1,0:T(8,128)(2,1)S(1)}, f16[2,32,3328]{2,1,0:T(8,128)(2,1)S(1)}, u32[]{:S(2)}, u32[]{:S(2)}) collective-permute-start(f16[2,32,3328]{2,1,0:T(8,128)(2,1)S(1)} %pad_maximum_fusion.6), channel_id=1, source_target_pairs={{0,4},{1,13},{4,0},{5,9},{8,12},{9,5},{12,8},{13,1},{2,6},{3,15},{... | collective-permute-start | bytes 1277960 | tf_op jit(solution)/shard_map/ppermute | solution.py:23
  48.2 4.1 %collective-permute-done.21 = f16[2,32,3328]{2,1,0:T(8,128)(2,1)S(1)} collective-permute-done((f16[2,32,3328]{2,1,0:T(8,128)(2,1)S(1)}, f16[2,32,3328]{2,1,0:T(8,128)(2,1)S(1)}, u32[]{:S(2)}, u32[]{:S(2)}) %collective-permute-start.21) | collective-permute-done | bytes 426016 | tf_op jit(solution)/shard_map/ppermute | solution.py:23
  53.5 6.4 %collective-permute-done.22 = f16[2,16,3328]{2,1,0:T(8,128)(2,1)S(1)} collective-permute-done((f16[2,16,3328]{2,1,0:T(8,128)(2,1)S(1)}, f16[2,16,3328]{2,1,0:T(8,128)(2,1)S(1)}, u32[]{:S(2)}, u32[]{:S(2)}) %collective-permute-start.22) | collective-permute-done | bytes 213024 | tf_op jit(solution)/shard_map/ppermute | solution.py:23
  61.5 2.2 %collective-permute-done.2 = f16[2,32,3328]{2,1,0:T(8,128)(2,1)S(1)} collective-permute-done((f16[2,32,3328]{2,1,0:T(8,128)(2,1)S(1)}, f16[2,32,3328]{2,1,0:T(8,128)(2,1)S(1)}, u32[]{:S(2)}, u32[]{:S(2)}) %collective-permute-start.2) | collective-permute-done | bytes 426016 | tf_op jit(solution)/shard_map/ppermute | solution.py:23
  65.0 1.9 %collective-permute-start.24 = (bf16[16,3328]{1,0:T(8,128)(2,1)S(1)}, bf16[16,3328]{1,0:T(8,128)(2,1)S(1)}, u32[]{:S(2)}, u32[]{:S(2)}) collective-permute-start(bf16[16,3328]{1,0:T(8,128)(2,1)S(1)} %fusion.54), channel_id=1, source_target_pairs={{0,12},{1,5},{4,8},{5,1},{8,4},{9,13},{12,0},{13,9},{2,14},{3,7},{... | collective-permute-start | bytes 319496 | tf_op jit(solution)/shard_map/ppermute | solution.py:23
  67.3 1.0 collective-permute-start.14
  68.4 2.6 %collective-permute-done.3 = f16[2,16,3328]{2,1,0:T(8,128)(2,1)S(1)} collective-permute-done((f16[2,16,3328]{2,1,0:T(8,128)(2,1)S(1)}, f16[2,16,3328]{2,1,0:T(8,128)(2,1)S(1)}, u32[]{:S(2)}, u32[]{:S(2)}) %collective-permute-start.3) | collective-permute-done | bytes 213024 | tf_op jit(solution)/shard_map/ppermute | solution.py:23
  72.2 1.1 collective-permute-done.31
  73.3 0.9 collective-permute-start.32
  74.3 2.4 %collective-permute-start.25 = (bf16[32,3328]{1,0:T(8,128)(2,1)S(1)}, bf16[32,3328]{1,0:T(8,128)(2,1)S(1)}, u32[]{:S(2)}, u32[]{:S(2)}) collective-permute-start(bf16[32,3328]{1,0:T(8,128)(2,1)S(1)} %pad_maximum_fusion.20), channel_id=1, source_target_pairs={{0,4},{1,13},{4,0},{5,9},{8,12},{9,5},{12,8},{13,1},{2,6},{3,15},{... | collective-permute-start | bytes 638984 | tf_op jit(solution)/shard_map/ppermute | solution.py:23
  76.7 0.9 collective-permute-done.32
  77.7 1.1 collective-permute-start.33
  79.5 1.1 collective-permute-start.5
  80.6 1.0 collective-permute-done.33
  81.6 3.7 %collective-permute-start.34 = (bf16[32,3328]{1,0:T(8,128)(2,1)S(1)}, bf16[32,3328]{1,0:T(8,128)(2,1)S(1)}, u32[]{:S(2)}, u32[]{:S(2)}) collective-permute-start(bf16[32,3328]{1,0:T(8,128)(2,1)S(1)} %pad_maximum_fusion.22), channel_id=1, source_target_pairs={{0,4},{1,13},{4,0},{5,9},{8,12},{9,5},{12,8},{13,1},{2,6},{3,15},{... | collective-permute-start | bytes 638984 | tf_op jit(solution)/shard_map/ppermute | solution.py:23
  85.3 4.4 %collective-permute-start.26 = (bf16[64,3328]{1,0:T(8,128)(2,1)S(1)}, bf16[64,3328]{1,0:T(8,128)(2,1)S(1)}, u32[]{:S(2)}, u32[]{:S(2)}) collective-permute-start(bf16[64,3328]{1,0:T(8,128)(2,1)S(1)} %pad_maximum_fusion.9), channel_id=1, source_target_pairs={{0,1},{1,0},{2,3},{3,2},{4,5},{5,4},{6,7},{7,6},{8,9},{9,8},{10,11... | collective-permute-start | bytes 1277960 | tf_op jit(solution)/shard_map/ppermute | solution.py:23
  89.8 1.9 %collective-permute-start.16 = (bf16[32,3328]{1,0:T(8,128)(2,1)S(1)}, bf16[32,3328]{1,0:T(8,128)(2,1)S(1)}, u32[]{:S(2)}, u32[]{:S(2)}) collective-permute-start(bf16[32,3328]{1,0:T(8,128)(2,1)S(1)} %pad_maximum_fusion.17), channel_id=1, source_target_pairs={{0,4},{1,13},{4,0},{5,9},{8,12},{9,5},{12,8},{13,1},{2,6},{3,15},{... | collective-permute-start | bytes 638984 | tf_op jit(solution)/shard_map/ppermute | solution.py:23
  91.7 0.9 collective-permute-start.6
  92.7 2.9 %collective-permute-start.35 = (bf16[64,3328]{1,0:T(8,128)(2,1)S(1)}, bf16[64,3328]{1,0:T(8,128)(2,1)S(1)}, u32[]{:S(2)}, u32[]{:S(2)}) collective-permute-start(bf16[64,3328]{1,0:T(8,128)(2,1)S(1)} %pad_maximum_fusion.11), channel_id=1, source_target_pairs={{0,1},{1,0},{2,3},{3,2},{4,5},{5,4},{6,7},{7,6},{8,9},{9,8},{10,11... | collective-permute-start | bytes 1277960 | tf_op jit(solution)/shard_map/ppermute | solution.py:23
  95.8 2.1 %collective-permute-start.17 = (bf16[64,3328]{1,0:T(8,128)(2,1)S(1)}, bf16[64,3328]{1,0:T(8,128)(2,1)S(1)}, u32[]{:S(2)}, u32[]{:S(2)}) collective-permute-start(bf16[64,3328]{1,0:T(8,128)(2,1)S(1)} %pad_maximum_fusion.7), channel_id=1, source_target_pairs={{0,1},{1,0},{2,3},{3,2},{4,5},{5,4},{6,7},{7,6},{8,9},{9,8},{10,11... | collective-permute-start | bytes 1277960 | tf_op jit(solution)/shard_map/ppermute | solution.py:23
  98.1 2.3 %collective-permute-start.7 = (bf16[64,3328]{1,0:T(8,128)(2,1)S(1)}, bf16[64,3328]{1,0:T(8,128)(2,1)S(1)}, u32[]{:S(2)}, u32[]{:S(2)}) collective-permute-start(bf16[64,3328]{1,0:T(8,128)(2,1)S(1)} %pad_maximum_fusion.5), channel_id=1, source_target_pairs={{0,1},{1,0},{2,3},{3,2},{4,5},{5,4},{6,7},{7,6},{8,9},{9,8},{10,11... | collective-permute-start | bytes 1277960 | tf_op jit(solution)/shard_map/ppermute | solution.py:23
  100.4 1.0 fusion.16
  101.4 1.1 convolution_convert_fusion
  102.6 1.1 fusion.12
  103.7 3.1 %collective-permute-start.19 = (bf16[64,1024]{1,0:T(8,128)(2,1)S(1)}, bf16[64,1024]{1,0:T(8,128)(2,1)S(1)}, u32[]{:S(2)}, u32[]{:S(2)}) collective-permute-start(bf16[64,1024]{1,0:T(8,128)(2,1)S(1)} %get-tuple-element.86), channel_id=1, source_target_pairs={{0,112},{16,96},{32,80},{48,64},{64,48},{80,32},{96,16},{112,0},{1... | collective-permute-start | bytes 393224 | tf_op jit(solution)/shard_map/ppermute | solution.py:23
  106.8 0.9 collective-permute-start.18
  107.6 1.1 fusion.8
  108.7 3.1 %collective-permute-start.9 = (bf16[64,1024]{1,0:T(8,128)(2,1)S(1)}, bf16[64,1024]{1,0:T(8,128)(2,1)S(1)}, u32[]{:S(2)}, u32[]{:S(2)}) collective-permute-start(bf16[64,1024]{1,0:T(8,128)(2,1)S(1)} %get-tuple-element.72), channel_id=1, source_target_pairs={{0,80},{16,64},{32,112},{48,96},{64,16},{80,0},{96,48},{112,32},{1... | collective-permute-start | bytes 393224 | tf_op jit(solution)/shard_map/ppermute | solution.py:23
  111.8 1.2 collective-permute-start.8
  113.1 1.5 %collective-permute-start.37 = (bf16[64,1024]{1,0:T(8,128)(2,1)S(1)}, bf16[64,1024]{1,0:T(8,128)(2,1)S(1)}, u32[]{:S(2)}, u32[]{:S(2)}) collective-permute-start(bf16[64,1024]{1,0:T(8,128)(2,1)S(1)} %select_convert_fusion), channel_id=1, source_target_pairs={{0,16},{16,0},{32,48},{48,32},{64,80},{80,64},{96,112},{112,96},{1... | collective-permute-start | bytes 393224 | tf_op jit(solution)/shard_map/ppermute | solution.py:23
  114.7 2.6 %collective-permute-done.9 = bf16[64,1024]{1,0:T(8,128)(2,1)S(1)} collective-permute-done((bf16[64,1024]{1,0:T(8,128)(2,1)S(1)}, bf16[64,1024]{1,0:T(8,128)(2,1)S(1)}, u32[]{:S(2)}, u32[]{:S(2)}) %collective-permute-start.9) | collective-permute-done | bytes 131104 | tf_op jit(solution)/shard_map/ppermute | solution.py:23
  117.3 1.6 %collective-permute-done.8 = bf16[64,1024]{1,0:T(8,128)(2,1)S(1)} collective-permute-done((bf16[64,1024]{1,0:T(8,128)(2,1)S(1)}, bf16[64,1024]{1,0:T(8,128)(2,1)S(1)}, u32[]{:S(2)}, u32[]{:S(2)}) %collective-permute-start.8) | collective-permute-done | bytes 131104 | tf_op jit(solution)/shard_map/ppermute | solution.py:23
  118.9 1.4 %collective-permute-done.37 = bf16[64,1024]{1,0:T(8,128)(2,1)S(1)} collective-permute-done((bf16[64,1024]{1,0:T(8,128)(2,1)S(1)}, bf16[64,1024]{1,0:T(8,128)(2,1)S(1)}, u32[]{:S(2)}, u32[]{:S(2)}) %collective-permute-start.37) | collective-permute-done | bytes 131104 | tf_op jit(solution)/shard_map/ppermute | solution.py:23
  (141 shorter events, 14.4 us)
Async XLA Ops:
  1.8 18.5 %all-to-all-start = ((bf16[32,4,1024]{2,1,0:T(4,128)(2,1)}), bf16[32,4,1024]{2,1,0:T(4,128)(2,1)S(1)}, u32[]{:S(2)}, u32[]{:S(2)}) async-start(bf16[32,4,1024]{2,1,0:T(4,128)(2,1)} %all_to_all.6), calls=%async_computation | async-start | bytes 524288 | tf_op jit(solution)/shard_map/all_to_all | solution.py:48
  20.4 8.0 %slice-start.2 = ((s8[6815744]{0:T(1024)(128)(4,1)}), s8[4194304]{0:T(1024)(128)(4,1)S(1)}, s32[]{:S(2)}) async-start(s8[6815744]{0:T(1024)(128)(4,1)} %bitcast.208), calls=%async_computation.3 | async-start | bytes 8388608
  20.5 7.9 %slice-start.3 = ((s8[6815744]{0:T(1024)(128)(4,1)}), s8[2621440]{0:T(1024)(128)(4,1)S(1)}, s32[]{:S(2)}) async-start(s8[6815744]{0:T(1024)(128)(4,1)} %bitcast.208), calls=%async_computation.4 | async-start | bytes 5242880
  20.5 10.9 %collective-permute-start.27 = (bf16[128,1024]{1,0:T(8,128)(2,1)S(1)}, bf16[128,1024]{1,0:T(8,128)(2,1)S(1)}, u32[]{:S(2)}, u32[]{:S(2)}) collective-permute-start(bf16[128,1024]{1,0:T(8,128)(2,1)S(1)} %bitcast_dynamic-update-slice_fusion), channel_id=1, source_target_pairs={{0,32},{32,0},{64,96},{96,64},{1,33},{33,1},{65,97},{97,65},{2,34}... | collective-permute-start | bytes 786440 | tf_op jit(solution)/shard_map/ppermute | solution.py:23
  21.8 11.8 %collective-permute-start.10 = (bf16[128,1024]{1,0:T(8,128)(2,1)S(1)}, bf16[128,1024]{1,0:T(8,128)(2,1)S(1)}, u32[]{:S(2)}, u32[]{:S(2)}) collective-permute-start(bf16[128,1024]{1,0:T(8,128)(2,1)S(1)} %bitcast_dynamic-update-slice_fusion), channel_id=1, source_target_pairs={{0,96},{32,64},{64,32},{96,0},{1,97},{33,65},{65,33},{97,1},{2,98}... | collective-permute-start | bytes 786440 | tf_op jit(solution)/shard_map/ppermute | solution.py:23
  23.6 12.2 %collective-permute-start = (bf16[128,1024]{1,0:T(8,128)(2,1)S(1)}, bf16[128,1024]{1,0:T(8,128)(2,1)S(1)}, u32[]{:S(2)}, u32[]{:S(2)}) collective-permute-start(bf16[128,1024]{1,0:T(8,128)(2,1)S(1)} %bitcast_dynamic-update-slice_fusion), channel_id=1, source_target_pairs={{0,64},{32,96},{64,0},{96,32},{1,65},{33,97},{65,1},{97,33},{2,66}... | collective-permute-start | bytes 786440 | tf_op jit(solution)/shard_map/ppermute | solution.py:23
  24.3 7.2 %slice-start = ((s8[6815744]{0:T(1024)(128)(4,1)}), s8[4194304]{0:T(1024)(128)(4,1)S(1)}, s32[]{:S(2)}) async-start(s8[6815744]{0:T(1024)(128)(4,1)} %bitcast.206), calls=%async_computation.1 | async-start | bytes 8388608
  28.4 3.0 %slice-start.1 = ((s8[6815744]{0:T(1024)(128)(4,1)}), s8[2621440]{0:T(1024)(128)(4,1)S(1)}, s32[]{:S(2)}) async-start(s8[6815744]{0:T(1024)(128)(4,1)} %bitcast.206), calls=%async_computation.2 | async-start | bytes 5242880
  29.9 13.8 %collective-permute-start.20 = (f16[2,64,3328]{2,1,0:T(8,128)(2,1)S(1)}, f16[2,64,3328]{2,1,0:T(8,128)(2,1)S(1)}, u32[]{:S(2)}, u32[]{:S(2)}) collective-permute-start(f16[2,64,3328]{2,1,0:T(8,128)(2,1)S(1)} %pad_maximum_fusion.2), channel_id=1, source_target_pairs={{0,1},{1,0},{2,3},{3,2},{4,5},{5,4},{6,7},{7,6},{8,9},{9,8},{10,11... | collective-permute-start | bytes 2555912 | tf_op jit(solution)/shard_map/ppermute | solution.py:23
  38.3 6.6 %collective-permute-start.28 = (f16[2,64,3328]{2,1,0:T(8,128)(2,1)S(1)}, f16[2,64,3328]{2,1,0:T(8,128)(2,1)S(1)}, u32[]{:S(2)}, u32[]{:S(2)}) collective-permute-start(f16[2,64,3328]{2,1,0:T(8,128)(2,1)S(1)} %pad_maximum_fusion.3), channel_id=1, source_target_pairs={{0,1},{1,0},{2,3},{3,2},{4,5},{5,4},{6,7},{7,6},{8,9},{9,8},{10,11... | collective-permute-start | bytes 2555912 | tf_op jit(solution)/shard_map/ppermute | solution.py:23
  42.4 3.3 %collective-permute-start.11 = (f16[2,64,3328]{2,1,0:T(8,128)(2,1)S(1)}, f16[2,64,3328]{2,1,0:T(8,128)(2,1)S(1)}, u32[]{:S(2)}, u32[]{:S(2)}) collective-permute-start(f16[2,64,3328]{2,1,0:T(8,128)(2,1)S(1)} %pad_maximum_fusion.1), channel_id=1, source_target_pairs={{0,1},{1,0},{2,3},{3,2},{4,5},{5,4},{6,7},{7,6},{8,9},{9,8},{10,11... | collective-permute-start | bytes 2555912 | tf_op jit(solution)/shard_map/ppermute | solution.py:23
  42.9 5.0 %collective-permute-start.1 = (f16[2,64,3328]{2,1,0:T(8,128)(2,1)S(1)}, f16[2,64,3328]{2,1,0:T(8,128)(2,1)S(1)}, u32[]{:S(2)}, u32[]{:S(2)}) collective-permute-start(f16[2,64,3328]{2,1,0:T(8,128)(2,1)S(1)} %pad_maximum_fusion), channel_id=1, source_target_pairs={{0,1},{1,0},{2,3},{3,2},{4,5},{5,4},{6,7},{7,6},{8,9},{9,8},{10,11... | collective-permute-start | bytes 2555912 | tf_op jit(solution)/shard_map/ppermute | solution.py:23
  44.0 8.3 %collective-permute-start.21 = (f16[2,32,3328]{2,1,0:T(8,128)(2,1)S(1)}, f16[2,32,3328]{2,1,0:T(8,128)(2,1)S(1)}, u32[]{:S(2)}, u32[]{:S(2)}) collective-permute-start(f16[2,32,3328]{2,1,0:T(8,128)(2,1)S(1)} %pad_maximum_fusion.8), channel_id=1, source_target_pairs={{0,4},{1,13},{4,0},{5,9},{8,12},{9,5},{12,8},{13,1},{2,6},{3,15},{... | collective-permute-start | bytes 1277960 | tf_op jit(solution)/shard_map/ppermute | solution.py:23
  45.3 14.9 %collective-permute-start.29 = (f16[2,64,1664]{2,1,0:T(8,128)(2,1)S(1)}, f16[2,64,1664]{2,1,0:T(8,128)(2,1)S(1)}, u32[]{:S(2)}, u32[]{:S(2)}) collective-permute-start(f16[2,64,1664]{2,1,0:T(8,128)(2,1)S(1)} %pad_maximum_fusion.10), channel_id=1, source_target_pairs={{0,2},{2,0},{1,3},{3,1},{4,6},{6,4},{5,7},{7,5},{8,10},{10,8},{9,1... | collective-permute-start | bytes 1277960 | tf_op jit(solution)/shard_map/ppermute | solution.py:23
  46.1 15.0 %collective-permute-start.12 = (f16[2,32,3328]{2,1,0:T(8,128)(2,1)S(1)}, f16[2,32,3328]{2,1,0:T(8,128)(2,1)S(1)}, u32[]{:S(2)}, u32[]{:S(2)}) collective-permute-start(f16[2,32,3328]{2,1,0:T(8,128)(2,1)S(1)} %pad_maximum_fusion.6), channel_id=1, source_target_pairs={{0,4},{1,13},{4,0},{5,9},{8,12},{9,5},{12,8},{13,1},{2,6},{3,15},{... | collective-permute-start | bytes 1277960 | tf_op jit(solution)/shard_map/ppermute | solution.py:23
  52.5 7.4 %collective-permute-start.22 = (f16[2,16,3328]{2,1,0:T(8,128)(2,1)S(1)}, f16[2,16,3328]{2,1,0:T(8,128)(2,1)S(1)}, u32[]{:S(2)}, u32[]{:S(2)}) collective-permute-start(f16[2,16,3328]{2,1,0:T(8,128)(2,1)S(1)} %pad_maximum_fusion.18), channel_id=1, source_target_pairs={{0,12},{1,5},{4,8},{5,1},{8,4},{9,13},{12,0},{13,9},{2,14},{3,7},{... | collective-permute-start | bytes 638984 | tf_op jit(solution)/shard_map/ppermute | solution.py:23
  52.7 11.0 %collective-permute-start.2 = (f16[2,32,3328]{2,1,0:T(8,128)(2,1)S(1)}, f16[2,32,3328]{2,1,0:T(8,128)(2,1)S(1)}, u32[]{:S(2)}, u32[]{:S(2)}) collective-permute-start(f16[2,32,3328]{2,1,0:T(8,128)(2,1)S(1)} %pad_maximum_fusion.4), channel_id=1, source_target_pairs={{0,4},{1,13},{4,0},{5,9},{8,12},{9,5},{12,8},{13,1},{2,6},{3,15},{... | collective-permute-start | bytes 1277960 | tf_op jit(solution)/shard_map/ppermute | solution.py:23
  60.1 4.8 %collective-permute-start.23 = (f16[2,16,3328]{2,1,0:T(8,128)(2,1)S(1)}, f16[2,16,3328]{2,1,0:T(8,128)(2,1)S(1)}, u32[]{:S(2)}, u32[]{:S(2)}) collective-permute-start(f16[2,16,3328]{2,1,0:T(8,128)(2,1)S(1)} %pad_maximum_fusion.19), channel_id=1, source_target_pairs={{0,2},{2,0},{1,3},{3,1},{4,6},{6,4},{5,7},{7,5},{8,10},{10,8},{9,1... | collective-permute-start | bytes 638984 | tf_op jit(solution)/shard_map/ppermute | solution.py:23
  60.5 6.4 %collective-permute-start.30 = (f16[2,32,1664]{2,1,0:T(8,128)(2,1)S(1)}, f16[2,32,1664]{2,1,0:T(8,128)(2,1)S(1)}, u32[]{:S(2)}, u32[]{:S(2)}) collective-permute-start(f16[2,32,1664]{2,1,0:T(8,128)(2,1)S(1)} %pad_maximum_fusion.21), channel_id=1, source_target_pairs={{0,4},{1,13},{4,0},{5,9},{8,12},{9,5},{12,8},{13,1},{2,6},{3,15},{... | collective-permute-start | bytes 638984 | tf_op jit(solution)/shard_map/ppermute | solution.py:23
  61.4 5.8 %collective-permute-start.13 = (f16[2,16,3328]{2,1,0:T(8,128)(2,1)S(1)}, f16[2,16,3328]{2,1,0:T(8,128)(2,1)S(1)}, u32[]{:S(2)}, u32[]{:S(2)}) collective-permute-start(f16[2,16,3328]{2,1,0:T(8,128)(2,1)S(1)} %pad_maximum_fusion.15), channel_id=1, source_target_pairs={{0,12},{1,5},{4,8},{5,1},{8,4},{9,13},{12,0},{13,9},{2,14},{3,7},{... | collective-permute-start | bytes 638984 | tf_op jit(solution)/shard_map/ppermute | solution.py:23
  63.7 36.6 %slice-start.4 = ((s8[6815744]{0:T(1024)(128)(4,1)}), s8[4194304]{0:T(1024)(128)(4,1)S(1)}, s32[]{:S(2)}) async-start(s8[6815744]{0:T(1024)(128)(4,1)} %bitcast.210), calls=%async_computation.5 | async-start | bytes 8388608
  64.0 7.0 %collective-permute-start.3 = (f16[2,16,3328]{2,1,0:T(8,128)(2,1)S(1)}, f16[2,16,3328]{2,1,0:T(8,128)(2,1)S(1)}, u32[]{:S(2)}, u32[]{:S(2)}) collective-permute-start(f16[2,16,3328]{2,1,0:T(8,128)(2,1)S(1)} %pad_maximum_fusion.12), channel_id=1, source_target_pairs={{0,12},{1,5},{4,8},{5,1},{8,4},{9,13},{12,0},{13,9},{2,14},{3,7},{... | collective-permute-start | bytes 638984 | tf_op jit(solution)/shard_map/ppermute | solution.py:23
  65.0 7.2 %collective-permute-start.24 = (bf16[16,3328]{1,0:T(8,128)(2,1)S(1)}, bf16[16,3328]{1,0:T(8,128)(2,1)S(1)}, u32[]{:S(2)}, u32[]{:S(2)}) collective-permute-start(bf16[16,3328]{1,0:T(8,128)(2,1)S(1)} %fusion.54), channel_id=1, source_target_pairs={{0,12},{1,5},{4,8},{5,1},{8,4},{9,13},{12,0},{13,9},{2,14},{3,7},{... | collective-permute-start | bytes 319496 | tf_op jit(solution)/shard_map/ppermute | solution.py:23
  67.1 6.2 %collective-permute-start.31 = (f16[2,16,1664]{2,1,0:T(8,128)(2,1)S(1)}, f16[2,16,1664]{2,1,0:T(8,128)(2,1)S(1)}, u32[]{:S(2)}, u32[]{:S(2)}) collective-permute-start(f16[2,16,1664]{2,1,0:T(8,128)(2,1)S(1)} %pad_maximum_fusion.24), channel_id=1, source_target_pairs={{0,12},{1,5},{4,8},{5,1},{8,4},{9,13},{12,0},{13,9},{2,14},{3,7},{... | collective-permute-start | bytes 319496 | tf_op jit(solution)/shard_map/ppermute | solution.py:23
  67.3 33.0 %slice-start.5 = ((s8[6815744]{0:T(1024)(128)(4,1)}), s8[2621440]{0:T(1024)(128)(4,1)S(1)}, s32[]{:S(2)}) async-start(s8[6815744]{0:T(1024)(128)(4,1)} %bitcast.210), calls=%async_computation.6 | async-start | bytes 5242880
  67.3 11.4 %collective-permute-start.14 = (f16[2,16,3328]{2,1,0:T(8,128)(2,1)S(1)}, f16[2,16,3328]{2,1,0:T(8,128)(2,1)S(1)}, u32[]{:S(2)}, u32[]{:S(2)}) collective-permute-start(f16[2,16,3328]{2,1,0:T(8,128)(2,1)S(1)} %pad_maximum_fusion.16), channel_id=1, source_target_pairs={{0,2},{2,0},{1,3},{3,1},{4,6},{6,4},{5,7},{7,5},{8,10},{10,8},{9,1... | collective-permute-start | bytes 638984 | tf_op jit(solution)/shard_map/ppermute | solution.py:23
  71.2 8.3 %collective-permute-start.4 = (f16[2,16,3328]{2,1,0:T(8,128)(2,1)S(1)}, f16[2,16,3328]{2,1,0:T(8,128)(2,1)S(1)}, u32[]{:S(2)}, u32[]{:S(2)}) collective-permute-start(f16[2,16,3328]{2,1,0:T(8,128)(2,1)S(1)} %pad_maximum_fusion.13), channel_id=1, source_target_pairs={{0,2},{2,0},{1,3},{3,1},{4,6},{6,4},{5,7},{7,5},{8,10},{10,8},{9,1... | collective-permute-start | bytes 638984 | tf_op jit(solution)/shard_map/ppermute | solution.py:23
  73.3 4.3 %collective-permute-start.32 = (bf16[16,1664]{1,0:T(8,128)(2,1)S(1)}, bf16[16,1664]{1,0:T(8,128)(2,1)S(1)}, u32[]{:S(2)}, u32[]{:S(2)}) collective-permute-start(bf16[16,1664]{1,0:T(8,128)(2,1)S(1)} %fusion.76), channel_id=1, source_target_pairs={{0,2},{2,0},{1,3},{3,1},{4,6},{6,4},{5,7},{7,5},{8,10},{10,8},{9,1... | collective-permute-start | bytes 159752 | tf_op jit(solution)/shard_map/ppermute | solution.py:23
  74.3 11.0 %collective-permute-start.25 = (bf16[32,3328]{1,0:T(8,128)(2,1)S(1)}, bf16[32,3328]{1,0:T(8,128)(2,1)S(1)}, u32[]{:S(2)}, u32[]{:S(2)}) collective-permute-start(bf16[32,3328]{1,0:T(8,128)(2,1)S(1)} %pad_maximum_fusion.20), channel_id=1, source_target_pairs={{0,4},{1,13},{4,0},{5,9},{8,12},{9,5},{12,8},{13,1},{2,6},{3,15},{... | collective-permute-start | bytes 638984 | tf_op jit(solution)/shard_map/ppermute | solution.py:23
  77.7 3.9 %collective-permute-start.33 = (bf16[16,3328]{1,0:T(8,128)(2,1)S(1)}, bf16[16,3328]{1,0:T(8,128)(2,1)S(1)}, u32[]{:S(2)}, u32[]{:S(2)}) collective-permute-start(bf16[16,3328]{1,0:T(8,128)(2,1)S(1)} %pad_maximum_fusion.25), channel_id=1, source_target_pairs={{0,12},{1,5},{4,8},{5,1},{8,4},{9,13},{12,0},{13,9},{2,14},{3,7},{... | collective-permute-start | bytes 319496 | tf_op jit(solution)/shard_map/ppermute | solution.py:23
  78.9 10.9 %collective-permute-start.15 = (bf16[16,3328]{1,0:T(8,128)(2,1)S(1)}, bf16[16,3328]{1,0:T(8,128)(2,1)S(1)}, u32[]{:S(2)}, u32[]{:S(2)}) collective-permute-start(bf16[16,3328]{1,0:T(8,128)(2,1)S(1)} %fusion.56), channel_id=1, source_target_pairs={{0,12},{1,5},{4,8},{5,1},{8,4},{9,13},{12,0},{13,9},{2,14},{3,7},{... | collective-permute-start | bytes 319496 | tf_op jit(solution)/shard_map/ppermute | solution.py:23
  79.5 12.2 %collective-permute-start.5 = (bf16[16,3328]{1,0:T(8,128)(2,1)S(1)}, bf16[16,3328]{1,0:T(8,128)(2,1)S(1)}, u32[]{:S(2)}, u32[]{:S(2)}) collective-permute-start(bf16[16,3328]{1,0:T(8,128)(2,1)S(1)} %fusion.58), channel_id=1, source_target_pairs={{0,12},{1,5},{4,8},{5,1},{8,4},{9,13},{12,0},{13,9},{2,14},{3,7},{... | collective-permute-start | bytes 319496 | tf_op jit(solution)/shard_map/ppermute | solution.py:23
  81.6 11.0 %collective-permute-start.34 = (bf16[32,3328]{1,0:T(8,128)(2,1)S(1)}, bf16[32,3328]{1,0:T(8,128)(2,1)S(1)}, u32[]{:S(2)}, u32[]{:S(2)}) collective-permute-start(bf16[32,3328]{1,0:T(8,128)(2,1)S(1)} %pad_maximum_fusion.22), channel_id=1, source_target_pairs={{0,4},{1,13},{4,0},{5,9},{8,12},{9,5},{12,8},{13,1},{2,6},{3,15},{... | collective-permute-start | bytes 638984 | tf_op jit(solution)/shard_map/ppermute | solution.py:23
  85.3 15.0 %collective-permute-start.26 = (bf16[64,3328]{1,0:T(8,128)(2,1)S(1)}, bf16[64,3328]{1,0:T(8,128)(2,1)S(1)}, u32[]{:S(2)}, u32[]{:S(2)}) collective-permute-start(bf16[64,3328]{1,0:T(8,128)(2,1)S(1)} %pad_maximum_fusion.9), channel_id=1, source_target_pairs={{0,1},{1,0},{2,3},{3,2},{4,5},{5,4},{6,7},{7,6},{8,9},{9,8},{10,11... | collective-permute-start | bytes 1277960 | tf_op jit(solution)/shard_map/ppermute | solution.py:23
  89.8 6.0 %collective-permute-start.16 = (bf16[32,3328]{1,0:T(8,128)(2,1)S(1)}, bf16[32,3328]{1,0:T(8,128)(2,1)S(1)}, u32[]{:S(2)}, u32[]{:S(2)}) collective-permute-start(bf16[32,3328]{1,0:T(8,128)(2,1)S(1)} %pad_maximum_fusion.17), channel_id=1, source_target_pairs={{0,4},{1,13},{4,0},{5,9},{8,12},{9,5},{12,8},{13,1},{2,6},{3,15},{... | collective-permute-start | bytes 638984 | tf_op jit(solution)/shard_map/ppermute | solution.py:23
  91.7 6.3 %collective-permute-start.6 = (bf16[32,3328]{1,0:T(8,128)(2,1)S(1)}, bf16[32,3328]{1,0:T(8,128)(2,1)S(1)}, u32[]{:S(2)}, u32[]{:S(2)}) collective-permute-start(bf16[32,3328]{1,0:T(8,128)(2,1)S(1)} %pad_maximum_fusion.14), channel_id=1, source_target_pairs={{0,4},{1,13},{4,0},{5,9},{8,12},{9,5},{12,8},{13,1},{2,6},{3,15},{... | collective-permute-start | bytes 638984 | tf_op jit(solution)/shard_map/ppermute | solution.py:23
  92.7 8.8 %collective-permute-start.35 = (bf16[64,3328]{1,0:T(8,128)(2,1)S(1)}, bf16[64,3328]{1,0:T(8,128)(2,1)S(1)}, u32[]{:S(2)}, u32[]{:S(2)}) collective-permute-start(bf16[64,3328]{1,0:T(8,128)(2,1)S(1)} %pad_maximum_fusion.11), channel_id=1, source_target_pairs={{0,1},{1,0},{2,3},{3,2},{4,5},{5,4},{6,7},{7,6},{8,9},{9,8},{10,11... | collective-permute-start | bytes 1277960 | tf_op jit(solution)/shard_map/ppermute | solution.py:23
  95.8 6.8 %collective-permute-start.17 = (bf16[64,3328]{1,0:T(8,128)(2,1)S(1)}, bf16[64,3328]{1,0:T(8,128)(2,1)S(1)}, u32[]{:S(2)}, u32[]{:S(2)}) collective-permute-start(bf16[64,3328]{1,0:T(8,128)(2,1)S(1)} %pad_maximum_fusion.7), channel_id=1, source_target_pairs={{0,1},{1,0},{2,3},{3,2},{4,5},{5,4},{6,7},{7,6},{8,9},{9,8},{10,11... | collective-permute-start | bytes 1277960 | tf_op jit(solution)/shard_map/ppermute | solution.py:23
  98.1 9.6 %collective-permute-start.7 = (bf16[64,3328]{1,0:T(8,128)(2,1)S(1)}, bf16[64,3328]{1,0:T(8,128)(2,1)S(1)}, u32[]{:S(2)}, u32[]{:S(2)}) collective-permute-start(bf16[64,3328]{1,0:T(8,128)(2,1)S(1)} %pad_maximum_fusion.5), channel_id=1, source_target_pairs={{0,1},{1,0},{2,3},{3,2},{4,5},{5,4},{6,7},{7,6},{8,9},{9,8},{10,11... | collective-permute-start | bytes 1277960 | tf_op jit(solution)/shard_map/ppermute | solution.py:23
  102.5 10.5 %collective-permute-start.36 = (bf16[128,1024]{1,0:T(8,128)(2,1)S(1)}, bf16[128,1024]{1,0:T(8,128)(2,1)S(1)}, u32[]{:S(2)}, u32[]{:S(2)}) collective-permute-start(bf16[128,1024]{1,0:T(8,128)(2,1)S(1)} %convolution_convert_fusion), channel_id=1, source_target_pairs={{0,32},{32,0},{64,96},{96,64},{1,33},{33,1},{65,97},{97,65},{2,34}... | collective-permute-start | bytes 786440 | tf_op jit(solution)/shard_map/ppermute | solution.py:23
  103.7 11.0 %collective-permute-start.19 = (bf16[64,1024]{1,0:T(8,128)(2,1)S(1)}, bf16[64,1024]{1,0:T(8,128)(2,1)S(1)}, u32[]{:S(2)}, u32[]{:S(2)}) collective-permute-start(bf16[64,1024]{1,0:T(8,128)(2,1)S(1)} %get-tuple-element.86), channel_id=1, source_target_pairs={{0,112},{16,96},{32,80},{48,64},{64,48},{80,32},{96,16},{112,0},{1... | collective-permute-start | bytes 393224 | tf_op jit(solution)/shard_map/ppermute | solution.py:23
  106.8 7.9 %collective-permute-start.18 = (bf16[64,1024]{1,0:T(8,128)(2,1)S(1)}, bf16[64,1024]{1,0:T(8,128)(2,1)S(1)}, u32[]{:S(2)}, u32[]{:S(2)}) collective-permute-start(bf16[64,1024]{1,0:T(8,128)(2,1)S(1)} %get-tuple-element.85), channel_id=1, source_target_pairs={{0,96},{32,64},{64,32},{96,0},{1,97},{33,65},{65,33},{97,1},{2,98}... | collective-permute-start | bytes 393224 | tf_op jit(solution)/shard_map/ppermute | solution.py:23
  108.7 8.5 %collective-permute-start.9 = (bf16[64,1024]{1,0:T(8,128)(2,1)S(1)}, bf16[64,1024]{1,0:T(8,128)(2,1)S(1)}, u32[]{:S(2)}, u32[]{:S(2)}) collective-permute-start(bf16[64,1024]{1,0:T(8,128)(2,1)S(1)} %get-tuple-element.72), channel_id=1, source_target_pairs={{0,80},{16,64},{32,112},{48,96},{64,16},{80,0},{96,48},{112,32},{1... | collective-permute-start | bytes 393224 | tf_op jit(solution)/shard_map/ppermute | solution.py:23
  111.8 7.1 %collective-permute-start.8 = (bf16[64,1024]{1,0:T(8,128)(2,1)S(1)}, bf16[64,1024]{1,0:T(8,128)(2,1)S(1)}, u32[]{:S(2)}, u32[]{:S(2)}) collective-permute-start(bf16[64,1024]{1,0:T(8,128)(2,1)S(1)} %get-tuple-element.71), channel_id=1, source_target_pairs={{0,64},{32,96},{64,0},{96,32},{1,65},{33,97},{65,1},{97,33},{2,66}... | collective-permute-start | bytes 393224 | tf_op jit(solution)/shard_map/ppermute | solution.py:23
  113.1 7.2 %collective-permute-start.37 = (bf16[64,1024]{1,0:T(8,128)(2,1)S(1)}, bf16[64,1024]{1,0:T(8,128)(2,1)S(1)}, u32[]{:S(2)}, u32[]{:S(2)}) collective-permute-start(bf16[64,1024]{1,0:T(8,128)(2,1)S(1)} %select_convert_fusion), channel_id=1, source_target_pairs={{0,16},{16,0},{32,48},{48,32},{64,80},{80,64},{96,112},{112,96},{1... | collective-permute-start | bytes 393224 | tf_op jit(solution)/shard_map/ppermute | solution.py:23

commit v13 on v10

--- a/solution.py
+++ b/solution.py
@@ -100,7 +100,7 @@
                 part = slice(0 if over == 4 else got.shape[1] // 2, None)
                 send = jnp.stack([lifted(v[part]) for v in total])
                 swap = (swap_first, swap_second, swap_z)[over - 2]
-            send, *st["total"] = tie(send, *total)
+            send, st["total"] = tie(send), total
             st["flight"] = swap(send)
         elif s == 5:
             got = tie(st["flight"])

time: 120 us -> 120 us (level)
  transfers between devices with their start and end apart: 39 -> 39, of which waited for: 15 -> 15; matrix products, arithmetic and copies ran while one was open for 17% -> 18% of each run, Pallas kernels for 0% -> 0%
where the time goes in v13:
time: 120 us
  starting transfers between devices  61.4 us (51%)
  waiting for transfers between devices  34.1 us (28%)
  matrix products  15.8 us (13%)
  other arithmetic  6.12 us (5%)
  local copies, waits for them, and re-layouts  2 us (2%)
    ppermute x38, starting transfers between devices, permute(): return lambda v: lax.ppermute(v, axes, pairs)  51.8 us
    ppermute x38, waiting for transfers between devices, permute(): return lambda v: lax.ppermute(v, axes, pairs)  25.3 us
    dot_general x12, matrix products, product(): return jnp.dot(rows, weight, preferred_element_type=F32)  15.8 us
    all_to_all x1, starting transfers between devices, per_device(): lax.all_to_all(blocks, AXES[1:], split_axis=0, concat_axis=0, tiled=True)  9.6 us
    all_to_all x1, waiting for transfers between devices, per_device(): lax.all_to_all(blocks, AXES[1:], split_axis=0, concat_axis=0, tiled=True)  8.79 us
  transfers between devices with their start and end apart: 39, of which 15 were waited for; matrix products, arithmetic and copies ran while one was open for 18% of the time, Pallas kernels for 0%

profile of v13, /device:TPU:1, one launch (start us, length us, event | category | flops | bytes accessed | tf_op | source)
XLA Modules:
  0.0 120.3 jit_solution(1964423034313124456)
XLA Ops:
  0.0 0.9 broadcast_in_dim.7
  1.8 9.6 %all-to-all-start = ((bf16[32,4,1024]{2,1,0:T(4,128)(2,1)}), bf16[32,4,1024]{2,1,0:T(4,128)(2,1)S(1)}, u32[]{:S(2)}, u32[]{:S(2)}) async-start(bf16[32,4,1024]{2,1,0:T(4,128)(2,1)} %all_to_all.6), calls=%async_computation | async-start | bytes 524288 | tf_op jit(solution)/shard_map/all_to_all | solution.py:48
  11.4 8.8 %all-to-all-done = bf16[32,4,1024]{2,1,0:T(4,128)(2,1)S(1)} async-done(((bf16[32,4,1024]{2,1,0:T(4,128)(2,1)}), bf16[32,4,1024]{2,1,0:T(4,128)(2,1)S(1)}, u32[]{:S(2)}, u32[]{:S(2)}) %all-to-all-start) | async-done | bytes 262176 | tf_op jit(solution)/shard_map/all_to_all | solution.py:48
  20.5 2.6 %collective-permute-start.27 = (bf16[128,1024]{1,0:T(8,128)(2,1)S(1)}, bf16[128,1024]{1,0:T(8,128)(2,1)S(1)}, u32[]{:S(2)}, u32[]{:S(2)}) collective-permute-start(bf16[128,1024]{1,0:T(8,128)(2,1)S(1)} %bitcast_dynamic-update-slice_fusion), channel_id=1, source_target_pairs={{0,96},{32,64},{64,32},{96,0},{1,97},{33,65},{65,33},{97,1},{2,98}... | collective-permute-start | bytes 786440 | tf_op jit(solution)/shard_map/ppermute | solution.py:23
  23.1 1.4 %collective-permute-start = (bf16[128,1024]{1,0:T(8,128)(2,1)S(1)}, bf16[128,1024]{1,0:T(8,128)(2,1)S(1)}, u32[]{:S(2)}, u32[]{:S(2)}) collective-permute-start(bf16[128,1024]{1,0:T(8,128)(2,1)S(1)} %bitcast_dynamic-update-slice_fusion), channel_id=1, source_target_pairs={{0,64},{32,96},{64,0},{96,32},{1,65},{33,97},{65,1},{97,33},{2,66}... | collective-permute-start | bytes 786440 | tf_op jit(solution)/shard_map/ppermute | solution.py:23
  24.4 4.1 %fusion.87 = f32[128,3328]{1,0:T(8,128)S(1)} fusion(bf16[128,1024]{1,0:T(8,128)(2,1)S(1)} %bitcast_dynamic-update-slice_fusion, bf16[1024,3328]{1,0:T(8,128)(2,1)} %param.5), kind=kOutput, calls=%fused_computation.200 | convolution fusion | flops 872415232 | bytes 8781824 | tf_op jit(solution)/shard_map/dot_general | solution.py:74
  28.6 1.1 fusion.88
  30.1 1.9 %collective-permute-start.20 = (f16[2,64,3328]{2,1,0:T(8,128)(2,1)S(1)}, f16[2,64,3328]{2,1,0:T(8,128)(2,1)S(1)}, u32[]{:S(2)}, u32[]{:S(2)}) collective-permute-start(f16[2,64,3328]{2,1,0:T(8,128)(2,1)S(1)} %pad_maximum_fusion.2), channel_id=1, source_target_pairs={{0,1},{1,0},{2,3},{3,2},{4,5},{5,4},{6,7},{7,6},{8,9},{9,8},{10,11... | collective-permute-start | bytes 2555912 | tf_op jit(solution)/shard_map/ppermute | solution.py:23
  31.9 1.1 fusion.89
  33.0 1.1 fusion.90
  34.1 1.1 fusion.85
  35.2 1.1 fusion.86
  36.3 1.1 fusion.83
  37.3 1.1 fusion.84
  38.8 1.1 collective-permute-start.28
  44.1 1.8 %collective-permute-start.12 = (f16[2,32,3328]{2,1,0:T(8,128)(2,1)S(1)}, f16[2,32,3328]{2,1,0:T(8,128)(2,1)S(1)}, u32[]{:S(2)}, u32[]{:S(2)}) collective-permute-start(f16[2,32,3328]{2,1,0:T(8,128)(2,1)S(1)} %pad_maximum_fusion.6), channel_id=1, source_target_pairs={{0,4},{1,13},{4,0},{5,9},{8,12},{9,5},{12,8},{13,1},{2,6},{3,15},{... | collective-permute-start | bytes 1277960 | tf_op jit(solution)/shard_map/ppermute | solution.py:23
  46.1 4.0 %collective-permute-done.21 = f16[2,32,3328]{2,1,0:T(8,128)(2,1)S(1)} collective-permute-done((f16[2,32,3328]{2,1,0:T(8,128)(2,1)S(1)}, f16[2,32,3328]{2,1,0:T(8,128)(2,1)S(1)}, u32[]{:S(2)}, u32[]{:S(2)}) %collective-permute-start.21) | collective-permute-done | bytes 426016 | tf_op jit(solution)/shard_map/ppermute | solution.py:23
  51.4 6.4 %collective-permute-done.22 = f16[2,16,3328]{2,1,0:T(8,128)(2,1)S(1)} collective-permute-done((f16[2,16,3328]{2,1,0:T(8,128)(2,1)S(1)}, f16[2,16,3328]{2,1,0:T(8,128)(2,1)S(1)}, u32[]{:S(2)}, u32[]{:S(2)}) %collective-permute-start.22) | collective-permute-done | bytes 213024 | tf_op jit(solution)/shard_map/ppermute | solution.py:23
  59.3 2.2 %collective-permute-done.2 = f16[2,32,3328]{2,1,0:T(8,128)(2,1)S(1)} collective-permute-done((f16[2,32,3328]{2,1,0:T(8,128)(2,1)S(1)}, f16[2,32,3328]{2,1,0:T(8,128)(2,1)S(1)}, u32[]{:S(2)}, u32[]{:S(2)}) %collective-permute-start.2) | collective-permute-done | bytes 426016 | tf_op jit(solution)/shard_map/ppermute | solution.py:23
  62.9 2.0 %collective-permute-start.24 = (bf16[16,3328]{1,0:T(8,128)(2,1)S(1)}, bf16[16,3328]{1,0:T(8,128)(2,1)S(1)}, u32[]{:S(2)}, u32[]{:S(2)}) collective-permute-start(bf16[16,3328]{1,0:T(8,128)(2,1)S(1)} %fusion.54), channel_id=1, source_target_pairs={{0,12},{1,5},{4,8},{5,1},{8,4},{9,13},{12,0},{13,9},{2,14},{3,7},{... | collective-permute-start | bytes 319496 | tf_op jit(solution)/shard_map/ppermute | solution.py:23
  65.3 1.0 collective-permute-start.14
  66.3 2.6 %collective-permute-done.3 = f16[2,16,3328]{2,1,0:T(8,128)(2,1)S(1)} collective-permute-done((f16[2,16,3328]{2,1,0:T(8,128)(2,1)S(1)}, f16[2,16,3328]{2,1,0:T(8,128)(2,1)S(1)}, u32[]{:S(2)}, u32[]{:S(2)}) %collective-permute-start.3) | collective-permute-done | bytes 213024 | tf_op jit(solution)/shard_map/ppermute | solution.py:23
  70.0 1.1 collective-permute-done.31
  71.2 1.0 collective-permute-start.32
  72.2 2.4 %collective-permute-start.25 = (bf16[32,3328]{1,0:T(8,128)(2,1)S(1)}, bf16[32,3328]{1,0:T(8,128)(2,1)S(1)}, u32[]{:S(2)}, u32[]{:S(2)}) collective-permute-start(bf16[32,3328]{1,0:T(8,128)(2,1)S(1)} %pad_maximum_fusion.20), channel_id=1, source_target_pairs={{0,4},{1,13},{4,0},{5,9},{8,12},{9,5},{12,8},{13,1},{2,6},{3,15},{... | collective-permute-start | bytes 638984 | tf_op jit(solution)/shard_map/ppermute | solution.py:23
  74.7 0.9 collective-permute-done.32
  75.6 1.1 collective-permute-start.33
  77.5 1.1 collective-permute-start.5
  78.6 0.9 collective-permute-done.33
  79.5 3.8 %collective-permute-start.34 = (bf16[32,3328]{1,0:T(8,128)(2,1)S(1)}, bf16[32,3328]{1,0:T(8,128)(2,1)S(1)}, u32[]{:S(2)}, u32[]{:S(2)}) collective-permute-start(bf16[32,3328]{1,0:T(8,128)(2,1)S(1)} %pad_maximum_fusion.22), channel_id=1, source_target_pairs={{0,4},{1,13},{4,0},{5,9},{8,12},{9,5},{12,8},{13,1},{2,6},{3,15},{... | collective-permute-start | bytes 638984 | tf_op jit(solution)/shard_map/ppermute | solution.py:23
  83.3 4.3 %collective-permute-start.26 = (bf16[64,3328]{1,0:T(8,128)(2,1)S(1)}, bf16[64,3328]{1,0:T(8,128)(2,1)S(1)}, u32[]{:S(2)}, u32[]{:S(2)}) collective-permute-start(bf16[64,3328]{1,0:T(8,128)(2,1)S(1)} %pad_maximum_fusion.9), channel_id=1, source_target_pairs={{0,1},{1,0},{2,3},{3,2},{4,5},{5,4},{6,7},{7,6},{8,9},{9,8},{10,11... | collective-permute-start | bytes 1277960 | tf_op jit(solution)/shard_map/ppermute | solution.py:23
  87.7 1.9 %collective-permute-start.16 = (bf16[32,3328]{1,0:T(8,128)(2,1)S(1)}, bf16[32,3328]{1,0:T(8,128)(2,1)S(1)}, u32[]{:S(2)}, u32[]{:S(2)}) collective-permute-start(bf16[32,3328]{1,0:T(8,128)(2,1)S(1)} %pad_maximum_fusion.17), channel_id=1, source_target_pairs={{0,4},{1,13},{4,0},{5,9},{8,12},{9,5},{12,8},{13,1},{2,6},{3,15},{... | collective-permute-start | bytes 638984 | tf_op jit(solution)/shard_map/ppermute | solution.py:23
  89.6 0.9 collective-permute-start.6
  90.5 2.9 %collective-permute-start.35 = (bf16[64,3328]{1,0:T(8,128)(2,1)S(1)}, bf16[64,3328]{1,0:T(8,128)(2,1)S(1)}, u32[]{:S(2)}, u32[]{:S(2)}) collective-permute-start(bf16[64,3328]{1,0:T(8,128)(2,1)S(1)} %pad_maximum_fusion.11), channel_id=1, source_target_pairs={{0,1},{1,0},{2,3},{3,2},{4,5},{5,4},{6,7},{7,6},{8,9},{9,8},{10,11... | collective-permute-start | bytes 1277960 | tf_op jit(solution)/shard_map/ppermute | solution.py:23
  93.7 2.1 %collective-permute-start.17 = (bf16[64,3328]{1,0:T(8,128)(2,1)S(1)}, bf16[64,3328]{1,0:T(8,128)(2,1)S(1)}, u32[]{:S(2)}, u32[]{:S(2)}) collective-permute-start(bf16[64,3328]{1,0:T(8,128)(2,1)S(1)} %pad_maximum_fusion.7), channel_id=1, source_target_pairs={{0,1},{1,0},{2,3},{3,2},{4,5},{5,4},{6,7},{7,6},{8,9},{9,8},{10,11... | collective-permute-start | bytes 1277960 | tf_op jit(solution)/shard_map/ppermute | solution.py:23
  96.0 2.3 %collective-permute-start.7 = (bf16[64,3328]{1,0:T(8,128)(2,1)S(1)}, bf16[64,3328]{1,0:T(8,128)(2,1)S(1)}, u32[]{:S(2)}, u32[]{:S(2)}) collective-permute-start(bf16[64,3328]{1,0:T(8,128)(2,1)S(1)} %pad_maximum_fusion.5), channel_id=1, source_target_pairs={{0,1},{1,0},{2,3},{3,2},{4,5},{5,4},{6,7},{7,6},{8,9},{9,8},{10,11... | collective-permute-start | bytes 1277960 | tf_op jit(solution)/shard_map/ppermute | solution.py:23
  98.3 1.1 fusion.16
  99.3 1.1 convolution_convert_fusion
  100.4 2.6 %collective-permute-start.36 = (bf16[128,1024]{1,0:T(8,128)(2,1)S(1)}, bf16[128,1024]{1,0:T(8,128)(2,1)S(1)}, u32[]{:S(2)}, u32[]{:S(2)}) collective-permute-start(bf16[128,1024]{1,0:T(8,128)(2,1)S(1)} %convolution_convert_fusion), channel_id=1, source_target_pairs={{0,96},{32,64},{64,32},{96,0},{1,97},{33,65},{65,33},{97,1},{2,98}... | collective-permute-start | bytes 786440 | tf_op jit(solution)/shard_map/ppermute | solution.py:23
  102.9 1.1 fusion.12
  104.1 2.6 %collective-permute-start.18 = (bf16[64,1024]{1,0:T(8,128)(2,1)S(1)}, bf16[64,1024]{1,0:T(8,128)(2,1)S(1)}, u32[]{:S(2)}, u32[]{:S(2)}) collective-permute-start(bf16[64,1024]{1,0:T(8,128)(2,1)S(1)} %get-tuple-element.31), channel_id=1, source_target_pairs={{0,32},{32,0},{64,96},{96,64},{1,33},{33,1},{65,97},{97,65},{2,34}... | collective-permute-start | bytes 393224 | tf_op jit(solution)/shard_map/ppermute | solution.py:23
  106.8 1.1 fusion.8
  107.9 1.2 %collective-permute-start.9 = (bf16[64,1024]{1,0:T(8,128)(2,1)S(1)}, bf16[64,1024]{1,0:T(8,128)(2,1)S(1)}, u32[]{:S(2)}, u32[]{:S(2)}) collective-permute-start(bf16[64,1024]{1,0:T(8,128)(2,1)S(1)} %get-tuple-element.27), channel_id=1, source_target_pairs={{0,80},{16,64},{32,112},{48,96},{64,16},{80,0},{96,48},{112,32},{1... | collective-permute-start | bytes 393224 | tf_op jit(solution)/shard_map/ppermute | solution.py:23
  109.1 3.1 %collective-permute-start.8 = (bf16[64,1024]{1,0:T(8,128)(2,1)S(1)}, bf16[64,1024]{1,0:T(8,128)(2,1)S(1)}, u32[]{:S(2)}, u32[]{:S(2)}) collective-permute-start(bf16[64,1024]{1,0:T(8,128)(2,1)S(1)} %get-tuple-element.26), channel_id=1, source_target_pairs={{0,64},{32,96},{64,0},{96,32},{1,65},{33,97},{65,1},{97,33},{2,66}... | collective-permute-start | bytes 393224 | tf_op jit(solution)/shard_map/ppermute | solution.py:23
  112.3 1.5 %collective-permute-start.37 = (bf16[64,1024]{1,0:T(8,128)(2,1)S(1)}, bf16[64,1024]{1,0:T(8,128)(2,1)S(1)}, u32[]{:S(2)}, u32[]{:S(2)}) collective-permute-start(bf16[64,1024]{1,0:T(8,128)(2,1)S(1)} %select_convert_fusion), channel_id=1, source_target_pairs={{0,16},{16,0},{32,48},{48,32},{64,80},{80,64},{96,112},{112,96},{1... | collective-permute-start | bytes 393224 | tf_op jit(solution)/shard_map/ppermute | solution.py:23
  113.8 2.6 %collective-permute-done.9 = bf16[64,1024]{1,0:T(8,128)(2,1)S(1)} collective-permute-done((bf16[64,1024]{1,0:T(8,128)(2,1)S(1)}, bf16[64,1024]{1,0:T(8,128)(2,1)S(1)}, u32[]{:S(2)}, u32[]{:S(2)}) %collective-permute-start.9) | collective-permute-done | bytes 131104 | tf_op jit(solution)/shard_map/ppermute | solution.py:23
  116.4 1.6 %collective-permute-done.8 = bf16[64,1024]{1,0:T(8,128)(2,1)S(1)} collective-permute-done((bf16[64,1024]{1,0:T(8,128)(2,1)S(1)}, bf16[64,1024]{1,0:T(8,128)(2,1)S(1)}, u32[]{:S(2)}, u32[]{:S(2)}) %collective-permute-start.8) | collective-permute-done | bytes 131104 | tf_op jit(solution)/shard_map/ppermute | solution.py:23
  117.9 1.5 %collective-permute-done.37 = bf16[64,1024]{1,0:T(8,128)(2,1)S(1)} collective-permute-done((bf16[64,1024]{1,0:T(8,128)(2,1)S(1)}, bf16[64,1024]{1,0:T(8,128)(2,1)S(1)}, u32[]{:S(2)}, u32[]{:S(2)}) %collective-permute-start.37) | collective-permute-done | bytes 131104 | tf_op jit(solution)/shard_map/ppermute | solution.py:23
  (141 shorter events, 14.1 us)
Async XLA Ops:
  1.8 18.5 %all-to-all-start = ((bf16[32,4,1024]{2,1,0:T(4,128)(2,1)}), bf16[32,4,1024]{2,1,0:T(4,128)(2,1)S(1)}, u32[]{:S(2)}, u32[]{:S(2)}) async-start(bf16[32,4,1024]{2,1,0:T(4,128)(2,1)} %all_to_all.6), calls=%async_computation | async-start | bytes 524288 | tf_op jit(solution)/shard_map/all_to_all | solution.py:48
  20.4 8.2 %slice-start.2 = ((s8[6815744]{0:T(1024)(128)(4,1)}), s8[4194304]{0:T(1024)(128)(4,1)S(1)}, s32[]{:S(2)}) async-start(s8[6815744]{0:T(1024)(128)(4,1)} %bitcast.234), calls=%async_computation.3 | async-start | bytes 8388608
  20.5 8.1 %slice-start.3 = ((s8[6815744]{0:T(1024)(128)(4,1)}), s8[2621440]{0:T(1024)(128)(4,1)S(1)}, s32[]{:S(2)}) async-start(s8[6815744]{0:T(1024)(128)(4,1)} %bitcast.234), calls=%async_computation.4 | async-start | bytes 5242880
  20.5 11.4 %collective-permute-start.27 = (bf16[128,1024]{1,0:T(8,128)(2,1)S(1)}, bf16[128,1024]{1,0:T(8,128)(2,1)S(1)}, u32[]{:S(2)}, u32[]{:S(2)}) collective-permute-start(bf16[128,1024]{1,0:T(8,128)(2,1)S(1)} %bitcast_dynamic-update-slice_fusion), channel_id=1, source_target_pairs={{0,96},{32,64},{64,32},{96,0},{1,97},{33,65},{65,33},{97,1},{2,98}... | collective-permute-start | bytes 786440 | tf_op jit(solution)/shard_map/ppermute | solution.py:23
  23.1 11.0 %collective-permute-start.10 = (bf16[128,1024]{1,0:T(8,128)(2,1)S(1)}, bf16[128,1024]{1,0:T(8,128)(2,1)S(1)}, u32[]{:S(2)}, u32[]{:S(2)}) collective-permute-start(bf16[128,1024]{1,0:T(8,128)(2,1)S(1)} %bitcast_dynamic-update-slice_fusion), channel_id=1, source_target_pairs={{0,32},{32,0},{64,96},{96,64},{1,33},{33,1},{65,97},{97,65},{2,34}... | collective-permute-start | bytes 786440 | tf_op jit(solution)/shard_map/ppermute | solution.py:23
  23.1 13.2 %collective-permute-start = (bf16[128,1024]{1,0:T(8,128)(2,1)S(1)}, bf16[128,1024]{1,0:T(8,128)(2,1)S(1)}, u32[]{:S(2)}, u32[]{:S(2)}) collective-permute-start(bf16[128,1024]{1,0:T(8,128)(2,1)S(1)} %bitcast_dynamic-update-slice_fusion), channel_id=1, source_target_pairs={{0,64},{32,96},{64,0},{96,32},{1,65},{33,97},{65,1},{97,33},{2,66}... | collective-permute-start | bytes 786440 | tf_op jit(solution)/shard_map/ppermute | solution.py:23
  24.4 7.5 %slice-start = ((s8[6815744]{0:T(1024)(128)(4,1)}), s8[4194304]{0:T(1024)(128)(4,1)S(1)}, s32[]{:S(2)}) async-start(s8[6815744]{0:T(1024)(128)(4,1)} %bitcast.232), calls=%async_computation.1 | async-start | bytes 8388608
  28.6 3.3 %slice-start.1 = ((s8[6815744]{0:T(1024)(128)(4,1)}), s8[2621440]{0:T(1024)(128)(4,1)S(1)}, s32[]{:S(2)}) async-start(s8[6815744]{0:T(1024)(128)(4,1)} %bitcast.232), calls=%async_computation.2 | async-start | bytes 5242880
  30.1 11.4 %collective-permute-start.20 = (f16[2,64,3328]{2,1,0:T(8,128)(2,1)S(1)}, f16[2,64,3328]{2,1,0:T(8,128)(2,1)S(1)}, u32[]{:S(2)}, u32[]{:S(2)}) collective-permute-start(f16[2,64,3328]{2,1,0:T(8,128)(2,1)S(1)} %pad_maximum_fusion.2), channel_id=1, source_target_pairs={{0,1},{1,0},{2,3},{3,2},{4,5},{5,4},{6,7},{7,6},{8,9},{9,8},{10,11... | collective-permute-start | bytes 2555912 | tf_op jit(solution)/shard_map/ppermute | solution.py:23
  38.8 3.9 %collective-permute-start.28 = (f16[2,64,3328]{2,1,0:T(8,128)(2,1)S(1)}, f16[2,64,3328]{2,1,0:T(8,128)(2,1)S(1)}, u32[]{:S(2)}, u32[]{:S(2)}) collective-permute-start(f16[2,64,3328]{2,1,0:T(8,128)(2,1)S(1)} %pad_maximum_fusion.3), channel_id=1, source_target_pairs={{0,1},{1,0},{2,3},{3,2},{4,5},{5,4},{6,7},{7,6},{8,9},{9,8},{10,11... | collective-permute-start | bytes 2555912 | tf_op jit(solution)/shard_map/ppermute | solution.py:23
  40.2 3.4 %collective-permute-start.11 = (f16[2,64,3328]{2,1,0:T(8,128)(2,1)S(1)}, f16[2,64,3328]{2,1,0:T(8,128)(2,1)S(1)}, u32[]{:S(2)}, u32[]{:S(2)}) collective-permute-start(f16[2,64,3328]{2,1,0:T(8,128)(2,1)S(1)} %pad_maximum_fusion.1), channel_id=1, source_target_pairs={{0,1},{1,0},{2,3},{3,2},{4,5},{5,4},{6,7},{7,6},{8,9},{9,8},{10,11... | collective-permute-start | bytes 2555912 | tf_op jit(solution)/shard_map/ppermute | solution.py:23
  40.7 5.1 %collective-permute-start.1 = (f16[2,64,3328]{2,1,0:T(8,128)(2,1)S(1)}, f16[2,64,3328]{2,1,0:T(8,128)(2,1)S(1)}, u32[]{:S(2)}, u32[]{:S(2)}) collective-permute-start(f16[2,64,3328]{2,1,0:T(8,128)(2,1)S(1)} %pad_maximum_fusion), channel_id=1, source_target_pairs={{0,1},{1,0},{2,3},{3,2},{4,5},{5,4},{6,7},{7,6},{8,9},{9,8},{10,11... | collective-permute-start | bytes 2555912 | tf_op jit(solution)/shard_map/ppermute | solution.py:23
  41.9 8.3 %collective-permute-start.21 = (f16[2,32,3328]{2,1,0:T(8,128)(2,1)S(1)}, f16[2,32,3328]{2,1,0:T(8,128)(2,1)S(1)}, u32[]{:S(2)}, u32[]{:S(2)}) collective-permute-start(f16[2,32,3328]{2,1,0:T(8,128)(2,1)S(1)} %pad_maximum_fusion.8), channel_id=1, source_target_pairs={{0,4},{1,13},{4,0},{5,9},{8,12},{9,5},{12,8},{13,1},{2,6},{3,15},{... | collective-permute-start | bytes 1277960 | tf_op jit(solution)/shard_map/ppermute | solution.py:23
  43.2 14.9 %collective-permute-start.29 = (f16[2,64,1664]{2,1,0:T(8,128)(2,1)S(1)}, f16[2,64,1664]{2,1,0:T(8,128)(2,1)S(1)}, u32[]{:S(2)}, u32[]{:S(2)}) collective-permute-start(f16[2,64,1664]{2,1,0:T(8,128)(2,1)S(1)} %pad_maximum_fusion.10), channel_id=1, source_target_pairs={{0,2},{2,0},{1,3},{3,1},{4,6},{6,4},{5,7},{7,5},{8,10},{10,8},{9,1... | collective-permute-start | bytes 1277960 | tf_op jit(solution)/shard_map/ppermute | solution.py:23
  44.1 14.9 %collective-permute-start.12 = (f16[2,32,3328]{2,1,0:T(8,128)(2,1)S(1)}, f16[2,32,3328]{2,1,0:T(8,128)(2,1)S(1)}, u32[]{:S(2)}, u32[]{:S(2)}) collective-permute-start(f16[2,32,3328]{2,1,0:T(8,128)(2,1)S(1)} %pad_maximum_fusion.6), channel_id=1, source_target_pairs={{0,4},{1,13},{4,0},{5,9},{8,12},{9,5},{12,8},{13,1},{2,6},{3,15},{... | collective-permute-start | bytes 1277960 | tf_op jit(solution)/shard_map/ppermute | solution.py:23
  50.4 7.4 %collective-permute-start.22 = (f16[2,16,3328]{2,1,0:T(8,128)(2,1)S(1)}, f16[2,16,3328]{2,1,0:T(8,128)(2,1)S(1)}, u32[]{:S(2)}, u32[]{:S(2)}) collective-permute-start(f16[2,16,3328]{2,1,0:T(8,128)(2,1)S(1)} %pad_maximum_fusion.18), channel_id=1, source_target_pairs={{0,12},{1,5},{4,8},{5,1},{8,4},{9,13},{12,0},{13,9},{2,14},{3,7},{... | collective-permute-start | bytes 638984 | tf_op jit(solution)/shard_map/ppermute | solution.py:23
  50.6 11.0 %collective-permute-start.2 = (f16[2,32,3328]{2,1,0:T(8,128)(2,1)S(1)}, f16[2,32,3328]{2,1,0:T(8,128)(2,1)S(1)}, u32[]{:S(2)}, u32[]{:S(2)}) collective-permute-start(f16[2,32,3328]{2,1,0:T(8,128)(2,1)S(1)} %pad_maximum_fusion.4), channel_id=1, source_target_pairs={{0,4},{1,13},{4,0},{5,9},{8,12},{9,5},{12,8},{13,1},{2,6},{3,15},{... | collective-permute-start | bytes 1277960 | tf_op jit(solution)/shard_map/ppermute | solution.py:23
  58.0 4.8 %collective-permute-start.23 = (f16[2,16,3328]{2,1,0:T(8,128)(2,1)S(1)}, f16[2,16,3328]{2,1,0:T(8,128)(2,1)S(1)}, u32[]{:S(2)}, u32[]{:S(2)}) collective-permute-start(f16[2,16,3328]{2,1,0:T(8,128)(2,1)S(1)} %pad_maximum_fusion.19), channel_id=1, source_target_pairs={{0,2},{2,0},{1,3},{3,1},{4,6},{6,4},{5,7},{7,5},{8,10},{10,8},{9,1... | collective-permute-start | bytes 638984 | tf_op jit(solution)/shard_map/ppermute | solution.py:23
  58.4 6.5 %collective-permute-start.30 = (f16[2,32,1664]{2,1,0:T(8,128)(2,1)S(1)}, f16[2,32,1664]{2,1,0:T(8,128)(2,1)S(1)}, u32[]{:S(2)}, u32[]{:S(2)}) collective-permute-start(f16[2,32,1664]{2,1,0:T(8,128)(2,1)S(1)} %pad_maximum_fusion.21), channel_id=1, source_target_pairs={{0,4},{1,13},{4,0},{5,9},{8,12},{9,5},{12,8},{13,1},{2,6},{3,15},{... | collective-permute-start | bytes 638984 | tf_op jit(solution)/shard_map/ppermute | solution.py:23
  59.2 5.9 %collective-permute-start.13 = (f16[2,16,3328]{2,1,0:T(8,128)(2,1)S(1)}, f16[2,16,3328]{2,1,0:T(8,128)(2,1)S(1)}, u32[]{:S(2)}, u32[]{:S(2)}) collective-permute-start(f16[2,16,3328]{2,1,0:T(8,128)(2,1)S(1)} %pad_maximum_fusion.15), channel_id=1, source_target_pairs={{0,12},{1,5},{4,8},{5,1},{8,4},{9,13},{12,0},{13,9},{2,14},{3,7},{... | collective-permute-start | bytes 638984 | tf_op jit(solution)/shard_map/ppermute | solution.py:23
  61.5 36.7 %slice-start.4 = ((s8[6815744]{0:T(1024)(128)(4,1)}), s8[4194304]{0:T(1024)(128)(4,1)S(1)}, s32[]{:S(2)}) async-start(s8[6815744]{0:T(1024)(128)(4,1)} %bitcast.236), calls=%async_computation.5 | async-start | bytes 8388608
  61.8 7.1 %collective-permute-start.3 = (f16[2,16,3328]{2,1,0:T(8,128)(2,1)S(1)}, f16[2,16,3328]{2,1,0:T(8,128)(2,1)S(1)}, u32[]{:S(2)}, u32[]{:S(2)}) collective-permute-start(f16[2,16,3328]{2,1,0:T(8,128)(2,1)S(1)} %pad_maximum_fusion.12), channel_id=1, source_target_pairs={{0,12},{1,5},{4,8},{5,1},{8,4},{9,13},{12,0},{13,9},{2,14},{3,7},{... | collective-permute-start | bytes 638984 | tf_op jit(solution)/shard_map/ppermute | solution.py:23
  62.9 7.1 %collective-permute-start.24 = (bf16[16,3328]{1,0:T(8,128)(2,1)S(1)}, bf16[16,3328]{1,0:T(8,128)(2,1)S(1)}, u32[]{:S(2)}, u32[]{:S(2)}) collective-permute-start(bf16[16,3328]{1,0:T(8,128)(2,1)S(1)} %fusion.54), channel_id=1, source_target_pairs={{0,12},{1,5},{4,8},{5,1},{8,4},{9,13},{12,0},{13,9},{2,14},{3,7},{... | collective-permute-start | bytes 319496 | tf_op jit(solution)/shard_map/ppermute | solution.py:23
  65.0 6.1 %collective-permute-start.31 = (f16[2,16,1664]{2,1,0:T(8,128)(2,1)S(1)}, f16[2,16,1664]{2,1,0:T(8,128)(2,1)S(1)}, u32[]{:S(2)}, u32[]{:S(2)}) collective-permute-start(f16[2,16,1664]{2,1,0:T(8,128)(2,1)S(1)} %pad_maximum_fusion.24), channel_id=1, source_target_pairs={{0,12},{1,5},{4,8},{5,1},{8,4},{9,13},{12,0},{13,9},{2,14},{3,7},{... | collective-permute-start | bytes 319496 | tf_op jit(solution)/shard_map/ppermute | solution.py:23
  65.3 11.3 %collective-permute-start.14 = (f16[2,16,3328]{2,1,0:T(8,128)(2,1)S(1)}, f16[2,16,3328]{2,1,0:T(8,128)(2,1)S(1)}, u32[]{:S(2)}, u32[]{:S(2)}) collective-permute-start(f16[2,16,3328]{2,1,0:T(8,128)(2,1)S(1)} %pad_maximum_fusion.16), channel_id=1, source_target_pairs={{0,2},{2,0},{1,3},{3,1},{4,6},{6,4},{5,7},{7,5},{8,10},{10,8},{9,1... | collective-permute-start | bytes 638984 | tf_op jit(solution)/shard_map/ppermute | solution.py:23
  69.0 29.3 %slice-start.5 = ((s8[6815744]{0:T(1024)(128)(4,1)}), s8[2621440]{0:T(1024)(128)(4,1)S(1)}, s32[]{:S(2)}) async-start(s8[6815744]{0:T(1024)(128)(4,1)} %bitcast.236), calls=%async_computation.6 | async-start | bytes 5242880
  69.1 8.3 %collective-permute-start.4 = (f16[2,16,3328]{2,1,0:T(8,128)(2,1)S(1)}, f16[2,16,3328]{2,1,0:T(8,128)(2,1)S(1)}, u32[]{:S(2)}, u32[]{:S(2)}) collective-permute-start(f16[2,16,3328]{2,1,0:T(8,128)(2,1)S(1)} %pad_maximum_fusion.13), channel_id=1, source_target_pairs={{0,2},{2,0},{1,3},{3,1},{4,6},{6,4},{5,7},{7,5},{8,10},{10,8},{9,1... | collective-permute-start | bytes 638984 | tf_op jit(solution)/shard_map/ppermute | solution.py:23
  71.2 4.3 %collective-permute-start.32 = (bf16[16,1664]{1,0:T(8,128)(2,1)S(1)}, bf16[16,1664]{1,0:T(8,128)(2,1)S(1)}, u32[]{:S(2)}, u32[]{:S(2)}) collective-permute-start(bf16[16,1664]{1,0:T(8,128)(2,1)S(1)} %fusion.74), channel_id=1, source_target_pairs={{0,2},{2,0},{1,3},{3,1},{4,6},{6,4},{5,7},{7,5},{8,10},{10,8},{9,1... | collective-permute-start | bytes 159752 | tf_op jit(solution)/shard_map/ppermute | solution.py:23
  72.2 11.1 %collective-permute-start.25 = (bf16[32,3328]{1,0:T(8,128)(2,1)S(1)}, bf16[32,3328]{1,0:T(8,128)(2,1)S(1)}, u32[]{:S(2)}, u32[]{:S(2)}) collective-permute-start(bf16[32,3328]{1,0:T(8,128)(2,1)S(1)} %pad_maximum_fusion.20), channel_id=1, source_target_pairs={{0,4},{1,13},{4,0},{5,9},{8,12},{9,5},{12,8},{13,1},{2,6},{3,15},{... | collective-permute-start | bytes 638984 | tf_op jit(solution)/shard_map/ppermute | solution.py:23
  75.6 3.9 %collective-permute-start.33 = (bf16[16,3328]{1,0:T(8,128)(2,1)S(1)}, bf16[16,3328]{1,0:T(8,128)(2,1)S(1)}, u32[]{:S(2)}, u32[]{:S(2)}) collective-permute-start(bf16[16,3328]{1,0:T(8,128)(2,1)S(1)} %pad_maximum_fusion.25), channel_id=1, source_target_pairs={{0,12},{1,5},{4,8},{5,1},{8,4},{9,13},{12,0},{13,9},{2,14},{3,7},{... | collective-permute-start | bytes 319496 | tf_op jit(solution)/shard_map/ppermute | solution.py:23
  76.8 10.8 %collective-permute-start.15 = (bf16[16,3328]{1,0:T(8,128)(2,1)S(1)}, bf16[16,3328]{1,0:T(8,128)(2,1)S(1)}, u32[]{:S(2)}, u32[]{:S(2)}) collective-permute-start(bf16[16,3328]{1,0:T(8,128)(2,1)S(1)} %fusion.56), channel_id=1, source_target_pairs={{0,12},{1,5},{4,8},{5,1},{8,4},{9,13},{12,0},{13,9},{2,14},{3,7},{... | collective-permute-start | bytes 319496 | tf_op jit(solution)/shard_map/ppermute | solution.py:23
  77.5 12.1 %collective-permute-start.5 = (bf16[16,3328]{1,0:T(8,128)(2,1)S(1)}, bf16[16,3328]{1,0:T(8,128)(2,1)S(1)}, u32[]{:S(2)}, u32[]{:S(2)}) collective-permute-start(bf16[16,3328]{1,0:T(8,128)(2,1)S(1)} %fusion.58), channel_id=1, source_target_pairs={{0,12},{1,5},{4,8},{5,1},{8,4},{9,13},{12,0},{13,9},{2,14},{3,7},{... | collective-permute-start | bytes 319496 | tf_op jit(solution)/shard_map/ppermute | solution.py:23
  79.5 11.0 %collective-permute-start.34 = (bf16[32,3328]{1,0:T(8,128)(2,1)S(1)}, bf16[32,3328]{1,0:T(8,128)(2,1)S(1)}, u32[]{:S(2)}, u32[]{:S(2)}) collective-permute-start(bf16[32,3328]{1,0:T(8,128)(2,1)S(1)} %pad_maximum_fusion.22), channel_id=1, source_target_pairs={{0,4},{1,13},{4,0},{5,9},{8,12},{9,5},{12,8},{13,1},{2,6},{3,15},{... | collective-permute-start | bytes 638984 | tf_op jit(solution)/shard_map/ppermute | solution.py:23
  83.3 14.9 %collective-permute-start.26 = (bf16[64,3328]{1,0:T(8,128)(2,1)S(1)}, bf16[64,3328]{1,0:T(8,128)(2,1)S(1)}, u32[]{:S(2)}, u32[]{:S(2)}) collective-permute-start(bf16[64,3328]{1,0:T(8,128)(2,1)S(1)} %pad_maximum_fusion.9), channel_id=1, source_target_pairs={{0,1},{1,0},{2,3},{3,2},{4,5},{5,4},{6,7},{7,6},{8,9},{9,8},{10,11... | collective-permute-start | bytes 1277960 | tf_op jit(solution)/shard_map/ppermute | solution.py:23
  87.7 6.0 %collective-permute-start.16 = (bf16[32,3328]{1,0:T(8,128)(2,1)S(1)}, bf16[32,3328]{1,0:T(8,128)(2,1)S(1)}, u32[]{:S(2)}, u32[]{:S(2)}) collective-permute-start(bf16[32,3328]{1,0:T(8,128)(2,1)S(1)} %pad_maximum_fusion.17), channel_id=1, source_target_pairs={{0,4},{1,13},{4,0},{5,9},{8,12},{9,5},{12,8},{13,1},{2,6},{3,15},{... | collective-permute-start | bytes 638984 | tf_op jit(solution)/shard_map/ppermute | solution.py:23
  89.6 6.3 %collective-permute-start.6 = (bf16[32,3328]{1,0:T(8,128)(2,1)S(1)}, bf16[32,3328]{1,0:T(8,128)(2,1)S(1)}, u32[]{:S(2)}, u32[]{:S(2)}) collective-permute-start(bf16[32,3328]{1,0:T(8,128)(2,1)S(1)} %pad_maximum_fusion.14), channel_id=1, source_target_pairs={{0,4},{1,13},{4,0},{5,9},{8,12},{9,5},{12,8},{13,1},{2,6},{3,15},{... | collective-permute-start | bytes 638984 | tf_op jit(solution)/shard_map/ppermute | solution.py:23
  90.5 8.8 %collective-permute-start.35 = (bf16[64,3328]{1,0:T(8,128)(2,1)S(1)}, bf16[64,3328]{1,0:T(8,128)(2,1)S(1)}, u32[]{:S(2)}, u32[]{:S(2)}) collective-permute-start(bf16[64,3328]{1,0:T(8,128)(2,1)S(1)} %pad_maximum_fusion.11), channel_id=1, source_target_pairs={{0,1},{1,0},{2,3},{3,2},{4,5},{5,4},{6,7},{7,6},{8,9},{9,8},{10,11... | collective-permute-start | bytes 1277960 | tf_op jit(solution)/shard_map/ppermute | solution.py:23
  93.7 9.3 %collective-permute-start.17 = (bf16[64,3328]{1,0:T(8,128)(2,1)S(1)}, bf16[64,3328]{1,0:T(8,128)(2,1)S(1)}, u32[]{:S(2)}, u32[]{:S(2)}) collective-permute-start(bf16[64,3328]{1,0:T(8,128)(2,1)S(1)} %pad_maximum_fusion.7), channel_id=1, source_target_pairs={{0,1},{1,0},{2,3},{3,2},{4,5},{5,4},{6,7},{7,6},{8,9},{9,8},{10,11... | collective-permute-start | bytes 1277960 | tf_op jit(solution)/shard_map/ppermute | solution.py:23
  96.0 10.8 %collective-permute-start.7 = (bf16[64,3328]{1,0:T(8,128)(2,1)S(1)}, bf16[64,3328]{1,0:T(8,128)(2,1)S(1)}, u32[]{:S(2)}, u32[]{:S(2)}) collective-permute-start(bf16[64,3328]{1,0:T(8,128)(2,1)S(1)} %pad_maximum_fusion.5), channel_id=1, source_target_pairs={{0,1},{1,0},{2,3},{3,2},{4,5},{5,4},{6,7},{7,6},{8,9},{9,8},{10,11... | collective-permute-start | bytes 1277960 | tf_op jit(solution)/shard_map/ppermute | solution.py:23
  100.4 11.8 %collective-permute-start.36 = (bf16[128,1024]{1,0:T(8,128)(2,1)S(1)}, bf16[128,1024]{1,0:T(8,128)(2,1)S(1)}, u32[]{:S(2)}, u32[]{:S(2)}) collective-permute-start(bf16[128,1024]{1,0:T(8,128)(2,1)S(1)} %convolution_convert_fusion), channel_id=1, source_target_pairs={{0,96},{32,64},{64,32},{96,0},{1,97},{33,65},{65,33},{97,1},{2,98}... | collective-permute-start | bytes 786440 | tf_op jit(solution)/shard_map/ppermute | solution.py:23
  104.0 9.8 %collective-permute-start.19 = (bf16[64,1024]{1,0:T(8,128)(2,1)S(1)}, bf16[64,1024]{1,0:T(8,128)(2,1)S(1)}, u32[]{:S(2)}, u32[]{:S(2)}) collective-permute-start(bf16[64,1024]{1,0:T(8,128)(2,1)S(1)} %get-tuple-element.32), channel_id=1, source_target_pairs={{0,48},{16,32},{32,16},{48,0},{64,112},{80,96},{96,80},{112,64},{1... | collective-permute-start | bytes 393224 | tf_op jit(solution)/shard_map/ppermute | solution.py:23
  104.1 9.7 %collective-permute-start.18 = (bf16[64,1024]{1,0:T(8,128)(2,1)S(1)}, bf16[64,1024]{1,0:T(8,128)(2,1)S(1)}, u32[]{:S(2)}, u32[]{:S(2)}) collective-permute-start(bf16[64,1024]{1,0:T(8,128)(2,1)S(1)} %get-tuple-element.31), channel_id=1, source_target_pairs={{0,32},{32,0},{64,96},{96,64},{1,33},{33,1},{65,97},{97,65},{2,34}... | collective-permute-start | bytes 393224 | tf_op jit(solution)/shard_map/ppermute | solution.py:23
  107.9 8.5 %collective-permute-start.9 = (bf16[64,1024]{1,0:T(8,128)(2,1)S(1)}, bf16[64,1024]{1,0:T(8,128)(2,1)S(1)}, u32[]{:S(2)}, u32[]{:S(2)}) collective-permute-start(bf16[64,1024]{1,0:T(8,128)(2,1)S(1)} %get-tuple-element.27), channel_id=1, source_target_pairs={{0,80},{16,64},{32,112},{48,96},{64,16},{80,0},{96,48},{112,32},{1... | collective-permute-start | bytes 393224 | tf_op jit(solution)/shard_map/ppermute | solution.py:23
  109.1 8.9 %collective-permute-start.8 = (bf16[64,1024]{1,0:T(8,128)(2,1)S(1)}, bf16[64,1024]{1,0:T(8,128)(2,1)S(1)}, u32[]{:S(2)}, u32[]{:S(2)}) collective-permute-start(bf16[64,1024]{1,0:T(8,128)(2,1)S(1)} %get-tuple-element.26), channel_id=1, source_target_pairs={{0,64},{32,96},{64,0},{96,32},{1,65},{33,97},{65,1},{97,33},{2,66}... | collective-permute-start | bytes 393224 | tf_op jit(solution)/shard_map/ppermute | solution.py:23
  112.3 7.2 %collective-permute-start.37 = (bf16[64,1024]{1,0:T(8,128)(2,1)S(1)}, bf16[64,1024]{1,0:T(8,128)(2,1)S(1)}, u32[]{:S(2)}, u32[]{:S(2)}) collective-permute-start(bf16[64,1024]{1,0:T(8,128)(2,1)S(1)} %select_convert_fusion), channel_id=1, source_target_pairs={{0,16},{16,0},{32,48},{48,32},{64,80},{80,64},{96,112},{112,96},{1... | collective-permute-start | bytes 393224 | tf_op jit(solution)/shard_map/ppermute | solution.py:23
